TPU v7x, 256 devices: a whole 4x4x8 slice. The times are simulated.
256 devices in a mesh: tm: 32 (over y, x, z_lo), cam: 8 (over z_hi, core).
Axes of the slice: x: 4, y: 4, z: 8 (z_hi: 4, z_lo: 2; z = z_hi * 2 + z_lo), core: 2. Of those that a mesh axis runs over, the one named last changes fastest.
Arguments:
- tokens: bfloat16 [32, 8, 128, 1024], P('tm', 'cam'), may hold values from -6 to 6
- gain: float32 [1024], replicated, may hold values from 0.1 to 1.9
- w_qkv: bfloat16 [1024, 3072], replicated
- w_out: bfloat16 [1024, 1024], replicated, may hold values from -4.5 to 4.5
- window: int32 [8], replicated, may hold values from 1 to 8, as said below
- valid: int32 [32], P('tm'), may hold values 0 or 1
- cotangent: bfloat16 [32, 8, 128, 1024], P('tm', 'cam'), may hold values from -3 to 3
Outputs:
- mixed: bfloat16 [32, 8, 128, 1024], P('tm', 'cam')
- d_tokens: bfloat16 [32, 8, 128, 1024], P('tm', 'cam')
Inputs may be any that keep to these rules, and one draw needn't show every extreme that they name: At least one head has window 8.
All inputs are finite; a program needn't handle non-finite values. No bound on the sum of `valid` on one device may be relied on, other than what follows from the above.
Results may differ from a plain program's by a relative error of at most 0.02.
Values may be sent and summed in bfloat16 or wider, within the bound.
No kernel may reach another device: no remote copies, remote signals or barrier semaphores. Data moves between devices by JAX's collectives and lax.ppermute only.
A program may use at most 128 MiB of HBM per device.

v0:
```python
import jax
import jax.numpy as jnp
from jax import lax
from jax.sharding import PartitionSpec as P

D = 1024
H = 8
DH = 128
HW = 128
WIN = 8
F_DEV = 1


EPS = 1e-05


def shifted(value, axis, steps):
    count = lax.axis_size(axis)
    leading, last = (max(0, -steps), min(count, count - steps))
    return lax.ppermute(value, axis, [(source, source + steps) for source in range(leading, last)])


def relay_window(carried, reach):
    arrived = [
        shifted((carried[0], carried[1], carried[2]), "tm", offset)
        for offset in range(reach, 0, -1)
    ]
    return arrived


def per_device(tokens, gain, w_qkv, w_out, window, valid, cotangent):
    scale = DH ** (-0.5)
    cameras = lax.axis_size("cam")
    reach = WIN // F_DEV
    split = cameras * HW
    inputs = tokens[:, 0].astype(jnp.float32)
    rinv = lax.rsqrt(jnp.mean(inputs * inputs, axis=-1, keepdims=True) + EPS)
    normed = (inputs * rinv * gain).astype(jnp.bfloat16)
    proj = jnp.dot(normed.reshape(-1, D), w_qkv, preferred_element_type=jnp.float32).astype(
        jnp.bfloat16
    )
    proj = proj.reshape(F_DEV, HW, 3, D)
    query = proj[:, :, 0]
    keys = proj[:, :, 1]
    values = proj[:, :, 2]
    near_keys, near_values = (
        lax.all_gather(keys[:, None], "cam", axis=1, tiled=True),
        lax.all_gather(values[:, None], "cam", axis=1, tiled=True),
    )
    arrived = relay_window((keys, values, valid), reach)
    past_keys = jnp.concatenate([piece[0] for piece in arrived] + [keys], axis=0)
    past_values = jnp.concatenate([piece[1] for piece in arrived] + [values], axis=0)
    past_ok = jnp.concatenate([piece[2] for piece in arrived] + [valid], axis=0)
    offsets = jnp.arange(WIN, dtype=jnp.int32)
    head_ok = offsets[None, :] >= (WIN - window)[:, None]

    def frame_inputs(index):
        frame_keys = near_keys[index].reshape(split, H, DH)
        frame_values = near_values[index].reshape(split, H, DH)
        window_keys = past_keys[index : index + WIN].reshape(WIN * HW, H, DH)
        window_values = past_values[index : index + WIN].reshape(WIN * HW, H, DH)
        allowed = jnp.repeat(head_ok & (past_ok[index : index + WIN][None, :] == 1), HW, axis=1)
        return (frame_keys, frame_values, window_keys, window_values, allowed)

    def scores_of(queries, frame_keys, window_keys, allowed):
        near = (
            jnp.einsum("phd,khd->hpk", queries, frame_keys, preferred_element_type=jnp.float32)
            * scale
        )
        past = (
            jnp.einsum("phd,khd->hpk", queries, window_keys, preferred_element_type=jnp.float32)
            * scale
        )
        past = jnp.where(allowed[:, None, :], past, -jnp.inf)
        return jnp.concatenate([near, past], axis=-1)

    index = 0
    frame_keys, frame_values, window_keys, window_values, allowed = frame_inputs(index)
    queries = query[index].reshape(HW, H, DH)
    scores = scores_of(queries, frame_keys, window_keys, allowed)
    peak = jnp.max(scores, axis=-1, keepdims=True)
    expd = jnp.exp(scores - peak)
    total = jnp.sum(expd, axis=-1, keepdims=True)
    weights = (expd / total).astype(jnp.bfloat16)
    result = jnp.einsum(
        "hpk,khd->phd", weights[..., :split], frame_values, preferred_element_type=jnp.float32
    )
    result = result + jnp.einsum(
        "hpk,khd->phd", weights[..., split:], window_values, preferred_element_type=jnp.float32
    )
    attended_list = [result.astype(jnp.bfloat16)]
    peaks = [peak]
    totals = [total]
    attended = jnp.stack(attended_list)
    output = jnp.dot(attended.reshape(-1, D), w_out, preferred_element_type=jnp.float32).reshape(
        F_DEV, HW, D
    )
    mixed = (inputs + output).astype(jnp.bfloat16)
    d_attended = jnp.dot(
        cotangent[:, 0].reshape(-1, D), w_out.T, preferred_element_type=jnp.float32
    )
    d_attended = d_attended.astype(jnp.bfloat16).reshape(F_DEV, HW, H, DH)
    deltas = jnp.sum(d_attended.astype(jnp.float32) * attended.astype(jnp.float32), axis=-1)
    buffer_keys = jnp.zeros(((WIN + F_DEV) * HW, H, DH), jnp.float32)
    buffer_values = jnp.zeros(((WIN + F_DEV) * HW, H, DH), jnp.float32)
    index = 0
    frame_keys, frame_values, window_keys, window_values, allowed = frame_inputs(index)
    queries = query[index].reshape(HW, H, DH)
    scores = scores_of(queries, frame_keys, window_keys, allowed)
    probs = jnp.exp(scores - peaks[index]) / totals[index]
    weights = probs.astype(jnp.bfloat16)
    grads_out = d_attended[index]
    d_probs = jnp.concatenate(
        [
            jnp.einsum("phd,khd->hpk", grads_out, frame_values, preferred_element_type=jnp.float32),
            jnp.einsum(
                "phd,khd->hpk", grads_out, window_values, preferred_element_type=jnp.float32
            ),
        ],
        axis=-1,
    )
    d_scores = (probs * (d_probs - deltas[index].T[:, :, None]) * scale).astype(jnp.bfloat16)
    d_query = jnp.einsum(
        "hpk,khd->phd", d_scores[..., :split], frame_keys, preferred_element_type=jnp.float32
    )
    d_query = d_query + jnp.einsum(
        "hpk,khd->phd", d_scores[..., split:], window_keys, preferred_element_type=jnp.float32
    )
    query_grads = [d_query]
    near_key_grads = [
        jnp.einsum(
            "hpk,phd->khd", d_scores[..., :split], queries, preferred_element_type=jnp.float32
        )
    ]
    near_value_grads = [
        jnp.einsum(
            "hpk,phd->khd", weights[..., :split], grads_out, preferred_element_type=jnp.float32
        )
    ]
    buffer_keys = buffer_keys.at[index * HW : (index + WIN) * HW].add(
        jnp.einsum(
            "hpk,phd->khd", d_scores[..., split:], queries, preferred_element_type=jnp.float32
        )
    )
    buffer_values = buffer_values.at[index * HW : (index + WIN) * HW].add(
        jnp.einsum(
            "hpk,phd->khd", weights[..., split:], grads_out, preferred_element_type=jnp.float32
        )
    )
    near_key_terms = jnp.stack(near_key_grads).reshape(F_DEV, cameras, HW, D)
    near_value_terms = jnp.stack(near_value_grads).reshape(F_DEV, cameras, HW, D)
    summed_keys, summed_values = (
        lax.psum_scatter(
            near_key_terms.astype(jnp.bfloat16), "cam", scatter_dimension=1, tiled=True
        ).astype(jnp.float32),
        lax.psum_scatter(
            near_value_terms.astype(jnp.bfloat16), "cam", scatter_dimension=1, tiled=True
        ).astype(jnp.float32),
    )
    rounded_keys = buffer_keys.astype(jnp.bfloat16).reshape(reach + 1, F_DEV, HW, D)
    rounded_values = buffer_values.astype(jnp.bfloat16).reshape(reach + 1, F_DEV, HW, D)
    d_keys = summed_keys[:, 0] + rounded_keys[reach].astype(jnp.float32)
    d_values = summed_values[:, 0] + rounded_values[reach].astype(jnp.float32)
    for offset in range(1, reach + 1):
        back_keys, back_values = shifted(
            (rounded_keys[reach - offset], rounded_values[reach - offset]), "tm", -offset
        )
        d_keys = d_keys + back_keys.astype(jnp.float32)
        d_values = d_values + back_values.astype(jnp.float32)
    d_query_all = jnp.stack(query_grads).reshape(F_DEV, HW, D)
    grads = (
        jnp.stack([d_query_all, d_keys, d_values], axis=2).reshape(-1, 3 * D).astype(jnp.bfloat16)
    )
    d_normed = jnp.dot(grads, w_qkv.T, preferred_element_type=jnp.float32).reshape(F_DEV, HW, D)
    scaled = d_normed * gain
    d_inputs = rinv * scaled - inputs * rinv**3 * jnp.mean(scaled * inputs, axis=-1, keepdims=True)
    d_tokens = (cotangent[:, 0].astype(jnp.float32) + d_inputs).astype(jnp.bfloat16)
    return (mixed[:, None], d_tokens[:, None])


def solution(mesh):
    return jax.shard_map(
        per_device,
        mesh=mesh,
        in_specs=(
            P("tm", "cam", None, None),
            P(),
            P(),
            P(),
            P(),
            P("tm"),
            P("tm", "cam", None, None),
        ),
        out_specs=(P("tm", "cam", None, None), P("tm", "cam", None, None)),
        check_vma=False,
    )
```

profile of v0, /device:TPU:16, one launch (start us, length us, event | category | flops | bytes accessed | tf_op | source)
XLA Modules:
  0.0 356.4 jit_solution(2371343320844540109)
XLA Ops:
  8.5 4.0 %convolution_convert_fusion = bf16[128,3072]{1,0:T(8,128)(2,1)S(1)} fusion(bf16[1024,3072]{1,0:T(8,128)(2,1)} %param.13, bf16[1,1,128,1024]{3,2,1,0:T(8,128)(2,1)} %param.11, f32[1024]{0:T(1024)} %param.12, f32[128]{0:T(128)S(1)} %get-tuple-element.46), kind=kOutput, calls=%fused_computation.9 | convolution fusion | flops 806223872 | bytes 7344640 | tf_op jit(solution)/shard_map/dot_general | solution.py:39
  19.8 6.0 %collective-permute-start.17 = (bf16[1,128,1024]{2,1,0:T(8,128)(2,1)}, bf16[1,128,1024]{2,1,0:T(8,128)(2,1)}, u32[]{:S(2)}, u32[]{:S(2)}) collective-permute-start(bf16[1,128,1024]{2,1,0:T(8,128)(2,1)} %bitcast.5), channel_id=1, source_target_pairs={{0,56},{8,64},{16,72},{24,80},{32,88},{40,96},{48,104},{56,112},{6... | collective-permute-start | bytes 786440 | tf_op jit(solution)/shard_map/ppermute | solution.py:20
  32.7 9.7 %collective-permute-done = s32[1]{0:T(128)} collective-permute-done((s32[1]{0:T(128)}, s32[1]{0:T(128)}, u32[]{:S(2)}, u32[]{:S(2)}) %collective-permute-start) | collective-permute-done | bytes 36 | tf_op jit(solution)/shard_map/ppermute | solution.py:20
  44.4 6.8 %collective-permute-done.1 = s32[1]{0:T(128)} collective-permute-done((s32[1]{0:T(128)}, s32[1]{0:T(128)}, u32[]{:S(2)}, u32[]{:S(2)}) %collective-permute-start.1) | collective-permute-done | bytes 36 | tf_op jit(solution)/shard_map/ppermute | solution.py:20
  57.6 5.1 %collective-permute-start.3 = (s32[1]{0:T(128)}, s32[1]{0:T(128)}, u32[]{:S(2)}, u32[]{:S(2)}) collective-permute-start(s32[1]{0:T(128)} %param.16), channel_id=1, source_target_pairs={{0,40},{8,48},{16,56},{24,64},{32,72},{40,80},{48,88},{56,96},{64,... | collective-permute-start | bytes 20 | tf_op jit(solution)/shard_map/ppermute | solution.py:20
  68.7 4.3 %collective-permute-done.4 = s32[1]{0:T(128)} collective-permute-done((s32[1]{0:T(128)}, s32[1]{0:T(128)}, u32[]{:S(2)}, u32[]{:S(2)}) %collective-permute-start.4) | collective-permute-done | bytes 36 | tf_op jit(solution)/shard_map/ppermute | solution.py:20
  73.0 5.1 %collective-permute-start.5 = (s32[1]{0:T(128)}, s32[1]{0:T(128)}, u32[]{:S(2)}, u32[]{:S(2)}) collective-permute-start(s32[1]{0:T(128)} %param.16), channel_id=1, source_target_pairs={{0,24},{8,32},{16,40},{24,48},{32,56},{40,64},{48,72},{56,80},{64,... | collective-permute-start | bytes 20 | tf_op jit(solution)/shard_map/ppermute | solution.py:20
  78.1 4.1 %collective-permute-done.5 = s32[1]{0:T(128)} collective-permute-done((s32[1]{0:T(128)}, s32[1]{0:T(128)}, u32[]{:S(2)}, u32[]{:S(2)}) %collective-permute-start.5) | collective-permute-done | bytes 36 | tf_op jit(solution)/shard_map/ppermute | solution.py:20
  89.8 5.8 %collective-permute-start.7 = (s32[1]{0:T(128)}, s32[1]{0:T(128)}, u32[]{:S(2)}, u32[]{:S(2)}) collective-permute-start(s32[1]{0:T(128)} %param.16), channel_id=1, source_target_pairs={{0,8},{8,16},{16,24},{24,32},{32,40},{40,48},{48,56},{56,64},{64,7... | collective-permute-start | bytes 20 | tf_op jit(solution)/shard_map/ppermute | solution.py:20
  100.4 5.1 %concatenate.23 = s32[8]{0:T(128)S(1)} concatenate(s32[1]{0:T(128)} %collective-permute-done, s32[1]{0:T(128)} %collective-permute-done.1, s32[1]{0:T(128)} %collective-permute-done.2, s32[1]{0:T(128)} %collective-permute-done.3, s32[1]{0:T(128)} %collective-permute-done.4, s32[1]{0:T(128)} %collective-permute-done.5, s32[1]{0:T(128)} %collective-permute-done.6, ...), dimensions={0} | concatenate | bytes 64 | tf_op jit(solution)/shard_map/concatenate | solution.py:53
  108.8 5.1 %collective-permute-start.12 = (bf16[1,128,1024]{2,1,0:T(8,128)(2,1)S(1)}, bf16[1,128,1024]{2,1,0:T(8,128)(2,1)S(1)}, u32[]{:S(2)}, u32[]{:S(2)}) collective-permute-start(bf16[1,128,1024]{2,1,0:T(8,128)(2,1)S(1)} %bitcast.160), channel_id=1, source_target_pairs={{0,32},{8,40},{16,48},{24,56},{32,64},{40,72},{48,80},{56,88},{64,... | collective-permute-start | bytes 786440 | tf_op jit(solution)/shard_map/ppermute | solution.py:20
  119.6 7.7 %collective-permute-start.14 = (bf16[1,128,1024]{2,1,0:T(8,128)(2,1)S(1)}, bf16[1,128,1024]{2,1,0:T(8,128)(2,1)S(1)}, u32[]{:S(2)}, u32[]{:S(2)}) collective-permute-start(bf16[1,128,1024]{2,1,0:T(8,128)(2,1)S(1)} %bitcast.162), channel_id=1, source_target_pairs={{0,16},{8,24},{16,32},{24,40},{32,48},{40,56},{48,64},{56,72},{64,... | collective-permute-start | bytes 786440 | tf_op jit(solution)/shard_map/ppermute | solution.py:20
  130.9 6.2 %collective-permute-start.18 = (bf16[1,128,1024]{2,1,0:T(8,128)(2,1)}, bf16[1,128,1024]{2,1,0:T(8,128)(2,1)S(1)}, u32[]{:S(2)}, u32[]{:S(2)}) collective-permute-start(bf16[1,128,1024]{2,1,0:T(8,128)(2,1)} %bitcast.5), channel_id=1, source_target_pairs={{0,48},{8,56},{16,64},{24,72},{32,80},{40,88},{48,96},{56,104},{64... | collective-permute-start | bytes 786440 | tf_op jit(solution)/shard_map/ppermute | solution.py:20
  137.1 6.8 %collective-permute-start.19 = (bf16[1,128,1024]{2,1,0:T(8,128)(2,1)}, bf16[1,128,1024]{2,1,0:T(8,128)(2,1)}, u32[]{:S(2)}, u32[]{:S(2)}) collective-permute-start(bf16[1,128,1024]{2,1,0:T(8,128)(2,1)} %bitcast.5), channel_id=1, source_target_pairs={{0,40},{8,48},{16,56},{24,64},{32,72},{40,80},{48,88},{56,96},{64,... | collective-permute-start | bytes 786440 | tf_op jit(solution)/shard_map/ppermute | solution.py:20
  147.9 4.1 %copy.58 = bf16[1024,8,128]{0,2,1:T(8,128)(2,1)} copy(bf16[1024,8,128]{2,1,0:T(8,128)(2,1)} %bitcast.134) | data formatting | bytes 4194304 | tf_op jit(solution)/shard_map/reshape | solution.py:60
  152.0 4.5 %fusion.72 = (f32[8,128]{1,0:T(8,128)S(1)}, f32[8,128,1024]{2,1,0:T(8,128)}) fusion(bf16[128,8,128]{0,2,1:T(8,128)(2,1)S(1)} %bitcast.146, bf16[1024,8,128]{0,2,1:T(8,128)(2,1)} %copy.58, pred[8,1024]{1,0:T(8,128)(4,1)S(1)} %broadcast_bitcast_fusion), kind=kOutput, calls=%fused_computation.104 | convolution fusion | flops 271580160 | bytes 6565888 | tf_op jit(solution)/shard_map/phd,khd->hpk/dot_general | solution.py:71
  160.1 4.2 %copy.57 = bf16[1024,8,128]{0,2,1:T(8,128)(2,1)} copy(bf16[1024,8,128]{2,1,0:T(8,128)(2,1)} %bitcast.135) | data formatting | bytes 4194304 | tf_op jit(solution)/shard_map/reshape;squeeze | solution.py:58
  175.0 11.4 %collective-permute-start.21 = (bf16[1,128,1024]{2,1,0:T(8,128)(2,1)}, bf16[1,128,1024]{2,1,0:T(8,128)(2,1)S(1)}, u32[]{:S(2)}, u32[]{:S(2)}) collective-permute-start(bf16[1,128,1024]{2,1,0:T(8,128)(2,1)} %bitcast.5), channel_id=1, source_target_pairs={{0,24},{8,32},{16,40},{24,48},{32,56},{40,64},{48,72},{56,80},{64,... | collective-permute-start | bytes 786440 | tf_op jit(solution)/shard_map/ppermute | solution.py:20
  190.3 4.2 %collective-permute-start.23 = (bf16[1,128,1024]{2,1,0:T(8,128)(2,1)}, bf16[1,128,1024]{2,1,0:T(8,128)(2,1)S(1)}, u32[]{:S(2)}, u32[]{:S(2)}) collective-permute-start(bf16[1,128,1024]{2,1,0:T(8,128)(2,1)} %bitcast.5), channel_id=1, source_target_pairs={{0,8},{8,16},{16,24},{24,32},{32,40},{40,48},{48,56},{56,64},{64,7... | collective-permute-start | bytes 786440 | tf_op jit(solution)/shard_map/ppermute | solution.py:20
  198.0 8.6 %collective-permute-done.23 = bf16[1,128,1024]{2,1,0:T(8,128)(2,1)S(1)} collective-permute-done((bf16[1,128,1024]{2,1,0:T(8,128)(2,1)}, bf16[1,128,1024]{2,1,0:T(8,128)(2,1)S(1)}, u32[]{:S(2)}, u32[]{:S(2)}) %collective-permute-start.23) | collective-permute-done | bytes 262176 | tf_op jit(solution)/shard_map/ppermute | solution.py:20
  208.5 4.1 %copy.68 = bf16[1024,8,128]{0,2,1:T(8,128)(2,1)} copy(bf16[1024,8,128]{2,1,0:T(8,128)(2,1)} %bitcast.137) | data formatting | bytes 4194304 | tf_op jit(solution)/shard_map/reshape | solution.py:61
  212.7 4.4 %fusion.74 = f32[8,128,1024]{2,1,0:T(8,128)} fusion(bf16[128,8,128]{0,2,1:T(8,128)(2,1)S(1)} %bitcast.143, bf16[1024,8,128]{0,2,1:T(8,128)(2,1)} %copy.68), kind=kOutput, calls=%fused_computation.106 | convolution fusion | flops 268435456 | bytes 6553600 | tf_op jit(solution)/shard_map/phd,khd->hpk/dot_general | solution.py:116
  220.6 4.2 %copy.67 = bf16[1024,8,128]{0,2,1:T(8,128)(2,1)} copy(bf16[1024,8,128]{2,1,0:T(8,128)(2,1)} %bitcast.138) | data formatting | bytes 4194304 | tf_op jit(solution)/shard_map/reshape;squeeze | solution.py:59
  231.7 4.5 %fusion.73 = f32[8,128,1024]{2,1,0:T(8,128)} fusion(bf16[128,8,128]{0,2,1:T(8,128)(2,1)S(1)} %bitcast.144, bf16[1024,8,128]{0,2,1:T(8,128)(2,1)} %copy.67), kind=kOutput, calls=%fused_computation.105 | convolution fusion | flops 268435456 | bytes 6553600 | tf_op jit(solution)/shard_map/phd,khd->hpk/dot_general | solution.py:115
  236.3 4.5 %fusion.3 = bf16[8,128,2048]{2,1,0:T(8,128)(2,1)S(1)} fusion(f32[8,128,1024]{2,1,0:T(8,128)S(1)} %copy-done.9, f32[8,128,1024]{2,1,0:T(8,128)} %fusion.73, f32[8,128]{1,0:T(8,128)S(1)} %bitcast.177, f32[8,128]{1,0:T(8,128)S(1)} %fusion.5, f32[8,128]{1,0:T(8,128)S(1)} %reduce_max.22, f32[8,128,1024]{2,1,0:T(8,128)S(1)} %copy-done.2, ...), kind=kLoop, calls=%fused_computation.5 | loop fusion | flops 16777216 | bytes 20983808 | tf_op jit(solution)/shard_map/convert_element_type | solution.py:122
  252.8 3.9 %collective-permute-start.37 = (bf16[1,128,1024]{1,2,0:T(8,128)(2,1)S(1)}, bf16[1,128,1024]{1,2,0:T(8,128)(2,1)S(1)}, u32[]{:S(2)}, u32[]{:S(2)}) collective-permute-start(bf16[1,128,1024]{1,2,0:T(8,128)(2,1)S(1)} %bitcast.172), channel_id=1, source_target_pairs={{48,0},{56,8},{64,16},{72,24},{80,32},{88,40},{96,48},{104,56},{11... | collective-permute-start | bytes 786440 | tf_op jit(solution)/shard_map/ppermute | solution.py:20
  268.6 10.8 %collective-permute-start.33 = (bf16[1,128,1024]{1,2,0:T(8,128)(2,1)S(1)}, bf16[1,128,1024]{1,2,0:T(8,128)(2,1)S(1)}, u32[]{:S(2)}, u32[]{:S(2)}) collective-permute-start(bf16[1,128,1024]{1,2,0:T(8,128)(2,1)S(1)} %bitcast.165), channel_id=1, source_target_pairs={{16,0},{24,8},{32,16},{40,24},{48,32},{56,40},{64,48},{72,56},{80,... | collective-permute-start | bytes 786440 | tf_op jit(solution)/shard_map/ppermute | solution.py:20
  279.4 17.5 %collective-permute-start.32 = (bf16[1,128,1024]{1,2,0:T(8,128)(2,1)S(1)}, bf16[1,128,1024]{1,2,0:T(8,128)(2,1)S(1)}, u32[]{:S(2)}, u32[]{:S(2)}) collective-permute-start(bf16[1,128,1024]{1,2,0:T(8,128)(2,1)S(1)} %bitcast.164), channel_id=1, source_target_pairs={{8,0},{16,8},{24,16},{32,24},{40,32},{48,40},{56,48},{64,56},{72,6... | collective-permute-start | bytes 786440 | tf_op jit(solution)/shard_map/ppermute | solution.py:20
  296.9 3.9 %collective-permute-start.31 = (bf16[1,128,1024]{1,2,0:T(8,128)(2,1)S(1)}, bf16[1,128,1024]{1,2,0:T(8,128)(2,1)S(1)}, u32[]{:S(2)}, u32[]{:S(2)}) collective-permute-start(bf16[1,128,1024]{1,2,0:T(8,128)(2,1)S(1)} %bitcast.169), channel_id=1, source_target_pairs={{64,0},{72,8},{80,16},{88,24},{96,32},{104,40},{112,48},{120,56},{... | collective-permute-start | bytes 786440 | tf_op jit(solution)/shard_map/ppermute | solution.py:20
  311.9 15.4 %collective-permute-start.27 = (bf16[1,128,1024]{1,2,0:T(8,128)(2,1)}, bf16[1,128,1024]{1,2,0:T(8,128)(2,1)}, u32[]{:S(2)}, u32[]{:S(2)}) collective-permute-start(bf16[1,128,1024]{1,2,0:T(8,128)(2,1)} %bitcast.20), channel_id=1, source_target_pairs={{32,0},{40,8},{48,16},{56,24},{64,32},{72,40},{80,48},{88,56},{96,... | collective-permute-start | bytes 786440 | tf_op jit(solution)/shard_map/ppermute | solution.py:20
  329.3 4.0 %collective-permute-start.25 = (bf16[1,128,1024]{1,2,0:T(8,128)(2,1)}, bf16[1,128,1024]{1,2,0:T(8,128)(2,1)}, u32[]{:S(2)}, u32[]{:S(2)}) collective-permute-start(bf16[1,128,1024]{1,2,0:T(8,128)(2,1)} %bitcast.18), channel_id=1, source_target_pairs={{16,0},{24,8},{32,16},{40,24},{48,32},{56,40},{64,48},{72,56},{80,... | collective-permute-start | bytes 786440 | tf_op jit(solution)/shard_map/ppermute | solution.py:20
  343.9 5.1 %fusion.42 = (f32[128]{0:T(128)S(1)}, f32[128,1024]{1,0:T(8,128)S(1)}) fusion(bf16[1,1,128,1024]{3,2,1,0:T(8,128)(2,1)S(1)} %copy-done.10, f32[1024]{0:T(1024)S(1)} %copy-done.24, bf16[128,3072]{0,1:T(8,128)(2,1)S(1)} %bitcast.150, bf16[1024,3072]{1,0:T(8,128)(2,1)} %param.13), kind=kOutput, calls=%fused_computation.49 | convolution fusion | flops 805830528 | bytes 7868928 | tf_op jit(solution)/shard_map/dot_general | solution.py:174
  (179 shorter events, 140.7 us)
Async XLA Ops:
  7.2 149.4 %all-gather.7.cloned.1.call-start = ((), (), s32[]{:S(2)}) async-start(), calls=%async_computation.5 | async-start | bytes 2359296 | tf_op jit(solution)/shard_map/all_gather | solution.py:47
  15.7 201.3 %all-gather.5.cloned.1.call-start = ((), (), s32[]{:S(2)}) async-start(), calls=%async_computation.4 | async-start | bytes 2359296 | tf_op jit(solution)/shard_map/all_gather | solution.py:48
  16.6 158.4 %collective-permute-start.16 = (bf16[1,128,1024]{2,1,0:T(8,128)(2,1)}, bf16[1,128,1024]{2,1,0:T(8,128)(2,1)}, u32[]{:S(2)}, u32[]{:S(2)}) collective-permute-start(bf16[1,128,1024]{2,1,0:T(8,128)(2,1)} %bitcast.5), channel_id=1, source_target_pairs={{0,64},{8,72},{16,80},{24,88},{32,96},{40,104},{48,112},{56,120},{... | collective-permute-start | bytes 786440 | tf_op jit(solution)/shard_map/ppermute | solution.py:20
  19.8 167.6 %collective-permute-start.17 = (bf16[1,128,1024]{2,1,0:T(8,128)(2,1)}, bf16[1,128,1024]{2,1,0:T(8,128)(2,1)}, u32[]{:S(2)}, u32[]{:S(2)}) collective-permute-start(bf16[1,128,1024]{2,1,0:T(8,128)(2,1)} %bitcast.5), channel_id=1, source_target_pairs={{0,56},{8,64},{16,72},{24,80},{32,88},{40,96},{48,104},{56,112},{6... | collective-permute-start | bytes 786440 | tf_op jit(solution)/shard_map/ppermute | solution.py:20
  25.8 79.9 %collective-permute-start.8 = (bf16[1,128,1024]{2,1,0:T(8,128)(2,1)}, bf16[1,128,1024]{2,1,0:T(8,128)(2,1)}, u32[]{:S(2)}, u32[]{:S(2)}) collective-permute-start(bf16[1,128,1024]{2,1,0:T(8,128)(2,1)} %bitcast.156), channel_id=1, source_target_pairs={{0,64},{8,72},{16,80},{24,88},{32,96},{40,104},{48,112},{56,120},{... | collective-permute-start | bytes 786440 | tf_op jit(solution)/shard_map/ppermute | solution.py:20
  27.7 81.1 %collective-permute-start.9 = (bf16[1,128,1024]{2,1,0:T(8,128)(2,1)}, bf16[1,128,1024]{2,1,0:T(8,128)(2,1)}, u32[]{:S(2)}, u32[]{:S(2)}) collective-permute-start(bf16[1,128,1024]{2,1,0:T(8,128)(2,1)} %bitcast.157), channel_id=1, source_target_pairs={{0,56},{8,64},{16,72},{24,80},{32,88},{40,96},{48,104},{56,112},{6... | collective-permute-start | bytes 786440 | tf_op jit(solution)/shard_map/ppermute | solution.py:20
  31.6 303.8 %reduce-scatter.5.cloned.1.call-start = ((), (), s32[]{:S(2)}) async-start(), calls=%async_computation.3 | async-start | bytes 2359296 | tf_op jit(solution)/shard_map/reduce_scatter | solution.py:156
  98.5 16.4 %collective-permute-start.10 = (bf16[1,128,1024]{2,1,0:T(8,128)(2,1)S(1)}, bf16[1,128,1024]{2,1,0:T(8,128)(2,1)S(1)}, u32[]{:S(2)}, u32[]{:S(2)}) collective-permute-start(bf16[1,128,1024]{2,1,0:T(8,128)(2,1)S(1)} %bitcast.158), channel_id=1, source_target_pairs={{0,48},{8,56},{16,64},{24,72},{32,80},{40,88},{48,96},{56,104},{64... | collective-permute-start | bytes 786440 | tf_op jit(solution)/shard_map/ppermute | solution.py:20
  105.7 13.9 %collective-permute-start.11 = (bf16[1,128,1024]{2,1,0:T(8,128)(2,1)S(1)}, bf16[1,128,1024]{2,1,0:T(8,128)(2,1)S(1)}, u32[]{:S(2)}, u32[]{:S(2)}) collective-permute-start(bf16[1,128,1024]{2,1,0:T(8,128)(2,1)S(1)} %bitcast.159), channel_id=1, source_target_pairs={{0,40},{8,48},{16,56},{24,64},{32,72},{40,80},{48,88},{56,96},{64,... | collective-permute-start | bytes 786440 | tf_op jit(solution)/shard_map/ppermute | solution.py:20
  108.8 18.5 %collective-permute-start.12 = (bf16[1,128,1024]{2,1,0:T(8,128)(2,1)S(1)}, bf16[1,128,1024]{2,1,0:T(8,128)(2,1)S(1)}, u32[]{:S(2)}, u32[]{:S(2)}) collective-permute-start(bf16[1,128,1024]{2,1,0:T(8,128)(2,1)S(1)} %bitcast.160), channel_id=1, source_target_pairs={{0,32},{8,40},{16,48},{24,56},{32,64},{40,72},{48,80},{56,88},{64,... | collective-permute-start | bytes 786440 | tf_op jit(solution)/shard_map/ppermute | solution.py:20
  114.9 16.0 %collective-permute-start.13 = (bf16[1,128,1024]{2,1,0:T(8,128)(2,1)S(1)}, bf16[1,128,1024]{2,1,0:T(8,128)(2,1)S(1)}, u32[]{:S(2)}, u32[]{:S(2)}) collective-permute-start(bf16[1,128,1024]{2,1,0:T(8,128)(2,1)S(1)} %bitcast.161), channel_id=1, source_target_pairs={{0,24},{8,32},{16,40},{24,48},{32,56},{40,64},{48,72},{56,80},{64,... | collective-permute-start | bytes 786440 | tf_op jit(solution)/shard_map/ppermute | solution.py:20
  119.6 17.5 %collective-permute-start.14 = (bf16[1,128,1024]{2,1,0:T(8,128)(2,1)S(1)}, bf16[1,128,1024]{2,1,0:T(8,128)(2,1)S(1)}, u32[]{:S(2)}, u32[]{:S(2)}) collective-permute-start(bf16[1,128,1024]{2,1,0:T(8,128)(2,1)S(1)} %bitcast.162), channel_id=1, source_target_pairs={{0,16},{8,24},{16,32},{24,40},{32,48},{40,56},{48,64},{56,72},{64,... | collective-permute-start | bytes 786440 | tf_op jit(solution)/shard_map/ppermute | solution.py:20
  127.4 16.6 %collective-permute-start.15 = (bf16[1,128,1024]{2,1,0:T(8,128)(2,1)S(1)}, bf16[1,128,1024]{2,1,0:T(8,128)(2,1)S(1)}, u32[]{:S(2)}, u32[]{:S(2)}) collective-permute-start(bf16[1,128,1024]{2,1,0:T(8,128)(2,1)S(1)} %bitcast.163), channel_id=1, source_target_pairs={{0,8},{8,16},{16,24},{24,32},{32,40},{40,48},{48,56},{56,64},{64,7... | collective-permute-start | bytes 786440 | tf_op jit(solution)/shard_map/ppermute | solution.py:20
  130.9 59.4 %collective-permute-start.18 = (bf16[1,128,1024]{2,1,0:T(8,128)(2,1)}, bf16[1,128,1024]{2,1,0:T(8,128)(2,1)S(1)}, u32[]{:S(2)}, u32[]{:S(2)}) collective-permute-start(bf16[1,128,1024]{2,1,0:T(8,128)(2,1)} %bitcast.5), channel_id=1, source_target_pairs={{0,48},{8,56},{16,64},{24,72},{32,80},{40,88},{48,96},{56,104},{64... | collective-permute-start | bytes 786440 | tf_op jit(solution)/shard_map/ppermute | solution.py:20
  137.1 57.4 %collective-permute-start.19 = (bf16[1,128,1024]{2,1,0:T(8,128)(2,1)}, bf16[1,128,1024]{2,1,0:T(8,128)(2,1)}, u32[]{:S(2)}, u32[]{:S(2)}) collective-permute-start(bf16[1,128,1024]{2,1,0:T(8,128)(2,1)} %bitcast.5), channel_id=1, source_target_pairs={{0,40},{8,48},{16,56},{24,64},{32,72},{40,80},{48,88},{56,96},{64,... | collective-permute-start | bytes 786440 | tf_op jit(solution)/shard_map/ppermute | solution.py:20
  143.9 51.5 %collective-permute-start.20 = (bf16[1,128,1024]{2,1,0:T(8,128)(2,1)}, bf16[1,128,1024]{2,1,0:T(8,128)(2,1)S(1)}, u32[]{:S(2)}, u32[]{:S(2)}) collective-permute-start(bf16[1,128,1024]{2,1,0:T(8,128)(2,1)} %bitcast.5), channel_id=1, source_target_pairs={{0,32},{8,40},{16,48},{24,56},{32,64},{40,72},{48,80},{56,88},{64,... | collective-permute-start | bytes 786440 | tf_op jit(solution)/shard_map/ppermute | solution.py:20
  174.9 166.9 %reduce-scatter.3.cloned.1.call-start = ((), (), s32[]{:S(2)}) async-start(), calls=%async_computation.2 | async-start | bytes 2359296 | tf_op jit(solution)/shard_map/reduce_scatter | solution.py:153
  175.0 20.5 %collective-permute-start.21 = (bf16[1,128,1024]{2,1,0:T(8,128)(2,1)}, bf16[1,128,1024]{2,1,0:T(8,128)(2,1)S(1)}, u32[]{:S(2)}, u32[]{:S(2)}) collective-permute-start(bf16[1,128,1024]{2,1,0:T(8,128)(2,1)} %bitcast.5), channel_id=1, source_target_pairs={{0,24},{8,32},{16,40},{24,48},{32,56},{40,64},{48,72},{56,80},{64,... | collective-permute-start | bytes 786440 | tf_op jit(solution)/shard_map/ppermute | solution.py:20
  190.3 16.3 %collective-permute-start.23 = (bf16[1,128,1024]{2,1,0:T(8,128)(2,1)}, bf16[1,128,1024]{2,1,0:T(8,128)(2,1)S(1)}, u32[]{:S(2)}, u32[]{:S(2)}) collective-permute-start(bf16[1,128,1024]{2,1,0:T(8,128)(2,1)} %bitcast.5), channel_id=1, source_target_pairs={{0,8},{8,16},{16,24},{24,32},{32,40},{40,48},{48,56},{56,64},{64,7... | collective-permute-start | bytes 786440 | tf_op jit(solution)/shard_map/ppermute | solution.py:20
  248.3 14.2 %collective-permute-start.39 = (bf16[1,128,1024]{1,2,0:T(8,128)(2,1)S(1)}, bf16[1,128,1024]{1,2,0:T(8,128)(2,1)S(1)}, u32[]{:S(2)}, u32[]{:S(2)}) collective-permute-start(bf16[1,128,1024]{1,2,0:T(8,128)(2,1)S(1)} %bitcast.174), channel_id=1, source_target_pairs={{64,0},{72,8},{80,16},{88,24},{96,32},{104,40},{112,48},{120,56},{... | collective-permute-start | bytes 786440 | tf_op jit(solution)/shard_map/ppermute | solution.py:20
  250.9 17.7 %collective-permute-start.38 = (bf16[1,128,1024]{1,2,0:T(8,128)(2,1)S(1)}, bf16[1,128,1024]{1,2,0:T(8,128)(2,1)S(1)}, u32[]{:S(2)}, u32[]{:S(2)}) collective-permute-start(bf16[1,128,1024]{1,2,0:T(8,128)(2,1)S(1)} %bitcast.173), channel_id=1, source_target_pairs={{56,0},{64,8},{72,16},{80,24},{88,32},{96,40},{104,48},{112,56},{1... | collective-permute-start | bytes 786440 | tf_op jit(solution)/shard_map/ppermute | solution.py:20
  252.8 26.6 %collective-permute-start.37 = (bf16[1,128,1024]{1,2,0:T(8,128)(2,1)S(1)}, bf16[1,128,1024]{1,2,0:T(8,128)(2,1)S(1)}, u32[]{:S(2)}, u32[]{:S(2)}) collective-permute-start(bf16[1,128,1024]{1,2,0:T(8,128)(2,1)S(1)} %bitcast.172), channel_id=1, source_target_pairs={{48,0},{56,8},{64,16},{72,24},{80,32},{88,40},{96,48},{104,56},{11... | collective-permute-start | bytes 786440 | tf_op jit(solution)/shard_map/ppermute | solution.py:20
  256.7 40.2 %collective-permute-start.36 = (bf16[1,128,1024]{1,2,0:T(8,128)(2,1)S(1)}, bf16[1,128,1024]{1,2,0:T(8,128)(2,1)S(1)}, u32[]{:S(2)}, u32[]{:S(2)}) collective-permute-start(bf16[1,128,1024]{1,2,0:T(8,128)(2,1)S(1)} %bitcast.171), channel_id=1, source_target_pairs={{40,0},{48,8},{56,16},{64,24},{72,32},{80,40},{88,48},{96,56},{104... | collective-permute-start | bytes 786440 | tf_op jit(solution)/shard_map/ppermute | solution.py:20
  258.6 42.2 %collective-permute-start.35 = (bf16[1,128,1024]{1,2,0:T(8,128)(2,1)S(1)}, bf16[1,128,1024]{1,2,0:T(8,128)(2,1)S(1)}, u32[]{:S(2)}, u32[]{:S(2)}) collective-permute-start(bf16[1,128,1024]{1,2,0:T(8,128)(2,1)S(1)} %bitcast.170), channel_id=1, source_target_pairs={{32,0},{40,8},{48,16},{56,24},{64,32},{72,40},{80,48},{88,56},{96,... | collective-permute-start | bytes 786440 | tf_op jit(solution)/shard_map/ppermute | solution.py:20
  262.5 40.2 %collective-permute-start.34 = (bf16[1,128,1024]{1,2,0:T(8,128)(2,1)S(1)}, bf16[1,128,1024]{1,2,0:T(8,128)(2,1)S(1)}, u32[]{:S(2)}, u32[]{:S(2)}) collective-permute-start(bf16[1,128,1024]{1,2,0:T(8,128)(2,1)S(1)} %bitcast.168), channel_id=1, source_target_pairs={{24,0},{32,8},{40,16},{48,24},{56,32},{64,40},{72,48},{80,56},{88,... | collective-permute-start | bytes 786440 | tf_op jit(solution)/shard_map/ppermute | solution.py:20
  268.6 41.1 %collective-permute-start.33 = (bf16[1,128,1024]{1,2,0:T(8,128)(2,1)S(1)}, bf16[1,128,1024]{1,2,0:T(8,128)(2,1)S(1)}, u32[]{:S(2)}, u32[]{:S(2)}) collective-permute-start(bf16[1,128,1024]{1,2,0:T(8,128)(2,1)S(1)} %bitcast.165), channel_id=1, source_target_pairs={{16,0},{24,8},{32,16},{40,24},{48,32},{56,40},{64,48},{72,56},{80,... | collective-permute-start | bytes 786440 | tf_op jit(solution)/shard_map/ppermute | solution.py:20
  279.4 32.5 %collective-permute-start.32 = (bf16[1,128,1024]{1,2,0:T(8,128)(2,1)S(1)}, bf16[1,128,1024]{1,2,0:T(8,128)(2,1)S(1)}, u32[]{:S(2)}, u32[]{:S(2)}) collective-permute-start(bf16[1,128,1024]{1,2,0:T(8,128)(2,1)S(1)} %bitcast.164), channel_id=1, source_target_pairs={{8,0},{16,8},{24,16},{32,24},{40,32},{48,40},{56,48},{64,56},{72,6... | collective-permute-start | bytes 786440 | tf_op jit(solution)/shard_map/ppermute | solution.py:20
  296.9 30.4 %collective-permute-start.31 = (bf16[1,128,1024]{1,2,0:T(8,128)(2,1)S(1)}, bf16[1,128,1024]{1,2,0:T(8,128)(2,1)S(1)}, u32[]{:S(2)}, u32[]{:S(2)}) collective-permute-start(bf16[1,128,1024]{1,2,0:T(8,128)(2,1)S(1)} %bitcast.169), channel_id=1, source_target_pairs={{64,0},{72,8},{80,16},{88,24},{96,32},{104,40},{112,48},{120,56},{... | collective-permute-start | bytes 786440 | tf_op jit(solution)/shard_map/ppermute | solution.py:20
  300.8 28.4 %collective-permute-start.30 = (bf16[1,128,1024]{1,2,0:T(8,128)(2,1)S(1)}, bf16[1,128,1024]{1,2,0:T(8,128)(2,1)}, u32[]{:S(2)}, u32[]{:S(2)}) collective-permute-start(bf16[1,128,1024]{1,2,0:T(8,128)(2,1)S(1)} %bitcast.167), channel_id=1, source_target_pairs={{56,0},{64,8},{72,16},{80,24},{88,32},{96,40},{104,48},{112,56},{1... | collective-permute-start | bytes 786440 | tf_op jit(solution)/shard_map/ppermute | solution.py:20
  303.5 29.8 %collective-permute-start.29 = (bf16[1,128,1024]{1,2,0:T(8,128)(2,1)S(1)}, bf16[1,128,1024]{1,2,0:T(8,128)(2,1)}, u32[]{:S(2)}, u32[]{:S(2)}) collective-permute-start(bf16[1,128,1024]{1,2,0:T(8,128)(2,1)S(1)} %bitcast.166), channel_id=1, source_target_pairs={{48,0},{56,8},{64,16},{72,24},{80,32},{88,40},{96,48},{104,56},{11... | collective-permute-start | bytes 786440 | tf_op jit(solution)/shard_map/ppermute | solution.py:20
  309.6 27.6 %collective-permute-start.28 = (bf16[1,128,1024]{1,2,0:T(8,128)(2,1)}, bf16[1,128,1024]{1,2,0:T(8,128)(2,1)}, u32[]{:S(2)}, u32[]{:S(2)}) collective-permute-start(bf16[1,128,1024]{1,2,0:T(8,128)(2,1)} %bitcast.21), channel_id=1, source_target_pairs={{40,0},{48,8},{56,16},{64,24},{72,32},{80,40},{88,48},{96,56},{104... | collective-permute-start | bytes 786440 | tf_op jit(solution)/shard_map/ppermute | solution.py:20
  311.9 25.4 %collective-permute-start.27 = (bf16[1,128,1024]{1,2,0:T(8,128)(2,1)}, bf16[1,128,1024]{1,2,0:T(8,128)(2,1)}, u32[]{:S(2)}, u32[]{:S(2)}) collective-permute-start(bf16[1,128,1024]{1,2,0:T(8,128)(2,1)} %bitcast.20), channel_id=1, source_target_pairs={{32,0},{40,8},{48,16},{56,24},{64,32},{72,40},{80,48},{88,56},{96,... | collective-permute-start | bytes 786440 | tf_op jit(solution)/shard_map/ppermute | solution.py:20
  (38 other events, 481.0 us)
Sparse Core Ops, SparseCore 0:
  15.8 45.3 all-gather.6
  63.6 32.4 all-gather.4
  175.0 51.5 reduce-scatter.4
  245.4 52.0 reduce-scatter.2
where the time goes:
time: 358 us; the launch traced here: 356 us
  starting transfers between devices  178 us (50%)
  waiting for transfers between devices  56.9 us (16%)
  local copies, waits for them, and re-layouts  53.1 us (15%)
  matrix products  40.2 us (11%)
  between operations  14.8 us (4%)
  other arithmetic  13.6 us (4%)
    ppermute x40, starting transfers between devices, shifted(): lax.ppermute(value, axis, [(source, source + steps) for source in range(l...  178 us
    ppermute x40, waiting for transfers between devices, shifted(): lax.ppermute(value, axis, [(source, source + steps) for source in range(l...  56.8 us
    unnamed x72, local copies, waits for them, and re-layouts  21.7 us
  transfers between devices with their start and end apart: 44, of which 15 were waited for; matrix products, arithmetic and copies ran while one was open for 24% of the time, Pallas kernels for 0%

commit v1 on v0

v1 whole, which is shorter than its diff:
```python
import math

import jax
import jax.numpy as jnp
from jax import lax
from jax.experimental import pallas as pl
from jax.experimental.pallas import tpu as pltpu
from jax.sharding import Mesh
from jax.sharding import PartitionSpec as P

D = 1024
H = 8
DH = 128
HW = 128
WIN = 8
EPS = 1e-05

HALF = H // 2
PAIR = 2 * HW
GROUP = 8
SCALE = DH ** (-0.5)
SCALE2 = SCALE * math.log2(math.e)
FLOOR = -3.0e38
F32 = jnp.float32
BF16 = jnp.bfloat16
NT = (((1,), (1,)), ((), ()))
VMEM_LIMIT = 48 * 1024 * 1024

Q0, G0, K0, V0, OK0, ROWS = 0, 128, 256, 384, 512, 528
KEYS = (WIN + 1) * HW


def params(**kw):
    return pltpu.CompilerParams(vmem_limit_bytes=VMEM_LIMIT, **kw)


def mm(a, b):
    return jnp.dot(a, b, preferred_element_type=F32)


def mm_nt(a, b):
    return lax.dot_general(a, b, NT, preferred_element_type=F32)


def turn(a):
    return a.astype(F32).T


def project_kernel(core, valid, own, other, cot_own, cot_other, gain, wq, wk, wv, wo, packed, kv):
    del core
    x = jnp.concatenate([own[...], other[...]], axis=0).astype(F32)
    rinv = lax.rsqrt(jnp.mean(x * x, axis=-1, keepdims=True) + EPS)
    normed = (x * rinv * gain[...]).astype(BF16)
    cot = jnp.concatenate([cot_own[...], cot_other[...]], axis=0)
    flags = jnp.full((ROWS - OK0, DH), valid[0], jnp.int32).astype(F32).astype(BF16)
    for row, part in ((K0, wk), (V0, wv), (Q0, wq), (G0, wo)):
        if row == G0:
            got = mm_nt(cot, part[...]).astype(BF16)
        else:
            got = mm(normed, part[...]).astype(BF16)
        for h in range(HALF):
            block = got[:, h * DH : (h + 1) * DH]
            for s in range(2):
                packed[s, h, row : row + HW, :] = block[s * HW : (s + 1) * HW]
            if row == K0:
                kv[0, h] = block
            if row == V0:
                kv[1, h] = block
    for h in range(HALF):
        for s in range(2):
            packed[s, h, OK0:ROWS, :] = flags


def project(core, valid, own, other, cot_own, cot_other, gain, w_qkv, w_out):
    whole = lambda shape: pl.BlockSpec(shape, lambda i, core, valid: (0,) * len(shape))
    part = lambda at: pl.BlockSpec((D, HALF * DH), lambda i, core, valid: (0, at * 2 + core[0]))
    return pl.pallas_call(
        project_kernel,
        grid_spec=pltpu.PrefetchScalarGridSpec(
            num_scalar_prefetch=2,
            grid=(1,),
            in_specs=[whole((HW, D))] * 4
            + [whole((1, D)), part(0), part(1), part(2)]
            + [pl.BlockSpec((HALF * DH, D), lambda i, core, valid: (core[0], 0))],
            out_specs=[whole((2, HALF, ROWS, DH)), whole((2, HALF, PAIR, DH))],
        ),
        out_shape=[
            jax.ShapeDtypeStruct((2, HALF, ROWS, DH), BF16),
            jax.ShapeDtypeStruct((2, HALF, PAIR, DH), BF16),
        ],
        compiler_params=params(),
        cost_estimate=pl.CostEstimate(
            flops=2 * PAIR * D * 4 * HALF * DH, bytes_accessed=7_000_000, transcendentals=0
        ),
        name="project",
    )(core, valid, own, other, cot_own, cot_other, gain, w_qkv, w_qkv, w_qkv, w_out)


def split3(value):
    first = value.astype(BF16)
    rest = value - first.astype(F32)
    second = rest.astype(BF16)
    third = (rest - second.astype(F32)).astype(BF16)
    return [first.astype(F32), second.astype(F32), third.astype(F32)]


def far_forward_kernel(win, mine, past, sent, kept, keys, values_t, scores):
    width = win[0]
    for j in range(GROUP):
        keys[j * HW : (j + 1) * HW, :] = past[j, :HW, :]
        keys[(GROUP + j) * HW : (GROUP + j + 1) * HW, :] = mine[j, K0 : K0 + HW, :]
        values_t[:, j * HW : (j + 1) * HW] = turn(past[j, HW : 2 * HW, :]).astype(BF16)
        values_t[:, (GROUP + j) * HW : (GROUP + j + 1) * HW] = turn(
            mine[j, V0 : V0 + HW, :]
        ).astype(BF16)
    for p in range(GROUP // 2):
        query = jnp.concatenate([mine[2 * p, :HW, :], mine[2 * p + 1, :HW, :]], axis=0)
        grad_t = jnp.concatenate(
            [turn(mine[2 * p, G0 : G0 + HW, :]), turn(mine[2 * p + 1, G0 : G0 + HW, :])], axis=1
        )
        peak = jnp.full((1, PAIR), -jnp.inf, F32)
        for b in range(WIN + 1):
            j = 2 * p + b
            if j < GROUP:
                flag = past[j, 2 * HW : 2 * HW + 1, :].astype(F32)
            else:
                flag = mine[j - GROUP, OK0 : OK0 + 1, :].astype(F32)
            lower = jnp.where((flag > 0.5) & (b >= WIN - width) & (b < WIN), 0.0, -jnp.inf)
            upper = jnp.where((flag > 0.5) & (b >= WIN + 1 - width), 0.0, -jnp.inf)
            bias = jnp.concatenate([lower, upper], axis=1)
            block = mm_nt(keys[j * HW : (j + 1) * HW, :], query) + bias
            scores[b * HW : (b + 1) * HW, :] = block
            peak = jnp.maximum(peak, jnp.max(block, axis=0, keepdims=True))
        peak = jnp.maximum(peak * SCALE2, FLOOR)
        total = jnp.zeros((1, PAIR), F32)
        for b in range(WIN + 1):
            block = jnp.exp2(scores[b * HW : (b + 1) * HW, :] * SCALE2 - peak)
            total = total + jnp.sum(block, axis=0, keepdims=True)
            kept[p, b * HW : (b + 1) * HW, :] = block.astype(BF16)
        result = mm(values_t[:, p * PAIR : p * PAIR + KEYS], kept[p])
        delta = jnp.sum(result * grad_t, axis=0, keepdims=True)
        stats = split3(peak) + split3(total) + split3(delta)
        stats = jnp.concatenate(stats + [jnp.zeros((7, PAIR), F32)], axis=0)
        packed = jnp.concatenate([result, stats], axis=0).astype(BF16)
        sent[2 * p] = packed[:, :HW]
        sent[2 * p + 1] = packed[:, HW:]


VM = pl.BlockSpec(memory_space=pltpu.VMEM)
SM = pl.BlockSpec(memory_space=pltpu.SMEM)


def far_forward(width, mine, past):
    return pl.pallas_call(
        far_forward_kernel,
        in_specs=[SM, VM, VM],
        out_specs=[VM, VM],
        out_shape=[
            jax.ShapeDtypeStruct((GROUP, DH + 16, HW), BF16),
            jax.ShapeDtypeStruct((GROUP // 2, KEYS, PAIR), BF16),
        ],
        scratch_shapes=[
            pltpu.VMEM((2 * GROUP * HW, DH), BF16),
            pltpu.VMEM((DH, 2 * GROUP * HW), BF16),
            pltpu.VMEM((KEYS, PAIR), F32),
        ],
        compiler_params=params(),
        cost_estimate=pl.CostEstimate(
            flops=16 * KEYS * PAIR * DH, bytes_accessed=5_000_000, transcendentals=4 * KEYS * PAIR
        ),
        name="far_forward",
    )(width, mine, past)


def near_kernel(kv, packed, far, dkv, dq, attended, told, scores, kept, grads):
    query = jnp.concatenate([packed[0, 0, :HW, :], packed[1, 0, :HW, :]], axis=0)
    grad = jnp.concatenate([packed[0, 0, G0 : G0 + HW, :], packed[1, 0, G0 : G0 + HW, :]], axis=0)
    grad_t = turn(grad)
    peak = jnp.full((1, PAIR), -jnp.inf, F32)
    for z in range(4):
        block = mm_nt(kv[z, 0, 0], query)
        scores[z * PAIR : (z + 1) * PAIR, :] = block
        peak = jnp.maximum(peak, jnp.max(block, axis=0, keepdims=True))
    peak = peak * SCALE2
    total = jnp.zeros((1, PAIR), F32)
    for b in range(8):
        block = jnp.exp2(scores[b * HW : (b + 1) * HW, :] * SCALE2 - peak)
        total = total + jnp.sum(block, axis=0, keepdims=True)
        kept[b * HW : (b + 1) * HW, :] = block.astype(BF16)
    result = jnp.zeros((DH, PAIR), F32)
    for z in range(4):
        result = result + mm(turn(kv[z, 1, 0]).astype(BF16), kept[z * PAIR : (z + 1) * PAIR, :])
    delta = jnp.sum(result * grad_t, axis=0, keepdims=True)
    other = jnp.concatenate([far[0, 0], far[1, 0]], axis=1).astype(F32)
    row = lambda at: other[DH + at : DH + at + 1, :]
    far_peak = (row(0) + row(1)) + row(2)
    far_total = (row(3) + row(4)) + row(5)
    far_delta = (row(6) + row(7)) + row(8)
    top = jnp.maximum(peak, far_peak)
    near_weight = jnp.exp2(peak - top)
    far_weight = jnp.exp2(far_peak - top)
    inverse = 1.0 / (near_weight * total + far_weight * far_total)
    near_weight = near_weight * inverse
    far_weight = far_weight * inverse
    delta = near_weight * delta + far_weight * far_delta
    mixed_t = near_weight * result + far_weight * other[:DH, :]
    attended[0] = mixed_t.T.astype(BF16)
    far_delta = far_weight * delta
    for s in range(2):
        told[s, 0] = jnp.concatenate(
            [
                far_weight[:, s * HW : (s + 1) * HW],
                far_delta[:, s * HW : (s + 1) * HW],
                jnp.zeros((6, HW), F32),
            ],
            axis=0,
        )
    grad_t = (grad_t * near_weight).astype(BF16)
    delta = near_weight * delta
    back = jnp.zeros((DH, PAIR), F32)
    for z in range(4):
        rows = slice(z * PAIR, (z + 1) * PAIR)
        d_probs = mm(kv[z, 1, 0], grad_t)
        d_scores = (kept[rows, :].astype(F32) * (d_probs - delta)).astype(BF16)
        grads[rows, :] = d_scores
        dkv[z, 1, 0] = mm_nt(kept[rows, :], grad_t).astype(BF16)
        dkv[z, 0, 0] = (mm(d_scores, query) * SCALE).astype(BF16)
        back = back + mm(turn(kv[z, 0, 0]).astype(BF16), d_scores)
    dq[0] = (back * SCALE).T.astype(BF16)


def near(kv, packed, far):
    return pl.pallas_call(
        near_kernel,
        grid=(HALF,),
        in_specs=[
            pl.BlockSpec((4, 2, 1, PAIR, DH), lambda h: (0, 0, h, 0, 0)),
            pl.BlockSpec((2, 1, ROWS, DH), lambda h: (0, h, 0, 0)),
            pl.BlockSpec((2, 1, DH + 16, HW), lambda h: (0, h, 0, 0)),
        ],
        out_specs=[
            pl.BlockSpec((4, 2, 1, PAIR, DH), lambda h: (0, 0, h, 0, 0)),
            pl.BlockSpec((1, PAIR, DH), lambda h: (h, 0, 0)),
            pl.BlockSpec((1, PAIR, DH), lambda h: (h, 0, 0)),
            pl.BlockSpec((2, 1, 8, HW), lambda h: (0, h, 0, 0)),
        ],
        out_shape=[
            jax.ShapeDtypeStruct((4, 2, HALF, PAIR, DH), BF16),
            jax.ShapeDtypeStruct((HALF, PAIR, DH), BF16),
            jax.ShapeDtypeStruct((HALF, PAIR, DH), BF16),
            jax.ShapeDtypeStruct((2, HALF, 8, HW), F32),
        ],
        scratch_shapes=[
            pltpu.VMEM((4 * PAIR, PAIR), F32),
            pltpu.VMEM((4 * PAIR, PAIR), BF16),
            pltpu.VMEM((4 * PAIR, PAIR), BF16),
        ],
        compiler_params=params(),
        cost_estimate=pl.CostEstimate(
            flops=12 * HALF * 4 * PAIR * PAIR * DH,
            bytes_accessed=6_000_000,
            transcendentals=HALF * 4 * PAIR * PAIR,
        ),
        name="near",
    )(kv, packed, far)


def far_backward_kernel(mine, past, kept, told, own, back, keys_t, values, dk, dv, grads):
    for j in range(GROUP):
        keys_t[:, j * HW : (j + 1) * HW] = turn(past[j, :HW, :]).astype(BF16)
        keys_t[:, (GROUP + j) * HW : (GROUP + j + 1) * HW] = turn(
            mine[j, K0 : K0 + HW, :]
        ).astype(BF16)
        values[j * HW : (j + 1) * HW, :] = past[j, HW : 2 * HW, :]
        values[(GROUP + j) * HW : (GROUP + j + 1) * HW, :] = mine[j, V0 : V0 + HW, :]
    dk[...] = jnp.zeros_like(dk)
    dv[...] = jnp.zeros_like(dv)
    for p in range(GROUP // 2):
        query = jnp.concatenate([mine[2 * p, :HW, :], mine[2 * p + 1, :HW, :]], axis=0)
        grad_t = jnp.concatenate(
            [turn(mine[2 * p, G0 : G0 + HW, :]), turn(mine[2 * p + 1, G0 : G0 + HW, :])], axis=1
        )
        stats = jnp.concatenate([told[2 * p], told[2 * p + 1]], axis=1)
        weight = stats[0:1, :]
        delta = stats[1:2, :]
        grad_t = (grad_t * weight).astype(BF16)
        at = p * PAIR
        for lo, size in ((0, 384), (384, 384), (768, 384)):
            rows = slice(lo, lo + size)
            spot = slice(at + lo, at + lo + size)
            d_probs = mm(values[spot, :], grad_t)
            block = kept[p, rows, :]
            d_scores = (block.astype(F32) * (d_probs - delta)).astype(BF16)
            grads[rows, :] = d_scores
            dv[spot, :] += mm_nt(block, grad_t)
            dk[spot, :] += mm(d_scores, query)
        d_query = (mm(keys_t[:, at : at + KEYS], grads[...]) * SCALE).T.astype(BF16)
        own[2 * p, :HW, :] = d_query[:HW]
        own[2 * p + 1, :HW, :] = d_query[HW:]
    for j in range(GROUP):
        early = slice(j * HW, (j + 1) * HW)
        late = slice((GROUP + j) * HW, (GROUP + j + 1) * HW)
        back[j, :HW, :] = (dk[early, :] * SCALE).astype(BF16)
        back[j, HW:, :] = dv[early, :].astype(BF16)
        own[j, HW : 2 * HW, :] = (dk[late, :] * SCALE).astype(BF16)
        own[j, 2 * HW :, :] = dv[late, :].astype(BF16)


def far_backward(mine, past, kept, told):
    return pl.pallas_call(
        far_backward_kernel,
        in_specs=[VM] * 4,
        out_specs=[VM, VM],
        out_shape=[
            jax.ShapeDtypeStruct((GROUP, 3 * HW, DH), BF16),
            jax.ShapeDtypeStruct((GROUP, 2 * HW, DH), BF16),
        ],
        scratch_shapes=[
            pltpu.VMEM((DH, 2 * GROUP * HW), BF16),
            pltpu.VMEM((2 * GROUP * HW, DH), BF16),
            pltpu.VMEM((2 * GROUP * HW, DH), F32),
            pltpu.VMEM((2 * GROUP * HW, DH), F32),
            pltpu.VMEM((KEYS, PAIR), BF16),
        ],
        compiler_params=params(),
        cost_estimate=pl.CostEstimate(
            flops=32 * KEYS * PAIR * DH, bytes_accessed=6_000_000, transcendentals=0
        ),
        name="far_backward",
    )(mine, past, kept, told)


def mix_kernel(core, attended, wo, own, other):
    del core
    rows = jnp.concatenate([attended[h] for h in range(HALF)], axis=1)
    out = mm(rows, wo[...])
    own[...] = out[:HW]
    other[...] = out[HW:].astype(BF16)


def mix(core, attended, w_out):
    return pl.pallas_call(
        mix_kernel,
        grid_spec=pltpu.PrefetchScalarGridSpec(
            num_scalar_prefetch=1,
            grid=(1,),
            in_specs=[
                pl.BlockSpec((HALF, PAIR, DH), lambda i, core: (0, 0, 0)),
                pl.BlockSpec((HALF * DH, D), lambda i, core: (core[0], 0)),
            ],
            out_specs=[pl.BlockSpec((HW, D), lambda i, core: (0, 0))] * 2,
        ),
        out_shape=[jax.ShapeDtypeStruct((HW, D), F32), jax.ShapeDtypeStruct((HW, D), BF16)],
        compiler_params=params(),
        cost_estimate=pl.CostEstimate(
            flops=2 * PAIR * D * HALF * DH, bytes_accessed=2_000_000, transcendentals=0
        ),
        name="mix",
    )(core, attended, w_out)


def unproject_kernel(core, dq, dkv, far, wq, wk, wv, own, other):
    del core
    total = jnp.zeros((PAIR, D), F32)
    for part, weight in enumerate((wq, wk, wv)):
        pieces = []
        for h in range(HALF):
            rows = slice(part * HW, (part + 1) * HW)
            away = jnp.concatenate([far[0, h, rows, :], far[1, h, rows, :]], axis=0)
            close = dq[h] if part == 0 else dkv[part - 1, h]
            pieces.append((away.astype(F32) + close.astype(F32)).astype(BF16))
        total = total + mm_nt(jnp.concatenate(pieces, axis=1), weight[...])
    own[...] = total[:HW]
    other[...] = total[HW:].astype(BF16)


def unproject(core, dq, dkv, far, w_qkv):
    whole = lambda shape: pl.BlockSpec(shape, lambda i, core: (0,) * len(shape))
    part = lambda at: pl.BlockSpec((D, HALF * DH), lambda i, core: (0, at * 2 + core[0]))
    return pl.pallas_call(
        unproject_kernel,
        grid_spec=pltpu.PrefetchScalarGridSpec(
            num_scalar_prefetch=1,
            grid=(1,),
            in_specs=[
                whole((HALF, PAIR, DH)),
                whole((2, HALF, PAIR, DH)),
                whole((2, HALF, 3 * HW, DH)),
                part(0),
                part(1),
                part(2),
            ],
            out_specs=[whole((HW, D))] * 2,
        ),
        out_shape=[jax.ShapeDtypeStruct((HW, D), F32), jax.ShapeDtypeStruct((HW, D), BF16)],
        compiler_params=params(),
        cost_estimate=pl.CostEstimate(
            flops=2 * PAIR * D * 3 * HALF * DH, bytes_accessed=5_000_000, transcendentals=0
        ),
        name="unproject",
    )(core, dq, dkv, far, w_qkv, w_qkv, w_qkv)


def finish_kernel(tokens, cot, gain, own, other, out):
    x = tokens[...].astype(F32)
    rinv = lax.rsqrt(jnp.mean(x * x, axis=-1, keepdims=True) + EPS)
    scaled = (own[...] + other[...].astype(F32)) * gain[...]
    mean = jnp.mean(scaled * x, axis=-1, keepdims=True)
    grad = rinv * scaled - x * (rinv * rinv * rinv * mean)
    out[...] = (cot[...].astype(F32) + grad).astype(BF16)


def finish(tokens, cot, gain, own, other):
    return pl.pallas_call(
        finish_kernel,
        in_specs=[VM] * 5,
        out_specs=VM,
        out_shape=jax.ShapeDtypeStruct((HW, D), BF16),
        compiler_params=params(),
        cost_estimate=pl.CostEstimate(flops=HW * D * 10, bytes_accessed=2_000_000, transcendentals=0),
        name="finish",
    )(tokens, cot, gain, own, other)


SWAP = [(0, 1), (1, 0)]
LANE = ("x", "zl")


def swap(value):
    return lax.ppermute(value, "core", SWAP)


def exchange(value):
    return lax.all_to_all(value, LANE, 0, 0, tiled=True)


def per_device(tokens, gain, w_qkv, w_out, window, valid, cotangent):
    rows = lax.axis_size("y")
    core = lax.axis_index("core").astype(jnp.int32)
    lane = lax.axis_index(LANE).astype(jnp.int32)
    tokens = tokens.reshape(HW, D)
    cot = cotangent.reshape(HW, D)
    gain = gain.reshape(1, D)
    core_arg = core.reshape(1)
    other_tokens = swap(tokens)
    other_cot = swap(cot)
    width = lax.dynamic_slice(window, (core * HALF + lane % HALF,), (1,))
    packed, kv = project(
        core_arg, valid, tokens, other_tokens, cot, other_cot, gain, w_qkv, w_out
    )
    near_kv = lax.all_gather(kv, "zh", axis=0)
    mine = exchange(packed.reshape(2 * HALF, ROWS, DH))
    past = lax.ppermute(mine[:, K0:, :], "y", [(i, i + 1) for i in range(rows - 1)])
    sent, kept = far_forward(width, mine, past)
    far = exchange(sent).reshape(2, HALF, DH + 16, HW)
    dkv, dq, attended, told = near(near_kv, packed, far)
    dkv = lax.psum_scatter(dkv, "zh", scatter_dimension=0)
    told = exchange(told.reshape(2 * HALF, 8, HW))
    own, back = far_backward(mine, past, kept, told)
    back = lax.ppermute(back, "y", [(i + 1, i) for i in range(rows - 1)])
    summed = (own[:, HW:, :].astype(F32) + back.astype(F32)).astype(BF16)
    own = jnp.concatenate([own[:, :HW, :], summed], axis=1)
    far_grads = exchange(own).reshape(2, HALF, 3 * HW, DH)
    mixed_own, mixed_other = mix(core_arg, attended, w_out)
    mixed_other = swap(mixed_other)
    mixed = (tokens.astype(F32) + (mixed_own + mixed_other.astype(F32))).astype(BF16)
    grad_own, grad_other = unproject(core_arg, dq, dkv, far_grads, w_qkv)
    grad_other = swap(grad_other)
    d_tokens = finish(tokens, cot, gain, grad_own, grad_other)
    return mixed.reshape(1, 1, HW, D), d_tokens.reshape(1, 1, HW, D)


def solution(mesh):
    grid = Mesh(mesh.devices.reshape(4, 4, 2, 4, 2), ("y", "x", "zl", "zh", "core"))
    frames, cams = ("y", "x", "zl"), ("zh", "core")
    split = P(frames, cams, None, None)
    return jax.shard_map(
        per_device,
        mesh=grid,
        in_specs=(split, P(), P(), P(), P(), P(frames), split),
        out_specs=(split, split),
        check_vma=False,
    )
```

time: 358 us -> 163 us (0.46)
  starting transfers between devices: 178 us -> 9.96 us
  blocking collectives: 0 us -> 52.7 us
  matrix products: 40.2 us -> 0 us
  local copies, waits for them, and re-layouts: 53.1 us -> 13.9 us
  Pallas kernels: 0 us -> 22.1 us
  other arithmetic: 13.6 us -> 1.9 us
  waiting for transfers between devices: 56.9 us -> 45.7 us
    ppermute x40 -> x6, starting transfers between devices: 178 us -> 6.34 us  [the longest x1 3.29 us: per_device(): lax.ppermute(mine[:, K0:, :], 'y', [(i, i + 1) for i in range(rows - 1)])]
    all_to_all x0 -> x3, blocking collectives: none -> 52.7 us  [exchange(): return lax.all_to_all(value, LANE, 0, 0, tiled=True)]
    dot_general x16 -> x0, matrix products: 40.2 us -> none  [the longest x1 5.08 us: per_device(): jnp.dot(grads, w_qkv.T, preferred_element_type=jnp.float32)]
    ppermute x40 -> x6, waiting for transfers between devices: 56.8 us -> 21.1 us  [the longest x1 11.9 us: per_device(): back = lax.ppermute(back, 'y', [(i + 1, i) for i in range(rows - 1)])]
    all_to_all x0 -> x1, waiting for transfers between devices: none -> 24.1 us  [exchange(): return lax.all_to_all(value, LANE, 0, 0, tiled=True)]
    pallas_call x0 -> x7, Pallas kernels: none -> 22.1 us  [the longest x1 7.1 us: near(): pl.pallas_call(near_kernel, grid=(HALF,), in_specs=[pl.BlockSpec((4, 2, 1...]
    unnamed x72 -> x34, local copies, waits for them, and re-layouts: 21.7 us -> 13.2 us
    another operation x2 -> x0, local copies, waits for them, and re-layouts: 8.32 us -> none  [the longest x1 4.17 us: frame_inputs(): frame_values = near_values[index].reshape(split, H, DH)]
  transfers between devices with their start and end apart: 44 -> 9, of which waited for: 15 -> 7; matrix products, arithmetic and copies ran while one was open for 24% -> 2% of each run, Pallas kernels for 0% -> 6%
where the time goes in v1:
time: 163 us; the launch traced here: 161 us
  blocking collectives  52.7 us (32%)
  waiting for transfers between devices  45.7 us (28%)
  Pallas kernels  22.1 us (14%)
  between operations  14.9 us (9%)
  local copies, waits for them, and re-layouts  13.9 us (9%)
  starting transfers between devices  9.96 us (6%)
  other arithmetic  1.9 us (1%)
    all_to_all x3, blocking collectives, exchange(): return lax.all_to_all(value, LANE, 0, 0, tiled=True)  52.7 us
    all_to_all x1, waiting for transfers between devices, exchange(): return lax.all_to_all(value, LANE, 0, 0, tiled=True)  24.1 us
    unnamed x34, local copies, waits for them, and re-layouts  13.2 us
    ppermute x1, waiting for transfers between devices, per_device(): back = lax.ppermute(back, 'y', [(i + 1, i) for i in range(rows - 1)])  11.9 us
    ppermute x1, waiting for transfers between devices, per_device(): lax.ppermute(mine[:, K0:, :], 'y', [(i, i + 1) for i in range(rows - 1)])  7.51 us
    pallas_call x1, Pallas kernels, near(): pl.pallas_call(near_kernel, grid=(HALF,), in_specs=[pl.BlockSpec((4, 2, 1...  7.1 us
    pallas_call x1, Pallas kernels, project(): pl.pallas_call(project_kernel, grid_spec=pltpu.PrefetchScalarGridSpec(num...  3.86 us
    all_to_all x1, starting transfers between devices, exchange(): return lax.all_to_all(value, LANE, 0, 0, tiled=True)  3.55 us
  transfers between devices with their start and end apart: 9, of which 7 were waited for; matrix products, arithmetic and copies ran while one was open for 2% of the time, Pallas kernels for 6%

profile of v1, /device:TPU:16, one launch (start us, length us, event | category | flops | bytes accessed | tf_op | source)
XLA Modules:
  0.0 161.2 jit_solution(8131723751968924591)
XLA Ops:
  9.4 1.6 copy-done
  11.0 0.9 copy-done.2
  12.0 0.9 copy-done.4
  12.9 0.7 copy-done.11
  13.6 3.9 %project.1 = (bf16[2,4,528,128]{3,2,1,0:T(8,128)(2,1)S(1)}, bf16[2,4,256,128]{3,2,1,0:T(8,128)(2,1)}) custom-call(s32[1]{0:T(128)} %bitcast.1.core, s32[1]{0:T(128)S(6)} %copy.9.valid, bf16[128,1024]{1,0:T(8,128)(2,1)S(1)} %bitcast.16, bf16[128,1024]{1,0:T(8,128)(2,1)S(1)} %collective-permute-done.other, bf16[128,1024]{1,0:T(8,128)(2,1)S(1)} %bitcast.20, ...), custom_call_target="tpu_custom_call" | custom-call | flops 1073741824 | bytes 7000000 | tf_op jit(solution)/shard_map/project/pallas_call | solution.py:77
  17.5 31.4 %all_to_all.20.mine = bf16[8,528,128]{2,1,0:T(8,128)(2,1)S(1)} all-to-all(bf16[8,528,128]{2,1,0:T(8,128)(2,1)S(1)} %bitcast.18), channel_id=1, replica_groups=mesh['y'=4,'x'=4,'zl'=2,'zh'=4,'core'=2] {'x','zl'}, dimensions={0} | all-to-all | bytes 2162688 | tf_op jit(solution)/shard_map/all_to_all | solution.py:434
  48.9 3.3 %collective-permute-start.2 = (bf16[8,272,128]{2,1,0:T(8,128)(2,1)S(1)}, bf16[8,272,128]{2,1,0:T(8,128)(2,1)S(1)}, u32[]{:S(2)}, u32[]{:S(2)}) collective-permute-start(bf16[8,272,128]{2,1,0:T(8,128)(2,1)S(1)} %slice.12), channel_id=1, source_target_pairs={{0,64},{64,128},{128,192},{1,65},{65,129},{129,193},{2,66},{66,130... | collective-permute-start | bytes 1671176 | tf_op jit(solution)/shard_map/ppermute | solution.py:453
  52.3 0.6 dynamic_slice.3.win
  52.9 7.5 %collective-permute-done.2.past = bf16[8,272,128]{2,1,0:T(8,128)(2,1)S(1)} collective-permute-done((bf16[8,272,128]{2,1,0:T(8,128)(2,1)S(1)}, bf16[8,272,128]{2,1,0:T(8,128)(2,1)S(1)}, u32[]{:S(2)}, u32[]{:S(2)}) %collective-permute-start.2) | collective-permute-done | bytes 557088 | tf_op jit(solution)/shard_map/ppermute | solution.py:453
  60.4 3.3 %far_forward.1 = (bf16[8,144,128]{2,1,0:T(8,128)(2,1)S(1)}, bf16[4,1152,256]{2,1,0:T(8,128)(2,1)S(1)}) custom-call(s32[1]{0:T(128)} %dynamic_slice.3.win, bf16[8,528,128]{2,1,0:T(8,128)(2,1)S(1)} %all_to_all.20.mine, bf16[8,272,128]{2,1,0:T(8,128)(2,1)S(1)} %collective-permute-done.2.past), custom_call_target="tpu_custom_call" | custom-call | flops 603979776 | bytes 5000000 | tf_op jit(solution)/shard_map/far_forward/pallas_call | solution.py:154
  63.7 1.4 copy-done.14
  65.1 11.6 %all_to_all.21 = bf16[8,144,128]{2,1,0:T(8,128)(2,1)S(1)} all-to-all(bf16[8,144,128]{2,1,0:T(8,128)(2,1)S(1)} %get-tuple-element.18), channel_id=1, replica_groups=mesh['y'=4,'x'=4,'zl'=2,'zh'=4,'core'=2] {'x','zl'}, dimensions={0} | all-to-all | bytes 589824 | tf_op jit(solution)/shard_map/all_to_all | solution.py:434
  76.8 1.6 copy-done.13
  78.3 7.1 %near.1 = (bf16[4,2,4,256,128]{4,3,2,1,0:T(8,128)(2,1)}, bf16[4,256,128]{2,1,0:T(8,128)(2,1)S(1)}, bf16[4,256,128]{2,1,0:T(8,128)(2,1)S(1)}, f32[2,4,8,128]{3,2,1,0:T(8,128)S(1)}) custom-call(bf16[4,2,4,256,128]{4,3,2,1,0:T(8,128)(2,1)S(1)} %bitcast.27, bf16[2,4,528,128]{3,2,1,0:T(8,128)(2,1)S(1)} %get-tuple-element.17.packed, ...), custom_call_target="tpu_custom_call" | custom-call | flops 1610612736 | bytes 6000000 | tf_op jit(solution)/shard_map/near/pallas_call | solution.py:233
  85.4 0.7 copy-done.7
  86.1 0.7 copy-done.9
  86.9 9.8 %all_to_all.22.told = f32[8,8,128]{2,1,0:T(8,128)S(1)} all-to-all(f32[8,8,128]{2,1,0:T(8,128)S(1)} %bitcast.24), channel_id=1, replica_groups=mesh['y'=4,'x'=4,'zl'=2,'zh'=4,'core'=2] {'x','zl'}, dimensions={0} | all-to-all | bytes 65536 | tf_op jit(solution)/shard_map/all_to_all | solution.py:434
  96.6 1.7 %copy-done.15 = bf16[4,1152,256]{2,1,0:T(8,128)(2,1)S(1)} copy-done((bf16[4,1152,256]{2,1,0:T(8,128)(2,1)S(1)}, bf16[4,1152,256]{2,1,0:T(8,128)(2,1)}, u32[]{:S(2)}) %copy-start.15) | copy-done | bytes 2359320
  98.3 2.8 %far_backward.1 = (bf16[8,384,128]{2,1,0:T(8,128)(2,1)S(1)}, bf16[8,256,128]{2,1,0:T(8,128)(2,1)S(1)}) custom-call(bf16[8,528,128]{2,1,0:T(8,128)(2,1)S(1)} %all_to_all.20.mine, bf16[8,272,128]{2,1,0:T(8,128)(2,1)S(1)} %collective-permute-done.2.past, bf16[4,1152,256]{2,1,0:T(8,128)(2,1)S(1)} %copy-done.15, f32[8,8,128]{2,1,0:T(8,128)S(1)} %all_to_all.22.told), custom_call_target="tpu_custom_call" | custom-call | flops 1207959552 | bytes 6000000 | tf_op jit(solution)/shard_map/far_backward/pallas_call | solution.py:310
  101.1 2.4 %collective-permute-start.4 = (bf16[8,256,128]{2,1,0:T(8,128)(2,1)S(1)}, bf16[8,256,128]{2,1,0:T(8,128)(2,1)S(1)}, u32[]{:S(2)}, u32[]{:S(2)}) collective-permute-start(bf16[8,256,128]{2,1,0:T(8,128)(2,1)S(1)} %get-tuple-element.27), channel_id=1, source_target_pairs={{64,0},{128,64},{192,128},{65,1},{129,65},{193,129},{66,2},{130,66... | collective-permute-start | bytes 1572872 | tf_op jit(solution)/shard_map/ppermute | solution.py:460
  103.5 11.9 %collective-permute-done.4 = bf16[8,256,128]{2,1,0:T(8,128)(2,1)S(1)} collective-permute-done((bf16[8,256,128]{2,1,0:T(8,128)(2,1)S(1)}, bf16[8,256,128]{2,1,0:T(8,128)(2,1)S(1)}, u32[]{:S(2)}, u32[]{:S(2)}) %collective-permute-start.4) | collective-permute-done | bytes 524320 | tf_op jit(solution)/shard_map/ppermute | solution.py:460
  115.6 1.0 pad_maximum_fusion
  116.5 3.5 %all-to-all-start.3 = ((bf16[8,384,128]{2,1,0:T(8,128)(2,1)}), bf16[8,384,128]{2,1,0:T(8,128)(2,1)S(1)}, u32[]{:S(2)}, u32[]{:S(2)}) async-start(bf16[8,384,128]{2,1,0:T(8,128)(2,1)} %pad_maximum_fusion), calls=%async_computation.4 | async-start | bytes 1572864 | tf_op jit(solution)/shard_map/all_to_all | solution.py:434
  120.1 0.9 copy-done.10
  121.1 1.1 mix.1
  122.2 24.1 %all-to-all-done.3 = bf16[8,384,128]{2,1,0:T(8,128)(2,1)S(1)} async-done(((bf16[8,384,128]{2,1,0:T(8,128)(2,1)}), bf16[8,384,128]{2,1,0:T(8,128)(2,1)S(1)}, u32[]{:S(2)}, u32[]{:S(2)}) %all-to-all-start.3) | async-done | bytes 786464 | tf_op jit(solution)/shard_map/all_to_all | solution.py:434
  146.8 1.0 copy-done.6
  147.8 0.9 copy-done.8
  148.8 3.0 %unproject.1 = (f32[128,1024]{1,0:T(8,128)S(1)}, bf16[128,1024]{1,0:T(8,128)(2,1)S(1)}) custom-call(s32[1]{0:T(128)} %bitcast.1.core, bf16[4,256,128]{2,1,0:T(8,128)(2,1)S(1)} %copy-done.8, bf16[2,4,256,128]{3,2,1,0:T(8,128)(2,1)S(1)} %bitcast.22, bf16[2,4,384,128]{3,2,1,0:T(8,128)(2,1)S(1)} %bitcast.14, bf16[1024,3072]{1,0:T(8,128)(2,1)} %wv.3, ...), custom_call_target="tpu_custom_call" | custom-call | flops 805306368 | bytes 5000000 | tf_op jit(solution)/shard_map/unproject/pallas_call | solution.py:380
  151.9 0.8 fusion
  152.7 0.7 collective-permute-done.5.other
  153.4 1.0 finish.1
  (38 shorter events, 2.4 us)
Async XLA Ops:
  7.2 69.6 %all-gather.3.cloned.1.call-start = ((), (), s32[]{:S(2)}) async-start(), calls=%async_computation.6 | async-start | bytes 2621440 | tf_op jit(solution)/shard_map/all_gather | solution.py:451
  7.2 1.8 %collective-permute-start.1 = (bf16[128,1024]{1,0:T(8,128)(2,1)}, bf16[128,1024]{1,0:T(8,128)(2,1)S(1)}, u32[]{:S(2)}, u32[]{:S(2)}) collective-permute-start(bf16[128,1024]{1,0:T(8,128)(2,1)} %bitcast.19), channel_id=1, source_target_pairs={{0,1},{1,0},{2,3},{3,2},{4,5},{5,4},{6,7},{7,6},{8,9},{9,8},{10,11... | collective-permute-start | bytes 786440 | tf_op jit(solution)/shard_map/ppermute | solution.py:430
  7.3 2.1 %collective-permute-start = (bf16[128,1024]{1,0:T(8,128)(2,1)}, bf16[128,1024]{1,0:T(8,128)(2,1)S(1)}, u32[]{:S(2)}, u32[]{:S(2)}) collective-permute-start(bf16[128,1024]{1,0:T(8,128)(2,1)} %bitcast.15), channel_id=1, source_target_pairs={{0,1},{1,0},{2,3},{3,2},{4,5},{5,4},{6,7},{7,6},{8,9},{9,8},{10,11... | collective-permute-start | bytes 786440 | tf_op jit(solution)/shard_map/ppermute | solution.py:430
  9.4 1.6 copy-start
  11.0 0.9 copy-start.2
  12.0 0.9 copy-start.4
  12.9 0.7 copy-start.11
  17.5 34.8 %copy-start.16 = (s32[8]{0:T(128)S(1)}, s32[8]{0:T(128)}, u32[]{:S(2)}) copy-start(s32[8]{0:T(128)} %param.11) | copy-start | bytes 100
  17.5 129.3 %reduce-scatter.2.cloned.1.call-start = ((), (), s32[]{:S(2)}) async-start(), calls=%async_computation.5 | async-start | bytes 2621440 | tf_op jit(solution)/shard_map/reduce_scatter | solution.py:457
  48.9 11.4 %collective-permute-start.2 = (bf16[8,272,128]{2,1,0:T(8,128)(2,1)S(1)}, bf16[8,272,128]{2,1,0:T(8,128)(2,1)S(1)}, u32[]{:S(2)}, u32[]{:S(2)}) collective-permute-start(bf16[8,272,128]{2,1,0:T(8,128)(2,1)S(1)} %slice.12), channel_id=1, source_target_pairs={{0,64},{64,128},{128,192},{1,65},{65,129},{129,193},{2,66},{66,130... | collective-permute-start | bytes 1671176 | tf_op jit(solution)/shard_map/ppermute | solution.py:453
  63.7 1.4 copy-start.14
  76.7 1.6 copy-start.13
  85.4 0.7 copy-start.7
  86.1 0.7 copy-start.9
  96.6 1.7 %copy-start.15 = (bf16[4,1152,256]{2,1,0:T(8,128)(2,1)S(1)}, bf16[4,1152,256]{2,1,0:T(8,128)(2,1)}, u32[]{:S(2)}) copy-start(bf16[4,1152,256]{2,1,0:T(8,128)(2,1)} %copy-done.14) | copy-start | bytes 7077892
  101.1 14.4 %collective-permute-start.4 = (bf16[8,256,128]{2,1,0:T(8,128)(2,1)S(1)}, bf16[8,256,128]{2,1,0:T(8,128)(2,1)S(1)}, u32[]{:S(2)}, u32[]{:S(2)}) collective-permute-start(bf16[8,256,128]{2,1,0:T(8,128)(2,1)S(1)} %get-tuple-element.27), channel_id=1, source_target_pairs={{64,0},{128,64},{192,128},{65,1},{129,65},{193,129},{66,2},{130,66... | collective-permute-start | bytes 1572872 | tf_op jit(solution)/shard_map/ppermute | solution.py:460
  103.5 16.6 %copy-start.1 = (bf16[1024,1024]{1,0:T(8,128)(2,1)S(1)}, bf16[1024,1024]{1,0:T(8,128)(2,1)}, u32[]{:S(2)}) copy-start(bf16[1024,1024]{1,0:T(8,128)(2,1)} %wo.3) | copy-start | bytes 6291460
  116.5 29.8 %all-to-all-start.3 = ((bf16[8,384,128]{2,1,0:T(8,128)(2,1)}), bf16[8,384,128]{2,1,0:T(8,128)(2,1)S(1)}, u32[]{:S(2)}, u32[]{:S(2)}) async-start(bf16[8,384,128]{2,1,0:T(8,128)(2,1)} %pad_maximum_fusion), calls=%async_computation.4 | async-start | bytes 1572864 | tf_op jit(solution)/shard_map/all_to_all | solution.py:434
  120.1 1.0 copy-start.10
  122.2 29.6 %collective-permute-start.3 = (bf16[128,1024]{1,0:T(8,128)(2,1)}, bf16[128,1024]{1,0:T(8,128)(2,1)S(1)}, u32[]{:S(2)}, u32[]{:S(2)}) collective-permute-start(bf16[128,1024]{1,0:T(8,128)(2,1)} %get-tuple-element.21), channel_id=1, source_target_pairs={{0,1},{1,0},{2,3},{3,2},{4,5},{5,4},{6,7},{7,6},{8,9},{9,8},{10,11... | collective-permute-start | bytes 786440 | tf_op jit(solution)/shard_map/ppermute | solution.py:430
  146.8 1.0 copy-start.6
  147.8 0.9 copy-start.8
  148.8 3.1 %copy-start.3 = (bf16[1,1,128,1024]{3,2,1,0:T(8,128)(2,1)S(1)}, bf16[1,1,128,1024]{3,2,1,0:T(8,128)(2,1)}, u32[]{:S(2)}) copy-start(bf16[1,1,128,1024]{3,2,1,0:T(8,128)(2,1)} %param.7) | copy-start | bytes 786436
  148.8 4.6 %copy-start.5 = (bf16[1,1,128,1024]{3,2,1,0:T(8,128)(2,1)S(1)}, bf16[1,1,128,1024]{3,2,1,0:T(8,128)(2,1)}, u32[]{:S(2)}) copy-start(bf16[1,1,128,1024]{3,2,1,0:T(8,128)(2,1)} %param.13) | copy-start | bytes 786436
  148.8 4.6 %copy-start.12 = (f32[1024]{0:T(1024)S(1)}, f32[1024]{0:T(1024)}, u32[]{:S(2)}) copy-start(f32[1024]{0:T(1024)} %param.8) | copy-start | bytes 12292
  151.7 1.6 %collective-permute-start.5 = (bf16[128,1024]{1,0:T(8,128)(2,1)S(1)}, bf16[128,1024]{1,0:T(8,128)(2,1)S(1)}, u32[]{:S(2)}, u32[]{:S(2)}) collective-permute-start(bf16[128,1024]{1,0:T(8,128)(2,1)S(1)} %get-tuple-element.29), channel_id=1, source_target_pairs={{0,1},{1,0},{2,3},{3,2},{4,5},{5,4},{6,7},{7,6},{8,9},{9,8},{10,11... | collective-permute-start | bytes 786440 | tf_op jit(solution)/shard_map/ppermute | solution.py:430
Sparse Core Ops, SparseCore 0:
  17.6 58.2 all-gather.2
  87.0 59.7 reduce-scatter.1

commit v2 on v1

v2 whole, which is shorter than its diff:
```python
import math

import jax
import jax.numpy as jnp
from jax import lax
from jax.experimental import pallas as pl
from jax.experimental.pallas import tpu as pltpu
from jax.sharding import Mesh
from jax.sharding import PartitionSpec as P

D = 1024
H = 8
DH = 128
HW = 128
WIN = 8
EPS = 1e-05

HALF = H // 2
PAIR = 2 * HW
GROUP = 8
SCALE = DH ** (-0.5)
SCALE2 = SCALE * math.log2(math.e)
FLOOR = -3.0e38
F32 = jnp.float32
BF16 = jnp.bfloat16
NT = (((1,), (1,)), ((), ()))
VMEM_LIMIT = 20 * 1024 * 1024
STAGE_LIMIT = 48 * 1024 * 1024

Q0, G0, K0, V0, OK0, ROWS = 0, 128, 256, 384, 512, 528
TOKENS = 8 * HW
KEYS = (WIN + 1) * HW


def params(**kw):
    return pltpu.CompilerParams(vmem_limit_bytes=VMEM_LIMIT, **kw)


def mm(a, b):
    return jnp.dot(a, b, preferred_element_type=F32)


def mm_nt(a, b):
    return lax.dot_general(a, b, NT, preferred_element_type=F32)


def turn(a):
    return a.astype(F32).T


VM = pl.BlockSpec(memory_space=pltpu.VMEM)
SM = pl.BlockSpec(memory_space=pltpu.SMEM)
ANY = pl.BlockSpec(memory_space=pltpu.HBM)


def cost(flops, size, exps=0):
    return pl.CostEstimate(flops=flops, bytes_accessed=size, transcendentals=exps)


def stage_kernel(place, tokens, cot, gain, w_qkv, w_out, own, own_cot, own_gain, wq, wk, wv, out, sems):
    core = place[0]
    copies = [
        pltpu.make_async_copy(tokens, own, sems.at[0]),
        pltpu.make_async_copy(cot, own_cot, sems.at[1]),
        pltpu.make_async_copy(gain, own_gain, sems.at[2]),
        pltpu.make_async_copy(
            w_out.at[pl.ds(pl.multiple_of(core * HALF * DH, HALF * DH), HALF * DH), :],
            out,
            sems.at[3],
        ),
    ]
    for part in range(3):
        start = pl.multiple_of(part * D + core * HALF * DH, HALF * DH)
        copies.append(
            pltpu.make_async_copy(
                w_qkv.at[:, pl.ds(start, HALF * DH)], (wq, wk, wv)[part], sems.at[4 + part]
            )
        )
    for copy in copies:
        copy.start()
    for copy in copies:
        copy.wait()


def stage(place, tokens, cot, gain, w_qkv, w_out):
    return pl.pallas_call(
        stage_kernel,
        in_specs=[SM] + [ANY] * 5,
        out_specs=[VM] * 7,
        out_shape=[
            jax.ShapeDtypeStruct((HW, D), BF16),
            jax.ShapeDtypeStruct((HW, D), BF16),
            jax.ShapeDtypeStruct((1, D), F32),
        ]
        + [jax.ShapeDtypeStruct((D, HALF * DH), BF16)] * 3
        + [jax.ShapeDtypeStruct((HALF * DH, D), BF16)],
        scratch_shapes=[pltpu.SemaphoreType.DMA((7,))],
        compiler_params=pltpu.CompilerParams(vmem_limit_bytes=STAGE_LIMIT),
        cost_estimate=cost(0, 9_000_000),
        name="stage",
    )(place, tokens, cot, gain, w_qkv, w_out)


def project_kernel(
    place, valid, own, other, cot_own, cot_other, gain, wq, wk, wv, wo, packed, near0, near1, near2, near3
):
    x = jnp.concatenate([own[...], other[...]], axis=0).astype(F32)
    rinv = lax.rsqrt(jnp.mean(x * x, axis=-1, keepdims=True) + EPS)
    normed = (x * rinv * gain[...]).astype(BF16)
    cot = jnp.concatenate([cot_own[...], cot_other[...]], axis=0)
    flags = jnp.full((ROWS - OK0, DH), valid[0], jnp.int32).astype(F32).astype(BF16)
    for row in (Q0, K0, V0, G0):
        if row == G0:
            got = mm_nt(cot, wo[...]).astype(BF16)
        else:
            got = mm(normed, {Q0: wq, K0: wk, V0: wv}[row][...]).astype(BF16)
        for h in range(HALF):
            for s in range(2):
                packed[h, s, row : row + HW, :] = got[s * HW : (s + 1) * HW, h * DH : (h + 1) * DH]
    for h in range(HALF):
        for s in range(2):
            packed[h, s, OK0:ROWS, :] = flags
    for step, near in enumerate((near0, near1, near2, near3)):
        h = lax.rem(place[2] + step, HALF)
        for s in range(2):
            near[s] = packed[h, s, :OK0, :]


def project(place, valid, own, other, cot_own, cot_other, gain, weights):
    return pl.pallas_call(
        project_kernel,
        in_specs=[SM, SM] + [VM] * 9,
        out_specs=[VM] * 5,
        out_shape=[jax.ShapeDtypeStruct((HALF, 2, ROWS, DH), BF16)]
        + [jax.ShapeDtypeStruct((2, OK0, DH), BF16)] * 4,
        compiler_params=params(),
        cost_estimate=cost(2 * PAIR * D * 4 * HALF * DH, 7_000_000),
        name="project",
    )(place, valid, own, other, cot_own, cot_other, gain, *weights)


def both(block, row):
    return jnp.concatenate([block[0, row : row + HW, :], block[1, row : row + HW, :]], axis=0)


def near_forward_kernel(near0, near1, near2, near3, kept, result, stats, scores):
    blocks = (near0, near1, near2, near3)
    turned = [turn(both(block, V0)).astype(BF16) for block in blocks]
    for g in range(4):
        cols = slice(g * PAIR, (g + 1) * PAIR)
        query = both(blocks[g], Q0)
        grad_t = turn(both(blocks[g], G0))
        peak = jnp.full((1, PAIR), -jnp.inf, F32)
        for z in range(4):
            block = mm_nt(both(blocks[z], K0), query)
            scores[z * PAIR : (z + 1) * PAIR, :] = block
            peak = jnp.maximum(peak, jnp.max(block, axis=0, keepdims=True))
        peak = peak * SCALE2
        total = jnp.zeros((1, PAIR), F32)
        for b in range(8):
            rows = slice(b * HW, (b + 1) * HW)
            block = jnp.exp2(scores[rows, :] * SCALE2 - peak)
            total = total + jnp.sum(block, axis=0, keepdims=True)
            kept[rows, cols] = block.astype(BF16)
        got = jnp.zeros((DH, PAIR), F32)
        for z in range(4):
            got = got + mm(turned[z], kept[z * PAIR : (z + 1) * PAIR, cols])
        result[:, cols] = got
        delta = jnp.sum(got * grad_t, axis=0, keepdims=True)
        told = jnp.concatenate([peak, total, delta, jnp.zeros((1, PAIR), F32)], axis=0)
        stats[2 * g] = told[:, :HW]
        stats[2 * g + 1] = told[:, HW:]


def near_forward(*blocks):
    return pl.pallas_call(
        near_forward_kernel,
        in_specs=[VM] * 4,
        out_specs=[VM] * 3,
        out_shape=[
            jax.ShapeDtypeStruct((TOKENS, TOKENS), BF16),
            jax.ShapeDtypeStruct((DH, TOKENS), F32),
            jax.ShapeDtypeStruct((8, 4, HW), F32),
        ],
        scratch_shapes=[pltpu.VMEM((TOKENS, PAIR), F32)],
        compiler_params=params(),
        cost_estimate=cost(4 * TOKENS * TOKENS * DH, 4_000_000, TOKENS * TOKENS),
        name="near_forward",
    )(*blocks)


def slot_of_near(place, step, s):
    zh = place[2]
    cam = lax.rem(zh + 4 - step, 4)
    return (zh * 2 + s) * 4 + cam


def far_forward_kernel(place, win, mine, past, close, told, kept, result, keys, values_t, scores):
    width = win[place[0] * HALF + place[1]]
    told[...] = jnp.zeros_like(told)
    for step in range(4):
        for s in range(2):
            told[slot_of_near(place, step, s), 0:4, :] = close[2 * step + s]
    for j in range(GROUP):
        keys[j * HW : (j + 1) * HW, :] = past[j, :HW, :]
        keys[(GROUP + j) * HW : (GROUP + j + 1) * HW, :] = mine[j, K0 : K0 + HW, :]
        values_t[:, j * HW : (j + 1) * HW] = turn(past[j, HW : 2 * HW, :]).astype(BF16)
        values_t[:, (GROUP + j) * HW : (GROUP + j + 1) * HW] = turn(
            mine[j, V0 : V0 + HW, :]
        ).astype(BF16)
    for p in range(GROUP // 2):
        query = jnp.concatenate([mine[2 * p, :HW, :], mine[2 * p + 1, :HW, :]], axis=0)
        grad_t = jnp.concatenate(
            [turn(mine[2 * p, G0 : G0 + HW, :]), turn(mine[2 * p + 1, G0 : G0 + HW, :])], axis=1
        )
        peak = jnp.full((1, PAIR), -jnp.inf, F32)
        for b in range(WIN + 1):
            j = 2 * p + b
            if j < GROUP:
                flag = past[j, 2 * HW : 2 * HW + 1, :].astype(F32)
            else:
                flag = mine[j - GROUP, OK0 : OK0 + 1, :].astype(F32)
            lower = jnp.where((flag > 0.5) & (b >= WIN - width) & (b < WIN), 0.0, -jnp.inf)
            upper = jnp.where((flag > 0.5) & (b >= WIN + 1 - width), 0.0, -jnp.inf)
            bias = jnp.concatenate([lower, upper], axis=1)
            block = mm_nt(keys[j * HW : (j + 1) * HW, :], query) + bias
            scores[b * HW : (b + 1) * HW, :] = block
            peak = jnp.maximum(peak, jnp.max(block, axis=0, keepdims=True))
        peak = jnp.maximum(peak * SCALE2, FLOOR)
        total = jnp.zeros((1, PAIR), F32)
        for b in range(WIN + 1):
            block = jnp.exp2(scores[b * HW : (b + 1) * HW, :] * SCALE2 - peak)
            total = total + jnp.sum(block, axis=0, keepdims=True)
            kept[p, b * HW : (b + 1) * HW, :] = block.astype(BF16)
        got = mm(values_t[:, p * PAIR : p * PAIR + KEYS], kept[p])
        result[:, p * PAIR : (p + 1) * PAIR] = got
        delta = jnp.sum(got * grad_t, axis=0, keepdims=True)
        stats = jnp.concatenate([peak, total, delta, jnp.zeros((1, PAIR), F32)], axis=0)
        told[2 * p * 4 + place[1], 4:8, :] = stats[:, :HW]
        told[(2 * p + 1) * 4 + place[1], 4:8, :] = stats[:, HW:]


def far_forward(place, window, mine, past, close):
    return pl.pallas_call(
        far_forward_kernel,
        in_specs=[SM, SM, VM, VM, VM],
        out_specs=[VM] * 3,
        out_shape=[
            jax.ShapeDtypeStruct((32, 8, HW), F32),
            jax.ShapeDtypeStruct((GROUP // 2, KEYS, PAIR), BF16),
            jax.ShapeDtypeStruct((DH, GROUP * HW), F32),
        ],
        scratch_shapes=[
            pltpu.VMEM((2 * GROUP * HW, DH), BF16),
            pltpu.VMEM((DH, 2 * GROUP * HW), BF16),
            pltpu.VMEM((KEYS, PAIR), F32),
        ],
        compiler_params=params(),
        cost_estimate=cost(16 * KEYS * PAIR * DH, 5_000_000, 4 * KEYS * PAIR),
        name="far_forward",
    )(place, window, mine, past, close)


def merge(this, other):
    top = jnp.maximum(this[0:1], other[0:1])
    here = jnp.exp2(this[0:1] - top)
    there = jnp.exp2(other[0:1] - top)
    inverse = 1.0 / (here * this[1:2] + there * other[1:2])
    here = here * inverse
    delta = here * this[2:3] + there * inverse * other[2:3]
    return here, here * delta


def near_backward_kernel(
    place, near0, near1, near2, near3, kept, result, stats, told,
    back0, back1, back2, back3, grads, grad_all, query_all,
):
    blocks = (near0, near1, near2, near3)
    outs = (back0, back1, back2, back3)
    for g in range(4):
        cols = slice(g * PAIR, (g + 1) * PAIR)
        this = jnp.concatenate([stats[2 * g], stats[2 * g + 1]], axis=1)
        other = jnp.concatenate(
            [told[slot_of_near(place, g, s), 4:8, :] for s in range(2)], axis=1
        )
        weight, delta = merge(this, other)
        grad_t = (turn(both(blocks[g], G0)) * weight).astype(BF16)
        grad_all[:, cols] = grad_t
        query_all[cols, :] = both(blocks[g], Q0)
        attended = (result[:, cols] * weight).T.astype(BF16)
        for s in range(2):
            outs[g][s, :HW, :] = attended[s * HW : (s + 1) * HW]
        for z in range(4):
            rows = slice(z * PAIR, (z + 1) * PAIR)
            d_probs = mm(both(blocks[z], V0), grad_t)
            grads[rows, cols] = (kept[rows, cols].astype(F32) * (d_probs - delta)).astype(BF16)
    for z in range(4):
        rows = slice(z * PAIR, (z + 1) * PAIR)
        d_values = mm_nt(kept[rows, :], grad_all[...]).astype(BF16)
        d_keys = (mm(grads[rows, :], query_all[...]) * SCALE).astype(BF16)
        for s in range(2):
            outs[z][s, 2 * HW : 3 * HW, :] = d_keys[s * HW : (s + 1) * HW]
            outs[z][s, 3 * HW :, :] = d_values[s * HW : (s + 1) * HW]
    keys_t = jnp.concatenate([turn(both(block, K0)).astype(BF16) for block in blocks], axis=1)
    for g in range(4):
        cols = slice(g * PAIR, (g + 1) * PAIR)
        d_query = (mm(keys_t, grads[:, cols]) * SCALE).T.astype(BF16)
        for s in range(2):
            outs[g][s, HW : 2 * HW, :] = d_query[s * HW : (s + 1) * HW]


def near_backward(place, blocks, kept, result, stats, told):
    return pl.pallas_call(
        near_backward_kernel,
        in_specs=[SM] + [VM] * 8,
        out_specs=[VM] * 4,
        out_shape=[jax.ShapeDtypeStruct((2, 4 * HW, DH), BF16)] * 4,
        scratch_shapes=[
            pltpu.VMEM((TOKENS, TOKENS), BF16),
            pltpu.VMEM((DH, TOKENS), BF16),
            pltpu.VMEM((TOKENS, DH), BF16),
        ],
        compiler_params=params(),
        cost_estimate=cost(8 * TOKENS * TOKENS * DH, 5_000_000),
        name="near_backward",
    )(place, *blocks, kept, result, stats, told)


def far_backward_kernel(
    place, mine, past, kept, result, sent, told, own, back, keys_t, values, dk, dv, grads
):
    for j in range(GROUP):
        keys_t[:, j * HW : (j + 1) * HW] = turn(past[j, :HW, :]).astype(BF16)
        keys_t[:, (GROUP + j) * HW : (GROUP + j + 1) * HW] = turn(
            mine[j, K0 : K0 + HW, :]
        ).astype(BF16)
        values[j * HW : (j + 1) * HW, :] = past[j, HW : 2 * HW, :]
        values[(GROUP + j) * HW : (GROUP + j + 1) * HW, :] = mine[j, V0 : V0 + HW, :]
    dk[...] = jnp.zeros_like(dk)
    dv[...] = jnp.zeros_like(dv)
    for p in range(GROUP // 2):
        query = jnp.concatenate([mine[2 * p, :HW, :], mine[2 * p + 1, :HW, :]], axis=0)
        grad_t = jnp.concatenate(
            [turn(mine[2 * p, G0 : G0 + HW, :]), turn(mine[2 * p + 1, G0 : G0 + HW, :])], axis=1
        )
        slots = [(2 * p + i) * 4 + place[1] for i in range(2)]
        this = jnp.concatenate([sent[slot, 4:8, :] for slot in slots], axis=1)
        other = jnp.concatenate([told[slot, 0:4, :] for slot in slots], axis=1)
        weight, delta = merge(this, other)
        grad_t = (grad_t * weight).astype(BF16)
        at = p * PAIR
        attended = (result[:, at : at + PAIR] * weight).T.astype(BF16)
        for lo, size in ((0, 384), (384, 384), (768, 384)):
            rows = slice(lo, lo + size)
            spot = slice(at + lo, at + lo + size)
            d_probs = mm(values[spot, :], grad_t)
            block = kept[p, rows, :]
            d_scores = (block.astype(F32) * (d_probs - delta)).astype(BF16)
            grads[rows, :] = d_scores
            dv[spot, :] += mm_nt(block, grad_t)
            dk[spot, :] += mm(d_scores, query)
        d_query = (mm(keys_t[:, at : at + KEYS], grads[...]) * SCALE).T.astype(BF16)
        for i in range(2):
            own[2 * p + i, :HW, :] = attended[i * HW : (i + 1) * HW]
            own[2 * p + i, HW : 2 * HW, :] = d_query[i * HW : (i + 1) * HW]
    for j in range(GROUP):
        early = slice(j * HW, (j + 1) * HW)
        late = slice((GROUP + j) * HW, (GROUP + j + 1) * HW)
        back[j, :HW, :] = (dk[early, :] * SCALE).astype(BF16)
        back[j, HW:, :] = dv[early, :].astype(BF16)
        own[j, 2 * HW : 3 * HW, :] = (dk[late, :] * SCALE).astype(BF16)
        own[j, 3 * HW :, :] = dv[late, :].astype(BF16)


def far_backward(place, mine, past, kept, result, sent, told):
    return pl.pallas_call(
        far_backward_kernel,
        in_specs=[SM] + [VM] * 6,
        out_specs=[VM, VM],
        out_shape=[
            jax.ShapeDtypeStruct((GROUP, 4 * HW, DH), BF16),
            jax.ShapeDtypeStruct((GROUP, 2 * HW, DH), BF16),
        ],
        scratch_shapes=[
            pltpu.VMEM((DH, 2 * GROUP * HW), BF16),
            pltpu.VMEM((2 * GROUP * HW, DH), BF16),
            pltpu.VMEM((2 * GROUP * HW, DH), F32),
            pltpu.VMEM((2 * GROUP * HW, DH), F32),
            pltpu.VMEM((KEYS, PAIR), BF16),
        ],
        compiler_params=params(),
        cost_estimate=cost(32 * KEYS * PAIR * DH, 6_000_000),
        name="far_backward",
    )(place, mine, past, kept, result, sent, told)


def unproject_kernel(place, near0, near1, near2, near3, far, wq, wk, wv, wo, own, other, close):
    for step, near in enumerate((near0, near1, near2, near3)):
        close[lax.rem(place[2] + step, HALF)] = near[...]
    parts = []
    for part in range(4):
        rows = slice(part * HW, (part + 1) * HW)
        pieces = []
        for h in range(HALF):
            away = jnp.concatenate([far[h, 0, rows, :], far[h, 1, rows, :]], axis=0)
            here = jnp.concatenate([close[h, 0, rows, :], close[h, 1, rows, :]], axis=0)
            pieces.append((away.astype(F32) + here.astype(F32)).astype(BF16))
        parts.append(jnp.concatenate(pieces, axis=1))
    mixed = mm(parts[0], wo[...])
    total = mm_nt(parts[1], wq[...]) + mm_nt(parts[2], wk[...]) + mm_nt(parts[3], wv[...])
    own[0] = mixed[:HW]
    own[1] = total[:HW]
    other[0] = mixed[HW:].astype(BF16)
    other[1] = total[HW:].astype(BF16)


def unproject(place, blocks, far, weights):
    return pl.pallas_call(
        unproject_kernel,
        in_specs=[SM] + [VM] * 9,
        out_specs=[VM, VM],
        out_shape=[jax.ShapeDtypeStruct((2, HW, D), F32), jax.ShapeDtypeStruct((2, HW, D), BF16)],
        scratch_shapes=[pltpu.VMEM((HALF, 2, 4 * HW, DH), BF16)],
        compiler_params=params(),
        cost_estimate=cost(2 * PAIR * D * 4 * HALF * DH, 8_000_000),
        name="unproject",
    )(place, *blocks, far, *weights)


def finish_kernel(tokens, cot, gain, own, other, mixed, out):
    x = tokens[...].astype(F32)
    mixed[...] = (x + (own[0] + other[0].astype(F32))).astype(BF16)
    rinv = lax.rsqrt(jnp.mean(x * x, axis=-1, keepdims=True) + EPS)
    scaled = (own[1] + other[1].astype(F32)) * gain[...]
    mean = jnp.mean(scaled * x, axis=-1, keepdims=True)
    grad = rinv * scaled - x * (rinv * rinv * rinv * mean)
    out[...] = (cot[...].astype(F32) + grad).astype(BF16)


def finish(tokens, cot, gain, own, other):
    return pl.pallas_call(
        finish_kernel,
        in_specs=[VM] * 5,
        out_specs=[VM] * 2,
        out_shape=[jax.ShapeDtypeStruct((HW, D), BF16)] * 2,
        compiler_params=params(),
        cost_estimate=cost(HW * D * 10, 3_000_000),
        name="finish",
    )(tokens, cot, gain, own, other)


LANE = ("x", "zl")


def swap(value):
    return lax.ppermute(value, "core", [(0, 1), (1, 0)])


def turn_ring(value, steps):
    return lax.ppermute(value, "zh", [(i, (i + steps) % 4) for i in range(4)])


def exchange(value, axes):
    return lax.all_to_all(value, axes, 0, 0, tiled=True)


def per_device(tokens, gain, w_qkv, w_out, window, valid, cotangent):
    rows = lax.axis_size("y")
    place = jnp.stack(
        [lax.axis_index(axis) for axis in ("core", "x", "zh")]
    ).astype(jnp.int32)
    tokens = tokens.reshape(HW, D)
    cot = cotangent.reshape(HW, D)
    other_tokens = swap(tokens)
    other_cot = swap(cot)
    tokens, cot, gain, *weights = stage(place, tokens, cot, gain.reshape(1, D), w_qkv, w_out)
    packed, *blocks = project(
        place, valid, tokens, other_tokens, cot, other_cot, gain, weights
    )
    blocks = [blocks[0]] + [turn_ring(blocks[step], step) for step in (1, 2, 3)]
    mine = exchange(packed.reshape(2 * HALF, ROWS, DH), LANE)
    past = lax.ppermute(mine[:, K0:, :], "y", [(i, i + 1) for i in range(rows - 1)])
    near_kept, near_result, close = near_forward(*blocks)
    sent, far_kept, far_result = far_forward(place, window, mine, past, close)
    told = exchange(sent, ("x", "zl", "zh"))
    own, back = far_backward(place, mine, past, far_kept, far_result, sent, told)
    back = lax.ppermute(back, "y", [(i + 1, i) for i in range(rows - 1)])
    returned = near_backward(place, blocks, near_kept, near_result, close, told)
    returned = [returned[0]] + [turn_ring(returned[step], -step) for step in (1, 2, 3)]
    summed = (own[:, 2 * HW :, :].astype(F32) + back.astype(F32)).astype(BF16)
    own = jnp.concatenate([own[:, : 2 * HW, :], summed], axis=1)
    far = exchange(own, LANE).reshape(HALF, 2, 4 * HW, DH)
    out_own, out_other = unproject(place, returned, far, weights)
    mixed, d_tokens = finish(tokens, cot, gain, out_own, swap(out_other))
    return mixed.reshape(1, 1, HW, D), d_tokens.reshape(1, 1, HW, D)


def solution(mesh):
    grid = Mesh(mesh.devices.reshape(4, 4, 2, 4, 2), ("y", "x", "zl", "zh", "core"))
    frames, cams = ("y", "x", "zl"), ("zh", "core")
    split = P(frames, cams, None, None)
    return jax.shard_map(
        per_device,
        mesh=grid,
        in_specs=(split, P(), P(), P(), P(), P(frames), split),
        out_specs=(split, split),
        check_vma=False,
    )
```

time: 163 us -> 162 us (level)
  the two profiles are of different devices: /device:TPU:16 before, /device:TPU:43 now
where the time goes in v2:
time: 162 us; the launch traced here: 161 us
  waiting for transfers between devices  52.6 us (32%)
  blocking collectives  38.2 us (24%)
  starting transfers between devices  26.9 us (17%)
  Pallas kernels  21.8 us (13%)
  local copies, waits for them, and re-layouts  19 us (12%)
    ppermute x6, waiting for transfers between devices, turn_ring(): return lax.ppermute(value, 'zh', [(i, (i + steps) % 4) for i in range(4)])  40.2 us
    all_to_all x2, blocking collectives, exchange(): return lax.all_to_all(value, axes, 0, 0, tiled=True)  38.2 us
    unnamed x60, local copies, waits for them, and re-layouts  18.9 us
    ppermute x6, starting transfers between devices, turn_ring(): return lax.ppermute(value, 'zh', [(i, (i + steps) % 4) for i in range(4)])  14.7 us
    ppermute x1, waiting for transfers between devices, per_device(): back = lax.ppermute(back, 'y', [(i + 1, i) for i in range(rows - 1)])  10.8 us
    all_to_all x1, starting transfers between devices, exchange(): return lax.all_to_all(value, axes, 0, 0, tiled=True)  5.52 us
    pallas_call x1, Pallas kernels, far_forward(): pl.pallas_call(far_forward_kernel, in_specs=[SM, SM, VM, VM, VM], out_spe...  3.41 us
    pallas_call x1, Pallas kernels, far_backward(): pl.pallas_call(far_backward_kernel, in_specs=[SM] + [VM] * 6, out_specs=[...  3.38 us
  transfers between devices with their start and end apart: 12, of which 6 were waited for; matrix products, arithmetic and copies ran while one was open for 0% of the time, Pallas kernels for 5%

profile of v2, /device:TPU:43, one launch (start us, length us, event | category | flops | bytes accessed | tf_op | source)
XLA Modules:
  0.0 161.3 jit_solution(7521701453963319067)
XLA Ops:
  2.2 0.9 copy-done.4
  3.2 0.9 copy-done.5
  4.8 2.8 %stage.1 = (bf16[128,1024]{1,0:T(8,128)(2,1)S(1)}, bf16[128,1024]{1,0:T(8,128)(2,1)S(1)}, f32[1,1024]{1,0:T(1,128)S(1)}, bf16[1024,512]{1,0:T(8,128)(2,1)S(1)}, ...) custom-call(s32[3]{0:T(128)S(1)} %pad_add_fusion.place, ...), custom_call_target="tpu_custom_call" | custom-call | bytes 9000000 | tf_op jit(solution)/shard_map/stage/pallas_call | solution.py:86
  7.7 3.1 %project.1 = (bf16[4,2,528,128]{3,2,1,0:T(8,128)(2,1)S(1)}, bf16[2,512,128]{2,1,0:T(8,128)(2,1)S(1)}, bf16[2,512,128]{2,1,0:T(8,128)(2,1)S(1)}, bf16[2,512,128]{2,1,0:T(8,128)(2,1)S(1)}, bf16[2,512,128]{2,1,0:T(8,128)(2,1)S(1)}) custom-call(s32[3]{0:T(128)S(1)} %pad_add_fusion.place, s32[1]{0:T(128)S(6)} %copy.9.valid, ...), custom_call_target="tpu_custom_call" | custom-call | flops 1073741824 | bytes 7000000 | tf_op jit(solution)/shard_map/project/pallas_call | solution.py:130
  10.9 19.0 %all_to_all.15.mine = bf16[8,528,128]{2,1,0:T(8,128)(2,1)S(1)} all-to-all(bf16[8,528,128]{2,1,0:T(8,128)(2,1)S(1)} %bitcast.10), channel_id=1, replica_groups=mesh['y'=4,'x'=4,'zl'=2,'zh'=4,'core'=2] {'x','zl'}, dimensions={0} | all-to-all | bytes 2162688 | tf_op jit(solution)/shard_map/all_to_all | solution.py:464
  29.9 3.2 %collective-permute-start.5 = (bf16[8,272,128]{2,1,0:T(8,128)(2,1)S(1)}, bf16[8,272,128]{2,1,0:T(8,128)(2,1)S(1)}, u32[]{:S(2)}, u32[]{:S(2)}) collective-permute-start(bf16[8,272,128]{2,1,0:T(8,128)(2,1)S(1)} %slice.12), channel_id=1, source_target_pairs={{0,64},{64,128},{128,192},{1,65},{65,129},{129,193},{2,66},{66,130... | collective-permute-start | bytes 1671176 | tf_op jit(solution)/shard_map/ppermute | solution.py:482
  33.1 3.1 %collective-permute-start.2 = (bf16[2,512,128]{2,1,0:T(8,128)(2,1)S(1)}, bf16[2,512,128]{2,1,0:T(8,128)(2,1)S(1)}, u32[]{:S(2)}, u32[]{:S(2)}) collective-permute-start(bf16[2,512,128]{2,1,0:T(8,128)(2,1)S(1)} %get-tuple-element.38), channel_id=1, source_target_pairs={{0,2},{2,4},{4,6},{6,0},{1,3},{3,5},{5,7},{7,1},{8,10},{10,12},{12... | collective-permute-start | bytes 786440 | tf_op jit(solution)/shard_map/ppermute | solution.py:460
  36.2 4.3 %collective-permute-start.3 = (bf16[2,512,128]{2,1,0:T(8,128)(2,1)S(1)}, bf16[2,512,128]{2,1,0:T(8,128)(2,1)S(1)}, u32[]{:S(2)}, u32[]{:S(2)}) collective-permute-start(bf16[2,512,128]{2,1,0:T(8,128)(2,1)S(1)} %get-tuple-element.39), channel_id=1, source_target_pairs={{0,4},{2,6},{4,0},{6,2},{1,5},{3,7},{5,1},{7,3},{8,12},{10,14},{12... | collective-permute-start | bytes 786440 | tf_op jit(solution)/shard_map/ppermute | solution.py:460
  40.5 2.3 %collective-permute-start.4 = (bf16[2,512,128]{2,1,0:T(8,128)(2,1)S(1)}, bf16[2,512,128]{2,1,0:T(8,128)(2,1)S(1)}, u32[]{:S(2)}, u32[]{:S(2)}) collective-permute-start(bf16[2,512,128]{2,1,0:T(8,128)(2,1)S(1)} %get-tuple-element.40), channel_id=1, source_target_pairs={{0,6},{2,0},{4,2},{6,4},{1,7},{3,1},{5,3},{7,5},{8,14},{10,8},{12,... | collective-permute-start | bytes 786440 | tf_op jit(solution)/shard_map/ppermute | solution.py:460
  42.8 17.3 %collective-permute-done.2.near1 = bf16[2,512,128]{2,1,0:T(8,128)(2,1)S(1)} collective-permute-done((bf16[2,512,128]{2,1,0:T(8,128)(2,1)S(1)}, bf16[2,512,128]{2,1,0:T(8,128)(2,1)S(1)}, u32[]{:S(2)}, u32[]{:S(2)}) %collective-permute-start.2) | collective-permute-done | bytes 262176 | tf_op jit(solution)/shard_map/ppermute | solution.py:460
  60.1 2.5 %near_forward.1 = (bf16[1024,1024]{1,0:T(8,128)(2,1)S(1)}, f32[128,1024]{1,0:T(8,128)S(1)}, f32[8,4,128]{2,1,0:T(4,128)S(1)}) custom-call(bf16[2,512,128]{2,1,0:T(8,128)(2,1)S(1)} %get-tuple-element.37.near0, bf16[2,512,128]{2,1,0:T(8,128)(2,1)S(1)} %collective-permute-done.2.near1, bf16[2,512,128]{2,1,0:T(8,128)(2,1)S(1)} %collective-permute-done.3.near2, ...), custom_call_target="tpu_custom_call" | custom-call | flops 536870912 | bytes 4000000 | tf_op jit(solution)/shard_map/near_forward/pallas_call | solution.py:176
  62.6 1.3 copy-done.24
  64.0 3.4 %far_forward.1 = (f32[32,8,128]{2,1,0:T(8,128)S(1)}, bf16[4,1152,256]{2,1,0:T(8,128)(2,1)S(1)}, f32[128,1024]{1,0:T(8,128)S(1)}) custom-call(s32[3]{0:T(128)S(1)} %pad_add_fusion.place, s32[8]{0:T(128)S(1)} %copy-done.23, bf16[8,528,128]{2,1,0:T(8,128)(2,1)S(1)} %all_to_all.15.mine, bf16[8,272,128]{2,1,0:T(8,128)(2,1)S(1)} %collective-permute-done.5.past, ...), custom_call_target="tpu_custom_call" | custom-call | flops 603979776 | bytes 5000000 | tf_op jit(solution)/shard_map/far_forward/pallas_call | solution.py:244
  67.4 19.2 %all_to_all.16.told = f32[32,8,128]{2,1,0:T(8,128)S(1)} all-to-all(f32[32,8,128]{2,1,0:T(8,128)S(1)} %get-tuple-element.45.sent), channel_id=1, replica_groups=mesh['y'=4,'x'=4,'zl'=2,'zh'=4,'core'=2] {'x','zl','zh'}, dimensions={0} | all-to-all | bytes 262144 | tf_op jit(solution)/shard_map/all_to_all | solution.py:464
  86.6 3.4 %far_backward.1 = (bf16[8,512,128]{2,1,0:T(8,128)(2,1)S(1)}, bf16[8,256,128]{2,1,0:T(8,128)(2,1)S(1)}) custom-call(s32[3]{0:T(128)S(1)} %pad_add_fusion.place, bf16[8,528,128]{2,1,0:T(8,128)(2,1)S(1)} %all_to_all.15.mine, bf16[8,272,128]{2,1,0:T(8,128)(2,1)S(1)} %collective-permute-done.5.past, bf16[4,1152,256]{2,1,0:T(8,128)(2,1)S(1)} %get-tuple-element.50.kept, ...), custom_call_target="tpu_custom_call" | custom-call | flops 1207959552 | bytes 6000000 | tf_op jit(solution)/shard_map/far_backward/pallas_call | solution.py:376
  90.0 2.0 %collective-permute-start.9 = (bf16[8,256,128]{2,1,0:T(8,128)(2,1)S(1)}, bf16[8,256,128]{2,1,0:T(8,128)(2,1)S(1)}, u32[]{:S(2)}, u32[]{:S(2)}) collective-permute-start(bf16[8,256,128]{2,1,0:T(8,128)(2,1)S(1)} %get-tuple-element.53), channel_id=1, source_target_pairs={{64,0},{128,64},{192,128},{65,1},{129,65},{193,129},{66,2},{130,66... | collective-permute-start | bytes 1572872 | tf_op jit(solution)/shard_map/ppermute | solution.py:487
  92.1 10.8 %collective-permute-done.9 = bf16[8,256,128]{2,1,0:T(8,128)(2,1)S(1)} collective-permute-done((bf16[8,256,128]{2,1,0:T(8,128)(2,1)S(1)}, bf16[8,256,128]{2,1,0:T(8,128)(2,1)S(1)}, u32[]{:S(2)}, u32[]{:S(2)}) %collective-permute-start.9) | collective-permute-done | bytes 524320 | tf_op jit(solution)/shard_map/ppermute | solution.py:487
  103.0 1.1 pad_maximum_fusion
  104.1 5.5 %all-to-all-start.2 = ((bf16[8,512,128]{2,1,0:T(8,128)(2,1)}), bf16[8,512,128]{2,1,0:T(8,128)(2,1)}, u32[]{:S(2)}, u32[]{:S(2)}) async-start(bf16[8,512,128]{2,1,0:T(8,128)(2,1)} %pad_maximum_fusion), calls=%async_computation.2 | async-start | bytes 2097152 | tf_op jit(solution)/shard_map/all_to_all | solution.py:464
  110.6 0.9 copy-done.18
  113.4 1.6 copy-done.25
  115.0 1.0 copy-done.27
  116.8 2.9 %near_backward.1 = (bf16[2,512,128]{2,1,0:T(8,128)(2,1)S(1)}, bf16[2,512,128]{2,1,0:T(8,128)(2,1)S(1)}, bf16[2,512,128]{2,1,0:T(8,128)(2,1)S(1)}, bf16[2,512,128]{2,1,0:T(8,128)(2,1)S(1)}) custom-call(s32[3]{0:T(128)S(1)} %pad_add_fusion.place, bf16[2,512,128]{2,1,0:T(8,128)(2,1)S(1)} %copy-done.16, bf16[2,512,128]{2,1,0:T(8,128)(2,1)S(1)} %copy-done.18, ...), custom_call_target="tpu_custom_call" | custom-call | flops 1073741824 | bytes 5000000 | tf_op jit(solution)/shard_map/near_backward/pallas_call | solution.py:313
  120.4 1.3 collective-permute-start.6
  121.7 3.7 %collective-permute-start.7 = (bf16[2,512,128]{2,1,0:T(8,128)(2,1)S(1)}, bf16[2,512,128]{2,1,0:T(8,128)(2,1)S(1)}, u32[]{:S(2)}, u32[]{:S(2)}) collective-permute-start(bf16[2,512,128]{2,1,0:T(8,128)(2,1)S(1)} %get-tuple-element.48), channel_id=1, source_target_pairs={{0,4},{2,6},{4,0},{6,2},{1,5},{3,7},{5,1},{7,3},{8,12},{10,14},{12... | collective-permute-start | bytes 786440 | tf_op jit(solution)/shard_map/ppermute | solution.py:460
  125.4 4.7 %collective-permute-done.6.near1 = bf16[2,512,128]{2,1,0:T(8,128)(2,1)S(1)} collective-permute-done((bf16[2,512,128]{2,1,0:T(8,128)(2,1)S(1)}, bf16[2,512,128]{2,1,0:T(8,128)(2,1)S(1)}, u32[]{:S(2)}, u32[]{:S(2)}) %collective-permute-start.6) | collective-permute-done | bytes 262176 | tf_op jit(solution)/shard_map/ppermute | solution.py:460
  130.9 15.2 %collective-permute-done.7.near2 = bf16[2,512,128]{2,1,0:T(8,128)(2,1)S(1)} collective-permute-done((bf16[2,512,128]{2,1,0:T(8,128)(2,1)S(1)}, bf16[2,512,128]{2,1,0:T(8,128)(2,1)S(1)}, u32[]{:S(2)}, u32[]{:S(2)}) %collective-permute-start.7) | collective-permute-done | bytes 262176 | tf_op jit(solution)/shard_map/ppermute | solution.py:460
  146.8 3.0 %collective-permute-done.8.near3 = bf16[2,512,128]{2,1,0:T(8,128)(2,1)S(1)} collective-permute-done((bf16[2,512,128]{2,1,0:T(8,128)(2,1)S(1)}, bf16[2,512,128]{2,1,0:T(8,128)(2,1)S(1)}, u32[]{:S(2)}, u32[]{:S(2)}) %collective-permute-start.8) | collective-permute-done | bytes 262176 | tf_op jit(solution)/shard_map/ppermute | solution.py:460
  150.5 1.2 copy-done.1
  155.5 2.6 %unproject.1 = (f32[2,128,1024]{2,1,0:T(8,128)S(1)}, bf16[2,128,1024]{2,1,0:T(8,128)(2,1)S(1)}) custom-call(s32[3]{0:T(128)S(1)} %pad_add_fusion.place, bf16[2,512,128]{2,1,0:T(8,128)(2,1)S(1)} %copy-done.7, bf16[2,512,128]{2,1,0:T(8,128)(2,1)S(1)} %copy-done.9, bf16[2,512,128]{2,1,0:T(8,128)(2,1)S(1)} %copy-done.11, bf16[2,512,128]{2,1,0:T(8,128)(2,1)S(1)} %copy-done.13, ...), custom_call_target="tpu_custom_call" | custom-call | flops 1073741824 | bytes 8000000 | tf_op jit(solution)/shard_map/unproject/pallas_call | solution.py:418
  158.7 1.5 collective-permute-done.10.other
  160.2 1.0 finish.1
  (67 shorter events, 12.7 us)
Async XLA Ops:
  0.6 7.1 %collective-permute-start = (bf16[128,1024]{1,0:T(8,128)(2,1)}, bf16[128,1024]{1,0:T(8,128)(2,1)}, u32[]{:S(2)}, u32[]{:S(2)}) collective-permute-start(bf16[128,1024]{1,0:T(8,128)(2,1)} %bitcast.11), channel_id=1, source_target_pairs={{0,1},{1,0},{2,3},{3,2},{4,5},{5,4},{6,7},{7,6},{8,9},{9,8},{10,11... | collective-permute-start | bytes 786440 | tf_op jit(solution)/shard_map/ppermute | solution.py:456
  1.4 6.3 %collective-permute-start.1 = (bf16[128,1024]{1,0:T(8,128)(2,1)}, bf16[128,1024]{1,0:T(8,128)(2,1)}, u32[]{:S(2)}, u32[]{:S(2)}) collective-permute-start(bf16[128,1024]{1,0:T(8,128)(2,1)} %bitcast.13), channel_id=1, source_target_pairs={{0,1},{1,0},{2,3},{3,2},{4,5},{5,4},{6,7},{7,6},{8,9},{9,8},{10,11... | collective-permute-start | bytes 786440 | tf_op jit(solution)/shard_map/ppermute | solution.py:456
  2.2 1.0 copy-start.4
  3.2 0.9 copy-start.5
  7.7 3.2 %copy-start = (bf16[512,1024]{1,0:T(8,128)(2,1)}, bf16[512,1024]{1,0:T(8,128)(2,1)S(1)}, u32[]{:S(2)}) copy-start(bf16[512,1024]{1,0:T(8,128)(2,1)S(1)} %get-tuple-element.36.wo) | copy-start | bytes 3145732
  7.7 3.2 %copy-start.2 = (bf16[128,1024]{1,0:T(8,128)(2,1)}, bf16[128,1024]{1,0:T(8,128)(2,1)S(1)}, u32[]{:S(2)}) copy-start(bf16[128,1024]{1,0:T(8,128)(2,1)S(1)} %get-tuple-element.31.cot_own.cot) | copy-start | bytes 786436
  10.9 51.8 %copy-start.15 = (bf16[2,512,128]{2,1,0:T(8,128)(2,1)}, bf16[2,512,128]{2,1,0:T(8,128)(2,1)S(1)}, u32[]{:S(2)}) copy-start(bf16[2,512,128]{2,1,0:T(8,128)(2,1)S(1)} %get-tuple-element.37.near0) | copy-start | bytes 786436
  10.9 53.1 %copy-start.23 = (s32[8]{0:T(128)S(1)}, s32[8]{0:T(128)}, u32[]{:S(2)}) copy-start(s32[8]{0:T(128)} %win.1) | copy-start | bytes 100
  29.9 34.0 %collective-permute-start.5 = (bf16[8,272,128]{2,1,0:T(8,128)(2,1)S(1)}, bf16[8,272,128]{2,1,0:T(8,128)(2,1)S(1)}, u32[]{:S(2)}, u32[]{:S(2)}) collective-permute-start(bf16[8,272,128]{2,1,0:T(8,128)(2,1)S(1)} %slice.12), channel_id=1, source_target_pairs={{0,64},{64,128},{128,192},{1,65},{65,129},{129,193},{2,66},{66,130... | collective-permute-start | bytes 1671176 | tf_op jit(solution)/shard_map/ppermute | solution.py:482
  33.1 26.9 %collective-permute-start.2 = (bf16[2,512,128]{2,1,0:T(8,128)(2,1)S(1)}, bf16[2,512,128]{2,1,0:T(8,128)(2,1)S(1)}, u32[]{:S(2)}, u32[]{:S(2)}) collective-permute-start(bf16[2,512,128]{2,1,0:T(8,128)(2,1)S(1)} %get-tuple-element.38), channel_id=1, source_target_pairs={{0,2},{2,4},{4,6},{6,0},{1,3},{3,5},{5,7},{7,1},{8,10},{10,12},{12... | collective-permute-start | bytes 786440 | tf_op jit(solution)/shard_map/ppermute | solution.py:460
  36.2 23.9 %collective-permute-start.3 = (bf16[2,512,128]{2,1,0:T(8,128)(2,1)S(1)}, bf16[2,512,128]{2,1,0:T(8,128)(2,1)S(1)}, u32[]{:S(2)}, u32[]{:S(2)}) collective-permute-start(bf16[2,512,128]{2,1,0:T(8,128)(2,1)S(1)} %get-tuple-element.39), channel_id=1, source_target_pairs={{0,4},{2,6},{4,0},{6,2},{1,5},{3,7},{5,1},{7,3},{8,12},{10,14},{12... | collective-permute-start | bytes 786440 | tf_op jit(solution)/shard_map/ppermute | solution.py:460
  40.5 19.6 %collective-permute-start.4 = (bf16[2,512,128]{2,1,0:T(8,128)(2,1)S(1)}, bf16[2,512,128]{2,1,0:T(8,128)(2,1)S(1)}, u32[]{:S(2)}, u32[]{:S(2)}) collective-permute-start(bf16[2,512,128]{2,1,0:T(8,128)(2,1)S(1)} %get-tuple-element.40), channel_id=1, source_target_pairs={{0,6},{2,0},{4,2},{6,4},{1,7},{3,1},{5,3},{7,5},{8,14},{10,8},{12,... | collective-permute-start | bytes 786440 | tf_op jit(solution)/shard_map/ppermute | solution.py:460
  60.1 3.9 %copy-start.17 = (bf16[2,512,128]{2,1,0:T(8,128)(2,1)}, bf16[2,512,128]{2,1,0:T(8,128)(2,1)S(1)}, u32[]{:S(2)}) copy-start(bf16[2,512,128]{2,1,0:T(8,128)(2,1)S(1)} %collective-permute-done.2.near1) | copy-start | bytes 786436
  60.1 3.9 %copy-start.19 = (bf16[2,512,128]{2,1,0:T(8,128)(2,1)}, bf16[2,512,128]{2,1,0:T(8,128)(2,1)S(1)}, u32[]{:S(2)}) copy-start(bf16[2,512,128]{2,1,0:T(8,128)(2,1)S(1)} %collective-permute-done.3.near2) | copy-start | bytes 786436
  60.1 3.9 %copy-start.21 = (bf16[2,512,128]{2,1,0:T(8,128)(2,1)}, bf16[2,512,128]{2,1,0:T(8,128)(2,1)S(1)}, u32[]{:S(2)}) copy-start(bf16[2,512,128]{2,1,0:T(8,128)(2,1)S(1)} %collective-permute-done.4.near3) | copy-start | bytes 786436
  62.6 1.3 copy-start.24
  64.0 22.6 %copy-start.28 = (f32[8,4,128]{2,1,0:T(4,128)}, f32[8,4,128]{2,1,0:T(4,128)S(1)}, u32[]{:S(2)}) copy-start(f32[8,4,128]{2,1,0:T(4,128)S(1)} %get-tuple-element.43.close.stats) | copy-start | bytes 49156
  64.0 26.0 %copy-start.26 = (f32[128,1024]{1,0:T(8,128)}, f32[128,1024]{1,0:T(8,128)S(1)}, u32[]{:S(2)}) copy-start(f32[128,1024]{1,0:T(8,128)S(1)} %get-tuple-element.42.result) | copy-start | bytes 1572868
  90.0 12.9 %collective-permute-start.9 = (bf16[8,256,128]{2,1,0:T(8,128)(2,1)S(1)}, bf16[8,256,128]{2,1,0:T(8,128)(2,1)S(1)}, u32[]{:S(2)}, u32[]{:S(2)}) collective-permute-start(bf16[8,256,128]{2,1,0:T(8,128)(2,1)S(1)} %get-tuple-element.53), channel_id=1, source_target_pairs={{64,0},{128,64},{192,128},{65,1},{129,65},{193,129},{66,2},{130,66... | collective-permute-start | bytes 1572872 | tf_op jit(solution)/shard_map/ppermute | solution.py:487
  104.1 46.4 %all-to-all-start.2 = ((bf16[8,512,128]{2,1,0:T(8,128)(2,1)}), bf16[8,512,128]{2,1,0:T(8,128)(2,1)}, u32[]{:S(2)}, u32[]{:S(2)}) async-start(bf16[8,512,128]{2,1,0:T(8,128)(2,1)} %pad_maximum_fusion), calls=%async_computation.2 | async-start | bytes 2097152 | tf_op jit(solution)/shard_map/all_to_all | solution.py:464
  109.6 0.9 copy-start.16
  110.6 0.9 copy-start.18
  111.5 0.9 copy-start.20
  112.5 0.9 copy-start.22
  113.4 1.6 copy-start.25
  115.0 1.0 copy-start.27
  120.4 9.7 %collective-permute-start.6 = (bf16[2,512,128]{2,1,0:T(8,128)(2,1)S(1)}, bf16[2,512,128]{2,1,0:T(8,128)(2,1)S(1)}, u32[]{:S(2)}, u32[]{:S(2)}) collective-permute-start(bf16[2,512,128]{2,1,0:T(8,128)(2,1)S(1)} %get-tuple-element.47), channel_id=1, source_target_pairs={{0,6},{2,0},{4,2},{6,4},{1,7},{3,1},{5,3},{7,5},{8,14},{10,8},{12,... | collective-permute-start | bytes 786440 | tf_op jit(solution)/shard_map/ppermute | solution.py:460
  121.7 24.4 %collective-permute-start.7 = (bf16[2,512,128]{2,1,0:T(8,128)(2,1)S(1)}, bf16[2,512,128]{2,1,0:T(8,128)(2,1)S(1)}, u32[]{:S(2)}, u32[]{:S(2)}) collective-permute-start(bf16[2,512,128]{2,1,0:T(8,128)(2,1)S(1)} %get-tuple-element.48), channel_id=1, source_target_pairs={{0,4},{2,6},{4,0},{6,2},{1,5},{3,7},{5,1},{7,3},{8,12},{10,14},{12... | collective-permute-start | bytes 786440 | tf_op jit(solution)/shard_map/ppermute | solution.py:460
  125.4 24.3 %collective-permute-start.8 = (bf16[2,512,128]{2,1,0:T(8,128)(2,1)S(1)}, bf16[2,512,128]{2,1,0:T(8,128)(2,1)S(1)}, u32[]{:S(2)}, u32[]{:S(2)}) collective-permute-start(bf16[2,512,128]{2,1,0:T(8,128)(2,1)S(1)} %get-tuple-element.49), channel_id=1, source_target_pairs={{0,2},{2,4},{4,6},{6,0},{1,3},{3,5},{5,7},{7,1},{8,10},{10,12},{12... | collective-permute-start | bytes 786440 | tf_op jit(solution)/shard_map/ppermute | solution.py:460
  150.5 1.2 copy-start.1
  155.5 4.7 %copy-start.3 = (bf16[128,1024]{1,0:T(8,128)(2,1)S(1)}, bf16[128,1024]{1,0:T(8,128)(2,1)}, u32[]{:S(2)}) copy-start(bf16[128,1024]{1,0:T(8,128)(2,1)} %copy-done.2) | copy-start | bytes 786436
  158.1 2.1 %collective-permute-start.10 = (bf16[2,128,1024]{2,1,0:T(8,128)(2,1)S(1)}, bf16[2,128,1024]{2,1,0:T(8,128)(2,1)S(1)}, u32[]{:S(2)}, u32[]{:S(2)}) collective-permute-start(bf16[2,128,1024]{2,1,0:T(8,128)(2,1)S(1)} %get-tuple-element.55), channel_id=1, source_target_pairs={{0,1},{1,0},{2,3},{3,2},{4,5},{5,4},{6,7},{7,6},{8,9},{9,8},{10,11... | collective-permute-start | bytes 1572872 | tf_op jit(solution)/shard_map/ppermute | solution.py:456
  (10 other events, 8.0 us)

commit v3 on v2

--- a/solution.py
+++ b/solution.py
@@ -184,7 +184,7 @@
         ],
         scratch_shapes=[pltpu.VMEM((TOKENS, PAIR), F32)],
         compiler_params=params(),
-        cost_estimate=cost(4 * TOKENS * TOKENS * DH, 4_000_000, TOKENS * TOKENS),
+        cost_estimate=cost(80 * TOKENS * TOKENS * DH, 4_000_000, TOKENS * TOKENS),
         name="near_forward",
     )(*blocks)
 
@@ -394,6 +394,27 @@
     )(place, mine, past, kept, result, sent, told)
 
 
+def add_back_kernel(own, back, out):
+    out[:, : 2 * HW, :] = own[:, : 2 * HW, :]
+    for j in range(GROUP):
+        out[j, 2 * HW : 4 * HW, :] = (
+            own[j, 2 * HW :, :].astype(F32) + back[j].astype(F32)
+        ).astype(BF16)
+        out[j, 4 * HW :, :] = jnp.zeros((ROWS - 4 * HW, DH), BF16)
+
+
+def add_back(own, back):
+    return pl.pallas_call(
+        add_back_kernel,
+        in_specs=[VM] * 2,
+        out_specs=VM,
+        out_shape=jax.ShapeDtypeStruct((GROUP, ROWS, DH), BF16),
+        compiler_params=params(),
+        cost_estimate=cost(GROUP * 2 * HW * DH, 2_500_000),
+        name="add_back",
+    )(own, back)
+
+
 def unproject_kernel(place, near0, near1, near2, near3, far, wq, wk, wv, wo, own, other, close):
     for step, near in enumerate((near0, near1, near2, near3)):
         close[lax.rem(place[2] + step, HALF)] = near[...]
@@ -486,10 +507,10 @@
     own, back = far_backward(place, mine, past, far_kept, far_result, sent, told)
     back = lax.ppermute(back, "y", [(i + 1, i) for i in range(rows - 1)])
     returned = near_backward(place, blocks, near_kept, near_result, close, told)
+    own, returned = lax.optimization_barrier((own, returned))
     returned = [returned[0]] + [turn_ring(returned[step], -step) for step in (1, 2, 3)]
-    summed = (own[:, 2 * HW :, :].astype(F32) + back.astype(F32)).astype(BF16)
-    own = jnp.concatenate([own[:, : 2 * HW, :], summed], axis=1)
-    far = exchange(own, LANE).reshape(HALF, 2, 4 * HW, DH)
+    own = add_back(own, back)
+    far = exchange(own, LANE).reshape(HALF, 2, ROWS, DH)
     out_own, out_other = unproject(place, returned, far, weights)
     mixed, d_tokens = finish(tokens, cot, gain, out_own, swap(out_other))
     return mixed.reshape(1, 1, HW, D), d_tokens.reshape(1, 1, HW, D)

time: 162 us -> 153 us (0.944)
  the two profiles are of different devices: /device:TPU:43 before, /device:TPU:16 now
where the time goes in v3:
time: 153 us; the launch traced here: 151 us
  waiting for transfers between devices  56.4 us (37%)
  starting transfers between devices  31 us (20%)
  Pallas kernels  23 us (15%)
  blocking collectives  20.4 us (13%)
  local copies, waits for them, and re-layouts  18.6 us (12%)
    ppermute x6, waiting for transfers between devices, turn_ring(): return lax.ppermute(value, 'zh', [(i, (i + steps) % 4) for i in range(4)])  37.2 us
    all_to_all x1, blocking collectives, exchange(): return lax.all_to_all(value, axes, 0, 0, tiled=True)  20.4 us
    unnamed x54, local copies, waits for them, and re-layouts  18.5 us
    ppermute x6, starting transfers between devices, turn_ring(): return lax.ppermute(value, 'zh', [(i, (i + steps) % 4) for i in range(4)])  15.5 us
    all_to_all x2, waiting for transfers between devices, exchange(): return lax.all_to_all(value, axes, 0, 0, tiled=True)  12.7 us
    all_to_all x2, starting transfers between devices, exchange(): return lax.all_to_all(value, axes, 0, 0, tiled=True)  9.28 us
    ppermute x1, waiting for transfers between devices, per_device(): back = lax.ppermute(back, 'y', [(i + 1, i) for i in range(rows - 1)])  4.6 us
    pallas_call x1, Pallas kernels, near_forward(): pl.pallas_call(near_forward_kernel, in_specs=[VM] * 4, out_specs=[VM] * 3...  3.58 us
  transfers between devices with their start and end apart: 13, of which 8 were waited for; matrix products, arithmetic and copies ran while one was open for 0% of the time, Pallas kernels for 7%

profile of v3, /device:TPU:16, one launch (start us, length us, event | category | flops | bytes accessed | tf_op | source)
XLA Modules:
  0.0 150.9 jit_solution(15692144563635882079)
XLA Ops:
  2.0 0.9 copy-done.7
  4.5 2.8 %stage.1 = (bf16[128,1024]{1,0:T(8,128)(2,1)S(1)}, bf16[128,1024]{1,0:T(8,128)(2,1)S(1)}, f32[1,1024]{1,0:T(1,128)S(1)}, bf16[1024,512]{1,0:T(8,128)(2,1)S(1)}, ...) custom-call(s32[3]{0:T(128)S(1)} %pad_add_fusion.place, ...), custom_call_target="tpu_custom_call" | custom-call | bytes 9000000 | tf_op jit(solution)/shard_map/stage/pallas_call | solution.py:86
  7.4 2.2 %project.1 = (bf16[4,2,528,128]{3,2,1,0:T(8,128)(2,1)S(1)}, bf16[2,512,128]{2,1,0:T(8,128)(2,1)S(1)}, bf16[2,512,128]{2,1,0:T(8,128)(2,1)S(1)}, bf16[2,512,128]{2,1,0:T(8,128)(2,1)S(1)}, bf16[2,512,128]{2,1,0:T(8,128)(2,1)S(1)}) custom-call(s32[3]{0:T(128)S(1)} %pad_add_fusion.place, s32[1]{0:T(128)S(6)} %copy.9.valid, ...), custom_call_target="tpu_custom_call" | custom-call | flops 1073741824 | bytes 7000000 | tf_op jit(solution)/shard_map/project/pallas_call | solution.py:130
  9.7 1.0 copy-done.4
  13.5 5.7 %all-to-all-start = ((bf16[8,528,128]{2,1,0:T(8,128)(2,1)}), bf16[8,528,128]{2,1,0:T(8,128)(2,1)S(1)}, u32[]{:S(2)}, u32[]{:S(2)}) async-start(bf16[8,528,128]{2,1,0:T(8,128)(2,1)} %bitcast.11), calls=%async_computation | async-start | bytes 2162688 | tf_op jit(solution)/shard_map/all_to_all | solution.py:485
  19.2 3.3 %collective-permute-start.3 = (bf16[2,512,128]{2,1,0:T(8,128)(2,1)}, bf16[2,512,128]{2,1,0:T(8,128)(2,1)}, u32[]{:S(2)}, u32[]{:S(2)}) collective-permute-start(bf16[2,512,128]{2,1,0:T(8,128)(2,1)} %copy-done.25), channel_id=1, source_target_pairs={{0,2},{2,4},{4,6},{6,0},{1,3},{3,5},{5,7},{7,1},{8,10},{10,12},{12... | collective-permute-start | bytes 786440 | tf_op jit(solution)/shard_map/ppermute | solution.py:481
  22.4 4.5 %collective-permute-start.4 = (bf16[2,512,128]{2,1,0:T(8,128)(2,1)}, bf16[2,512,128]{2,1,0:T(8,128)(2,1)}, u32[]{:S(2)}, u32[]{:S(2)}) collective-permute-start(bf16[2,512,128]{2,1,0:T(8,128)(2,1)} %copy-done.23), channel_id=1, source_target_pairs={{0,4},{2,6},{4,0},{6,2},{1,5},{3,7},{5,1},{7,3},{8,12},{10,14},{12... | collective-permute-start | bytes 786440 | tf_op jit(solution)/shard_map/ppermute | solution.py:481
  27.0 2.6 %collective-permute-start.5 = (bf16[2,512,128]{2,1,0:T(8,128)(2,1)}, bf16[2,512,128]{2,1,0:T(8,128)(2,1)}, u32[]{:S(2)}, u32[]{:S(2)}) collective-permute-start(bf16[2,512,128]{2,1,0:T(8,128)(2,1)} %copy-done.21), channel_id=1, source_target_pairs={{0,6},{2,0},{4,2},{6,4},{1,7},{3,1},{5,3},{7,5},{8,14},{10,8},{12,... | collective-permute-start | bytes 786440 | tf_op jit(solution)/shard_map/ppermute | solution.py:481
  29.6 12.7 %all-to-all-done.mine = bf16[8,528,128]{2,1,0:T(8,128)(2,1)S(1)} async-done(((bf16[8,528,128]{2,1,0:T(8,128)(2,1)}), bf16[8,528,128]{2,1,0:T(8,128)(2,1)S(1)}, u32[]{:S(2)}, u32[]{:S(2)}) %all-to-all-start) | async-done | bytes 1081376 | tf_op jit(solution)/shard_map/all_to_all | solution.py:485
  42.4 3.2 %collective-permute-start.2 = (bf16[8,272,128]{2,1,0:T(8,128)(2,1)S(1)}, bf16[8,272,128]{2,1,0:T(8,128)(2,1)S(1)}, u32[]{:S(2)}, u32[]{:S(2)}) collective-permute-start(bf16[8,272,128]{2,1,0:T(8,128)(2,1)S(1)} %slice.4), channel_id=1, source_target_pairs={{0,64},{64,128},{128,192},{1,65},{65,129},{129,193},{2,66},{66,130... | collective-permute-start | bytes 1671176 | tf_op jit(solution)/shard_map/ppermute | solution.py:503
  45.6 4.5 %collective-permute-done.3.near1 = bf16[2,512,128]{2,1,0:T(8,128)(2,1)} collective-permute-done((bf16[2,512,128]{2,1,0:T(8,128)(2,1)}, bf16[2,512,128]{2,1,0:T(8,128)(2,1)}, u32[]{:S(2)}, u32[]{:S(2)}) %collective-permute-start.3) | collective-permute-done | bytes 262176 | tf_op jit(solution)/shard_map/ppermute | solution.py:481
  50.1 5.8 %collective-permute-done.4.near2 = bf16[2,512,128]{2,1,0:T(8,128)(2,1)} collective-permute-done((bf16[2,512,128]{2,1,0:T(8,128)(2,1)}, bf16[2,512,128]{2,1,0:T(8,128)(2,1)}, u32[]{:S(2)}, u32[]{:S(2)}) %collective-permute-start.4) | collective-permute-done | bytes 262176 | tf_op jit(solution)/shard_map/ppermute | solution.py:481
  55.8 0.9 copy-done.19
  56.8 3.6 %near_forward.1 = (bf16[1024,1024]{1,0:T(8,128)(2,1)S(1)}, f32[128,1024]{1,0:T(8,128)S(1)}, f32[8,4,128]{2,1,0:T(4,128)S(1)}) custom-call(bf16[2,512,128]{2,1,0:T(8,128)(2,1)S(1)} %copy-done.19, bf16[2,512,128]{2,1,0:T(8,128)(2,1)} %collective-permute-done.3.near1, bf16[2,512,128]{2,1,0:T(8,128)(2,1)} %collective-permute-done.4.near2, ...), custom_call_target="tpu_custom_call" | custom-call | flops 10737418240 | bytes 4000000 | tf_op jit(solution)/shard_map/near_forward/pallas_call | solution.py:176
  60.4 3.4 %far_forward.1 = (f32[32,8,128]{2,1,0:T(8,128)S(1)}, bf16[4,1152,256]{2,1,0:T(8,128)(2,1)S(1)}, f32[128,1024]{1,0:T(8,128)S(1)}) custom-call(s32[3]{0:T(128)S(1)} %pad_add_fusion.place, s32[8]{0:T(128)S(1)} %copy-done.26, bf16[8,528,128]{2,1,0:T(8,128)(2,1)S(1)} %all-to-all-done.mine, bf16[8,272,128]{2,1,0:T(8,128)(2,1)S(1)} %collective-permute-done.2.past, ...), custom_call_target="tpu_custom_call" | custom-call | flops 603979776 | bytes 5000000 | tf_op jit(solution)/shard_map/far_forward/pallas_call | solution.py:244
  63.8 20.4 %all_to_all.15.told = f32[32,8,128]{2,1,0:T(8,128)S(1)} all-to-all(f32[32,8,128]{2,1,0:T(8,128)S(1)} %get-tuple-element.50.sent), channel_id=1, replica_groups=mesh['y'=4,'x'=4,'zl'=2,'zh'=4,'core'=2] {'x','zl','zh'}, dimensions={0} | all-to-all | bytes 262144 | tf_op jit(solution)/shard_map/all_to_all | solution.py:485
  84.2 3.4 %far_backward.1 = (bf16[8,512,128]{2,1,0:T(8,128)(2,1)S(1)}, bf16[8,256,128]{2,1,0:T(8,128)(2,1)S(1)}) custom-call(s32[3]{0:T(128)S(1)} %pad_add_fusion.place, bf16[8,528,128]{2,1,0:T(8,128)(2,1)S(1)} %all-to-all-done.mine, bf16[8,272,128]{2,1,0:T(8,128)(2,1)S(1)} %collective-permute-done.2.past, bf16[4,1152,256]{2,1,0:T(8,128)(2,1)S(1)} %get-tuple-element.48.kept, ...), custom_call_target="tpu_custom_call" | custom-call | flops 1207959552 | bytes 6000000 | tf_op jit(solution)/shard_map/far_backward/pallas_call | solution.py:376
  87.6 2.4 %collective-permute-start.9 = (bf16[8,256,128]{2,1,0:T(8,128)(2,1)S(1)}, bf16[8,256,128]{2,1,0:T(8,128)(2,1)S(1)}, u32[]{:S(2)}, u32[]{:S(2)}) collective-permute-start(bf16[8,256,128]{2,1,0:T(8,128)(2,1)S(1)} %get-tuple-element.63), channel_id=1, source_target_pairs={{64,0},{128,64},{192,128},{65,1},{129,65},{193,129},{66,2},{130,66... | collective-permute-start | bytes 1572872 | tf_op jit(solution)/shard_map/ppermute | solution.py:508
  89.9 3.5 %near_backward.1 = (bf16[2,512,128]{2,1,0:T(8,128)(2,1)S(1)}, bf16[2,512,128]{2,1,0:T(8,128)(2,1)S(1)}, bf16[2,512,128]{2,1,0:T(8,128)(2,1)S(1)}, bf16[2,512,128]{2,1,0:T(8,128)(2,1)S(1)}) custom-call(s32[3]{0:T(128)S(1)} %pad_add_fusion.place, bf16[2,512,128]{2,1,0:T(8,128)(2,1)S(1)} %copy-done.19, bf16[2,512,128]{2,1,0:T(8,128)(2,1)} %collective-permute-done.3.near1, ...), custom_call_target="tpu_custom_call" | custom-call | flops 1073741824 | bytes 5000000 | tf_op jit(solution)/shard_map/near_backward/pallas_call | solution.py:313
  96.3 4.6 %collective-permute-done.9.back = bf16[8,256,128]{2,1,0:T(8,128)(2,1)S(1)} collective-permute-done((bf16[8,256,128]{2,1,0:T(8,128)(2,1)S(1)}, bf16[8,256,128]{2,1,0:T(8,128)(2,1)S(1)}, u32[]{:S(2)}, u32[]{:S(2)}) %collective-permute-start.9) | collective-permute-done | bytes 524320 | tf_op jit(solution)/shard_map/ppermute | solution.py:508
  100.9 1.2 add_back.1
  102.0 3.6 %all-to-all-start.2 = ((bf16[8,528,128]{2,1,0:T(8,128)(2,1)}), bf16[8,528,128]{2,1,0:T(8,128)(2,1)S(1)}, u32[]{:S(2)}, u32[]{:S(2)}) async-start(bf16[8,528,128]{2,1,0:T(8,128)(2,1)} %add_back.1), calls=%async_computation.2 | async-start | bytes 2162688 | tf_op jit(solution)/shard_map/all_to_all | solution.py:485
  105.7 1.6 %collective-permute-start.6 = (bf16[2,512,128]{2,1,0:T(8,128)(2,1)}, bf16[2,512,128]{2,1,0:T(8,128)(2,1)S(1)}, u32[]{:S(2)}, u32[]{:S(2)}) collective-permute-start(bf16[2,512,128]{2,1,0:T(8,128)(2,1)} %copy-done.24), channel_id=1, source_target_pairs={{0,6},{2,0},{4,2},{6,4},{1,7},{3,1},{5,3},{7,5},{8,14},{10,8},{12,... | collective-permute-start | bytes 786440 | tf_op jit(solution)/shard_map/ppermute | solution.py:481
  107.2 3.5 %collective-permute-start.7 = (bf16[2,512,128]{2,1,0:T(8,128)(2,1)}, bf16[2,512,128]{2,1,0:T(8,128)(2,1)S(1)}, u32[]{:S(2)}, u32[]{:S(2)}) collective-permute-start(bf16[2,512,128]{2,1,0:T(8,128)(2,1)} %copy-done.22), channel_id=1, source_target_pairs={{0,4},{2,6},{4,0},{6,2},{1,5},{3,7},{5,1},{7,3},{8,12},{10,14},{12... | collective-permute-start | bytes 786440 | tf_op jit(solution)/shard_map/ppermute | solution.py:481
  110.7 2.6 %collective-permute-done.6.near1 = bf16[2,512,128]{2,1,0:T(8,128)(2,1)S(1)} collective-permute-done((bf16[2,512,128]{2,1,0:T(8,128)(2,1)}, bf16[2,512,128]{2,1,0:T(8,128)(2,1)S(1)}, u32[]{:S(2)}, u32[]{:S(2)}) %collective-permute-start.6) | collective-permute-done | bytes 262176 | tf_op jit(solution)/shard_map/ppermute | solution.py:481
  114.0 19.7 %collective-permute-done.7.near2 = bf16[2,512,128]{2,1,0:T(8,128)(2,1)S(1)} collective-permute-done((bf16[2,512,128]{2,1,0:T(8,128)(2,1)}, bf16[2,512,128]{2,1,0:T(8,128)(2,1)S(1)}, u32[]{:S(2)}, u32[]{:S(2)}) %collective-permute-start.7) | collective-permute-done | bytes 262176 | tf_op jit(solution)/shard_map/ppermute | solution.py:481
  134.4 4.7 %collective-permute-done.8.near3 = bf16[2,512,128]{2,1,0:T(8,128)(2,1)S(1)} collective-permute-done((bf16[2,512,128]{2,1,0:T(8,128)(2,1)}, bf16[2,512,128]{2,1,0:T(8,128)(2,1)S(1)}, u32[]{:S(2)}, u32[]{:S(2)}) %collective-permute-start.8) | collective-permute-done | bytes 262176 | tf_op jit(solution)/shard_map/ppermute | solution.py:481
  139.7 1.2 copy-done.1
  141.0 1.2 copy-done.3
  146.0 1.8 %unproject.1 = (f32[2,128,1024]{2,1,0:T(8,128)S(1)}, bf16[2,128,1024]{2,1,0:T(8,128)(2,1)S(1)}) custom-call(s32[3]{0:T(128)S(1)} %pad_add_fusion.place, bf16[2,512,128]{2,1,0:T(8,128)(2,1)S(1)} %copy-done.10, bf16[2,512,128]{2,1,0:T(8,128)(2,1)S(1)} %copy-done.12, bf16[2,512,128]{2,1,0:T(8,128)(2,1)S(1)} %copy-done.14, bf16[2,512,128]{2,1,0:T(8,128)(2,1)S(1)} %copy-done.16, ...), custom_call_target="tpu_custom_call" | custom-call | flops 1073741824 | bytes 8000000 | tf_op jit(solution)/shard_map/unproject/pallas_call | solution.py:439
  147.9 1.9 %collective-permute-done.10.other = bf16[2,128,1024]{2,1,0:T(8,128)(2,1)S(1)} collective-permute-done((bf16[2,128,1024]{2,1,0:T(8,128)(2,1)S(1)}, bf16[2,128,1024]{2,1,0:T(8,128)(2,1)S(1)}, u32[]{:S(2)}, u32[]{:S(2)}) %collective-permute-start.10) | collective-permute-done | bytes 524320 | tf_op jit(solution)/shard_map/ppermute | solution.py:477
  149.8 1.0 finish.1
  (60 shorter events, 14.0 us)
Async XLA Ops:
  0.6 6.8 %collective-permute-start = (bf16[128,1024]{1,0:T(8,128)(2,1)}, bf16[128,1024]{1,0:T(8,128)(2,1)S(1)}, u32[]{:S(2)}, u32[]{:S(2)}) collective-permute-start(bf16[128,1024]{1,0:T(8,128)(2,1)} %bitcast.12), channel_id=1, source_target_pairs={{0,1},{1,0},{2,3},{3,2},{4,5},{5,4},{6,7},{7,6},{8,9},{9,8},{10,11... | collective-permute-start | bytes 786440 | tf_op jit(solution)/shard_map/ppermute | solution.py:477
  0.7 6.7 %collective-permute-start.1 = (bf16[128,1024]{1,0:T(8,128)(2,1)}, bf16[128,1024]{1,0:T(8,128)(2,1)S(1)}, u32[]{:S(2)}, u32[]{:S(2)}) collective-permute-start(bf16[128,1024]{1,0:T(8,128)(2,1)} %bitcast.14), channel_id=1, source_target_pairs={{0,1},{1,0},{2,3},{3,2},{4,5},{5,4},{6,7},{7,6},{8,9},{9,8},{10,11... | collective-permute-start | bytes 786440 | tf_op jit(solution)/shard_map/ppermute | solution.py:477
  2.0 1.0 copy-start.7
  2.9 0.9 copy-start.8
  7.4 2.3 %copy-start = (bf16[1024,512]{1,0:T(8,128)(2,1)}, bf16[1024,512]{1,0:T(8,128)(2,1)S(1)}, u32[]{:S(2)}) copy-start(bf16[1024,512]{1,0:T(8,128)(2,1)S(1)} %get-tuple-element.40.wv) | copy-start | bytes 3145732
  7.4 2.3 %copy-start.2 = (bf16[512,1024]{1,0:T(8,128)(2,1)}, bf16[512,1024]{1,0:T(8,128)(2,1)S(1)}, u32[]{:S(2)}) copy-start(bf16[512,1024]{1,0:T(8,128)(2,1)S(1)} %get-tuple-element.41.wo) | copy-start | bytes 3145732
  7.4 2.3 %copy-start.5 = (bf16[128,1024]{1,0:T(8,128)(2,1)}, bf16[128,1024]{1,0:T(8,128)(2,1)S(1)}, u32[]{:S(2)}) copy-start(bf16[128,1024]{1,0:T(8,128)(2,1)S(1)} %get-tuple-element.36.cot_own.cot) | copy-start | bytes 786436
  9.7 1.0 copy-start.4
  12.1 0.7 copy-start.23
  13.5 28.8 %all-to-all-start = ((bf16[8,528,128]{2,1,0:T(8,128)(2,1)}), bf16[8,528,128]{2,1,0:T(8,128)(2,1)S(1)}, u32[]{:S(2)}, u32[]{:S(2)}) async-start(bf16[8,528,128]{2,1,0:T(8,128)(2,1)} %bitcast.11), calls=%async_computation | async-start | bytes 2162688 | tf_op jit(solution)/shard_map/all_to_all | solution.py:485
  19.2 30.9 %collective-permute-start.3 = (bf16[2,512,128]{2,1,0:T(8,128)(2,1)}, bf16[2,512,128]{2,1,0:T(8,128)(2,1)}, u32[]{:S(2)}, u32[]{:S(2)}) collective-permute-start(bf16[2,512,128]{2,1,0:T(8,128)(2,1)} %copy-done.25), channel_id=1, source_target_pairs={{0,2},{2,4},{4,6},{6,0},{1,3},{3,5},{5,7},{7,1},{8,10},{10,12},{12... | collective-permute-start | bytes 786440 | tf_op jit(solution)/shard_map/ppermute | solution.py:481
  22.4 33.4 %collective-permute-start.4 = (bf16[2,512,128]{2,1,0:T(8,128)(2,1)}, bf16[2,512,128]{2,1,0:T(8,128)(2,1)}, u32[]{:S(2)}, u32[]{:S(2)}) collective-permute-start(bf16[2,512,128]{2,1,0:T(8,128)(2,1)} %copy-done.23), channel_id=1, source_target_pairs={{0,4},{2,6},{4,0},{6,2},{1,5},{3,7},{5,1},{7,3},{8,12},{10,14},{12... | collective-permute-start | bytes 786440 | tf_op jit(solution)/shard_map/ppermute | solution.py:481
  27.0 28.9 %collective-permute-start.5 = (bf16[2,512,128]{2,1,0:T(8,128)(2,1)}, bf16[2,512,128]{2,1,0:T(8,128)(2,1)}, u32[]{:S(2)}, u32[]{:S(2)}) collective-permute-start(bf16[2,512,128]{2,1,0:T(8,128)(2,1)} %copy-done.21), channel_id=1, source_target_pairs={{0,6},{2,0},{4,2},{6,4},{1,7},{3,1},{5,3},{7,5},{8,14},{10,8},{12,... | collective-permute-start | bytes 786440 | tf_op jit(solution)/shard_map/ppermute | solution.py:481
  42.4 18.0 %collective-permute-start.2 = (bf16[8,272,128]{2,1,0:T(8,128)(2,1)S(1)}, bf16[8,272,128]{2,1,0:T(8,128)(2,1)S(1)}, u32[]{:S(2)}, u32[]{:S(2)}) collective-permute-start(bf16[8,272,128]{2,1,0:T(8,128)(2,1)S(1)} %slice.4), channel_id=1, source_target_pairs={{0,64},{64,128},{128,192},{1,65},{65,129},{129,193},{2,66},{66,130... | collective-permute-start | bytes 1671176 | tf_op jit(solution)/shard_map/ppermute | solution.py:503
  55.8 1.0 copy-start.19
  56.8 3.6 %copy-start.26 = (s32[8]{0:T(128)S(1)}, s32[8]{0:T(128)}, u32[]{:S(2)}) copy-start(s32[8]{0:T(128)} %win.1) | copy-start | bytes 100
  87.6 13.3 %collective-permute-start.9 = (bf16[8,256,128]{2,1,0:T(8,128)(2,1)S(1)}, bf16[8,256,128]{2,1,0:T(8,128)(2,1)S(1)}, u32[]{:S(2)}, u32[]{:S(2)}) collective-permute-start(bf16[8,256,128]{2,1,0:T(8,128)(2,1)S(1)} %get-tuple-element.63), channel_id=1, source_target_pairs={{64,0},{128,64},{192,128},{65,1},{129,65},{193,129},{66,2},{130,66... | collective-permute-start | bytes 1572872 | tf_op jit(solution)/shard_map/ppermute | solution.py:508
  94.9 0.7 copy-start.22
  102.0 37.7 %all-to-all-start.2 = ((bf16[8,528,128]{2,1,0:T(8,128)(2,1)}), bf16[8,528,128]{2,1,0:T(8,128)(2,1)S(1)}, u32[]{:S(2)}, u32[]{:S(2)}) async-start(bf16[8,528,128]{2,1,0:T(8,128)(2,1)} %add_back.1), calls=%async_computation.2 | async-start | bytes 2162688 | tf_op jit(solution)/shard_map/all_to_all | solution.py:485
  105.7 7.6 %collective-permute-start.6 = (bf16[2,512,128]{2,1,0:T(8,128)(2,1)}, bf16[2,512,128]{2,1,0:T(8,128)(2,1)S(1)}, u32[]{:S(2)}, u32[]{:S(2)}) collective-permute-start(bf16[2,512,128]{2,1,0:T(8,128)(2,1)} %copy-done.24), channel_id=1, source_target_pairs={{0,6},{2,0},{4,2},{6,4},{1,7},{3,1},{5,3},{7,5},{8,14},{10,8},{12,... | collective-permute-start | bytes 786440 | tf_op jit(solution)/shard_map/ppermute | solution.py:481
  107.2 26.4 %collective-permute-start.7 = (bf16[2,512,128]{2,1,0:T(8,128)(2,1)}, bf16[2,512,128]{2,1,0:T(8,128)(2,1)S(1)}, u32[]{:S(2)}, u32[]{:S(2)}) collective-permute-start(bf16[2,512,128]{2,1,0:T(8,128)(2,1)} %copy-done.22), channel_id=1, source_target_pairs={{0,4},{2,6},{4,0},{6,2},{1,5},{3,7},{5,1},{7,3},{8,12},{10,14},{12... | collective-permute-start | bytes 786440 | tf_op jit(solution)/shard_map/ppermute | solution.py:481
  110.7 28.4 %collective-permute-start.8 = (bf16[2,512,128]{2,1,0:T(8,128)(2,1)}, bf16[2,512,128]{2,1,0:T(8,128)(2,1)S(1)}, u32[]{:S(2)}, u32[]{:S(2)}) collective-permute-start(bf16[2,512,128]{2,1,0:T(8,128)(2,1)} %copy-done.20), channel_id=1, source_target_pairs={{0,2},{2,4},{4,6},{6,0},{1,3},{3,5},{5,7},{7,1},{8,10},{10,12},{12... | collective-permute-start | bytes 786440 | tf_op jit(solution)/shard_map/ppermute | solution.py:481
  113.3 0.7 copy-start.11
  133.6 0.7 copy-start.13
  139.7 1.2 copy-start.1
  141.0 1.2 copy-start.3
  142.2 0.9 copy-start.10
  143.1 0.9 copy-start.12
  144.1 0.9 copy-start.14
  145.0 0.9 copy-start.16
  146.0 3.9 %copy-start.6 = (bf16[128,1024]{1,0:T(8,128)(2,1)S(1)}, bf16[128,1024]{1,0:T(8,128)(2,1)}, u32[]{:S(2)}) copy-start(bf16[128,1024]{1,0:T(8,128)(2,1)} %copy-done.5) | copy-start | bytes 786436
  147.8 2.0 %collective-permute-start.10 = (bf16[2,128,1024]{2,1,0:T(8,128)(2,1)S(1)}, bf16[2,128,1024]{2,1,0:T(8,128)(2,1)S(1)}, u32[]{:S(2)}, u32[]{:S(2)}) collective-permute-start(bf16[2,128,1024]{2,1,0:T(8,128)(2,1)S(1)} %get-tuple-element.65), channel_id=1, source_target_pairs={{0,1},{1,0},{2,3},{3,2},{4,5},{5,4},{6,7},{7,6},{8,9},{9,8},{10,11... | collective-permute-start | bytes 1572872 | tf_op jit(solution)/shard_map/ppermute | solution.py:477
  (8 other events, 5.6 us)

commit v4 on v3

--- a/solution.py
+++ b/solution.py
@@ -485,11 +485,16 @@
     return lax.all_to_all(value, axes, 0, 0, tiled=True)
 
 
+def exchange_alone(value, go):
+    return lax.cond(go, lambda v: exchange(v, LANE), jnp.zeros_like, value)
+
+
 def per_device(tokens, gain, w_qkv, w_out, window, valid, cotangent):
     rows = lax.axis_size("y")
     place = jnp.stack(
         [lax.axis_index(axis) for axis in ("core", "x", "zh")]
     ).astype(jnp.int32)
+    go = window[0] > 0
     tokens = tokens.reshape(HW, D)
     cot = cotangent.reshape(HW, D)
     other_tokens = swap(tokens)
@@ -499,7 +504,7 @@
         place, valid, tokens, other_tokens, cot, other_cot, gain, weights
     )
     blocks = [blocks[0]] + [turn_ring(blocks[step], step) for step in (1, 2, 3)]
-    mine = exchange(packed.reshape(2 * HALF, ROWS, DH), LANE)
+    mine = exchange_alone(packed.reshape(2 * HALF, ROWS, DH), go)
     past = lax.ppermute(mine[:, K0:, :], "y", [(i, i + 1) for i in range(rows - 1)])
     near_kept, near_result, close = near_forward(*blocks)
     sent, far_kept, far_result = far_forward(place, window, mine, past, close)
@@ -510,7 +515,7 @@
     own, returned = lax.optimization_barrier((own, returned))
     returned = [returned[0]] + [turn_ring(returned[step], -step) for step in (1, 2, 3)]
     own = add_back(own, back)
-    far = exchange(own, LANE).reshape(HALF, 2, ROWS, DH)
+    far = exchange_alone(own, go).reshape(HALF, 2, ROWS, DH)
     out_own, out_other = unproject(place, returned, far, weights)
     mixed, d_tokens = finish(tokens, cot, gain, out_own, swap(out_other))
     return mixed.reshape(1, 1, HW, D), d_tokens.reshape(1, 1, HW, D)

time: 153 us -> 150 us (0.980)
  blocking collectives: 20.4 us -> 78.2 us
  waiting for transfers between devices: 56.4 us -> 11.9 us
  local copies, waits for them, and re-layouts: 18.6 us -> 6.63 us
  starting transfers between devices: 31 us -> 22.7 us
  Pallas kernels: 23 us -> 27 us
    all_to_all x1 -> x3, blocking collectives: 20.4 us -> 78.2 us  [exchange(): return lax.all_to_all(value, axes, 0, 0, tiled=True)]
    ppermute x6, waiting for transfers between devices: 37.2 us -> 0.02 us  [turn_ring(): return lax.ppermute(value, 'zh', [(i, (i + steps) % 4) for i in range(4)])]
    unnamed x54 -> x26, local copies, waits for them, and re-layouts: 18.5 us -> 5.49 us
    all_to_all x2 -> x0, waiting for transfers between devices: 12.7 us -> none  [exchange(): return lax.all_to_all(value, axes, 0, 0, tiled=True)]
    all_to_all x2 -> x0, starting transfers between devices: 9.28 us -> none  [exchange(): return lax.all_to_all(value, axes, 0, 0, tiled=True)]
    ppermute x1, waiting for transfers between devices: 0.01 us -> 9.25 us  [per_device(): lax.ppermute(mine[:, K0:, :], 'y', [(i, i + 1) for i in range(rows - 1)])]
    ppermute x1, waiting for transfers between devices: 4.6 us -> 0.69 us  [per_device(): back = lax.ppermute(back, 'y', [(i + 1, i) for i in range(rows - 1)])]
    pallas_call x1, Pallas kernels: 2.24 us -> 4.37 us  [project(): pl.pallas_call(project_kernel, in_specs=[SM, SM] + [VM] * 9, out_specs=[V...]
  transfers between devices with their start and end apart: 13 -> 11, of which waited for: 8 -> 3; matrix products, arithmetic and copies ran while one was open for 0% -> 1% of each run, Pallas kernels for 7% -> 8%
where the time goes in v4:
time: 150 us; the launch traced here: 148 us
  blocking collectives  78.2 us (52%)
  Pallas kernels  27 us (18%)
  starting transfers between devices  22.7 us (15%)
  waiting for transfers between devices  11.9 us (8%)
  local copies, waits for them, and re-layouts  6.63 us (4%)
  between operations  1.51 us (1%)
    all_to_all x3, blocking collectives, exchange(): return lax.all_to_all(value, axes, 0, 0, tiled=True)  78.2 us
    ppermute x6, starting transfers between devices, turn_ring(): return lax.ppermute(value, 'zh', [(i, (i + steps) % 4) for i in range(4)])  16.5 us
    ppermute x1, waiting for transfers between devices, per_device(): lax.ppermute(mine[:, K0:, :], 'y', [(i, i + 1) for i in range(rows - 1)])  9.25 us
    unnamed x26, local copies, waits for them, and re-layouts  5.49 us
    pallas_call x1, Pallas kernels, project(): pl.pallas_call(project_kernel, in_specs=[SM, SM] + [VM] * 9, out_specs=[V...  4.37 us
    pallas_call x1, Pallas kernels, near_backward(): pl.pallas_call(near_backward_kernel, in_specs=[SM] + [VM] * 8, out_specs=...  4.3 us
    pallas_call x1, Pallas kernels, near_forward(): pl.pallas_call(near_forward_kernel, in_specs=[VM] * 4, out_specs=[VM] * 3...  3.67 us
    pallas_call x1, Pallas kernels, far_forward(): pl.pallas_call(far_forward_kernel, in_specs=[SM, SM, VM, VM, VM], out_spe...  3.42 us
  transfers between devices with their start and end apart: 11, of which 3 were waited for; matrix products, arithmetic and copies ran while one was open for 1% of the time, Pallas kernels for 8%

profile of v4, /device:TPU:16, one launch (start us, length us, event | category | flops | bytes accessed | tf_op | source)
XLA Modules:
  0.0 148.0 jit_solution(17784285533238465839)
XLA Ops:
  0.7 0.5 collective-permute-start.1
  2.0 0.9 copy-done.4
  2.9 0.9 copy-done.5
  3.9 0.7 copy-done.8
  4.5 2.8 %stage.1 = (bf16[128,1024]{1,0:T(8,128)(2,1)S(1)}, bf16[128,1024]{1,0:T(8,128)(2,1)S(1)}, f32[1,1024]{1,0:T(1,128)S(1)}, bf16[1024,512]{1,0:T(8,128)(2,1)S(1)}, ...) custom-call(s32[3]{0:T(128)S(1)} %pad_add_fusion.place, ...), custom_call_target="tpu_custom_call" | custom-call | bytes 9000000 | tf_op jit(solution)/shard_map/stage/pallas_call | solution.py:86
  7.4 4.4 %project.1 = (bf16[4,2,528,128]{3,2,1,0:T(8,128)(2,1)}, bf16[2,512,128]{2,1,0:T(8,128)(2,1)S(1)}, bf16[2,512,128]{2,1,0:T(8,128)(2,1)}, bf16[2,512,128]{2,1,0:T(8,128)(2,1)}, bf16[2,512,128]{2,1,0:T(8,128)(2,1)}) custom-call(s32[3]{0:T(128)S(1)} %pad_add_fusion.place, s32[1]{0:T(128)S(6)} %copy.13.valid, bf16[128,1024]{1,0:T(8,128)(2,1)S(1)} %get-tuple-element.45.own.tokens, ...), custom_call_target="tpu_custom_call" | custom-call | flops 1073741824 | bytes 7000000 | tf_op jit(solution)/shard_map/project/pallas_call | solution.py:130
  11.8 0.7 copy-done.9
  12.5 3.3 %collective-permute-start.3 = (bf16[2,512,128]{2,1,0:T(8,128)(2,1)}, bf16[2,512,128]{2,1,0:T(8,128)(2,1)}, u32[]{:S(2)}, u32[]{:S(2)}) collective-permute-start(bf16[2,512,128]{2,1,0:T(8,128)(2,1)} %get-tuple-element.54), channel_id=1, source_target_pairs={{0,2},{2,4},{4,6},{6,0},{1,3},{3,5},{5,7},{7,1},{8,10},{10,12},{12... | collective-permute-start | bytes 786440 | tf_op jit(solution)/shard_map/ppermute | solution.py:481
  15.8 5.4 %collective-permute-start.4 = (bf16[2,512,128]{2,1,0:T(8,128)(2,1)}, bf16[2,512,128]{2,1,0:T(8,128)(2,1)}, u32[]{:S(2)}, u32[]{:S(2)}) collective-permute-start(bf16[2,512,128]{2,1,0:T(8,128)(2,1)} %get-tuple-element.55), channel_id=1, source_target_pairs={{0,4},{2,6},{4,0},{6,2},{1,5},{3,7},{5,1},{7,3},{8,12},{10,14},{12... | collective-permute-start | bytes 786440 | tf_op jit(solution)/shard_map/ppermute | solution.py:481
  21.2 2.6 %collective-permute-start.5 = (bf16[2,512,128]{2,1,0:T(8,128)(2,1)}, bf16[2,512,128]{2,1,0:T(8,128)(2,1)}, u32[]{:S(2)}, u32[]{:S(2)}) collective-permute-start(bf16[2,512,128]{2,1,0:T(8,128)(2,1)} %get-tuple-element.56), channel_id=1, source_target_pairs={{0,6},{2,0},{4,2},{6,4},{1,7},{3,1},{5,3},{7,5},{8,14},{10,8},{12,... | collective-permute-start | bytes 786440 | tf_op jit(solution)/shard_map/ppermute | solution.py:481
  23.9 35.2 %conditional.2 = (bf16[8,528,128]{2,1,0:T(8,128)(2,1)}) conditional(s32[]{:T(128)} %bitcast.8, () %tuple.23, bf16[4,2,528,128]{3,2,1,0:T(8,128)(2,1)} %get-tuple-element.52), branch_computations={%region_0.0_spmd, %region_1.0_spmd} | conditional | bytes 2162696 | solution.py:489
  23.9 35.2 %all_to_all.13 = bf16[8,528,128]{2,1,0:T(8,128)(2,1)} all-to-all(bf16[8,528,128]{2,1,0:T(8,128)(2,1)} %bitcast.19), channel_id=1, replica_groups=mesh['y'=4,'x'=4,'zl'=2,'zh'=4,'core'=2] {'x','zl'}, dimensions={0} | all-to-all | bytes 2162688 | tf_op jit(solution)/shard_map/cond/branch_1_fun/all_to_all | solution.py:485
  59.1 1.1 slice.8
  60.3 3.2 %collective-permute-start.2 = (bf16[8,272,128]{2,1,0:T(8,128)(2,1)S(1)}, bf16[8,272,128]{2,1,0:T(8,128)(2,1)S(1)}, u32[]{:S(2)}, u32[]{:S(2)}) collective-permute-start(bf16[8,272,128]{2,1,0:T(8,128)(2,1)S(1)} %slice.8), channel_id=1, source_target_pairs={{0,64},{64,128},{128,192},{1,65},{65,129},{129,193},{2,66},{66,130... | collective-permute-start | bytes 1671176 | tf_op jit(solution)/shard_map/ppermute | solution.py:508
  63.5 3.7 %near_forward.1 = (bf16[1024,1024]{1,0:T(8,128)(2,1)S(1)}, f32[128,1024]{1,0:T(8,128)S(1)}, f32[8,4,128]{2,1,0:T(4,128)S(1)}) custom-call(bf16[2,512,128]{2,1,0:T(8,128)(2,1)S(1)} %copy-done.10, bf16[2,512,128]{2,1,0:T(8,128)(2,1)} %collective-permute-done.3.near1, bf16[2,512,128]{2,1,0:T(8,128)(2,1)} %collective-permute-done.4.near2, ...), custom_call_target="tpu_custom_call" | custom-call | flops 10737418240 | bytes 4000000 | tf_op jit(solution)/shard_map/near_forward/pallas_call | solution.py:176
  67.2 9.2 %collective-permute-done.2.past = bf16[8,272,128]{2,1,0:T(8,128)(2,1)S(1)} collective-permute-done((bf16[8,272,128]{2,1,0:T(8,128)(2,1)S(1)}, bf16[8,272,128]{2,1,0:T(8,128)(2,1)S(1)}, u32[]{:S(2)}, u32[]{:S(2)}) %collective-permute-start.2) | collective-permute-done | bytes 557088 | tf_op jit(solution)/shard_map/ppermute | solution.py:508
  76.4 3.4 %far_forward.1 = (f32[32,8,128]{2,1,0:T(8,128)S(1)}, bf16[4,1152,256]{2,1,0:T(8,128)(2,1)S(1)}, f32[128,1024]{1,0:T(8,128)S(1)}) custom-call(s32[3]{0:T(128)S(1)} %pad_add_fusion.place, s32[8]{0:T(128)S(1)} %copy-done.11, bf16[8,528,128]{2,1,0:T(8,128)(2,1)S(1)} %copy-done.12, bf16[8,272,128]{2,1,0:T(8,128)(2,1)S(1)} %collective-permute-done.2.past, ...), custom_call_target="tpu_custom_call" | custom-call | flops 603979776 | bytes 5000000 | tf_op jit(solution)/shard_map/far_forward/pallas_call | solution.py:244
  79.9 14.4 %all_to_all.15.told = f32[32,8,128]{2,1,0:T(8,128)S(1)} all-to-all(f32[32,8,128]{2,1,0:T(8,128)S(1)} %get-tuple-element.60.sent), channel_id=1, replica_groups=mesh['y'=4,'x'=4,'zl'=2,'zh'=4,'core'=2] {'x','zl','zh'}, dimensions={0} | all-to-all | bytes 262144 | tf_op jit(solution)/shard_map/all_to_all | solution.py:485
  94.2 3.4 %far_backward.1 = (bf16[8,512,128]{2,1,0:T(8,128)(2,1)S(1)}, bf16[8,256,128]{2,1,0:T(8,128)(2,1)S(1)}) custom-call(s32[3]{0:T(128)S(1)} %pad_add_fusion.place, bf16[8,528,128]{2,1,0:T(8,128)(2,1)S(1)} %copy-done.12, bf16[8,272,128]{2,1,0:T(8,128)(2,1)S(1)} %collective-permute-done.2.past, bf16[4,1152,256]{2,1,0:T(8,128)(2,1)S(1)} %get-tuple-element.58.kept, ...), custom_call_target="tpu_custom_call" | custom-call | flops 1207959552 | bytes 6000000 | tf_op jit(solution)/shard_map/far_backward/pallas_call | solution.py:376
  97.6 2.3 %collective-permute-start.9 = (bf16[8,256,128]{2,1,0:T(8,128)(2,1)S(1)}, bf16[8,256,128]{2,1,0:T(8,128)(2,1)S(1)}, u32[]{:S(2)}, u32[]{:S(2)}) collective-permute-start(bf16[8,256,128]{2,1,0:T(8,128)(2,1)S(1)} %get-tuple-element.73), channel_id=1, source_target_pairs={{64,0},{128,64},{192,128},{65,1},{129,65},{193,129},{66,2},{130,66... | collective-permute-start | bytes 1572872 | tf_op jit(solution)/shard_map/ppermute | solution.py:513
  99.9 4.3 %near_backward.1 = (bf16[2,512,128]{2,1,0:T(8,128)(2,1)S(1)}, bf16[2,512,128]{2,1,0:T(8,128)(2,1)}, bf16[2,512,128]{2,1,0:T(8,128)(2,1)}, bf16[2,512,128]{2,1,0:T(8,128)(2,1)}) custom-call(s32[3]{0:T(128)S(1)} %pad_add_fusion.place, bf16[2,512,128]{2,1,0:T(8,128)(2,1)S(1)} %copy-done.10, bf16[2,512,128]{2,1,0:T(8,128)(2,1)} %collective-permute-done.3.near1, ...), custom_call_target="tpu_custom_call" | custom-call | flops 1073741824 | bytes 5000000 | tf_op jit(solution)/shard_map/near_backward/pallas_call | solution.py:313
  104.2 1.6 %collective-permute-start.6 = (bf16[2,512,128]{2,1,0:T(8,128)(2,1)}, bf16[2,512,128]{2,1,0:T(8,128)(2,1)}, u32[]{:S(2)}, u32[]{:S(2)}) collective-permute-start(bf16[2,512,128]{2,1,0:T(8,128)(2,1)} %get-tuple-element.69), channel_id=1, source_target_pairs={{0,6},{2,0},{4,2},{6,4},{1,7},{3,1},{5,3},{7,5},{8,14},{10,8},{12,... | collective-permute-start | bytes 786440 | tf_op jit(solution)/shard_map/ppermute | solution.py:481
  105.9 3.5 %collective-permute-start.7 = (bf16[2,512,128]{2,1,0:T(8,128)(2,1)}, bf16[2,512,128]{2,1,0:T(8,128)(2,1)}, u32[]{:S(2)}, u32[]{:S(2)}) collective-permute-start(bf16[2,512,128]{2,1,0:T(8,128)(2,1)} %get-tuple-element.70), channel_id=1, source_target_pairs={{0,4},{2,6},{4,0},{6,2},{1,5},{3,7},{5,1},{7,3},{8,12},{10,14},{12... | collective-permute-start | bytes 786440 | tf_op jit(solution)/shard_map/ppermute | solution.py:481
  109.4 0.7 collective-permute-done.9.back
  110.0 1.1 add_back.1
  111.2 28.7 %conditional.3 = (bf16[4,2,528,128]{3,2,1,0:T(8,128)(2,1)}) conditional(s32[]{:T(128)} %bitcast.8, () %tuple.25, bf16[8,528,128]{2,1,0:T(8,128)(2,1)} %add_back.1), branch_computations={%region_2.0_spmd, %region_3.0_spmd} | conditional | bytes 2162696 | solution.py:489
  111.2 28.7 %all_to_all.14 = bf16[8,528,128]{2,1,0:T(8,128)(2,1)} all-to-all(bf16[8,528,128]{2,1,0:T(8,128)(2,1)} %param.3), channel_id=1, replica_groups=mesh['y'=4,'x'=4,'zl'=2,'zh'=4,'core'=2] {'x','zl'}, dimensions={0} | all-to-all | bytes 2162688 | tf_op jit(solution)/shard_map/cond/branch_1_fun/all_to_all | solution.py:485
  139.9 1.2 copy-done.1
  141.1 0.9 copy-done.7
  142.1 2.8 %unproject.1 = (f32[2,128,1024]{2,1,0:T(8,128)S(1)}, bf16[2,128,1024]{2,1,0:T(8,128)(2,1)S(1)}) custom-call(s32[3]{0:T(128)S(1)} %pad_add_fusion.place, bf16[2,512,128]{2,1,0:T(8,128)(2,1)S(1)} %copy-done.7, bf16[2,512,128]{2,1,0:T(8,128)(2,1)} %collective-permute-done.6.near1, bf16[2,512,128]{2,1,0:T(8,128)(2,1)} %collective-permute-done.7.near2, ...), custom_call_target="tpu_custom_call" | custom-call | flops 1073741824 | bytes 8000000 | tf_op jit(solution)/shard_map/unproject/pallas_call | solution.py:439
  145.0 1.9 %collective-permute-done.10.other = bf16[2,128,1024]{2,1,0:T(8,128)(2,1)S(1)} collective-permute-done((bf16[2,128,1024]{2,1,0:T(8,128)(2,1)S(1)}, bf16[2,128,1024]{2,1,0:T(8,128)(2,1)S(1)}, u32[]{:S(2)}, u32[]{:S(2)}) %collective-permute-start.10) | collective-permute-done | bytes 524320 | tf_op jit(solution)/shard_map/ppermute | solution.py:477
  146.9 1.0 finish.1
  (32 shorter events, 0.3 us)
Async XLA Ops:
  0.6 6.8 %collective-permute-start = (bf16[128,1024]{1,0:T(8,128)(2,1)}, bf16[128,1024]{1,0:T(8,128)(2,1)}, u32[]{:S(2)}, u32[]{:S(2)}) collective-permute-start(bf16[128,1024]{1,0:T(8,128)(2,1)} %bitcast.12), channel_id=1, source_target_pairs={{0,1},{1,0},{2,3},{3,2},{4,5},{5,4},{6,7},{7,6},{8,9},{9,8},{10,11... | collective-permute-start | bytes 786440 | tf_op jit(solution)/shard_map/ppermute | solution.py:477
  0.7 6.7 %collective-permute-start.1 = (bf16[128,1024]{1,0:T(8,128)(2,1)}, bf16[128,1024]{1,0:T(8,128)(2,1)}, u32[]{:S(2)}, u32[]{:S(2)}) collective-permute-start(bf16[128,1024]{1,0:T(8,128)(2,1)} %bitcast.14), channel_id=1, source_target_pairs={{0,1},{1,0},{2,3},{3,2},{4,5},{5,4},{6,7},{7,6},{8,9},{9,8},{10,11... | collective-permute-start | bytes 786440 | tf_op jit(solution)/shard_map/ppermute | solution.py:477
  2.0 1.0 copy-start.4
  2.9 0.9 copy-start.5
  3.9 0.7 copy-start.8
  7.4 4.4 %copy-start = (bf16[512,1024]{1,0:T(8,128)(2,1)}, bf16[512,1024]{1,0:T(8,128)(2,1)S(1)}, u32[]{:S(2)}) copy-start(bf16[512,1024]{1,0:T(8,128)(2,1)S(1)} %get-tuple-element.51.wo) | copy-start | bytes 3145732
  7.4 4.4 %copy-start.2 = (bf16[128,1024]{1,0:T(8,128)(2,1)}, bf16[128,1024]{1,0:T(8,128)(2,1)S(1)}, u32[]{:S(2)}) copy-start(bf16[128,1024]{1,0:T(8,128)(2,1)S(1)} %get-tuple-element.46.cot_own.cot) | copy-start | bytes 786436
  7.4 16.4 %copy-start.11 = (s32[8]{0:T(128)S(1)}, s32[8]{0:T(128)}, u32[]{:S(2)}) copy-start(s32[8]{0:T(128)} %win.1) | copy-start | bytes 100
  11.8 0.7 copy-start.9
  12.5 50.9 %collective-permute-start.3 = (bf16[2,512,128]{2,1,0:T(8,128)(2,1)}, bf16[2,512,128]{2,1,0:T(8,128)(2,1)}, u32[]{:S(2)}, u32[]{:S(2)}) collective-permute-start(bf16[2,512,128]{2,1,0:T(8,128)(2,1)} %get-tuple-element.54), channel_id=1, source_target_pairs={{0,2},{2,4},{4,6},{6,0},{1,3},{3,5},{5,7},{7,1},{8,10},{10,12},{12... | collective-permute-start | bytes 786440 | tf_op jit(solution)/shard_map/ppermute | solution.py:481
  15.8 47.6 %collective-permute-start.4 = (bf16[2,512,128]{2,1,0:T(8,128)(2,1)}, bf16[2,512,128]{2,1,0:T(8,128)(2,1)}, u32[]{:S(2)}, u32[]{:S(2)}) collective-permute-start(bf16[2,512,128]{2,1,0:T(8,128)(2,1)} %get-tuple-element.55), channel_id=1, source_target_pairs={{0,4},{2,6},{4,0},{6,2},{1,5},{3,7},{5,1},{7,3},{8,12},{10,14},{12... | collective-permute-start | bytes 786440 | tf_op jit(solution)/shard_map/ppermute | solution.py:481
  21.2 42.2 %collective-permute-start.5 = (bf16[2,512,128]{2,1,0:T(8,128)(2,1)}, bf16[2,512,128]{2,1,0:T(8,128)(2,1)}, u32[]{:S(2)}, u32[]{:S(2)}) collective-permute-start(bf16[2,512,128]{2,1,0:T(8,128)(2,1)} %get-tuple-element.56), channel_id=1, source_target_pairs={{0,6},{2,0},{4,2},{6,4},{1,7},{3,1},{5,3},{7,5},{8,14},{10,8},{12,... | collective-permute-start | bytes 786440 | tf_op jit(solution)/shard_map/ppermute | solution.py:481
  59.1 4.4 %copy-start.10 = (bf16[2,512,128]{2,1,0:T(8,128)(2,1)S(1)}, bf16[2,512,128]{2,1,0:T(8,128)(2,1)}, u32[]{:S(2)}) copy-start(bf16[2,512,128]{2,1,0:T(8,128)(2,1)} %copy-done.9) | copy-start | bytes 786436
  60.3 16.2 %collective-permute-start.2 = (bf16[8,272,128]{2,1,0:T(8,128)(2,1)S(1)}, bf16[8,272,128]{2,1,0:T(8,128)(2,1)S(1)}, u32[]{:S(2)}, u32[]{:S(2)}) collective-permute-start(bf16[8,272,128]{2,1,0:T(8,128)(2,1)S(1)} %slice.8), channel_id=1, source_target_pairs={{0,64},{64,128},{128,192},{1,65},{65,129},{129,193},{2,66},{66,130... | collective-permute-start | bytes 1671176 | tf_op jit(solution)/shard_map/ppermute | solution.py:508
  63.5 12.9 %copy-start.12 = (bf16[8,528,128]{2,1,0:T(8,128)(2,1)S(1)}, bf16[8,528,128]{2,1,0:T(8,128)(2,1)}, u32[]{:S(2)}) copy-start(bf16[8,528,128]{2,1,0:T(8,128)(2,1)} %get-tuple-element.78.mine) | copy-start | bytes 3244036
  97.6 12.4 %collective-permute-start.9 = (bf16[8,256,128]{2,1,0:T(8,128)(2,1)S(1)}, bf16[8,256,128]{2,1,0:T(8,128)(2,1)S(1)}, u32[]{:S(2)}, u32[]{:S(2)}) collective-permute-start(bf16[8,256,128]{2,1,0:T(8,128)(2,1)S(1)} %get-tuple-element.73), channel_id=1, source_target_pairs={{64,0},{128,64},{192,128},{65,1},{129,65},{193,129},{66,2},{130,66... | collective-permute-start | bytes 1572872 | tf_op jit(solution)/shard_map/ppermute | solution.py:513
  104.2 7.0 %copy-start.6 = (bf16[2,512,128]{2,1,0:T(8,128)(2,1)}, bf16[2,512,128]{2,1,0:T(8,128)(2,1)S(1)}, u32[]{:S(2)}) copy-start(bf16[2,512,128]{2,1,0:T(8,128)(2,1)S(1)} %get-tuple-element.68.near0) | copy-start | bytes 786436
  104.2 35.6 %collective-permute-start.6 = (bf16[2,512,128]{2,1,0:T(8,128)(2,1)}, bf16[2,512,128]{2,1,0:T(8,128)(2,1)}, u32[]{:S(2)}, u32[]{:S(2)}) collective-permute-start(bf16[2,512,128]{2,1,0:T(8,128)(2,1)} %get-tuple-element.69), channel_id=1, source_target_pairs={{0,6},{2,0},{4,2},{6,4},{1,7},{3,1},{5,3},{7,5},{8,14},{10,8},{12,... | collective-permute-start | bytes 786440 | tf_op jit(solution)/shard_map/ppermute | solution.py:481
  105.9 34.0 %collective-permute-start.7 = (bf16[2,512,128]{2,1,0:T(8,128)(2,1)}, bf16[2,512,128]{2,1,0:T(8,128)(2,1)}, u32[]{:S(2)}, u32[]{:S(2)}) collective-permute-start(bf16[2,512,128]{2,1,0:T(8,128)(2,1)} %get-tuple-element.70), channel_id=1, source_target_pairs={{0,4},{2,6},{4,0},{6,2},{1,5},{3,7},{5,1},{7,3},{8,12},{10,14},{12... | collective-permute-start | bytes 786440 | tf_op jit(solution)/shard_map/ppermute | solution.py:481
  109.4 30.5 %collective-permute-start.8 = (bf16[2,512,128]{2,1,0:T(8,128)(2,1)}, bf16[2,512,128]{2,1,0:T(8,128)(2,1)}, u32[]{:S(2)}, u32[]{:S(2)}) collective-permute-start(bf16[2,512,128]{2,1,0:T(8,128)(2,1)} %get-tuple-element.71), channel_id=1, source_target_pairs={{0,2},{2,4},{4,6},{6,0},{1,3},{3,5},{5,7},{7,1},{8,10},{10,12},{12... | collective-permute-start | bytes 786440 | tf_op jit(solution)/shard_map/ppermute | solution.py:481
  139.9 1.2 copy-start.1
  141.1 0.9 copy-start.7
  142.1 4.8 %copy-start.3 = (bf16[128,1024]{1,0:T(8,128)(2,1)S(1)}, bf16[128,1024]{1,0:T(8,128)(2,1)}, u32[]{:S(2)}) copy-start(bf16[128,1024]{1,0:T(8,128)(2,1)} %copy-done.2) | copy-start | bytes 786436
  144.9 2.0 %collective-permute-start.10 = (bf16[2,128,1024]{2,1,0:T(8,128)(2,1)S(1)}, bf16[2,128,1024]{2,1,0:T(8,128)(2,1)S(1)}, u32[]{:S(2)}, u32[]{:S(2)}) collective-permute-start(bf16[2,128,1024]{2,1,0:T(8,128)(2,1)S(1)} %get-tuple-element.75), channel_id=1, source_target_pairs={{0,1},{1,0},{2,3},{3,2},{4,5},{5,4},{6,7},{7,6},{8,9},{9,8},{10,11... | collective-permute-start | bytes 1572872 | tf_op jit(solution)/shard_map/ppermute | solution.py:477

commit v5 on v4

--- a/solution.py
+++ b/solution.py
@@ -57,12 +57,9 @@
     return pl.CostEstimate(flops=flops, bytes_accessed=size, transcendentals=exps)
 
 
-def stage_kernel(place, tokens, cot, gain, w_qkv, w_out, own, own_cot, own_gain, wq, wk, wv, out, sems):
+def stage_kernel(place, w_qkv, w_out, wq, wk, wv, out, sems):
     core = place[0]
     copies = [
-        pltpu.make_async_copy(tokens, own, sems.at[0]),
-        pltpu.make_async_copy(cot, own_cot, sems.at[1]),
-        pltpu.make_async_copy(gain, own_gain, sems.at[2]),
         pltpu.make_async_copy(
             w_out.at[pl.ds(pl.multiple_of(core * HALF * DH, HALF * DH), HALF * DH), :],
             out,
@@ -73,7 +70,7 @@
         start = pl.multiple_of(part * D + core * HALF * DH, HALF * DH)
         copies.append(
             pltpu.make_async_copy(
-                w_qkv.at[:, pl.ds(start, HALF * DH)], (wq, wk, wv)[part], sems.at[4 + part]
+                w_qkv.at[:, pl.ds(start, HALF * DH)], (wq, wk, wv)[part], sems.at[part]
             )
         )
     for copy in copies:
@@ -82,23 +79,26 @@
         copy.wait()
 
 
-def stage(place, tokens, cot, gain, w_qkv, w_out):
+def stage(place, w_qkv, w_out):
     return pl.pallas_call(
         stage_kernel,
-        in_specs=[SM] + [ANY] * 5,
-        out_specs=[VM] * 7,
-        out_shape=[
-            jax.ShapeDtypeStruct((HW, D), BF16),
-            jax.ShapeDtypeStruct((HW, D), BF16),
-            jax.ShapeDtypeStruct((1, D), F32),
-        ]
-        + [jax.ShapeDtypeStruct((D, HALF * DH), BF16)] * 3
+        in_specs=[SM] + [ANY] * 2,
+        out_specs=[VM] * 4,
+        out_shape=[jax.ShapeDtypeStruct((D, HALF * DH), BF16)] * 3
         + [jax.ShapeDtypeStruct((HALF * DH, D), BF16)],
-        scratch_shapes=[pltpu.SemaphoreType.DMA((7,))],
+        scratch_shapes=[pltpu.SemaphoreType.DMA((4,))],
         compiler_params=pltpu.CompilerParams(vmem_limit_bytes=STAGE_LIMIT),
         cost_estimate=cost(0, 9_000_000),
         name="stage",
-    )(place, tokens, cot, gain, w_qkv, w_out)
+    )(place, w_qkv, w_out)
+
+
+def slot_of_head(place, h):
+    return lax.rem(h + HALF - place[2], HALF)
+
+
+def head_here(place, step=0):
+    return lax.rem(place[1] + place[2] + step, HALF)
 
 
 def project_kernel(
@@ -116,14 +116,16 @@
             got = mm(normed, {Q0: wq, K0: wk, V0: wv}[row][...]).astype(BF16)
         for h in range(HALF):
             for s in range(2):
-                packed[h, s, row : row + HW, :] = got[s * HW : (s + 1) * HW, h * DH : (h + 1) * DH]
+                packed[slot_of_head(place, h), s, row : row + HW, :] = (
+                    got[s * HW : (s + 1) * HW, h * DH : (h + 1) * DH]
+                )
     for h in range(HALF):
         for s in range(2):
             packed[h, s, OK0:ROWS, :] = flags
     for step, near in enumerate((near0, near1, near2, near3)):
-        h = lax.rem(place[2] + step, HALF)
+        slot = lax.rem(place[1] + step, HALF)
         for s in range(2):
-            near[s] = packed[h, s, :OK0, :]
+            near[s] = packed[slot, s, :OK0, :]
 
 
 def project(place, valid, own, other, cot_own, cot_other, gain, weights):
@@ -190,14 +192,11 @@
 
 
 def slot_of_near(place, step, s):
-    zh = place[2]
-    cam = lax.rem(zh + 4 - step, 4)
-    return (zh * 2 + s) * 4 + cam
+    return lax.rem(place[1] + step, 4) * 2 + s
 
 
 def far_forward_kernel(place, win, mine, past, close, told, kept, result, keys, values_t, scores):
-    width = win[place[0] * HALF + place[1]]
-    told[...] = jnp.zeros_like(told)
+    width = win[place[0] * HALF + head_here(place)]
     for step in range(4):
         for s in range(2):
             told[slot_of_near(place, step, s), 0:4, :] = close[2 * step + s]
@@ -236,8 +235,8 @@
         result[:, p * PAIR : (p + 1) * PAIR] = got
         delta = jnp.sum(got * grad_t, axis=0, keepdims=True)
         stats = jnp.concatenate([peak, total, delta, jnp.zeros((1, PAIR), F32)], axis=0)
-        told[2 * p * 4 + place[1], 4:8, :] = stats[:, :HW]
-        told[(2 * p + 1) * 4 + place[1], 4:8, :] = stats[:, HW:]
+        told[2 * p, 4:8, :] = stats[:, :HW]
+        told[2 * p + 1, 4:8, :] = stats[:, HW:]
 
 
 def far_forward(place, window, mine, past, close):
@@ -246,7 +245,7 @@
         in_specs=[SM, SM, VM, VM, VM],
         out_specs=[VM] * 3,
         out_shape=[
-            jax.ShapeDtypeStruct((32, 8, HW), F32),
+            jax.ShapeDtypeStruct((GROUP, 8, HW), F32),
             jax.ShapeDtypeStruct((GROUP // 2, KEYS, PAIR), BF16),
             jax.ShapeDtypeStruct((DH, GROUP * HW), F32),
         ],
@@ -343,9 +342,8 @@
         grad_t = jnp.concatenate(
             [turn(mine[2 * p, G0 : G0 + HW, :]), turn(mine[2 * p + 1, G0 : G0 + HW, :])], axis=1
         )
-        slots = [(2 * p + i) * 4 + place[1] for i in range(2)]
-        this = jnp.concatenate([sent[slot, 4:8, :] for slot in slots], axis=1)
-        other = jnp.concatenate([told[slot, 0:4, :] for slot in slots], axis=1)
+        this = jnp.concatenate([sent[2 * p, 4:8, :], sent[2 * p + 1, 4:8, :]], axis=1)
+        other = jnp.concatenate([told[2 * p, 0:4, :], told[2 * p + 1, 0:4, :]], axis=1)
         weight, delta = merge(this, other)
         grad_t = (grad_t * weight).astype(BF16)
         at = p * PAIR
@@ -417,13 +415,14 @@
 
 def unproject_kernel(place, near0, near1, near2, near3, far, wq, wk, wv, wo, own, other, close):
     for step, near in enumerate((near0, near1, near2, near3)):
-        close[lax.rem(place[2] + step, HALF)] = near[...]
+        close[head_here(place, step)] = near[...]
     parts = []
     for part in range(4):
         rows = slice(part * HW, (part + 1) * HW)
         pieces = []
         for h in range(HALF):
-            away = jnp.concatenate([far[h, 0, rows, :], far[h, 1, rows, :]], axis=0)
+            slot = slot_of_head(place, h)
+            away = jnp.concatenate([far[slot, 0, rows, :], far[slot, 1, rows, :]], axis=0)
             here = jnp.concatenate([close[h, 0, rows, :], close[h, 1, rows, :]], axis=0)
             pieces.append((away.astype(F32) + here.astype(F32)).astype(BF16))
         parts.append(jnp.concatenate(pieces, axis=1))
@@ -435,17 +434,25 @@
     other[1] = total[HW:].astype(BF16)
 
 
-def unproject(place, blocks, far, weights):
+def unproject(place, blocks, far, w_qkv, w_out):
+    whole = lambda shape: pl.BlockSpec(shape, lambda i, place: (0,) * len(shape))
+    part = lambda at: pl.BlockSpec((D, HALF * DH), lambda i, place: (0, at * 2 + place[0]))
     return pl.pallas_call(
         unproject_kernel,
-        in_specs=[SM] + [VM] * 9,
-        out_specs=[VM, VM],
+        grid_spec=pltpu.PrefetchScalarGridSpec(
+            num_scalar_prefetch=1,
+            grid=(1,),
+            in_specs=[whole((2, 4 * HW, DH))] * 4
+            + [whole((HALF, 2, ROWS, DH)), part(0), part(1), part(2)]
+            + [pl.BlockSpec((HALF * DH, D), lambda i, place: (place[0], 0))],
+            out_specs=[whole((2, HW, D))] * 2,
+            scratch_shapes=[pltpu.VMEM((HALF, 2, 4 * HW, DH), BF16)],
+        ),
         out_shape=[jax.ShapeDtypeStruct((2, HW, D), F32), jax.ShapeDtypeStruct((2, HW, D), BF16)],
-        scratch_shapes=[pltpu.VMEM((HALF, 2, 4 * HW, DH), BF16)],
-        compiler_params=params(),
+        compiler_params=pltpu.CompilerParams(vmem_limit_bytes=50 * 1024 * 1024),
         cost_estimate=cost(2 * PAIR * D * 4 * HALF * DH, 8_000_000),
         name="unproject",
-    )(place, *blocks, far, *weights)
+    )(place, *blocks, far, w_qkv, w_qkv, w_qkv, w_out)
 
 
 def finish_kernel(tokens, cot, gain, own, other, mixed, out):
@@ -471,6 +478,9 @@
 
 
 LANE = ("x", "zl")
+SAME_HEAD = [
+    [(x * 2 + zl) * 4 + (h + 4 - x) % 4 for x in range(4) for zl in range(2)] for h in range(4)
+]
 
 
 def swap(value):
@@ -481,8 +491,8 @@
     return lax.ppermute(value, "zh", [(i, (i + steps) % 4) for i in range(4)])
 
 
-def exchange(value, axes):
-    return lax.all_to_all(value, axes, 0, 0, tiled=True)
+def exchange(value, axes, groups=None):
+    return lax.all_to_all(value, axes, 0, 0, axis_index_groups=groups, tiled=True)
 
 
 def exchange_alone(value, go):
@@ -499,16 +509,17 @@
     cot = cotangent.reshape(HW, D)
     other_tokens = swap(tokens)
     other_cot = swap(cot)
-    tokens, cot, gain, *weights = stage(place, tokens, cot, gain.reshape(1, D), w_qkv, w_out)
+    gain = gain.reshape(1, D)
+    weights = stage(place, w_qkv, w_out)
     packed, *blocks = project(
         place, valid, tokens, other_tokens, cot, other_cot, gain, weights
     )
     blocks = [blocks[0]] + [turn_ring(blocks[step], step) for step in (1, 2, 3)]
-    mine = exchange_alone(packed.reshape(2 * HALF, ROWS, DH), go)
+    mine = exchange(packed.reshape(2 * HALF, ROWS, DH), LANE)
     past = lax.ppermute(mine[:, K0:, :], "y", [(i, i + 1) for i in range(rows - 1)])
     near_kept, near_result, close = near_forward(*blocks)
     sent, far_kept, far_result = far_forward(place, window, mine, past, close)
-    told = exchange(sent, ("x", "zl", "zh"))
+    told = exchange(sent, ("x", "zl", "zh"), SAME_HEAD)
     own, back = far_backward(place, mine, past, far_kept, far_result, sent, told)
     back = lax.ppermute(back, "y", [(i + 1, i) for i in range(rows - 1)])
     returned = near_backward(place, blocks, near_kept, near_result, close, told)
@@ -516,7 +527,7 @@
     returned = [returned[0]] + [turn_ring(returned[step], -step) for step in (1, 2, 3)]
     own = add_back(own, back)
     far = exchange_alone(own, go).reshape(HALF, 2, ROWS, DH)
-    out_own, out_other = unproject(place, returned, far, weights)
+    out_own, out_other = unproject(place, returned, far, w_qkv, w_out)
     mixed, d_tokens = finish(tokens, cot, gain, out_own, swap(out_other))
     return mixed.reshape(1, 1, HW, D), d_tokens.reshape(1, 1, HW, D)
 

time: 150 us -> 131 us (0.87)
  blocking collectives: 78.2 us -> 47.7 us
  waiting for transfers between devices: 11.9 us -> 26.5 us
  local copies, waits for them, and re-layouts: 6.63 us -> 0.05 us
  starting transfers between devices: 22.7 us -> 28.4 us
  Pallas kernels: 27 us -> 24.7 us
    all_to_all x3 -> x2, blocking collectives: 78.2 us -> 47.7 us  [exchange(): lax.all_to_all(value, axes, 0, 0, axis_index_groups=groups, tiled=True)]
    all_to_all x0 -> x1, waiting for transfers between devices: none -> 12.8 us  [exchange(): lax.all_to_all(value, axes, 0, 0, axis_index_groups=groups, tiled=True)]
    ppermute x6, waiting for transfers between devices: 0.02 us -> 9.98 us  [turn_ring(): return lax.ppermute(value, 'zh', [(i, (i + steps) % 4) for i in range(4)])]
    ppermute x1, waiting for transfers between devices: 9.25 us -> 0.01 us  [per_device(): lax.ppermute(mine[:, K0:, :], 'y', [(i, i + 1) for i in range(rows - 1)])]
    all_to_all x0 -> x1, starting transfers between devices: none -> 5.73 us  [exchange(): lax.all_to_all(value, axes, 0, 0, axis_index_groups=groups, tiled=True)]
    unnamed x26 -> x8, local copies, waits for them, and re-layouts: 5.49 us -> 0.01 us
  transfers between devices with their start and end apart: 11 -> 12, of which waited for: 3 -> 5; matrix products, arithmetic and copies ran while one was open for 1% -> 0% of each run, Pallas kernels for 8% -> 7%
where the time goes in v5:
time: 131 us; the launch traced here: 129 us
  blocking collectives  47.7 us (36%)
  starting transfers between devices  28.4 us (22%)
  waiting for transfers between devices  26.5 us (20%)
  Pallas kernels  24.7 us (19%)
  between operations  1.47 us (1%)
    all_to_all x2, blocking collectives, exchange(): lax.all_to_all(value, axes, 0, 0, axis_index_groups=groups, tiled=True)  47.7 us
    ppermute x6, starting transfers between devices, turn_ring(): return lax.ppermute(value, 'zh', [(i, (i + steps) % 4) for i in range(4)])  16.5 us
    all_to_all x1, waiting for transfers between devices, exchange(): lax.all_to_all(value, axes, 0, 0, axis_index_groups=groups, tiled=True)  12.8 us
    ppermute x6, waiting for transfers between devices, turn_ring(): return lax.ppermute(value, 'zh', [(i, (i + steps) % 4) for i in range(4)])  9.98 us
    all_to_all x1, starting transfers between devices, exchange(): lax.all_to_all(value, axes, 0, 0, axis_index_groups=groups, tiled=True)  5.73 us
    pallas_call x1, Pallas kernels, unproject(): pl.pallas_call(unproject_kernel, grid_spec=pltpu.PrefetchScalarGridSpec(n...  4.36 us
    pallas_call x1, Pallas kernels, far_forward(): pl.pallas_call(far_forward_kernel, in_specs=[SM, SM, VM, VM, VM], out_spe...  3.41 us
    pallas_call x1, Pallas kernels, far_backward(): pl.pallas_call(far_backward_kernel, in_specs=[SM] + [VM] * 6, out_specs=[...  3.37 us
  transfers between devices with their start and end apart: 12, of which 5 were waited for; matrix products, arithmetic and copies ran while one was open for 0% of the time, Pallas kernels for 7%

profile of v5, /device:TPU:16, one launch (start us, length us, event | category | flops | bytes accessed | tf_op | source)
XLA Modules:
  0.0 128.9 jit_solution(16146126522000780557)
XLA Ops:
  0.6 0.1 collective-permute-start
  0.7 0.5 collective-permute-start.1
  1.9 0.1 pad_add_fusion.place
  2.0 2.8 %stage.1 = (bf16[1024,512]{1,0:T(8,128)(2,1)S(1)}, bf16[1024,512]{1,0:T(8,128)(2,1)S(1)}, bf16[1024,512]{1,0:T(8,128)(2,1)S(1)}, bf16[512,1024]{1,0:T(8,128)(2,1)S(1)}) custom-call(s32[3]{0:T(128)S(1)} %pad_add_fusion.place, bf16[1024,3072]{1,0:T(8,128)(2,1)} %wv.1, bf16[1024,1024]{1,0:T(8,128)(2,1)} %wo.1), custom_call_target="tpu_custom_call" | custom-call | bytes 9000000 | tf_op jit(solution)/shard_map/stage/pallas_call | solution.py:83
  4.7 0.0 collective-permute-done.1.cot_other
  4.8 3.2 %project.1 = (bf16[4,2,528,128]{3,2,1,0:T(8,128)(2,1)}, bf16[2,512,128]{2,1,0:T(8,128)(2,1)S(1)}, bf16[2,512,128]{2,1,0:T(8,128)(2,1)S(1)}, bf16[2,512,128]{2,1,0:T(8,128)(2,1)S(1)}, bf16[2,512,128]{2,1,0:T(8,128)(2,1)S(1)}) custom-call(s32[3]{0:T(128)S(1)} %pad_add_fusion.place, s32[1]{0:T(128)S(6)} %copy.11.valid, bf16[128,1024]{1,0:T(8,128)(2,1)S(1)} %bitcast.13, ...), custom_call_target="tpu_custom_call" | custom-call | flops 1073741824 | bytes 7000000 | tf_op jit(solution)/shard_map/project/pallas_call | solution.py:132
  8.0 5.7 %all-to-all-start.1 = ((bf16[8,528,128]{2,1,0:T(8,128)(2,1)}), bf16[8,528,128]{2,1,0:T(8,128)(2,1)S(1)}, u32[]{:S(2)}, u32[]{:S(2)}) async-start(bf16[8,528,128]{2,1,0:T(8,128)(2,1)} %bitcast.7), calls=%async_computation.1 | async-start | bytes 2162688 | tf_op jit(solution)/shard_map/all_to_all | solution.py:495
  13.7 3.3 %collective-permute-start.3 = (bf16[2,512,128]{2,1,0:T(8,128)(2,1)S(1)}, bf16[2,512,128]{2,1,0:T(8,128)(2,1)S(1)}, u32[]{:S(2)}, u32[]{:S(2)}) collective-permute-start(bf16[2,512,128]{2,1,0:T(8,128)(2,1)S(1)} %get-tuple-element.43), channel_id=1, source_target_pairs={{0,2},{2,4},{4,6},{6,0},{1,3},{3,5},{5,7},{7,1},{8,10},{10,12},{12... | collective-permute-start | bytes 786440 | tf_op jit(solution)/shard_map/ppermute | solution.py:491
  17.0 4.4 %collective-permute-start.4 = (bf16[2,512,128]{2,1,0:T(8,128)(2,1)S(1)}, bf16[2,512,128]{2,1,0:T(8,128)(2,1)S(1)}, u32[]{:S(2)}, u32[]{:S(2)}) collective-permute-start(bf16[2,512,128]{2,1,0:T(8,128)(2,1)S(1)} %get-tuple-element.44), channel_id=1, source_target_pairs={{0,4},{2,6},{4,0},{6,2},{1,5},{3,7},{5,1},{7,3},{8,12},{10,14},{12... | collective-permute-start | bytes 786440 | tf_op jit(solution)/shard_map/ppermute | solution.py:491
  21.4 2.6 %collective-permute-start.5 = (bf16[2,512,128]{2,1,0:T(8,128)(2,1)S(1)}, bf16[2,512,128]{2,1,0:T(8,128)(2,1)S(1)}, u32[]{:S(2)}, u32[]{:S(2)}) collective-permute-start(bf16[2,512,128]{2,1,0:T(8,128)(2,1)S(1)} %get-tuple-element.45), channel_id=1, source_target_pairs={{0,6},{2,0},{4,2},{6,4},{1,7},{3,1},{5,3},{7,5},{8,14},{10,8},{12,... | collective-permute-start | bytes 786440 | tf_op jit(solution)/shard_map/ppermute | solution.py:491
  24.0 12.8 %all-to-all-done.1.mine = bf16[8,528,128]{2,1,0:T(8,128)(2,1)S(1)} async-done(((bf16[8,528,128]{2,1,0:T(8,128)(2,1)}), bf16[8,528,128]{2,1,0:T(8,128)(2,1)S(1)}, u32[]{:S(2)}, u32[]{:S(2)}) %all-to-all-start.1) | async-done | bytes 1081376 | tf_op jit(solution)/shard_map/all_to_all | solution.py:495
  36.9 3.2 %collective-permute-start.2 = (bf16[8,272,128]{2,1,0:T(8,128)(2,1)S(1)}, bf16[8,272,128]{2,1,0:T(8,128)(2,1)S(1)}, u32[]{:S(2)}, u32[]{:S(2)}) collective-permute-start(bf16[8,272,128]{2,1,0:T(8,128)(2,1)S(1)} %slice.8), channel_id=1, source_target_pairs={{0,64},{64,128},{128,192},{1,65},{65,129},{129,193},{2,66},{66,130... | collective-permute-start | bytes 1671176 | tf_op jit(solution)/shard_map/ppermute | solution.py:519
  40.1 4.4 %collective-permute-done.3.near1 = bf16[2,512,128]{2,1,0:T(8,128)(2,1)S(1)} collective-permute-done((bf16[2,512,128]{2,1,0:T(8,128)(2,1)S(1)}, bf16[2,512,128]{2,1,0:T(8,128)(2,1)S(1)}, u32[]{:S(2)}, u32[]{:S(2)}) %collective-permute-start.3) | collective-permute-done | bytes 262176 | tf_op jit(solution)/shard_map/ppermute | solution.py:491
  44.5 5.6 %collective-permute-done.4.near2 = bf16[2,512,128]{2,1,0:T(8,128)(2,1)S(1)} collective-permute-done((bf16[2,512,128]{2,1,0:T(8,128)(2,1)S(1)}, bf16[2,512,128]{2,1,0:T(8,128)(2,1)S(1)}, u32[]{:S(2)}, u32[]{:S(2)}) %collective-permute-start.4) | collective-permute-done | bytes 262176 | tf_op jit(solution)/shard_map/ppermute | solution.py:491
  50.1 0.0 collective-permute-done.5.near3
  50.1 2.5 %near_forward.1 = (bf16[1024,1024]{1,0:T(8,128)(2,1)S(1)}, f32[128,1024]{1,0:T(8,128)S(1)}, f32[8,4,128]{2,1,0:T(4,128)S(1)}) custom-call(bf16[2,512,128]{2,1,0:T(8,128)(2,1)S(1)} %get-tuple-element.42.near0, bf16[2,512,128]{2,1,0:T(8,128)(2,1)S(1)} %collective-permute-done.3.near1, bf16[2,512,128]{2,1,0:T(8,128)(2,1)S(1)} %collective-permute-done.4.near2, ...), custom_call_target="tpu_custom_call" | custom-call | flops 10737418240 | bytes 4000000 | tf_op jit(solution)/shard_map/near_forward/pallas_call | solution.py:178
  52.6 3.4 %far_forward.1 = (f32[8,8,128]{2,1,0:T(8,128)S(1)}, bf16[4,1152,256]{2,1,0:T(8,128)(2,1)S(1)}, f32[128,1024]{1,0:T(8,128)S(1)}) custom-call(s32[3]{0:T(128)S(1)} %pad_add_fusion.place, s32[8]{0:T(128)S(1)} %copy-done.3, bf16[8,528,128]{2,1,0:T(8,128)(2,1)S(1)} %all-to-all-done.1.mine, bf16[8,272,128]{2,1,0:T(8,128)(2,1)S(1)} %collective-permute-done.2.past, ...), custom_call_target="tpu_custom_call" | custom-call | flops 603979776 | bytes 5000000 | tf_op jit(solution)/shard_map/far_forward/pallas_call | solution.py:243
  56.0 20.3 %all_to_all.15.told = f32[8,8,128]{2,1,0:T(8,128)S(1)} all-to-all(f32[8,8,128]{2,1,0:T(8,128)S(1)} %get-tuple-element.49.sent), channel_id=1, replica_groups={{0,8,22,30,36,44,50,58},{2,10,16,24,38,46,52,60},{4,12,18,26,32,40,54,6..., dimensions={0} | all-to-all | bytes 65536 | tf_op jit(solution)/shard_map/all_to_all | solution.py:495
  76.3 3.4 %far_backward.1 = (bf16[8,512,128]{2,1,0:T(8,128)(2,1)S(1)}, bf16[8,256,128]{2,1,0:T(8,128)(2,1)S(1)}) custom-call(s32[3]{0:T(128)S(1)} %pad_add_fusion.place, bf16[8,528,128]{2,1,0:T(8,128)(2,1)S(1)} %all-to-all-done.1.mine, bf16[8,272,128]{2,1,0:T(8,128)(2,1)S(1)} %collective-permute-done.2.past, bf16[4,1152,256]{2,1,0:T(8,128)(2,1)S(1)} %get-tuple-element.47.kept, ...), custom_call_target="tpu_custom_call" | custom-call | flops 1207959552 | bytes 6000000 | tf_op jit(solution)/shard_map/far_backward/pallas_call | solution.py:374
  79.7 2.3 %collective-permute-start.9 = (bf16[8,256,128]{2,1,0:T(8,128)(2,1)S(1)}, bf16[8,256,128]{2,1,0:T(8,128)(2,1)S(1)}, u32[]{:S(2)}, u32[]{:S(2)}) collective-permute-start(bf16[8,256,128]{2,1,0:T(8,128)(2,1)S(1)} %get-tuple-element.62), channel_id=1, source_target_pairs={{64,0},{128,64},{192,128},{65,1},{129,65},{193,129},{66,2},{130,66... | collective-permute-start | bytes 1572872 | tf_op jit(solution)/shard_map/ppermute | solution.py:524
  82.0 2.9 %near_backward.1 = (bf16[2,512,128]{2,1,0:T(8,128)(2,1)S(1)}, bf16[2,512,128]{2,1,0:T(8,128)(2,1)S(1)}, bf16[2,512,128]{2,1,0:T(8,128)(2,1)S(1)}, bf16[2,512,128]{2,1,0:T(8,128)(2,1)S(1)}) custom-call(s32[3]{0:T(128)S(1)} %pad_add_fusion.place, bf16[2,512,128]{2,1,0:T(8,128)(2,1)S(1)} %get-tuple-element.42.near0, ...), custom_call_target="tpu_custom_call" | custom-call | flops 1073741824 | bytes 5000000 | tf_op jit(solution)/shard_map/near_backward/pallas_call | solution.py:312
  85.0 3.7 %collective-permute-start.6 = (bf16[2,512,128]{2,1,0:T(8,128)(2,1)S(1)}, bf16[2,512,128]{2,1,0:T(8,128)(2,1)S(1)}, u32[]{:S(2)}, u32[]{:S(2)}) collective-permute-start(bf16[2,512,128]{2,1,0:T(8,128)(2,1)S(1)} %get-tuple-element.58), channel_id=1, source_target_pairs={{0,6},{2,0},{4,2},{6,4},{1,7},{3,1},{5,3},{7,5},{8,14},{10,8},{12,... | collective-permute-start | bytes 786440 | tf_op jit(solution)/shard_map/ppermute | solution.py:491
  88.7 1.5 %collective-permute-start.7 = (bf16[2,512,128]{2,1,0:T(8,128)(2,1)S(1)}, bf16[2,512,128]{2,1,0:T(8,128)(2,1)S(1)}, u32[]{:S(2)}, u32[]{:S(2)}) collective-permute-start(bf16[2,512,128]{2,1,0:T(8,128)(2,1)S(1)} %get-tuple-element.59), channel_id=1, source_target_pairs={{0,4},{2,6},{4,0},{6,2},{1,5},{3,7},{5,1},{7,3},{8,12},{10,14},{12... | collective-permute-start | bytes 786440 | tf_op jit(solution)/shard_map/ppermute | solution.py:491
  90.2 0.9 collective-permute-start.8
  91.2 1.8 %collective-permute-done.9.back = bf16[8,256,128]{2,1,0:T(8,128)(2,1)S(1)} collective-permute-done((bf16[8,256,128]{2,1,0:T(8,128)(2,1)S(1)}, bf16[8,256,128]{2,1,0:T(8,128)(2,1)S(1)}, u32[]{:S(2)}, u32[]{:S(2)}) %collective-permute-start.9) | collective-permute-done | bytes 524320 | tf_op jit(solution)/shard_map/ppermute | solution.py:524
  92.9 1.2 add_back.1
  94.1 27.4 %conditional.1 = (bf16[4,2,528,128]{3,2,1,0:T(8,128)(2,1)}) conditional(s32[]{:T(128)} %bitcast.8, () %tuple.18, bf16[8,528,128]{2,1,0:T(8,128)(2,1)} %add_back.1), branch_computations={%region_0.0_spmd, %region_1.0_spmd} | conditional | bytes 2162696 | solution.py:499
  94.1 27.4 %all_to_all.14 = bf16[8,528,128]{2,1,0:T(8,128)(2,1)} all-to-all(bf16[8,528,128]{2,1,0:T(8,128)(2,1)} %param.1), channel_id=1, replica_groups=mesh['y'=4,'x'=4,'zl'=2,'zh'=4,'core'=2] {'x','zl'}, dimensions={0} | all-to-all | bytes 2162688 | tf_op jit(solution)/shard_map/cond/branch_1_fun/all_to_all | solution.py:495
  121.5 4.4 %unproject.1 = (f32[2,128,1024]{2,1,0:T(8,128)S(1)}, bf16[2,128,1024]{2,1,0:T(8,128)(2,1)S(1)}) custom-call(s32[3]{0:T(128)S(1)} %pad_add_fusion.place, bf16[2,512,128]{2,1,0:T(8,128)(2,1)S(1)} %get-tuple-element.57.near0, bf16[2,512,128]{2,1,0:T(8,128)(2,1)S(1)} %collective-permute-done.6.near1, bf16[2,512,128]{2,1,0:T(8,128)(2,1)S(1)} %collective-permute-done.7.near2, ...), custom_call_target="tpu_custom_call" | custom-call | flops 1073741824 | bytes 8000000 | tf_op jit(solution)/shard_map/unproject/pallas_call | solution.py:440
  125.9 0.1 collective-permute-start.10
  126.0 1.9 %collective-permute-done.10.other = bf16[2,128,1024]{2,1,0:T(8,128)(2,1)S(1)} collective-permute-done((bf16[2,128,1024]{2,1,0:T(8,128)(2,1)S(1)}, bf16[2,128,1024]{2,1,0:T(8,128)(2,1)S(1)}, u32[]{:S(2)}, u32[]{:S(2)}) %collective-permute-start.10) | collective-permute-done | bytes 524320 | tf_op jit(solution)/shard_map/ppermute | solution.py:487
  127.9 1.0 finish.1
  (14 shorter events, 0.1 us)
Async XLA Ops:
  0.6 4.1 %collective-permute-start = (bf16[128,1024]{1,0:T(8,128)(2,1)}, bf16[128,1024]{1,0:T(8,128)(2,1)S(1)}, u32[]{:S(2)}, u32[]{:S(2)}) collective-permute-start(bf16[128,1024]{1,0:T(8,128)(2,1)} %bitcast.12), channel_id=1, source_target_pairs={{0,1},{1,0},{2,3},{3,2},{4,5},{5,4},{6,7},{7,6},{8,9},{9,8},{10,11... | collective-permute-start | bytes 786440 | tf_op jit(solution)/shard_map/ppermute | solution.py:487
  0.7 4.0 %collective-permute-start.1 = (bf16[128,1024]{1,0:T(8,128)(2,1)}, bf16[128,1024]{1,0:T(8,128)(2,1)S(1)}, u32[]{:S(2)}, u32[]{:S(2)}) collective-permute-start(bf16[128,1024]{1,0:T(8,128)(2,1)} %bitcast.15), channel_id=1, source_target_pairs={{0,1},{1,0},{2,3},{3,2},{4,5},{5,4},{6,7},{7,6},{8,9},{9,8},{10,11... | collective-permute-start | bytes 786440 | tf_op jit(solution)/shard_map/ppermute | solution.py:487
  2.0 2.8 %copy-start = (bf16[1,1,128,1024]{3,2,1,0:T(8,128)(2,1)S(1)}, bf16[1,1,128,1024]{3,2,1,0:T(8,128)(2,1)}, u32[]{:S(2)}) copy-start(bf16[1,1,128,1024]{3,2,1,0:T(8,128)(2,1)} %param.9) | copy-start | bytes 786436
  2.0 2.8 %copy-start.1 = (bf16[1,1,128,1024]{3,2,1,0:T(8,128)(2,1)S(1)}, bf16[1,1,128,1024]{3,2,1,0:T(8,128)(2,1)}, u32[]{:S(2)}) copy-start(bf16[1,1,128,1024]{3,2,1,0:T(8,128)(2,1)} %param.15) | copy-start | bytes 786436
  2.0 2.8 %copy-start.2 = (f32[1024]{0:T(1024)S(1)}, f32[1024]{0:T(1024)}, u32[]{:S(2)}) copy-start(f32[1024]{0:T(1024)} %param.10) | copy-start | bytes 12292
  8.0 28.9 %all-to-all-start.1 = ((bf16[8,528,128]{2,1,0:T(8,128)(2,1)}), bf16[8,528,128]{2,1,0:T(8,128)(2,1)S(1)}, u32[]{:S(2)}, u32[]{:S(2)}) async-start(bf16[8,528,128]{2,1,0:T(8,128)(2,1)} %bitcast.7), calls=%async_computation.1 | async-start | bytes 2162688 | tf_op jit(solution)/shard_map/all_to_all | solution.py:495
  13.7 30.8 %collective-permute-start.3 = (bf16[2,512,128]{2,1,0:T(8,128)(2,1)S(1)}, bf16[2,512,128]{2,1,0:T(8,128)(2,1)S(1)}, u32[]{:S(2)}, u32[]{:S(2)}) collective-permute-start(bf16[2,512,128]{2,1,0:T(8,128)(2,1)S(1)} %get-tuple-element.43), channel_id=1, source_target_pairs={{0,2},{2,4},{4,6},{6,0},{1,3},{3,5},{5,7},{7,1},{8,10},{10,12},{12... | collective-permute-start | bytes 786440 | tf_op jit(solution)/shard_map/ppermute | solution.py:491
  17.0 33.1 %collective-permute-start.4 = (bf16[2,512,128]{2,1,0:T(8,128)(2,1)S(1)}, bf16[2,512,128]{2,1,0:T(8,128)(2,1)S(1)}, u32[]{:S(2)}, u32[]{:S(2)}) collective-permute-start(bf16[2,512,128]{2,1,0:T(8,128)(2,1)S(1)} %get-tuple-element.44), channel_id=1, source_target_pairs={{0,4},{2,6},{4,0},{6,2},{1,5},{3,7},{5,1},{7,3},{8,12},{10,14},{12... | collective-permute-start | bytes 786440 | tf_op jit(solution)/shard_map/ppermute | solution.py:491
  21.4 28.6 %collective-permute-start.5 = (bf16[2,512,128]{2,1,0:T(8,128)(2,1)S(1)}, bf16[2,512,128]{2,1,0:T(8,128)(2,1)S(1)}, u32[]{:S(2)}, u32[]{:S(2)}) collective-permute-start(bf16[2,512,128]{2,1,0:T(8,128)(2,1)S(1)} %get-tuple-element.45), channel_id=1, source_target_pairs={{0,6},{2,0},{4,2},{6,4},{1,7},{3,1},{5,3},{7,5},{8,14},{10,8},{12,... | collective-permute-start | bytes 786440 | tf_op jit(solution)/shard_map/ppermute | solution.py:491
  36.9 15.7 %collective-permute-start.2 = (bf16[8,272,128]{2,1,0:T(8,128)(2,1)S(1)}, bf16[8,272,128]{2,1,0:T(8,128)(2,1)S(1)}, u32[]{:S(2)}, u32[]{:S(2)}) collective-permute-start(bf16[8,272,128]{2,1,0:T(8,128)(2,1)S(1)} %slice.8), channel_id=1, source_target_pairs={{0,64},{64,128},{128,192},{1,65},{65,129},{129,193},{2,66},{66,130... | collective-permute-start | bytes 1671176 | tf_op jit(solution)/shard_map/ppermute | solution.py:519
  50.1 2.5 %copy-start.3 = (s32[8]{0:T(128)S(1)}, s32[8]{0:T(128)}, u32[]{:S(2)}) copy-start(s32[8]{0:T(128)} %win.1) | copy-start | bytes 100
  79.7 13.2 %collective-permute-start.9 = (bf16[8,256,128]{2,1,0:T(8,128)(2,1)S(1)}, bf16[8,256,128]{2,1,0:T(8,128)(2,1)S(1)}, u32[]{:S(2)}, u32[]{:S(2)}) collective-permute-start(bf16[8,256,128]{2,1,0:T(8,128)(2,1)S(1)} %get-tuple-element.62), channel_id=1, source_target_pairs={{64,0},{128,64},{192,128},{65,1},{129,65},{193,129},{66,2},{130,66... | collective-permute-start | bytes 1572872 | tf_op jit(solution)/shard_map/ppermute | solution.py:524
  85.0 36.5 %collective-permute-start.6 = (bf16[2,512,128]{2,1,0:T(8,128)(2,1)S(1)}, bf16[2,512,128]{2,1,0:T(8,128)(2,1)S(1)}, u32[]{:S(2)}, u32[]{:S(2)}) collective-permute-start(bf16[2,512,128]{2,1,0:T(8,128)(2,1)S(1)} %get-tuple-element.58), channel_id=1, source_target_pairs={{0,6},{2,0},{4,2},{6,4},{1,7},{3,1},{5,3},{7,5},{8,14},{10,8},{12,... | collective-permute-start | bytes 786440 | tf_op jit(solution)/shard_map/ppermute | solution.py:491
  88.7 32.8 %collective-permute-start.7 = (bf16[2,512,128]{2,1,0:T(8,128)(2,1)S(1)}, bf16[2,512,128]{2,1,0:T(8,128)(2,1)S(1)}, u32[]{:S(2)}, u32[]{:S(2)}) collective-permute-start(bf16[2,512,128]{2,1,0:T(8,128)(2,1)S(1)} %get-tuple-element.59), channel_id=1, source_target_pairs={{0,4},{2,6},{4,0},{6,2},{1,5},{3,7},{5,1},{7,3},{8,12},{10,14},{12... | collective-permute-start | bytes 786440 | tf_op jit(solution)/shard_map/ppermute | solution.py:491
  90.2 31.3 %collective-permute-start.8 = (bf16[2,512,128]{2,1,0:T(8,128)(2,1)S(1)}, bf16[2,512,128]{2,1,0:T(8,128)(2,1)S(1)}, u32[]{:S(2)}, u32[]{:S(2)}) collective-permute-start(bf16[2,512,128]{2,1,0:T(8,128)(2,1)S(1)} %get-tuple-element.60), channel_id=1, source_target_pairs={{0,2},{2,4},{4,6},{6,0},{1,3},{3,5},{5,7},{7,1},{8,10},{10,12},{12... | collective-permute-start | bytes 786440 | tf_op jit(solution)/shard_map/ppermute | solution.py:491
  125.9 2.0 %collective-permute-start.10 = (bf16[2,128,1024]{2,1,0:T(8,128)(2,1)S(1)}, bf16[2,128,1024]{2,1,0:T(8,128)(2,1)S(1)}, u32[]{:S(2)}, u32[]{:S(2)}) collective-permute-start(bf16[2,128,1024]{2,1,0:T(8,128)(2,1)S(1)} %get-tuple-element.64), channel_id=1, source_target_pairs={{0,1},{1,0},{2,3},{3,2},{4,5},{5,4},{6,7},{7,6},{8,9},{9,8},{10,11... | collective-permute-start | bytes 1572872 | tf_op jit(solution)/shard_map/ppermute | solution.py:487

commit v6 on v5

--- a/solution.py
+++ b/solution.py
@@ -57,22 +57,24 @@
     return pl.CostEstimate(flops=flops, bytes_accessed=size, transcendentals=exps)
 
 
-def stage_kernel(place, w_qkv, w_out, wq, wk, wv, out, sems):
-    core = place[0]
+def weight_copies(place, w_qkv, w_out, parts, out, sems):
+    begin = pl.multiple_of(place[0] * HALF * DH, HALF * DH)
     copies = [
         pltpu.make_async_copy(
-            w_out.at[pl.ds(pl.multiple_of(core * HALF * DH, HALF * DH), HALF * DH), :],
-            out,
-            sems.at[3],
-        ),
+            w_qkv.at[:, pl.ds(pl.multiple_of(begin + part * D, HALF * DH), HALF * DH)],
+            parts[part],
+            sems.at[part],
+        )
+        for part in range(3)
     ]
-    for part in range(3):
-        start = pl.multiple_of(part * D + core * HALF * DH, HALF * DH)
-        copies.append(
-            pltpu.make_async_copy(
-                w_qkv.at[:, pl.ds(start, HALF * DH)], (wq, wk, wv)[part], sems.at[part]
-            )
-        )
+    copies.append(
+        pltpu.make_async_copy(w_out.at[pl.ds(begin, HALF * DH), :], out, sems.at[3])
+    )
+    return copies
+
+
+def stage_kernel(place, w_qkv, w_out, wq, wk, wv, out, sems):
+    copies = weight_copies(place, w_qkv, w_out, (wq, wk, wv), out, sems)
     for copy in copies:
         copy.start()
     for copy in copies:
@@ -91,6 +93,9 @@
         cost_estimate=cost(0, 9_000_000),
         name="stage",
     )(place, w_qkv, w_out)
+
+
+STEPS = (0, 2, 1, 3)
 
 
 def slot_of_head(place, h):
@@ -122,7 +127,7 @@
     for h in range(HALF):
         for s in range(2):
             packed[h, s, OK0:ROWS, :] = flags
-    for step, near in enumerate((near0, near1, near2, near3)):
+    for step, near in zip(STEPS, (near0, near1, near2, near3)):
         slot = lax.rem(place[1] + step, HALF)
         for s in range(2):
             near[s] = packed[slot, s, :OK0, :]
@@ -197,9 +202,9 @@
 
 def far_forward_kernel(place, win, mine, past, close, told, kept, result, keys, values_t, scores):
     width = win[place[0] * HALF + head_here(place)]
-    for step in range(4):
+    for g in range(4):
         for s in range(2):
-            told[slot_of_near(place, step, s), 0:4, :] = close[2 * step + s]
+            told[slot_of_near(place, STEPS[g], s), 0:4, :] = close[2 * g + s]
     for j in range(GROUP):
         keys[j * HW : (j + 1) * HW, :] = past[j, :HW, :]
         keys[(GROUP + j) * HW : (GROUP + j + 1) * HW, :] = mine[j, K0 : K0 + HW, :]
@@ -280,7 +285,7 @@
         cols = slice(g * PAIR, (g + 1) * PAIR)
         this = jnp.concatenate([stats[2 * g], stats[2 * g + 1]], axis=1)
         other = jnp.concatenate(
-            [told[slot_of_near(place, g, s), 4:8, :] for s in range(2)], axis=1
+            [told[slot_of_near(place, STEPS[g], s), 4:8, :] for s in range(2)], axis=1
         )
         weight, delta = merge(this, other)
         grad_t = (turn(both(blocks[g], G0)) * weight).astype(BF16)
@@ -367,7 +372,8 @@
         back[j, :HW, :] = (dk[early, :] * SCALE).astype(BF16)
         back[j, HW:, :] = dv[early, :].astype(BF16)
         own[j, 2 * HW : 3 * HW, :] = (dk[late, :] * SCALE).astype(BF16)
-        own[j, 3 * HW :, :] = dv[late, :].astype(BF16)
+        own[j, 3 * HW : 4 * HW, :] = dv[late, :].astype(BF16)
+        own[j, 4 * HW :, :] = jnp.zeros((ROWS - 4 * HW, DH), BF16)
 
 
 def far_backward(place, mine, past, kept, result, sent, told):
@@ -376,7 +382,7 @@
         in_specs=[SM] + [VM] * 6,
         out_specs=[VM, VM],
         out_shape=[
-            jax.ShapeDtypeStruct((GROUP, 4 * HW, DH), BF16),
+            jax.ShapeDtypeStruct((GROUP, ROWS, DH), BF16),
             jax.ShapeDtypeStruct((GROUP, 2 * HW, DH), BF16),
         ],
         scratch_shapes=[
@@ -393,12 +399,10 @@
 
 
 def add_back_kernel(own, back, out):
-    out[:, : 2 * HW, :] = own[:, : 2 * HW, :]
     for j in range(GROUP):
         out[j, 2 * HW : 4 * HW, :] = (
-            own[j, 2 * HW :, :].astype(F32) + back[j].astype(F32)
+            own[j, 2 * HW : 4 * HW, :].astype(F32) + back[j].astype(F32)
         ).astype(BF16)
-        out[j, 4 * HW :, :] = jnp.zeros((ROWS - 4 * HW, DH), BF16)
 
 
 def add_back(own, back):
@@ -407,14 +411,20 @@
         in_specs=[VM] * 2,
         out_specs=VM,
         out_shape=jax.ShapeDtypeStruct((GROUP, ROWS, DH), BF16),
+        input_output_aliases={0: 0},
         compiler_params=params(),
         cost_estimate=cost(GROUP * 2 * HW * DH, 2_500_000),
         name="add_back",
     )(own, back)
 
 
-def unproject_kernel(place, near0, near1, near2, near3, far, wq, wk, wv, wo, own, other, close):
-    for step, near in enumerate((near0, near1, near2, near3)):
+def unproject_kernel(
+    place, near0, near1, near2, near3, far, w_qkv, w_out, own, other, close, wq, wk, wv, wo, sems
+):
+    copies = weight_copies(place, w_qkv, w_out, (wq, wk, wv), wo, sems)
+    for copy in copies:
+        copy.start()
+    for step, near in zip(STEPS, (near0, near1, near2, near3)):
         close[head_here(place, step)] = near[...]
     parts = []
     for part in range(4):
@@ -426,8 +436,14 @@
             here = jnp.concatenate([close[h, 0, rows, :], close[h, 1, rows, :]], axis=0)
             pieces.append((away.astype(F32) + here.astype(F32)).astype(BF16))
         parts.append(jnp.concatenate(pieces, axis=1))
+    copies[0].wait()
+    total = mm_nt(parts[1], wq[...])
+    copies[1].wait()
+    total = total + mm_nt(parts[2], wk[...])
+    copies[2].wait()
+    total = total + mm_nt(parts[3], wv[...])
+    copies[3].wait()
     mixed = mm(parts[0], wo[...])
-    total = mm_nt(parts[1], wq[...]) + mm_nt(parts[2], wk[...]) + mm_nt(parts[3], wv[...])
     own[0] = mixed[:HW]
     own[1] = total[:HW]
     other[0] = mixed[HW:].astype(BF16)
@@ -435,24 +451,18 @@
 
 
 def unproject(place, blocks, far, w_qkv, w_out):
-    whole = lambda shape: pl.BlockSpec(shape, lambda i, place: (0,) * len(shape))
-    part = lambda at: pl.BlockSpec((D, HALF * DH), lambda i, place: (0, at * 2 + place[0]))
     return pl.pallas_call(
         unproject_kernel,
-        grid_spec=pltpu.PrefetchScalarGridSpec(
-            num_scalar_prefetch=1,
-            grid=(1,),
-            in_specs=[whole((2, 4 * HW, DH))] * 4
-            + [whole((HALF, 2, ROWS, DH)), part(0), part(1), part(2)]
-            + [pl.BlockSpec((HALF * DH, D), lambda i, place: (place[0], 0))],
-            out_specs=[whole((2, HW, D))] * 2,
-            scratch_shapes=[pltpu.VMEM((HALF, 2, 4 * HW, DH), BF16)],
-        ),
+        in_specs=[SM] + [VM] * 5 + [ANY] * 2,
+        out_specs=[VM, VM],
+        scratch_shapes=[pltpu.VMEM((HALF, 2, 4 * HW, DH), BF16)]
+        + [pltpu.VMEM((D, HALF * DH), BF16)] * 3
+        + [pltpu.VMEM((HALF * DH, D), BF16), pltpu.SemaphoreType.DMA((4,))],
         out_shape=[jax.ShapeDtypeStruct((2, HW, D), F32), jax.ShapeDtypeStruct((2, HW, D), BF16)],
         compiler_params=pltpu.CompilerParams(vmem_limit_bytes=50 * 1024 * 1024),
         cost_estimate=cost(2 * PAIR * D * 4 * HALF * DH, 8_000_000),
         name="unproject",
-    )(place, *blocks, far, w_qkv, w_qkv, w_qkv, w_out)
+    )(place, *blocks, far, w_qkv, w_out)
 
 
 def finish_kernel(tokens, cot, gain, own, other, mixed, out):
@@ -489,6 +499,10 @@
 
 def turn_ring(value, steps):
     return lax.ppermute(value, "zh", [(i, (i + steps) % 4) for i in range(4)])
+
+
+def all_round(blocks, sign):
+    return [blocks[0]] + [turn_ring(blocks[g], sign * STEPS[g]) for g in (1, 2, 3)]
 
 
 def exchange(value, axes, groups=None):
@@ -514,7 +528,7 @@
     packed, *blocks = project(
         place, valid, tokens, other_tokens, cot, other_cot, gain, weights
     )
-    blocks = [blocks[0]] + [turn_ring(blocks[step], step) for step in (1, 2, 3)]
+    blocks = all_round(blocks, 1)
     mine = exchange(packed.reshape(2 * HALF, ROWS, DH), LANE)
     past = lax.ppermute(mine[:, K0:, :], "y", [(i, i + 1) for i in range(rows - 1)])
     near_kept, near_result, close = near_forward(*blocks)
@@ -524,7 +538,7 @@
     back = lax.ppermute(back, "y", [(i + 1, i) for i in range(rows - 1)])
     returned = near_backward(place, blocks, near_kept, near_result, close, told)
     own, returned = lax.optimization_barrier((own, returned))
-    returned = [returned[0]] + [turn_ring(returned[step], -step) for step in (1, 2, 3)]
+    returned = all_round(returned, -1)
     own = add_back(own, back)
     far = exchange_alone(own, go).reshape(HALF, 2, ROWS, DH)
     out_own, out_other = unproject(place, returned, far, w_qkv, w_out)

time: 131 us -> 130 us (level)
  blocking collectives: 47.7 us -> 44.2 us
  waiting for transfers between devices: 26.5 us -> 29.9 us
    ppermute x6, waiting for transfers between devices: 9.98 us -> 14 us  [turn_ring(): return lax.ppermute(value, 'zh', [(i, (i + steps) % 4) for i in range(4)])]
    all_to_all x2, blocking collectives: 47.7 us -> 44.2 us  [exchange(): lax.all_to_all(value, axes, 0, 0, axis_index_groups=groups, tiled=True)]
where the time goes in v6:
time: 130 us; the launch traced here: 129 us
  blocking collectives  44.2 us (34%)
  waiting for transfers between devices  29.9 us (23%)
  starting transfers between devices  29 us (22%)
  Pallas kernels  24 us (18%)
  between operations  1.47 us (1%)
    all_to_all x2, blocking collectives, exchange(): lax.all_to_all(value, axes, 0, 0, axis_index_groups=groups, tiled=True)  44.2 us
    ppermute x6, starting transfers between devices, turn_ring(): return lax.ppermute(value, 'zh', [(i, (i + steps) % 4) for i in range(4)])  17.1 us
    ppermute x6, waiting for transfers between devices, turn_ring(): return lax.ppermute(value, 'zh', [(i, (i + steps) % 4) for i in range(4)])  14 us
    all_to_all x1, waiting for transfers between devices, exchange(): lax.all_to_all(value, axes, 0, 0, axis_index_groups=groups, tiled=True)  12.8 us
    all_to_all x1, starting transfers between devices, exchange(): lax.all_to_all(value, axes, 0, 0, axis_index_groups=groups, tiled=True)  5.7 us
    pallas_call x1, Pallas kernels, unproject(): pl.pallas_call(unproject_kernel, in_specs=[SM] + [VM] * 5 + [ANY] * 2, ou...  4.43 us
    pallas_call x1, Pallas kernels, far_forward(): pl.pallas_call(far_forward_kernel, in_specs=[SM, SM, VM, VM, VM], out_spe...  3.41 us
    pallas_call x1, Pallas kernels, far_backward(): pl.pallas_call(far_backward_kernel, in_specs=[SM] + [VM] * 6, out_specs=[...  3.37 us
  transfers between devices with their start and end apart: 12, of which 5 were waited for; matrix products, arithmetic and copies ran while one was open for 0% of the time, Pallas kernels for 7%

profile of v6, /device:TPU:16, one launch (start us, length us, event | category | flops | bytes accessed | tf_op | source)
XLA Modules:
  0.0 128.8 jit_solution(2564695202131434142)
XLA Ops:
  0.6 0.1 collective-permute-start
  0.7 0.5 collective-permute-start.1
  1.9 0.1 pad_add_fusion.place
  2.0 2.8 %stage.1 = (bf16[1024,512]{1,0:T(8,128)(2,1)S(1)}, bf16[1024,512]{1,0:T(8,128)(2,1)S(1)}, bf16[1024,512]{1,0:T(8,128)(2,1)S(1)}, bf16[512,1024]{1,0:T(8,128)(2,1)S(1)}) custom-call(s32[3]{0:T(128)S(1)} %pad_add_fusion.place, bf16[1024,3072]{1,0:T(8,128)(2,1)} %w_qkv.3, bf16[1024,1024]{1,0:T(8,128)(2,1)} %w_out.3), custom_call_target="tpu_custom_call" | custom-call | bytes 9000000 | tf_op jit(solution)/shard_map/stage/pallas_call | solution.py:85
  4.8 3.2 %project.1 = (bf16[4,2,528,128]{3,2,1,0:T(8,128)(2,1)}, bf16[2,512,128]{2,1,0:T(8,128)(2,1)S(1)}, bf16[2,512,128]{2,1,0:T(8,128)(2,1)S(1)}, bf16[2,512,128]{2,1,0:T(8,128)(2,1)S(1)}, bf16[2,512,128]{2,1,0:T(8,128)(2,1)S(1)}) custom-call(s32[3]{0:T(128)S(1)} %pad_add_fusion.place, s32[1]{0:T(128)S(6)} %copy.13.valid, bf16[128,1024]{1,0:T(8,128)(2,1)S(1)} %bitcast.13, ...), custom_call_target="tpu_custom_call" | custom-call | flops 1073741824 | bytes 7000000 | tf_op jit(solution)/shard_map/project/pallas_call | solution.py:137
  8.0 5.7 %all-to-all-start.1 = ((bf16[8,528,128]{2,1,0:T(8,128)(2,1)}), bf16[8,528,128]{2,1,0:T(8,128)(2,1)S(1)}, u32[]{:S(2)}, u32[]{:S(2)}) async-start(bf16[8,528,128]{2,1,0:T(8,128)(2,1)} %bitcast.7), calls=%async_computation.1 | async-start | bytes 2162688 | tf_op jit(solution)/shard_map/all_to_all | solution.py:509
  13.7 6.2 %collective-permute-start.3 = (bf16[2,512,128]{2,1,0:T(8,128)(2,1)S(1)}, bf16[2,512,128]{2,1,0:T(8,128)(2,1)S(1)}, u32[]{:S(2)}, u32[]{:S(2)}) collective-permute-start(bf16[2,512,128]{2,1,0:T(8,128)(2,1)S(1)} %get-tuple-element.43), channel_id=1, source_target_pairs={{0,4},{2,6},{4,0},{6,2},{1,5},{3,7},{5,1},{7,3},{8,12},{10,14},{12... | collective-permute-start | bytes 786440 | tf_op jit(solution)/shard_map/ppermute | solution.py:501
  19.9 1.6 %collective-permute-start.4 = (bf16[2,512,128]{2,1,0:T(8,128)(2,1)S(1)}, bf16[2,512,128]{2,1,0:T(8,128)(2,1)S(1)}, u32[]{:S(2)}, u32[]{:S(2)}) collective-permute-start(bf16[2,512,128]{2,1,0:T(8,128)(2,1)S(1)} %get-tuple-element.44), channel_id=1, source_target_pairs={{0,2},{2,4},{4,6},{6,0},{1,3},{3,5},{5,7},{7,1},{8,10},{10,12},{12... | collective-permute-start | bytes 786440 | tf_op jit(solution)/shard_map/ppermute | solution.py:501
  21.5 2.6 %collective-permute-start.5 = (bf16[2,512,128]{2,1,0:T(8,128)(2,1)S(1)}, bf16[2,512,128]{2,1,0:T(8,128)(2,1)S(1)}, u32[]{:S(2)}, u32[]{:S(2)}) collective-permute-start(bf16[2,512,128]{2,1,0:T(8,128)(2,1)S(1)} %get-tuple-element.45), channel_id=1, source_target_pairs={{0,6},{2,0},{4,2},{6,4},{1,7},{3,1},{5,3},{7,5},{8,14},{10,8},{12,... | collective-permute-start | bytes 786440 | tf_op jit(solution)/shard_map/ppermute | solution.py:501
  24.1 12.8 %all-to-all-done.1.mine = bf16[8,528,128]{2,1,0:T(8,128)(2,1)S(1)} async-done(((bf16[8,528,128]{2,1,0:T(8,128)(2,1)}), bf16[8,528,128]{2,1,0:T(8,128)(2,1)S(1)}, u32[]{:S(2)}, u32[]{:S(2)}) %all-to-all-start.1) | async-done | bytes 1081376 | tf_op jit(solution)/shard_map/all_to_all | solution.py:509
  36.9 3.2 %collective-permute-start.2 = (bf16[8,272,128]{2,1,0:T(8,128)(2,1)S(1)}, bf16[8,272,128]{2,1,0:T(8,128)(2,1)S(1)}, u32[]{:S(2)}, u32[]{:S(2)}) collective-permute-start(bf16[8,272,128]{2,1,0:T(8,128)(2,1)S(1)} %slice.8), channel_id=1, source_target_pairs={{0,64},{64,128},{128,192},{1,65},{65,129},{129,193},{2,66},{66,130... | collective-permute-start | bytes 1671176 | tf_op jit(solution)/shard_map/ppermute | solution.py:533
  40.1 9.9 %collective-permute-done.3.near1 = bf16[2,512,128]{2,1,0:T(8,128)(2,1)S(1)} collective-permute-done((bf16[2,512,128]{2,1,0:T(8,128)(2,1)S(1)}, bf16[2,512,128]{2,1,0:T(8,128)(2,1)S(1)}, u32[]{:S(2)}, u32[]{:S(2)}) %collective-permute-start.3) | collective-permute-done | bytes 262176 | tf_op jit(solution)/shard_map/ppermute | solution.py:501
  50.0 4.1 %collective-permute-done.4.near2 = bf16[2,512,128]{2,1,0:T(8,128)(2,1)S(1)} collective-permute-done((bf16[2,512,128]{2,1,0:T(8,128)(2,1)S(1)}, bf16[2,512,128]{2,1,0:T(8,128)(2,1)S(1)}, u32[]{:S(2)}, u32[]{:S(2)}) %collective-permute-start.4) | collective-permute-done | bytes 262176 | tf_op jit(solution)/shard_map/ppermute | solution.py:501
  54.1 0.0 collective-permute-done.5.near3
  54.1 2.5 %near_forward.1 = (bf16[1024,1024]{1,0:T(8,128)(2,1)S(1)}, f32[128,1024]{1,0:T(8,128)S(1)}, f32[8,4,128]{2,1,0:T(4,128)S(1)}) custom-call(bf16[2,512,128]{2,1,0:T(8,128)(2,1)S(1)} %get-tuple-element.42.near0, bf16[2,512,128]{2,1,0:T(8,128)(2,1)S(1)} %collective-permute-done.3.near1, bf16[2,512,128]{2,1,0:T(8,128)(2,1)S(1)} %collective-permute-done.4.near2, ...), custom_call_target="tpu_custom_call" | custom-call | flops 10737418240 | bytes 4000000 | tf_op jit(solution)/shard_map/near_forward/pallas_call | solution.py:183
  56.6 0.0 collective-permute-done.2.past
  56.6 3.4 %far_forward.1 = (f32[8,8,128]{2,1,0:T(8,128)S(1)}, bf16[4,1152,256]{2,1,0:T(8,128)(2,1)S(1)}, f32[128,1024]{1,0:T(8,128)S(1)}) custom-call(s32[3]{0:T(128)S(1)} %pad_add_fusion.place, s32[8]{0:T(128)S(1)} %copy-done.3, bf16[8,528,128]{2,1,0:T(8,128)(2,1)S(1)} %all-to-all-done.1.mine, bf16[8,272,128]{2,1,0:T(8,128)(2,1)S(1)} %collective-permute-done.2.past, ...), custom_call_target="tpu_custom_call" | custom-call | flops 603979776 | bytes 5000000 | tf_op jit(solution)/shard_map/far_forward/pallas_call | solution.py:248
  60.0 16.3 %all_to_all.15.told = f32[8,8,128]{2,1,0:T(8,128)S(1)} all-to-all(f32[8,8,128]{2,1,0:T(8,128)S(1)} %get-tuple-element.49.sent), channel_id=1, replica_groups={{0,8,22,30,36,44,50,58},{2,10,16,24,38,46,52,60},{4,12,18,26,32,40,54,6..., dimensions={0} | all-to-all | bytes 65536 | tf_op jit(solution)/shard_map/all_to_all | solution.py:509
  76.4 3.4 %far_backward.1 = (bf16[8,528,128]{2,1,0:T(8,128)(2,1)S(1)}, bf16[8,256,128]{2,1,0:T(8,128)(2,1)S(1)}) custom-call(s32[3]{0:T(128)S(1)} %pad_add_fusion.place, bf16[8,528,128]{2,1,0:T(8,128)(2,1)S(1)} %all-to-all-done.1.mine, bf16[8,272,128]{2,1,0:T(8,128)(2,1)S(1)} %collective-permute-done.2.past, bf16[4,1152,256]{2,1,0:T(8,128)(2,1)S(1)} %get-tuple-element.47.kept, ...), custom_call_target="tpu_custom_call" | custom-call | flops 1207959552 | bytes 6000000 | tf_op jit(solution)/shard_map/far_backward/pallas_call | solution.py:380
  79.7 2.3 %collective-permute-start.9 = (bf16[8,256,128]{2,1,0:T(8,128)(2,1)S(1)}, bf16[8,256,128]{2,1,0:T(8,128)(2,1)S(1)}, u32[]{:S(2)}, u32[]{:S(2)}) collective-permute-start(bf16[8,256,128]{2,1,0:T(8,128)(2,1)S(1)} %get-tuple-element.62), channel_id=1, source_target_pairs={{64,0},{128,64},{192,128},{65,1},{129,65},{193,129},{66,2},{130,66... | collective-permute-start | bytes 1572872 | tf_op jit(solution)/shard_map/ppermute | solution.py:538
  82.1 2.9 %near_backward.1 = (bf16[2,512,128]{2,1,0:T(8,128)(2,1)S(1)}, bf16[2,512,128]{2,1,0:T(8,128)(2,1)S(1)}, bf16[2,512,128]{2,1,0:T(8,128)(2,1)S(1)}, bf16[2,512,128]{2,1,0:T(8,128)(2,1)S(1)}) custom-call(s32[3]{0:T(128)S(1)} %pad_add_fusion.place, bf16[2,512,128]{2,1,0:T(8,128)(2,1)S(1)} %get-tuple-element.42.near0, ...), custom_call_target="tpu_custom_call" | custom-call | flops 1073741824 | bytes 5000000 | tf_op jit(solution)/shard_map/near_backward/pallas_call | solution.py:317
  85.0 3.8 %collective-permute-start.6 = (bf16[2,512,128]{2,1,0:T(8,128)(2,1)S(1)}, bf16[2,512,128]{2,1,0:T(8,128)(2,1)S(1)}, u32[]{:S(2)}, u32[]{:S(2)}) collective-permute-start(bf16[2,512,128]{2,1,0:T(8,128)(2,1)S(1)} %get-tuple-element.58), channel_id=1, source_target_pairs={{0,4},{2,6},{4,0},{6,2},{1,5},{3,7},{5,1},{7,3},{8,12},{10,14},{12... | collective-permute-start | bytes 786440 | tf_op jit(solution)/shard_map/ppermute | solution.py:501
  88.8 1.5 %collective-permute-start.7 = (bf16[2,512,128]{2,1,0:T(8,128)(2,1)S(1)}, bf16[2,512,128]{2,1,0:T(8,128)(2,1)S(1)}, u32[]{:S(2)}, u32[]{:S(2)}) collective-permute-start(bf16[2,512,128]{2,1,0:T(8,128)(2,1)S(1)} %get-tuple-element.59), channel_id=1, source_target_pairs={{0,6},{2,0},{4,2},{6,4},{1,7},{3,1},{5,3},{7,5},{8,14},{10,8},{12,... | collective-permute-start | bytes 786440 | tf_op jit(solution)/shard_map/ppermute | solution.py:501
  90.2 1.5 %collective-permute-start.8 = (bf16[2,512,128]{2,1,0:T(8,128)(2,1)S(1)}, bf16[2,512,128]{2,1,0:T(8,128)(2,1)S(1)}, u32[]{:S(2)}, u32[]{:S(2)}) collective-permute-start(bf16[2,512,128]{2,1,0:T(8,128)(2,1)S(1)} %get-tuple-element.60), channel_id=1, source_target_pairs={{0,2},{2,4},{4,6},{6,0},{1,3},{3,5},{5,7},{7,1},{8,10},{10,12},{12... | collective-permute-start | bytes 786440 | tf_op jit(solution)/shard_map/ppermute | solution.py:501
  91.8 1.2 collective-permute-done.9.back
  93.0 0.4 add_back.1
  93.4 27.9 %conditional.1 = (bf16[4,2,528,128]{3,2,1,0:T(8,128)(2,1)}) conditional(s32[]{:T(128)} %bitcast.8, () %tuple.18, bf16[8,528,128]{2,1,0:T(8,128)(2,1)S(1)} %add_back.1), branch_computations={%region_0.0_spmd, %region_1.0_spmd} | conditional | bytes 2162696 | solution.py:513
  93.4 27.9 %all_to_all.14 = bf16[8,528,128]{2,1,0:T(8,128)(2,1)} all-to-all(bf16[8,528,128]{2,1,0:T(8,128)(2,1)S(1)} %param.1), channel_id=1, replica_groups=mesh['y'=4,'x'=4,'zl'=2,'zh'=4,'core'=2] {'x','zl'}, dimensions={0} | all-to-all | bytes 2162688 | tf_op jit(solution)/shard_map/cond/branch_1_fun/all_to_all | solution.py:509
  121.3 4.4 %unproject.1 = (f32[2,128,1024]{2,1,0:T(8,128)S(1)}, bf16[2,128,1024]{2,1,0:T(8,128)(2,1)S(1)}) custom-call(s32[3]{0:T(128)S(1)} %pad_add_fusion.place, bf16[2,512,128]{2,1,0:T(8,128)(2,1)S(1)} %get-tuple-element.57.near0, bf16[2,512,128]{2,1,0:T(8,128)(2,1)S(1)} %collective-permute-done.6.near1, bf16[2,512,128]{2,1,0:T(8,128)(2,1)S(1)} %collective-permute-done.7.near2, ...), custom_call_target="tpu_custom_call" | custom-call | flops 1073741824 | bytes 8000000 | tf_op jit(solution)/shard_map/unproject/pallas_call | solution.py:454
  125.7 0.1 collective-permute-start.10
  125.8 1.9 %collective-permute-done.10.other = bf16[2,128,1024]{2,1,0:T(8,128)(2,1)S(1)} collective-permute-done((bf16[2,128,1024]{2,1,0:T(8,128)(2,1)S(1)}, bf16[2,128,1024]{2,1,0:T(8,128)(2,1)S(1)}, u32[]{:S(2)}, u32[]{:S(2)}) %collective-permute-start.10) | collective-permute-done | bytes 524320 | tf_op jit(solution)/shard_map/ppermute | solution.py:497
  127.7 1.0 finish.1
  (14 shorter events, 0.1 us)
Async XLA Ops:
  0.6 4.1 %collective-permute-start = (bf16[128,1024]{1,0:T(8,128)(2,1)}, bf16[128,1024]{1,0:T(8,128)(2,1)S(1)}, u32[]{:S(2)}, u32[]{:S(2)}) collective-permute-start(bf16[128,1024]{1,0:T(8,128)(2,1)} %bitcast.12), channel_id=1, source_target_pairs={{0,1},{1,0},{2,3},{3,2},{4,5},{5,4},{6,7},{7,6},{8,9},{9,8},{10,11... | collective-permute-start | bytes 786440 | tf_op jit(solution)/shard_map/ppermute | solution.py:497
  0.7 4.0 %collective-permute-start.1 = (bf16[128,1024]{1,0:T(8,128)(2,1)}, bf16[128,1024]{1,0:T(8,128)(2,1)S(1)}, u32[]{:S(2)}, u32[]{:S(2)}) collective-permute-start(bf16[128,1024]{1,0:T(8,128)(2,1)} %bitcast.15), channel_id=1, source_target_pairs={{0,1},{1,0},{2,3},{3,2},{4,5},{5,4},{6,7},{7,6},{8,9},{9,8},{10,11... | collective-permute-start | bytes 786440 | tf_op jit(solution)/shard_map/ppermute | solution.py:497
  2.0 2.8 %copy-start = (bf16[1,1,128,1024]{3,2,1,0:T(8,128)(2,1)S(1)}, bf16[1,1,128,1024]{3,2,1,0:T(8,128)(2,1)}, u32[]{:S(2)}) copy-start(bf16[1,1,128,1024]{3,2,1,0:T(8,128)(2,1)} %param.9) | copy-start | bytes 786436
  2.0 2.8 %copy-start.1 = (bf16[1,1,128,1024]{3,2,1,0:T(8,128)(2,1)S(1)}, bf16[1,1,128,1024]{3,2,1,0:T(8,128)(2,1)}, u32[]{:S(2)}) copy-start(bf16[1,1,128,1024]{3,2,1,0:T(8,128)(2,1)} %param.15) | copy-start | bytes 786436
  2.0 2.8 %copy-start.2 = (f32[1024]{0:T(1024)S(1)}, f32[1024]{0:T(1024)}, u32[]{:S(2)}) copy-start(f32[1024]{0:T(1024)} %param.10) | copy-start | bytes 12292
  8.0 28.8 %all-to-all-start.1 = ((bf16[8,528,128]{2,1,0:T(8,128)(2,1)}), bf16[8,528,128]{2,1,0:T(8,128)(2,1)S(1)}, u32[]{:S(2)}, u32[]{:S(2)}) async-start(bf16[8,528,128]{2,1,0:T(8,128)(2,1)} %bitcast.7), calls=%async_computation.1 | async-start | bytes 2162688 | tf_op jit(solution)/shard_map/all_to_all | solution.py:509
  13.7 36.3 %collective-permute-start.3 = (bf16[2,512,128]{2,1,0:T(8,128)(2,1)S(1)}, bf16[2,512,128]{2,1,0:T(8,128)(2,1)S(1)}, u32[]{:S(2)}, u32[]{:S(2)}) collective-permute-start(bf16[2,512,128]{2,1,0:T(8,128)(2,1)S(1)} %get-tuple-element.43), channel_id=1, source_target_pairs={{0,4},{2,6},{4,0},{6,2},{1,5},{3,7},{5,1},{7,3},{8,12},{10,14},{12... | collective-permute-start | bytes 786440 | tf_op jit(solution)/shard_map/ppermute | solution.py:501
  19.9 34.2 %collective-permute-start.4 = (bf16[2,512,128]{2,1,0:T(8,128)(2,1)S(1)}, bf16[2,512,128]{2,1,0:T(8,128)(2,1)S(1)}, u32[]{:S(2)}, u32[]{:S(2)}) collective-permute-start(bf16[2,512,128]{2,1,0:T(8,128)(2,1)S(1)} %get-tuple-element.44), channel_id=1, source_target_pairs={{0,2},{2,4},{4,6},{6,0},{1,3},{3,5},{5,7},{7,1},{8,10},{10,12},{12... | collective-permute-start | bytes 786440 | tf_op jit(solution)/shard_map/ppermute | solution.py:501
  21.5 32.6 %collective-permute-start.5 = (bf16[2,512,128]{2,1,0:T(8,128)(2,1)S(1)}, bf16[2,512,128]{2,1,0:T(8,128)(2,1)S(1)}, u32[]{:S(2)}, u32[]{:S(2)}) collective-permute-start(bf16[2,512,128]{2,1,0:T(8,128)(2,1)S(1)} %get-tuple-element.45), channel_id=1, source_target_pairs={{0,6},{2,0},{4,2},{6,4},{1,7},{3,1},{5,3},{7,5},{8,14},{10,8},{12,... | collective-permute-start | bytes 786440 | tf_op jit(solution)/shard_map/ppermute | solution.py:501
  36.9 19.7 %collective-permute-start.2 = (bf16[8,272,128]{2,1,0:T(8,128)(2,1)S(1)}, bf16[8,272,128]{2,1,0:T(8,128)(2,1)S(1)}, u32[]{:S(2)}, u32[]{:S(2)}) collective-permute-start(bf16[8,272,128]{2,1,0:T(8,128)(2,1)S(1)} %slice.8), channel_id=1, source_target_pairs={{0,64},{64,128},{128,192},{1,65},{65,129},{129,193},{2,66},{66,130... | collective-permute-start | bytes 1671176 | tf_op jit(solution)/shard_map/ppermute | solution.py:533
  54.1 2.5 %copy-start.3 = (s32[8]{0:T(128)S(1)}, s32[8]{0:T(128)}, u32[]{:S(2)}) copy-start(s32[8]{0:T(128)} %win.1) | copy-start | bytes 100
  79.7 13.2 %collective-permute-start.9 = (bf16[8,256,128]{2,1,0:T(8,128)(2,1)S(1)}, bf16[8,256,128]{2,1,0:T(8,128)(2,1)S(1)}, u32[]{:S(2)}, u32[]{:S(2)}) collective-permute-start(bf16[8,256,128]{2,1,0:T(8,128)(2,1)S(1)} %get-tuple-element.62), channel_id=1, source_target_pairs={{64,0},{128,64},{192,128},{65,1},{129,65},{193,129},{66,2},{130,66... | collective-permute-start | bytes 1572872 | tf_op jit(solution)/shard_map/ppermute | solution.py:538
  85.0 36.3 %collective-permute-start.6 = (bf16[2,512,128]{2,1,0:T(8,128)(2,1)S(1)}, bf16[2,512,128]{2,1,0:T(8,128)(2,1)S(1)}, u32[]{:S(2)}, u32[]{:S(2)}) collective-permute-start(bf16[2,512,128]{2,1,0:T(8,128)(2,1)S(1)} %get-tuple-element.58), channel_id=1, source_target_pairs={{0,4},{2,6},{4,0},{6,2},{1,5},{3,7},{5,1},{7,3},{8,12},{10,14},{12... | collective-permute-start | bytes 786440 | tf_op jit(solution)/shard_map/ppermute | solution.py:501
  88.8 32.5 %collective-permute-start.7 = (bf16[2,512,128]{2,1,0:T(8,128)(2,1)S(1)}, bf16[2,512,128]{2,1,0:T(8,128)(2,1)S(1)}, u32[]{:S(2)}, u32[]{:S(2)}) collective-permute-start(bf16[2,512,128]{2,1,0:T(8,128)(2,1)S(1)} %get-tuple-element.59), channel_id=1, source_target_pairs={{0,6},{2,0},{4,2},{6,4},{1,7},{3,1},{5,3},{7,5},{8,14},{10,8},{12,... | collective-permute-start | bytes 786440 | tf_op jit(solution)/shard_map/ppermute | solution.py:501
  90.2 31.1 %collective-permute-start.8 = (bf16[2,512,128]{2,1,0:T(8,128)(2,1)S(1)}, bf16[2,512,128]{2,1,0:T(8,128)(2,1)S(1)}, u32[]{:S(2)}, u32[]{:S(2)}) collective-permute-start(bf16[2,512,128]{2,1,0:T(8,128)(2,1)S(1)} %get-tuple-element.60), channel_id=1, source_target_pairs={{0,2},{2,4},{4,6},{6,0},{1,3},{3,5},{5,7},{7,1},{8,10},{10,12},{12... | collective-permute-start | bytes 786440 | tf_op jit(solution)/shard_map/ppermute | solution.py:501
  125.7 2.0 %collective-permute-start.10 = (bf16[2,128,1024]{2,1,0:T(8,128)(2,1)S(1)}, bf16[2,128,1024]{2,1,0:T(8,128)(2,1)S(1)}, u32[]{:S(2)}, u32[]{:S(2)}) collective-permute-start(bf16[2,128,1024]{2,1,0:T(8,128)(2,1)S(1)} %get-tuple-element.64), channel_id=1, source_target_pairs={{0,1},{1,0},{2,3},{3,2},{4,5},{5,4},{6,7},{7,6},{8,9},{9,8},{10,11... | collective-permute-start | bytes 1572872 | tf_op jit(solution)/shard_map/ppermute | solution.py:497

commit v7 on v6

--- a/solution.py
+++ b/solution.py
@@ -57,28 +57,55 @@
     return pl.CostEstimate(flops=flops, bytes_accessed=size, transcendentals=exps)
 
 
+PIECES = 4
+
+
 def weight_copies(place, w_qkv, w_out, parts, out, sems):
     begin = pl.multiple_of(place[0] * HALF * DH, HALF * DH)
-    copies = [
-        pltpu.make_async_copy(
-            w_qkv.at[:, pl.ds(pl.multiple_of(begin + part * D, HALF * DH), HALF * DH)],
-            parts[part],
-            sems.at[part],
+    groups = []
+    for part in range(3):
+        columns = pl.ds(pl.multiple_of(begin + part * D, HALF * DH), HALF * DH)
+        size = D // PIECES
+        groups.append(
+            [
+                pltpu.make_async_copy(
+                    w_qkv.at[pl.ds(n * size, size), columns],
+                    parts[part].at[pl.ds(n * size, size), :],
+                    sems.at[part * PIECES + n],
+                )
+                for n in range(PIECES)
+            ]
         )
-        for part in range(3)
-    ]
-    copies.append(
-        pltpu.make_async_copy(w_out.at[pl.ds(begin, HALF * DH), :], out, sems.at[3])
+    size = HALF * DH // PIECES
+    groups.append(
+        [
+            pltpu.make_async_copy(
+                w_out.at[pl.ds(pl.multiple_of(begin + n * size, size), size), :],
+                out.at[pl.ds(n * size, size), :],
+                sems.at[3 * PIECES + n],
+            )
+            for n in range(PIECES)
+        ]
     )
-    return copies
+    return groups
+
+
+def start_all(groups):
+    for group in groups:
+        for copy in group:
+            copy.start()
+
+
+def wait_all(group):
+    for copy in group:
+        copy.wait()
 
 
 def stage_kernel(place, w_qkv, w_out, wq, wk, wv, out, sems):
-    copies = weight_copies(place, w_qkv, w_out, (wq, wk, wv), out, sems)
-    for copy in copies:
-        copy.start()
-    for copy in copies:
-        copy.wait()
+    groups = weight_copies(place, w_qkv, w_out, (wq, wk, wv), out, sems)
+    start_all(groups)
+    for group in groups:
+        wait_all(group)
 
 
 def stage(place, w_qkv, w_out):
@@ -88,7 +115,7 @@
         out_specs=[VM] * 4,
         out_shape=[jax.ShapeDtypeStruct((D, HALF * DH), BF16)] * 3
         + [jax.ShapeDtypeStruct((HALF * DH, D), BF16)],
-        scratch_shapes=[pltpu.SemaphoreType.DMA((4,))],
+        scratch_shapes=[pltpu.SemaphoreType.DMA((4 * PIECES,))],
         compiler_params=pltpu.CompilerParams(vmem_limit_bytes=STAGE_LIMIT),
         cost_estimate=cost(0, 9_000_000),
         name="stage",
@@ -331,7 +358,7 @@
 
 
 def far_backward_kernel(
-    place, mine, past, kept, result, sent, told, own, back, keys_t, values, dk, dv, grads
+    place, mine, past, kept, result, sent, told, own, back0, back1, keys_t, values, dk, dv, grads
 ):
     for j in range(GROUP):
         keys_t[:, j * HW : (j + 1) * HW] = turn(past[j, :HW, :]).astype(BF16)
@@ -369,8 +396,10 @@
     for j in range(GROUP):
         early = slice(j * HW, (j + 1) * HW)
         late = slice((GROUP + j) * HW, (GROUP + j + 1) * HW)
-        back[j, :HW, :] = (dk[early, :] * SCALE).astype(BF16)
-        back[j, HW:, :] = dv[early, :].astype(BF16)
+        d_keys = (dk[early, :] * SCALE).astype(BF16)
+        d_values = dv[early, :].astype(BF16)
+        back0[j] = d_keys
+        back1[j] = d_values
         own[j, 2 * HW : 3 * HW, :] = (dk[late, :] * SCALE).astype(BF16)
         own[j, 3 * HW : 4 * HW, :] = dv[late, :].astype(BF16)
         own[j, 4 * HW :, :] = jnp.zeros((ROWS - 4 * HW, DH), BF16)
@@ -380,11 +409,9 @@
     return pl.pallas_call(
         far_backward_kernel,
         in_specs=[SM] + [VM] * 6,
-        out_specs=[VM, VM],
-        out_shape=[
-            jax.ShapeDtypeStruct((GROUP, ROWS, DH), BF16),
-            jax.ShapeDtypeStruct((GROUP, 2 * HW, DH), BF16),
-        ],
+        out_specs=[VM] * 3,
+        out_shape=[jax.ShapeDtypeStruct((GROUP, ROWS, DH), BF16)]
+        + [jax.ShapeDtypeStruct((GROUP, HW, DH), BF16)] * 2,
         scratch_shapes=[
             pltpu.VMEM((DH, 2 * GROUP * HW), BF16),
             pltpu.VMEM((2 * GROUP * HW, DH), BF16),
@@ -398,32 +425,31 @@
     )(place, mine, past, kept, result, sent, told)
 
 
-def add_back_kernel(own, back, out):
-    for j in range(GROUP):
-        out[j, 2 * HW : 4 * HW, :] = (
-            own[j, 2 * HW : 4 * HW, :].astype(F32) + back[j].astype(F32)
-        ).astype(BF16)
-
-
-def add_back(own, back):
+def add_back_kernel(own, back0, back1, out):
+    for n, back in enumerate((back0, back1)):
+        rows = slice((2 + n) * HW, (3 + n) * HW)
+        for j in range(GROUP):
+            out[j, rows, :] = (own[j, rows, :].astype(F32) + back[j].astype(F32)).astype(BF16)
+
+
+def add_back(own, *back):
     return pl.pallas_call(
         add_back_kernel,
-        in_specs=[VM] * 2,
+        in_specs=[VM] * 3,
         out_specs=VM,
         out_shape=jax.ShapeDtypeStruct((GROUP, ROWS, DH), BF16),
         input_output_aliases={0: 0},
         compiler_params=params(),
         cost_estimate=cost(GROUP * 2 * HW * DH, 2_500_000),
         name="add_back",
-    )(own, back)
+    )(own, *back)
 
 
 def unproject_kernel(
     place, near0, near1, near2, near3, far, w_qkv, w_out, own, other, close, wq, wk, wv, wo, sems
 ):
-    copies = weight_copies(place, w_qkv, w_out, (wq, wk, wv), wo, sems)
-    for copy in copies:
-        copy.start()
+    groups = weight_copies(place, w_qkv, w_out, (wq, wk, wv), wo, sems)
+    start_all(groups)
     for step, near in zip(STEPS, (near0, near1, near2, near3)):
         close[head_here(place, step)] = near[...]
     parts = []
@@ -436,13 +462,13 @@
             here = jnp.concatenate([close[h, 0, rows, :], close[h, 1, rows, :]], axis=0)
             pieces.append((away.astype(F32) + here.astype(F32)).astype(BF16))
         parts.append(jnp.concatenate(pieces, axis=1))
-    copies[0].wait()
+    wait_all(groups[0])
     total = mm_nt(parts[1], wq[...])
-    copies[1].wait()
+    wait_all(groups[1])
     total = total + mm_nt(parts[2], wk[...])
-    copies[2].wait()
+    wait_all(groups[2])
     total = total + mm_nt(parts[3], wv[...])
-    copies[3].wait()
+    wait_all(groups[3])
     mixed = mm(parts[0], wo[...])
     own[0] = mixed[:HW]
     own[1] = total[:HW]
@@ -457,7 +483,7 @@
         out_specs=[VM, VM],
         scratch_shapes=[pltpu.VMEM((HALF, 2, 4 * HW, DH), BF16)]
         + [pltpu.VMEM((D, HALF * DH), BF16)] * 3
-        + [pltpu.VMEM((HALF * DH, D), BF16), pltpu.SemaphoreType.DMA((4,))],
+        + [pltpu.VMEM((HALF * DH, D), BF16), pltpu.SemaphoreType.DMA((4 * PIECES,))],
         out_shape=[jax.ShapeDtypeStruct((2, HW, D), F32), jax.ShapeDtypeStruct((2, HW, D), BF16)],
         compiler_params=pltpu.CompilerParams(vmem_limit_bytes=50 * 1024 * 1024),
         cost_estimate=cost(2 * PAIR * D * 4 * HALF * DH, 8_000_000),
@@ -534,12 +560,13 @@
     near_kept, near_result, close = near_forward(*blocks)
     sent, far_kept, far_result = far_forward(place, window, mine, past, close)
     told = exchange(sent, ("x", "zl", "zh"), SAME_HEAD)
-    own, back = far_backward(place, mine, past, far_kept, far_result, sent, told)
-    back = lax.ppermute(back, "y", [(i + 1, i) for i in range(rows - 1)])
     returned = near_backward(place, blocks, near_kept, near_result, close, told)
+    told, returned = lax.optimization_barrier((told, returned))
+    own, *back = far_backward(place, mine, past, far_kept, far_result, sent, told)
+    back = [lax.ppermute(b, "y", [(i + 1, i) for i in range(rows - 1)]) for b in back]
+    returned = all_round(returned, -1)
     own, returned = lax.optimization_barrier((own, returned))
-    returned = all_round(returned, -1)
-    own = add_back(own, back)
+    own = add_back(own, *back)
     far = exchange_alone(own, go).reshape(HALF, 2, ROWS, DH)
     out_own, out_other = unproject(place, returned, far, w_qkv, w_out)
     mixed, d_tokens = finish(tokens, cot, gain, out_own, swap(out_other))

time: 130 us -> 133 us (1.023)
  waiting for transfers between devices: 29.9 us -> 39.6 us
  blocking collectives: 44.2 us -> 35.4 us
  starting transfers between devices: 29 us -> 31.5 us
    ppermute x6, waiting for transfers between devices: 14 us -> 24.9 us  [turn_ring(): return lax.ppermute(value, 'zh', [(i, (i + steps) % 4) for i in range(4)])]
    all_to_all x2, blocking collectives: 44.2 us -> 35.4 us  [exchange(): lax.all_to_all(value, axes, 0, 0, axis_index_groups=groups, tiled=True)]
    ppermute x1 -> x2, starting transfers between devices: 2.35 us -> 4.71 us  [per_device(): lax.ppermute(b, 'y', [(i + 1, i) for i in range(rows - 1)])]
  transfers between devices with their start and end apart: 12 -> 13, of which waited for: 5 -> 6; matrix products, arithmetic and copies ran while one was open for 0% -> 0% of each run, Pallas kernels for 7% -> 7%
where the time goes in v7:
time: 133 us; the launch traced here: 132 us
  waiting for transfers between devices  39.6 us (30%)
  blocking collectives  35.4 us (27%)
  starting transfers between devices  31.5 us (24%)
  Pallas kernels  23.5 us (18%)
  between operations  1.47 us (1%)
    all_to_all x2, blocking collectives, exchange(): lax.all_to_all(value, axes, 0, 0, axis_index_groups=groups, tiled=True)  35.4 us
    ppermute x6, waiting for transfers between devices, turn_ring(): return lax.ppermute(value, 'zh', [(i, (i + steps) % 4) for i in range(4)])  24.9 us
    ppermute x6, starting transfers between devices, turn_ring(): return lax.ppermute(value, 'zh', [(i, (i + steps) % 4) for i in range(4)])  17.2 us
    all_to_all x1, waiting for transfers between devices, exchange(): lax.all_to_all(value, axes, 0, 0, axis_index_groups=groups, tiled=True)  12.8 us
    all_to_all x1, starting transfers between devices, exchange(): lax.all_to_all(value, axes, 0, 0, axis_index_groups=groups, tiled=True)  5.7 us
    ppermute x2, starting transfers between devices, per_device(): lax.ppermute(b, 'y', [(i + 1, i) for i in range(rows - 1)])  4.71 us
    pallas_call x1, Pallas kernels, unproject(): pl.pallas_call(unproject_kernel, in_specs=[SM] + [VM] * 5 + [ANY] * 2, ou...  3.8 us
    pallas_call x1, Pallas kernels, far_forward(): pl.pallas_call(far_forward_kernel, in_specs=[SM, SM, VM, VM, VM], out_spe...  3.4 us
  transfers between devices with their start and end apart: 13, of which 6 were waited for; matrix products, arithmetic and copies ran while one was open for 0% of the time, Pallas kernels for 7%

profile of v7, /device:TPU:16, one launch (start us, length us, event | category | flops | bytes accessed | tf_op | source)
XLA Modules:
  0.0 131.6 jit_solution(10213386879872909277)
XLA Ops:
  0.6 0.1 collective-permute-start
  0.7 0.5 collective-permute-start.1
  1.9 0.1 pad_add_fusion.place
  2.0 2.8 %stage.1 = (bf16[1024,512]{1,0:T(8,128)(2,1)S(1)}, bf16[1024,512]{1,0:T(8,128)(2,1)S(1)}, bf16[1024,512]{1,0:T(8,128)(2,1)S(1)}, bf16[512,1024]{1,0:T(8,128)(2,1)S(1)}) custom-call(s32[3]{0:T(128)S(1)} %pad_add_fusion.place, bf16[1024,3072]{1,0:T(8,128)(2,1)} %w_qkv.3, bf16[1024,1024]{1,0:T(8,128)(2,1)} %w_out.3), custom_call_target="tpu_custom_call" | custom-call | bytes 9000000 | tf_op jit(solution)/shard_map/stage/pallas_call | solution.py:112
  4.9 3.2 %project.1 = (bf16[4,2,528,128]{3,2,1,0:T(8,128)(2,1)}, bf16[2,512,128]{2,1,0:T(8,128)(2,1)S(1)}, bf16[2,512,128]{2,1,0:T(8,128)(2,1)S(1)}, bf16[2,512,128]{2,1,0:T(8,128)(2,1)S(1)}, bf16[2,512,128]{2,1,0:T(8,128)(2,1)S(1)}) custom-call(s32[3]{0:T(128)S(1)} %pad_add_fusion.place, s32[1]{0:T(128)S(6)} %copy.13.valid, bf16[128,1024]{1,0:T(8,128)(2,1)S(1)} %bitcast.13, ...), custom_call_target="tpu_custom_call" | custom-call | flops 1073741824 | bytes 7000000 | tf_op jit(solution)/shard_map/project/pallas_call | solution.py:164
  8.1 5.7 %all-to-all-start.1 = ((bf16[8,528,128]{2,1,0:T(8,128)(2,1)}), bf16[8,528,128]{2,1,0:T(8,128)(2,1)S(1)}, u32[]{:S(2)}, u32[]{:S(2)}) async-start(bf16[8,528,128]{2,1,0:T(8,128)(2,1)} %bitcast.7), calls=%async_computation.1 | async-start | bytes 2162688 | tf_op jit(solution)/shard_map/all_to_all | solution.py:535
  13.8 6.2 %collective-permute-start.3 = (bf16[2,512,128]{2,1,0:T(8,128)(2,1)S(1)}, bf16[2,512,128]{2,1,0:T(8,128)(2,1)S(1)}, u32[]{:S(2)}, u32[]{:S(2)}) collective-permute-start(bf16[2,512,128]{2,1,0:T(8,128)(2,1)S(1)} %get-tuple-element.49), channel_id=1, source_target_pairs={{0,4},{2,6},{4,0},{6,2},{1,5},{3,7},{5,1},{7,3},{8,12},{10,14},{12... | collective-permute-start | bytes 786440 | tf_op jit(solution)/shard_map/ppermute | solution.py:527
  20.0 1.5 %collective-permute-start.4 = (bf16[2,512,128]{2,1,0:T(8,128)(2,1)S(1)}, bf16[2,512,128]{2,1,0:T(8,128)(2,1)S(1)}, u32[]{:S(2)}, u32[]{:S(2)}) collective-permute-start(bf16[2,512,128]{2,1,0:T(8,128)(2,1)S(1)} %get-tuple-element.50), channel_id=1, source_target_pairs={{0,2},{2,4},{4,6},{6,0},{1,3},{3,5},{5,7},{7,1},{8,10},{10,12},{12... | collective-permute-start | bytes 786440 | tf_op jit(solution)/shard_map/ppermute | solution.py:527
  21.5 2.6 %collective-permute-start.5 = (bf16[2,512,128]{2,1,0:T(8,128)(2,1)S(1)}, bf16[2,512,128]{2,1,0:T(8,128)(2,1)S(1)}, u32[]{:S(2)}, u32[]{:S(2)}) collective-permute-start(bf16[2,512,128]{2,1,0:T(8,128)(2,1)S(1)} %get-tuple-element.51), channel_id=1, source_target_pairs={{0,6},{2,0},{4,2},{6,4},{1,7},{3,1},{5,3},{7,5},{8,14},{10,8},{12,... | collective-permute-start | bytes 786440 | tf_op jit(solution)/shard_map/ppermute | solution.py:527
  24.1 12.8 %all-to-all-done.1.mine = bf16[8,528,128]{2,1,0:T(8,128)(2,1)S(1)} async-done(((bf16[8,528,128]{2,1,0:T(8,128)(2,1)}), bf16[8,528,128]{2,1,0:T(8,128)(2,1)S(1)}, u32[]{:S(2)}, u32[]{:S(2)}) %all-to-all-start.1) | async-done | bytes 1081376 | tf_op jit(solution)/shard_map/all_to_all | solution.py:535
  36.9 3.2 %collective-permute-start.2 = (bf16[8,272,128]{2,1,0:T(8,128)(2,1)S(1)}, bf16[8,272,128]{2,1,0:T(8,128)(2,1)S(1)}, u32[]{:S(2)}, u32[]{:S(2)}) collective-permute-start(bf16[8,272,128]{2,1,0:T(8,128)(2,1)S(1)} %slice.8), channel_id=1, source_target_pairs={{0,64},{64,128},{128,192},{1,65},{65,129},{129,193},{2,66},{66,130... | collective-permute-start | bytes 1671176 | tf_op jit(solution)/shard_map/ppermute | solution.py:559
  40.1 9.9 %collective-permute-done.3.near1 = bf16[2,512,128]{2,1,0:T(8,128)(2,1)S(1)} collective-permute-done((bf16[2,512,128]{2,1,0:T(8,128)(2,1)S(1)}, bf16[2,512,128]{2,1,0:T(8,128)(2,1)S(1)}, u32[]{:S(2)}, u32[]{:S(2)}) %collective-permute-start.3) | collective-permute-done | bytes 262176 | tf_op jit(solution)/shard_map/ppermute | solution.py:527
  50.1 4.1 %collective-permute-done.4.near2 = bf16[2,512,128]{2,1,0:T(8,128)(2,1)S(1)} collective-permute-done((bf16[2,512,128]{2,1,0:T(8,128)(2,1)S(1)}, bf16[2,512,128]{2,1,0:T(8,128)(2,1)S(1)}, u32[]{:S(2)}, u32[]{:S(2)}) %collective-permute-start.4) | collective-permute-done | bytes 262176 | tf_op jit(solution)/shard_map/ppermute | solution.py:527
  54.2 2.5 %near_forward.1 = (bf16[1024,1024]{1,0:T(8,128)(2,1)S(1)}, f32[128,1024]{1,0:T(8,128)S(1)}, f32[8,4,128]{2,1,0:T(4,128)S(1)}) custom-call(bf16[2,512,128]{2,1,0:T(8,128)(2,1)S(1)} %get-tuple-element.48.near0, bf16[2,512,128]{2,1,0:T(8,128)(2,1)S(1)} %collective-permute-done.3.near1, bf16[2,512,128]{2,1,0:T(8,128)(2,1)S(1)} %collective-permute-done.4.near2, ...), custom_call_target="tpu_custom_call" | custom-call | flops 10737418240 | bytes 4000000 | tf_op jit(solution)/shard_map/near_forward/pallas_call | solution.py:210
  56.7 3.4 %far_forward.1 = (f32[8,8,128]{2,1,0:T(8,128)S(1)}, bf16[4,1152,256]{2,1,0:T(8,128)(2,1)S(1)}, f32[128,1024]{1,0:T(8,128)S(1)}) custom-call(s32[3]{0:T(128)S(1)} %pad_add_fusion.place, s32[8]{0:T(128)S(1)} %copy-done.3, bf16[8,528,128]{2,1,0:T(8,128)(2,1)S(1)} %all-to-all-done.1.mine, bf16[8,272,128]{2,1,0:T(8,128)(2,1)S(1)} %collective-permute-done.2.past, ...), custom_call_target="tpu_custom_call" | custom-call | flops 603979776 | bytes 5000000 | tf_op jit(solution)/shard_map/far_forward/pallas_call | solution.py:275
  60.1 16.3 %all_to_all.15.told = f32[8,8,128]{2,1,0:T(8,128)S(1)} all-to-all(f32[8,8,128]{2,1,0:T(8,128)S(1)} %get-tuple-element.55.sent), channel_id=1, replica_groups={{0,8,22,30,36,44,50,58},{2,10,16,24,38,46,52,60},{4,12,18,26,32,40,54,6..., dimensions={0} | all-to-all | bytes 65536 | tf_op jit(solution)/shard_map/all_to_all | solution.py:535
  76.4 2.9 %near_backward.1 = (bf16[2,512,128]{2,1,0:T(8,128)(2,1)S(1)}, bf16[2,512,128]{2,1,0:T(8,128)(2,1)S(1)}, bf16[2,512,128]{2,1,0:T(8,128)(2,1)S(1)}, bf16[2,512,128]{2,1,0:T(8,128)(2,1)S(1)}) custom-call(s32[3]{0:T(128)S(1)} %pad_add_fusion.place, bf16[2,512,128]{2,1,0:T(8,128)(2,1)S(1)} %get-tuple-element.48.near0, ...), custom_call_target="tpu_custom_call" | custom-call | flops 1073741824 | bytes 5000000 | tf_op jit(solution)/shard_map/near_backward/pallas_call | solution.py:344
  79.4 3.9 %collective-permute-start.6 = (bf16[2,512,128]{2,1,0:T(8,128)(2,1)S(1)}, bf16[2,512,128]{2,1,0:T(8,128)(2,1)S(1)}, u32[]{:S(2)}, u32[]{:S(2)}) collective-permute-start(bf16[2,512,128]{2,1,0:T(8,128)(2,1)S(1)} %get-tuple-element.65), channel_id=1, source_target_pairs={{0,4},{2,6},{4,0},{6,2},{1,5},{3,7},{5,1},{7,3},{8,12},{10,14},{12... | collective-permute-start | bytes 786440 | tf_op jit(solution)/shard_map/ppermute | solution.py:527
  83.3 1.5 %collective-permute-start.7 = (bf16[2,512,128]{2,1,0:T(8,128)(2,1)S(1)}, bf16[2,512,128]{2,1,0:T(8,128)(2,1)S(1)}, u32[]{:S(2)}, u32[]{:S(2)}) collective-permute-start(bf16[2,512,128]{2,1,0:T(8,128)(2,1)S(1)} %get-tuple-element.66), channel_id=1, source_target_pairs={{0,6},{2,0},{4,2},{6,4},{1,7},{3,1},{5,3},{7,5},{8,14},{10,8},{12,... | collective-permute-start | bytes 786440 | tf_op jit(solution)/shard_map/ppermute | solution.py:527
  84.7 1.5 %collective-permute-start.8 = (bf16[2,512,128]{2,1,0:T(8,128)(2,1)S(1)}, bf16[2,512,128]{2,1,0:T(8,128)(2,1)S(1)}, u32[]{:S(2)}, u32[]{:S(2)}) collective-permute-start(bf16[2,512,128]{2,1,0:T(8,128)(2,1)S(1)} %get-tuple-element.67), channel_id=1, source_target_pairs={{0,2},{2,4},{4,6},{6,0},{1,3},{3,5},{5,7},{7,1},{8,10},{10,12},{12... | collective-permute-start | bytes 786440 | tf_op jit(solution)/shard_map/ppermute | solution.py:527
  86.2 3.4 %far_backward.1 = (bf16[8,528,128]{2,1,0:T(8,128)(2,1)S(1)}, bf16[8,128,128]{2,1,0:T(8,128)(2,1)S(1)}, bf16[8,128,128]{2,1,0:T(8,128)(2,1)S(1)}) custom-call(s32[3]{0:T(128)S(1)} %pad_add_fusion.place, bf16[8,528,128]{2,1,0:T(8,128)(2,1)S(1)} %all-to-all-done.1.mine, bf16[8,272,128]{2,1,0:T(8,128)(2,1)S(1)} %collective-permute-done.2.past, ...), custom_call_target="tpu_custom_call" | custom-call | flops 1207959552 | bytes 6000000 | tf_op jit(solution)/shard_map/far_backward/pallas_call | solution.py:409
  89.6 2.4 %collective-permute-start.9 = (bf16[8,128,128]{2,1,0:T(8,128)(2,1)S(1)}, bf16[8,128,128]{2,1,0:T(8,128)(2,1)S(1)}, u32[]{:S(2)}, u32[]{:S(2)}) collective-permute-start(bf16[8,128,128]{2,1,0:T(8,128)(2,1)S(1)} %get-tuple-element.73), channel_id=1, source_target_pairs={{64,0},{128,64},{192,128},{65,1},{129,65},{193,129},{66,2},{130,66... | collective-permute-start | bytes 786440 | tf_op jit(solution)/shard_map/ppermute | solution.py:566
  91.9 2.3 %collective-permute-start.10 = (bf16[8,128,128]{2,1,0:T(8,128)(2,1)S(1)}, bf16[8,128,128]{2,1,0:T(8,128)(2,1)S(1)}, u32[]{:S(2)}, u32[]{:S(2)}) collective-permute-start(bf16[8,128,128]{2,1,0:T(8,128)(2,1)S(1)} %get-tuple-element.74), channel_id=1, source_target_pairs={{64,0},{128,64},{192,128},{65,1},{129,65},{193,129},{66,2},{130,66... | collective-permute-start | bytes 786440 | tf_op jit(solution)/shard_map/ppermute | solution.py:566
  94.3 2.7 %collective-permute-done.6.near1 = bf16[2,512,128]{2,1,0:T(8,128)(2,1)S(1)} collective-permute-done((bf16[2,512,128]{2,1,0:T(8,128)(2,1)S(1)}, bf16[2,512,128]{2,1,0:T(8,128)(2,1)S(1)}, u32[]{:S(2)}, u32[]{:S(2)}) %collective-permute-start.6) | collective-permute-done | bytes 262176 | tf_op jit(solution)/shard_map/ppermute | solution.py:527
  97.0 8.3 %collective-permute-done.7.near2 = bf16[2,512,128]{2,1,0:T(8,128)(2,1)S(1)} collective-permute-done((bf16[2,512,128]{2,1,0:T(8,128)(2,1)S(1)}, bf16[2,512,128]{2,1,0:T(8,128)(2,1)S(1)}, u32[]{:S(2)}, u32[]{:S(2)}) %collective-permute-start.7) | collective-permute-done | bytes 262176 | tf_op jit(solution)/shard_map/ppermute | solution.py:527
  105.3 0.4 add_back.1
  105.7 19.1 %conditional.1 = (bf16[4,2,528,128]{3,2,1,0:T(8,128)(2,1)S(1)}) conditional(s32[]{:T(128)} %bitcast.8, () %tuple.20, bf16[8,528,128]{2,1,0:T(8,128)(2,1)S(1)} %add_back.1), branch_computations={%region_0.0_spmd, %region_1.0_spmd} | conditional | bytes 2162696 | solution.py:539
  105.7 19.1 %all_to_all.14 = bf16[8,528,128]{2,1,0:T(8,128)(2,1)S(1)} all-to-all(bf16[8,528,128]{2,1,0:T(8,128)(2,1)S(1)} %param.1), channel_id=1, replica_groups=mesh['y'=4,'x'=4,'zl'=2,'zh'=4,'core'=2] {'x','zl'}, dimensions={0} | all-to-all | bytes 2162688 | tf_op jit(solution)/shard_map/cond/branch_1_fun/all_to_all | solution.py:535
  124.8 3.8 %unproject.1 = (f32[2,128,1024]{2,1,0:T(8,128)S(1)}, bf16[2,128,1024]{2,1,0:T(8,128)(2,1)S(1)}) custom-call(s32[3]{0:T(128)S(1)} %pad_add_fusion.place, bf16[2,512,128]{2,1,0:T(8,128)(2,1)S(1)} %get-tuple-element.68.near0, bf16[2,512,128]{2,1,0:T(8,128)(2,1)S(1)} %collective-permute-done.6.near1, bf16[2,512,128]{2,1,0:T(8,128)(2,1)S(1)} %collective-permute-done.7.near2, ...), custom_call_target="tpu_custom_call" | custom-call | flops 1073741824 | bytes 8000000 | tf_op jit(solution)/shard_map/unproject/pallas_call | solution.py:480
  128.6 0.1 collective-permute-start.11
  128.7 1.9 %collective-permute-done.11.other = bf16[2,128,1024]{2,1,0:T(8,128)(2,1)S(1)} collective-permute-done((bf16[2,128,1024]{2,1,0:T(8,128)(2,1)S(1)}, bf16[2,128,1024]{2,1,0:T(8,128)(2,1)S(1)}, u32[]{:S(2)}, u32[]{:S(2)}) %collective-permute-start.11) | collective-permute-done | bytes 524320 | tf_op jit(solution)/shard_map/ppermute | solution.py:523
  130.6 1.0 finish.1
  (16 shorter events, 0.1 us)
Async XLA Ops:
  0.6 4.2 %collective-permute-start = (bf16[128,1024]{1,0:T(8,128)(2,1)}, bf16[128,1024]{1,0:T(8,128)(2,1)S(1)}, u32[]{:S(2)}, u32[]{:S(2)}) collective-permute-start(bf16[128,1024]{1,0:T(8,128)(2,1)} %bitcast.12), channel_id=1, source_target_pairs={{0,1},{1,0},{2,3},{3,2},{4,5},{5,4},{6,7},{7,6},{8,9},{9,8},{10,11... | collective-permute-start | bytes 786440 | tf_op jit(solution)/shard_map/ppermute | solution.py:523
  0.7 4.1 %collective-permute-start.1 = (bf16[128,1024]{1,0:T(8,128)(2,1)}, bf16[128,1024]{1,0:T(8,128)(2,1)S(1)}, u32[]{:S(2)}, u32[]{:S(2)}) collective-permute-start(bf16[128,1024]{1,0:T(8,128)(2,1)} %bitcast.15), channel_id=1, source_target_pairs={{0,1},{1,0},{2,3},{3,2},{4,5},{5,4},{6,7},{7,6},{8,9},{9,8},{10,11... | collective-permute-start | bytes 786440 | tf_op jit(solution)/shard_map/ppermute | solution.py:523
  2.0 2.9 %copy-start = (bf16[1,1,128,1024]{3,2,1,0:T(8,128)(2,1)S(1)}, bf16[1,1,128,1024]{3,2,1,0:T(8,128)(2,1)}, u32[]{:S(2)}) copy-start(bf16[1,1,128,1024]{3,2,1,0:T(8,128)(2,1)} %param.9) | copy-start | bytes 786436
  2.0 2.9 %copy-start.1 = (bf16[1,1,128,1024]{3,2,1,0:T(8,128)(2,1)S(1)}, bf16[1,1,128,1024]{3,2,1,0:T(8,128)(2,1)}, u32[]{:S(2)}) copy-start(bf16[1,1,128,1024]{3,2,1,0:T(8,128)(2,1)} %param.15) | copy-start | bytes 786436
  2.0 2.9 %copy-start.2 = (f32[1024]{0:T(1024)S(1)}, f32[1024]{0:T(1024)}, u32[]{:S(2)}) copy-start(f32[1024]{0:T(1024)} %param.10) | copy-start | bytes 12292
  8.1 28.8 %all-to-all-start.1 = ((bf16[8,528,128]{2,1,0:T(8,128)(2,1)}), bf16[8,528,128]{2,1,0:T(8,128)(2,1)S(1)}, u32[]{:S(2)}, u32[]{:S(2)}) async-start(bf16[8,528,128]{2,1,0:T(8,128)(2,1)} %bitcast.7), calls=%async_computation.1 | async-start | bytes 2162688 | tf_op jit(solution)/shard_map/all_to_all | solution.py:535
  13.8 36.3 %collective-permute-start.3 = (bf16[2,512,128]{2,1,0:T(8,128)(2,1)S(1)}, bf16[2,512,128]{2,1,0:T(8,128)(2,1)S(1)}, u32[]{:S(2)}, u32[]{:S(2)}) collective-permute-start(bf16[2,512,128]{2,1,0:T(8,128)(2,1)S(1)} %get-tuple-element.49), channel_id=1, source_target_pairs={{0,4},{2,6},{4,0},{6,2},{1,5},{3,7},{5,1},{7,3},{8,12},{10,14},{12... | collective-permute-start | bytes 786440 | tf_op jit(solution)/shard_map/ppermute | solution.py:527
  20.0 34.2 %collective-permute-start.4 = (bf16[2,512,128]{2,1,0:T(8,128)(2,1)S(1)}, bf16[2,512,128]{2,1,0:T(8,128)(2,1)S(1)}, u32[]{:S(2)}, u32[]{:S(2)}) collective-permute-start(bf16[2,512,128]{2,1,0:T(8,128)(2,1)S(1)} %get-tuple-element.50), channel_id=1, source_target_pairs={{0,2},{2,4},{4,6},{6,0},{1,3},{3,5},{5,7},{7,1},{8,10},{10,12},{12... | collective-permute-start | bytes 786440 | tf_op jit(solution)/shard_map/ppermute | solution.py:527
  21.5 32.6 %collective-permute-start.5 = (bf16[2,512,128]{2,1,0:T(8,128)(2,1)S(1)}, bf16[2,512,128]{2,1,0:T(8,128)(2,1)S(1)}, u32[]{:S(2)}, u32[]{:S(2)}) collective-permute-start(bf16[2,512,128]{2,1,0:T(8,128)(2,1)S(1)} %get-tuple-element.51), channel_id=1, source_target_pairs={{0,6},{2,0},{4,2},{6,4},{1,7},{3,1},{5,3},{7,5},{8,14},{10,8},{12,... | collective-permute-start | bytes 786440 | tf_op jit(solution)/shard_map/ppermute | solution.py:527
  36.9 19.7 %collective-permute-start.2 = (bf16[8,272,128]{2,1,0:T(8,128)(2,1)S(1)}, bf16[8,272,128]{2,1,0:T(8,128)(2,1)S(1)}, u32[]{:S(2)}, u32[]{:S(2)}) collective-permute-start(bf16[8,272,128]{2,1,0:T(8,128)(2,1)S(1)} %slice.8), channel_id=1, source_target_pairs={{0,64},{64,128},{128,192},{1,65},{65,129},{129,193},{2,66},{66,130... | collective-permute-start | bytes 1671176 | tf_op jit(solution)/shard_map/ppermute | solution.py:559
  54.2 2.5 %copy-start.3 = (s32[8]{0:T(128)S(1)}, s32[8]{0:T(128)}, u32[]{:S(2)}) copy-start(s32[8]{0:T(128)} %win.1) | copy-start | bytes 100
  79.4 17.6 %collective-permute-start.6 = (bf16[2,512,128]{2,1,0:T(8,128)(2,1)S(1)}, bf16[2,512,128]{2,1,0:T(8,128)(2,1)S(1)}, u32[]{:S(2)}, u32[]{:S(2)}) collective-permute-start(bf16[2,512,128]{2,1,0:T(8,128)(2,1)S(1)} %get-tuple-element.65), channel_id=1, source_target_pairs={{0,4},{2,6},{4,0},{6,2},{1,5},{3,7},{5,1},{7,3},{8,12},{10,14},{12... | collective-permute-start | bytes 786440 | tf_op jit(solution)/shard_map/ppermute | solution.py:527
  83.3 22.0 %collective-permute-start.7 = (bf16[2,512,128]{2,1,0:T(8,128)(2,1)S(1)}, bf16[2,512,128]{2,1,0:T(8,128)(2,1)S(1)}, u32[]{:S(2)}, u32[]{:S(2)}) collective-permute-start(bf16[2,512,128]{2,1,0:T(8,128)(2,1)S(1)} %get-tuple-element.66), channel_id=1, source_target_pairs={{0,6},{2,0},{4,2},{6,4},{1,7},{3,1},{5,3},{7,5},{8,14},{10,8},{12,... | collective-permute-start | bytes 786440 | tf_op jit(solution)/shard_map/ppermute | solution.py:527
  84.7 20.5 %collective-permute-start.8 = (bf16[2,512,128]{2,1,0:T(8,128)(2,1)S(1)}, bf16[2,512,128]{2,1,0:T(8,128)(2,1)S(1)}, u32[]{:S(2)}, u32[]{:S(2)}) collective-permute-start(bf16[2,512,128]{2,1,0:T(8,128)(2,1)S(1)} %get-tuple-element.67), channel_id=1, source_target_pairs={{0,2},{2,4},{4,6},{6,0},{1,3},{3,5},{5,7},{7,1},{8,10},{10,12},{12... | collective-permute-start | bytes 786440 | tf_op jit(solution)/shard_map/ppermute | solution.py:527
  89.6 15.7 %collective-permute-start.9 = (bf16[8,128,128]{2,1,0:T(8,128)(2,1)S(1)}, bf16[8,128,128]{2,1,0:T(8,128)(2,1)S(1)}, u32[]{:S(2)}, u32[]{:S(2)}) collective-permute-start(bf16[8,128,128]{2,1,0:T(8,128)(2,1)S(1)} %get-tuple-element.73), channel_id=1, source_target_pairs={{64,0},{128,64},{192,128},{65,1},{129,65},{193,129},{66,2},{130,66... | collective-permute-start | bytes 786440 | tf_op jit(solution)/shard_map/ppermute | solution.py:566
  91.9 13.3 %collective-permute-start.10 = (bf16[8,128,128]{2,1,0:T(8,128)(2,1)S(1)}, bf16[8,128,128]{2,1,0:T(8,128)(2,1)S(1)}, u32[]{:S(2)}, u32[]{:S(2)}) collective-permute-start(bf16[8,128,128]{2,1,0:T(8,128)(2,1)S(1)} %get-tuple-element.74), channel_id=1, source_target_pairs={{64,0},{128,64},{192,128},{65,1},{129,65},{193,129},{66,2},{130,66... | collective-permute-start | bytes 786440 | tf_op jit(solution)/shard_map/ppermute | solution.py:566
  128.6 2.0 %collective-permute-start.11 = (bf16[2,128,1024]{2,1,0:T(8,128)(2,1)S(1)}, bf16[2,128,1024]{2,1,0:T(8,128)(2,1)S(1)}, u32[]{:S(2)}, u32[]{:S(2)}) collective-permute-start(bf16[2,128,1024]{2,1,0:T(8,128)(2,1)S(1)} %get-tuple-element.76), channel_id=1, source_target_pairs={{0,1},{1,0},{2,3},{3,2},{4,5},{5,4},{6,7},{7,6},{8,9},{9,8},{10,11... | collective-permute-start | bytes 1572872 | tf_op jit(solution)/shard_map/ppermute | solution.py:523

commit v8 on v7

--- a/solution.py
+++ b/solution.py
@@ -26,6 +26,7 @@
 NT = (((1,), (1,)), ((), ()))
 VMEM_LIMIT = 20 * 1024 * 1024
 STAGE_LIMIT = 48 * 1024 * 1024
+LAST_LIMIT = 46 * 1024 * 1024
 
 Q0, G0, K0, V0, OK0, ROWS = 0, 128, 256, 384, 512, 528
 TOKENS = 8 * HW
@@ -358,7 +359,7 @@
 
 
 def far_backward_kernel(
-    place, mine, past, kept, result, sent, told, own, back0, back1, keys_t, values, dk, dv, grads
+    place, mine, past, kept, result, sent, told, own, back, keys_t, values, dk, dv, grads
 ):
     for j in range(GROUP):
         keys_t[:, j * HW : (j + 1) * HW] = turn(past[j, :HW, :]).astype(BF16)
@@ -396,10 +397,8 @@
     for j in range(GROUP):
         early = slice(j * HW, (j + 1) * HW)
         late = slice((GROUP + j) * HW, (GROUP + j + 1) * HW)
-        d_keys = (dk[early, :] * SCALE).astype(BF16)
-        d_values = dv[early, :].astype(BF16)
-        back0[j] = d_keys
-        back1[j] = d_values
+        back[j, :HW, :] = (dk[early, :] * SCALE).astype(BF16)
+        back[j, HW:, :] = dv[early, :].astype(BF16)
         own[j, 2 * HW : 3 * HW, :] = (dk[late, :] * SCALE).astype(BF16)
         own[j, 3 * HW : 4 * HW, :] = dv[late, :].astype(BF16)
         own[j, 4 * HW :, :] = jnp.zeros((ROWS - 4 * HW, DH), BF16)
@@ -409,9 +408,11 @@
     return pl.pallas_call(
         far_backward_kernel,
         in_specs=[SM] + [VM] * 6,
-        out_specs=[VM] * 3,
-        out_shape=[jax.ShapeDtypeStruct((GROUP, ROWS, DH), BF16)]
-        + [jax.ShapeDtypeStruct((GROUP, HW, DH), BF16)] * 2,
+        out_specs=[VM, VM],
+        out_shape=[
+            jax.ShapeDtypeStruct((GROUP, ROWS, DH), BF16),
+            jax.ShapeDtypeStruct((GROUP, 2 * HW, DH), BF16),
+        ],
         scratch_shapes=[
             pltpu.VMEM((DH, 2 * GROUP * HW), BF16),
             pltpu.VMEM((2 * GROUP * HW, DH), BF16),
@@ -425,28 +426,28 @@
     )(place, mine, past, kept, result, sent, told)
 
 
-def add_back_kernel(own, back0, back1, out):
-    for n, back in enumerate((back0, back1)):
-        rows = slice((2 + n) * HW, (3 + n) * HW)
-        for j in range(GROUP):
-            out[j, rows, :] = (own[j, rows, :].astype(F32) + back[j].astype(F32)).astype(BF16)
-
-
-def add_back(own, *back):
+def add_back_kernel(own, back, out):
+    for j in range(GROUP):
+        out[j, 2 * HW : 4 * HW, :] = (
+            own[j, 2 * HW : 4 * HW, :].astype(F32) + back[j].astype(F32)
+        ).astype(BF16)
+
+
+def add_back(own, back):
     return pl.pallas_call(
         add_back_kernel,
-        in_specs=[VM] * 3,
+        in_specs=[VM] * 2,
         out_specs=VM,
         out_shape=jax.ShapeDtypeStruct((GROUP, ROWS, DH), BF16),
         input_output_aliases={0: 0},
         compiler_params=params(),
         cost_estimate=cost(GROUP * 2 * HW * DH, 2_500_000),
         name="add_back",
-    )(own, *back)
-
-
-def unproject_kernel(
-    place, near0, near1, near2, near3, far, w_qkv, w_out, own, other, close, wq, wk, wv, wo, sems
+    )(own, back)
+
+
+def unproject_other_kernel(
+    place, near0, near1, near2, near3, far, w_qkv, w_out, other, rows, wq, wk, wv, wo, close, sems
 ):
     groups = weight_copies(place, w_qkv, w_out, (wq, wk, wv), wo, sems)
     start_all(groups)
@@ -454,13 +455,16 @@
         close[head_here(place, step)] = near[...]
     parts = []
     for part in range(4):
-        rows = slice(part * HW, (part + 1) * HW)
+        span = slice(part * HW, (part + 1) * HW)
         pieces = []
         for h in range(HALF):
             slot = slot_of_head(place, h)
-            away = jnp.concatenate([far[slot, 0, rows, :], far[slot, 1, rows, :]], axis=0)
-            here = jnp.concatenate([close[h, 0, rows, :], close[h, 1, rows, :]], axis=0)
-            pieces.append((away.astype(F32) + here.astype(F32)).astype(BF16))
+            sums = [
+                far[slot, s, span, :].astype(F32) + close[h, s, span, :].astype(F32)
+                for s in range(2)
+            ]
+            rows[part, :, h * DH : (h + 1) * DH] = sums[0].astype(BF16)
+            pieces.append(sums[1].astype(BF16))
         parts.append(jnp.concatenate(pieces, axis=1))
     wait_all(groups[0])
     total = mm_nt(parts[1], wq[...])
@@ -470,25 +474,46 @@
     total = total + mm_nt(parts[3], wv[...])
     wait_all(groups[3])
     mixed = mm(parts[0], wo[...])
-    own[0] = mixed[:HW]
-    own[1] = total[:HW]
-    other[0] = mixed[HW:].astype(BF16)
-    other[1] = total[HW:].astype(BF16)
-
-
-def unproject(place, blocks, far, w_qkv, w_out):
-    return pl.pallas_call(
-        unproject_kernel,
+    other[0] = mixed.astype(BF16)
+    other[1] = total.astype(BF16)
+
+
+def unproject_other(place, blocks, far, w_qkv, w_out):
+    return pl.pallas_call(
+        unproject_other_kernel,
         in_specs=[SM] + [VM] * 5 + [ANY] * 2,
-        out_specs=[VM, VM],
-        scratch_shapes=[pltpu.VMEM((HALF, 2, 4 * HW, DH), BF16)]
-        + [pltpu.VMEM((D, HALF * DH), BF16)] * 3
-        + [pltpu.VMEM((HALF * DH, D), BF16), pltpu.SemaphoreType.DMA((4 * PIECES,))],
-        out_shape=[jax.ShapeDtypeStruct((2, HW, D), F32), jax.ShapeDtypeStruct((2, HW, D), BF16)],
-        compiler_params=pltpu.CompilerParams(vmem_limit_bytes=50 * 1024 * 1024),
-        cost_estimate=cost(2 * PAIR * D * 4 * HALF * DH, 8_000_000),
-        name="unproject",
+        out_specs=[VM] * 6,
+        scratch_shapes=[
+            pltpu.VMEM((HALF, 2, 4 * HW, DH), BF16),
+            pltpu.SemaphoreType.DMA((4 * PIECES,)),
+        ],
+        out_shape=[
+            jax.ShapeDtypeStruct((2, HW, D), BF16),
+            jax.ShapeDtypeStruct((4, HW, HALF * DH), BF16),
+        ]
+        + [jax.ShapeDtypeStruct((D, HALF * DH), BF16)] * 3
+        + [jax.ShapeDtypeStruct((HALF * DH, D), BF16)],
+        compiler_params=pltpu.CompilerParams(vmem_limit_bytes=LAST_LIMIT),
+        cost_estimate=cost(PAIR * D * 4 * HALF * DH, 8_000_000),
+        name="unproject_other",
     )(place, *blocks, far, w_qkv, w_out)
+
+
+def unproject_own_kernel(rows, wq, wk, wv, wo, own):
+    own[0] = mm(rows[0], wo[...])
+    own[1] = mm_nt(rows[1], wq[...]) + mm_nt(rows[2], wk[...]) + mm_nt(rows[3], wv[...])
+
+
+def unproject_own(rows, weights):
+    return pl.pallas_call(
+        unproject_own_kernel,
+        in_specs=[VM] * 5,
+        out_specs=VM,
+        out_shape=jax.ShapeDtypeStruct((2, HW, D), F32),
+        compiler_params=params(),
+        cost_estimate=cost(PAIR * D * 4 * HALF * DH, 6_000_000),
+        name="unproject_own",
+    )(rows, *weights)
 
 
 def finish_kernel(tokens, cot, gain, own, other, mixed, out):
@@ -560,16 +585,17 @@
     near_kept, near_result, close = near_forward(*blocks)
     sent, far_kept, far_result = far_forward(place, window, mine, past, close)
     told = exchange(sent, ("x", "zl", "zh"), SAME_HEAD)
+    own, back = far_backward(place, mine, past, far_kept, far_result, sent, told)
+    back = lax.ppermute(back, "y", [(i + 1, i) for i in range(rows - 1)])
     returned = near_backward(place, blocks, near_kept, near_result, close, told)
-    told, returned = lax.optimization_barrier((told, returned))
-    own, *back = far_backward(place, mine, past, far_kept, far_result, sent, told)
-    back = [lax.ppermute(b, "y", [(i + 1, i) for i in range(rows - 1)]) for b in back]
+    own, returned = lax.optimization_barrier((own, returned))
     returned = all_round(returned, -1)
-    own, returned = lax.optimization_barrier((own, returned))
-    own = add_back(own, *back)
+    own = add_back(own, back)
     far = exchange_alone(own, go).reshape(HALF, 2, ROWS, DH)
-    out_own, out_other = unproject(place, returned, far, w_qkv, w_out)
-    mixed, d_tokens = finish(tokens, cot, gain, out_own, swap(out_other))
+    out_other, own_rows, *weights = unproject_other(place, returned, far, w_qkv, w_out)
+    out_other = swap(out_other)
+    out_own = unproject_own(own_rows, weights)
+    mixed, d_tokens = finish(tokens, cot, gain, out_own, out_other)
     return mixed.reshape(1, 1, HW, D), d_tokens.reshape(1, 1, HW, D)
 
 

time: 133 us -> 130 us (0.977)
  waiting for transfers between devices: 39.6 us -> 28.6 us
  blocking collectives: 35.4 us -> 44.2 us
  starting transfers between devices: 31.5 us -> 29 us
  Pallas kernels: 23.5 us -> 25.4 us
    ppermute x6, waiting for transfers between devices: 24.9 us -> 14 us  [turn_ring(): return lax.ppermute(value, 'zh', [(i, (i + steps) % 4) for i in range(4)])]
    all_to_all x2, blocking collectives: 35.4 us -> 44.2 us  [exchange(): lax.all_to_all(value, axes, 0, 0, axis_index_groups=groups, tiled=True)]
    ppermute x2 -> x1, starting transfers between devices: 4.71 us -> 2.35 us  [per_device(): back = lax.ppermute(back, 'y', [(i + 1, i) for i in range(rows - 1)])]
    pallas_call x2 -> x3, Pallas kernels: 4.21 us -> 6.12 us  [the longest x1 4.43 us: unproject_other(): pl.pallas_call(unproject_other_kernel, in_specs=[SM] + [VM] * 5 + [ANY] *...]
  transfers between devices with their start and end apart: 13 -> 12, of which waited for: 6 -> 5; matrix products, arithmetic and copies ran while one was open for 0% -> 0% of each run, Pallas kernels for 7% -> 8%
where the time goes in v8:
time: 130 us; the launch traced here: 129 us
  blocking collectives  44.2 us (34%)
  starting transfers between devices  29 us (22%)
  waiting for transfers between devices  28.6 us (22%)
  Pallas kernels  25.4 us (20%)
  between operations  1.48 us (1%)
    all_to_all x2, blocking collectives, exchange(): lax.all_to_all(value, axes, 0, 0, axis_index_groups=groups, tiled=True)  44.2 us
    ppermute x6, starting transfers between devices, turn_ring(): return lax.ppermute(value, 'zh', [(i, (i + steps) % 4) for i in range(4)])  17.1 us
    ppermute x6, waiting for transfers between devices, turn_ring(): return lax.ppermute(value, 'zh', [(i, (i + steps) % 4) for i in range(4)])  14 us
    all_to_all x1, waiting for transfers between devices, exchange(): lax.all_to_all(value, axes, 0, 0, axis_index_groups=groups, tiled=True)  12.8 us
    all_to_all x1, starting transfers between devices, exchange(): lax.all_to_all(value, axes, 0, 0, axis_index_groups=groups, tiled=True)  5.7 us
    pallas_call x1, Pallas kernels, unproject_other(): pl.pallas_call(unproject_other_kernel, in_specs=[SM] + [VM] * 5 + [ANY] *...  4.43 us
    pallas_call x1, Pallas kernels, far_forward(): pl.pallas_call(far_forward_kernel, in_specs=[SM, SM, VM, VM, VM], out_spe...  3.4 us
    pallas_call x1, Pallas kernels, far_backward(): pl.pallas_call(far_backward_kernel, in_specs=[SM] + [VM] * 6, out_specs=[...  3.37 us
  transfers between devices with their start and end apart: 12, of which 5 were waited for; matrix products, arithmetic and copies ran while one was open for 0% of the time, Pallas kernels for 8%

profile of v8, /device:TPU:16, one launch (start us, length us, event | category | flops | bytes accessed | tf_op | source)
XLA Modules:
  0.0 128.9 jit_solution(17332436498375623144)
XLA Ops:
  0.6 0.1 collective-permute-start
  0.7 0.5 collective-permute-start.1
  1.9 0.1 pad_add_fusion.place
  2.0 2.8 %stage.1 = (bf16[1024,512]{1,0:T(8,128)(2,1)S(1)}, bf16[1024,512]{1,0:T(8,128)(2,1)S(1)}, bf16[1024,512]{1,0:T(8,128)(2,1)S(1)}, bf16[512,1024]{1,0:T(8,128)(2,1)S(1)}) custom-call(s32[3]{0:T(128)S(1)} %pad_add_fusion.place, bf16[1024,3072]{1,0:T(8,128)(2,1)} %w_qkv.3, bf16[1024,1024]{1,0:T(8,128)(2,1)} %w_out.3), custom_call_target="tpu_custom_call" | custom-call | bytes 9000000 | tf_op jit(solution)/shard_map/stage/pallas_call | solution.py:113
  4.8 0.0 collective-permute-done.other
  4.9 3.2 %project.1 = (bf16[4,2,528,128]{3,2,1,0:T(8,128)(2,1)}, bf16[2,512,128]{2,1,0:T(8,128)(2,1)S(1)}, bf16[2,512,128]{2,1,0:T(8,128)(2,1)S(1)}, bf16[2,512,128]{2,1,0:T(8,128)(2,1)S(1)}, bf16[2,512,128]{2,1,0:T(8,128)(2,1)S(1)}) custom-call(s32[3]{0:T(128)S(1)} %pad_add_fusion.place, s32[1]{0:T(128)S(6)} %copy.13.valid, bf16[128,1024]{1,0:T(8,128)(2,1)S(1)} %bitcast.13, ...), custom_call_target="tpu_custom_call" | custom-call | flops 1073741824 | bytes 7000000 | tf_op jit(solution)/shard_map/project/pallas_call | solution.py:165
  8.1 5.7 %all-to-all-start.1 = ((bf16[8,528,128]{2,1,0:T(8,128)(2,1)}), bf16[8,528,128]{2,1,0:T(8,128)(2,1)S(1)}, u32[]{:S(2)}, u32[]{:S(2)}) async-start(bf16[8,528,128]{2,1,0:T(8,128)(2,1)} %bitcast.7), calls=%async_computation.1 | async-start | bytes 2162688 | tf_op jit(solution)/shard_map/all_to_all | solution.py:560
  13.8 6.2 %collective-permute-start.3 = (bf16[2,512,128]{2,1,0:T(8,128)(2,1)S(1)}, bf16[2,512,128]{2,1,0:T(8,128)(2,1)S(1)}, u32[]{:S(2)}, u32[]{:S(2)}) collective-permute-start(bf16[2,512,128]{2,1,0:T(8,128)(2,1)S(1)} %get-tuple-element.47), channel_id=1, source_target_pairs={{0,4},{2,6},{4,0},{6,2},{1,5},{3,7},{5,1},{7,3},{8,12},{10,14},{12... | collective-permute-start | bytes 786440 | tf_op jit(solution)/shard_map/ppermute | solution.py:552
  20.0 1.5 %collective-permute-start.4 = (bf16[2,512,128]{2,1,0:T(8,128)(2,1)S(1)}, bf16[2,512,128]{2,1,0:T(8,128)(2,1)S(1)}, u32[]{:S(2)}, u32[]{:S(2)}) collective-permute-start(bf16[2,512,128]{2,1,0:T(8,128)(2,1)S(1)} %get-tuple-element.48), channel_id=1, source_target_pairs={{0,2},{2,4},{4,6},{6,0},{1,3},{3,5},{5,7},{7,1},{8,10},{10,12},{12... | collective-permute-start | bytes 786440 | tf_op jit(solution)/shard_map/ppermute | solution.py:552
  21.6 2.6 %collective-permute-start.5 = (bf16[2,512,128]{2,1,0:T(8,128)(2,1)S(1)}, bf16[2,512,128]{2,1,0:T(8,128)(2,1)S(1)}, u32[]{:S(2)}, u32[]{:S(2)}) collective-permute-start(bf16[2,512,128]{2,1,0:T(8,128)(2,1)S(1)} %get-tuple-element.49), channel_id=1, source_target_pairs={{0,6},{2,0},{4,2},{6,4},{1,7},{3,1},{5,3},{7,5},{8,14},{10,8},{12,... | collective-permute-start | bytes 786440 | tf_op jit(solution)/shard_map/ppermute | solution.py:552
  24.1 12.8 %all-to-all-done.1.mine = bf16[8,528,128]{2,1,0:T(8,128)(2,1)S(1)} async-done(((bf16[8,528,128]{2,1,0:T(8,128)(2,1)}), bf16[8,528,128]{2,1,0:T(8,128)(2,1)S(1)}, u32[]{:S(2)}, u32[]{:S(2)}) %all-to-all-start.1) | async-done | bytes 1081376 | tf_op jit(solution)/shard_map/all_to_all | solution.py:560
  37.0 3.2 %collective-permute-start.2 = (bf16[8,272,128]{2,1,0:T(8,128)(2,1)S(1)}, bf16[8,272,128]{2,1,0:T(8,128)(2,1)S(1)}, u32[]{:S(2)}, u32[]{:S(2)}) collective-permute-start(bf16[8,272,128]{2,1,0:T(8,128)(2,1)S(1)} %slice.8), channel_id=1, source_target_pairs={{0,64},{64,128},{128,192},{1,65},{65,129},{129,193},{2,66},{66,130... | collective-permute-start | bytes 1671176 | tf_op jit(solution)/shard_map/ppermute | solution.py:584
  40.1 9.9 %collective-permute-done.3.near1 = bf16[2,512,128]{2,1,0:T(8,128)(2,1)S(1)} collective-permute-done((bf16[2,512,128]{2,1,0:T(8,128)(2,1)S(1)}, bf16[2,512,128]{2,1,0:T(8,128)(2,1)S(1)}, u32[]{:S(2)}, u32[]{:S(2)}) %collective-permute-start.3) | collective-permute-done | bytes 262176 | tf_op jit(solution)/shard_map/ppermute | solution.py:552
  50.1 4.1 %collective-permute-done.4.near2 = bf16[2,512,128]{2,1,0:T(8,128)(2,1)S(1)} collective-permute-done((bf16[2,512,128]{2,1,0:T(8,128)(2,1)S(1)}, bf16[2,512,128]{2,1,0:T(8,128)(2,1)S(1)}, u32[]{:S(2)}, u32[]{:S(2)}) %collective-permute-start.4) | collective-permute-done | bytes 262176 | tf_op jit(solution)/shard_map/ppermute | solution.py:552
  54.2 2.5 %near_forward.1 = (bf16[1024,1024]{1,0:T(8,128)(2,1)S(1)}, f32[128,1024]{1,0:T(8,128)S(1)}, f32[8,4,128]{2,1,0:T(4,128)S(1)}) custom-call(bf16[2,512,128]{2,1,0:T(8,128)(2,1)S(1)} %get-tuple-element.46.near0, bf16[2,512,128]{2,1,0:T(8,128)(2,1)S(1)} %collective-permute-done.3.near1, bf16[2,512,128]{2,1,0:T(8,128)(2,1)S(1)} %collective-permute-done.4.near2, ...), custom_call_target="tpu_custom_call" | custom-call | flops 10737418240 | bytes 4000000 | tf_op jit(solution)/shard_map/near_forward/pallas_call | solution.py:211
  56.7 3.4 %far_forward.1 = (f32[8,8,128]{2,1,0:T(8,128)S(1)}, bf16[4,1152,256]{2,1,0:T(8,128)(2,1)S(1)}, f32[128,1024]{1,0:T(8,128)S(1)}) custom-call(s32[3]{0:T(128)S(1)} %pad_add_fusion.place, s32[8]{0:T(128)S(1)} %copy-done.3, bf16[8,528,128]{2,1,0:T(8,128)(2,1)S(1)} %all-to-all-done.1.mine, bf16[8,272,128]{2,1,0:T(8,128)(2,1)S(1)} %collective-permute-done.2.past, ...), custom_call_target="tpu_custom_call" | custom-call | flops 603979776 | bytes 5000000 | tf_op jit(solution)/shard_map/far_forward/pallas_call | solution.py:276
  60.1 16.3 %all_to_all.15.told = f32[8,8,128]{2,1,0:T(8,128)S(1)} all-to-all(f32[8,8,128]{2,1,0:T(8,128)S(1)} %get-tuple-element.53.sent), channel_id=1, replica_groups={{0,8,22,30,36,44,50,58},{2,10,16,24,38,46,52,60},{4,12,18,26,32,40,54,6..., dimensions={0} | all-to-all | bytes 65536 | tf_op jit(solution)/shard_map/all_to_all | solution.py:560
  76.4 3.4 %far_backward.1 = (bf16[8,528,128]{2,1,0:T(8,128)(2,1)S(1)}, bf16[8,256,128]{2,1,0:T(8,128)(2,1)S(1)}) custom-call(s32[3]{0:T(128)S(1)} %pad_add_fusion.place, bf16[8,528,128]{2,1,0:T(8,128)(2,1)S(1)} %all-to-all-done.1.mine, bf16[8,272,128]{2,1,0:T(8,128)(2,1)S(1)} %collective-permute-done.2.past, bf16[4,1152,256]{2,1,0:T(8,128)(2,1)S(1)} %get-tuple-element.51.kept, ...), custom_call_target="tpu_custom_call" | custom-call | flops 1207959552 | bytes 6000000 | tf_op jit(solution)/shard_map/far_backward/pallas_call | solution.py:408
  79.8 2.3 %collective-permute-start.9 = (bf16[8,256,128]{2,1,0:T(8,128)(2,1)S(1)}, bf16[8,256,128]{2,1,0:T(8,128)(2,1)S(1)}, u32[]{:S(2)}, u32[]{:S(2)}) collective-permute-start(bf16[8,256,128]{2,1,0:T(8,128)(2,1)S(1)} %get-tuple-element.66), channel_id=1, source_target_pairs={{64,0},{128,64},{192,128},{65,1},{129,65},{193,129},{66,2},{130,66... | collective-permute-start | bytes 1572872 | tf_op jit(solution)/shard_map/ppermute | solution.py:589
  82.2 2.9 %near_backward.1 = (bf16[2,512,128]{2,1,0:T(8,128)(2,1)S(1)}, bf16[2,512,128]{2,1,0:T(8,128)(2,1)S(1)}, bf16[2,512,128]{2,1,0:T(8,128)(2,1)S(1)}, bf16[2,512,128]{2,1,0:T(8,128)(2,1)S(1)}) custom-call(s32[3]{0:T(128)S(1)} %pad_add_fusion.place, bf16[2,512,128]{2,1,0:T(8,128)(2,1)S(1)} %get-tuple-element.46.near0, ...), custom_call_target="tpu_custom_call" | custom-call | flops 1073741824 | bytes 5000000 | tf_op jit(solution)/shard_map/near_backward/pallas_call | solution.py:345
  85.1 3.8 %collective-permute-start.6 = (bf16[2,512,128]{2,1,0:T(8,128)(2,1)S(1)}, bf16[2,512,128]{2,1,0:T(8,128)(2,1)S(1)}, u32[]{:S(2)}, u32[]{:S(2)}) collective-permute-start(bf16[2,512,128]{2,1,0:T(8,128)(2,1)S(1)} %get-tuple-element.62), channel_id=1, source_target_pairs={{0,4},{2,6},{4,0},{6,2},{1,5},{3,7},{5,1},{7,3},{8,12},{10,14},{12... | collective-permute-start | bytes 786440 | tf_op jit(solution)/shard_map/ppermute | solution.py:552
  88.9 1.5 %collective-permute-start.7 = (bf16[2,512,128]{2,1,0:T(8,128)(2,1)S(1)}, bf16[2,512,128]{2,1,0:T(8,128)(2,1)S(1)}, u32[]{:S(2)}, u32[]{:S(2)}) collective-permute-start(bf16[2,512,128]{2,1,0:T(8,128)(2,1)S(1)} %get-tuple-element.63), channel_id=1, source_target_pairs={{0,6},{2,0},{4,2},{6,4},{1,7},{3,1},{5,3},{7,5},{8,14},{10,8},{12,... | collective-permute-start | bytes 786440 | tf_op jit(solution)/shard_map/ppermute | solution.py:552
  90.3 1.5 %collective-permute-start.8 = (bf16[2,512,128]{2,1,0:T(8,128)(2,1)S(1)}, bf16[2,512,128]{2,1,0:T(8,128)(2,1)S(1)}, u32[]{:S(2)}, u32[]{:S(2)}) collective-permute-start(bf16[2,512,128]{2,1,0:T(8,128)(2,1)S(1)} %get-tuple-element.64), channel_id=1, source_target_pairs={{0,2},{2,4},{4,6},{6,0},{1,3},{3,5},{5,7},{7,1},{8,10},{10,12},{12... | collective-permute-start | bytes 786440 | tf_op jit(solution)/shard_map/ppermute | solution.py:552
  91.8 1.2 collective-permute-done.9.back
  93.0 0.4 add_back.1
  93.5 27.9 %conditional.1 = (bf16[4,2,528,128]{3,2,1,0:T(8,128)(2,1)}) conditional(s32[]{:T(128)} %bitcast.8, () %tuple.18, bf16[8,528,128]{2,1,0:T(8,128)(2,1)S(1)} %add_back.1), branch_computations={%region_0.0_spmd, %region_1.0_spmd} | conditional | bytes 2162696 | solution.py:564
  93.5 27.9 %all_to_all.14 = bf16[8,528,128]{2,1,0:T(8,128)(2,1)} all-to-all(bf16[8,528,128]{2,1,0:T(8,128)(2,1)S(1)} %param.1), channel_id=1, replica_groups=mesh['y'=4,'x'=4,'zl'=2,'zh'=4,'core'=2] {'x','zl'}, dimensions={0} | all-to-all | bytes 2162688 | tf_op jit(solution)/shard_map/cond/branch_1_fun/all_to_all | solution.py:560
  121.4 4.4 %unproject_other.1 = (bf16[2,128,1024]{2,1,0:T(8,128)(2,1)S(1)}, bf16[4,128,512]{2,1,0:T(8,128)(2,1)S(1)}, bf16[1024,512]{1,0:T(8,128)(2,1)S(1)}, bf16[1024,512]...) custom-call(s32[3]{0:T(128)S(1)} %pad_add_fusion.place, ...), custom_call_target="tpu_custom_call" | custom-call | flops 536870912 | bytes 8000000 | tf_op jit(solution)/shard_map/unproject_other/pallas_call | solution.py:482
  125.8 0.1 collective-permute-start.10
  125.9 1.3 unproject_own.1.own
  127.2 0.6 collective-permute-done.10.other
  127.8 1.0 finish.1
  (15 shorter events, 0.1 us)
Async XLA Ops:
  0.6 4.2 %collective-permute-start = (bf16[128,1024]{1,0:T(8,128)(2,1)}, bf16[128,1024]{1,0:T(8,128)(2,1)S(1)}, u32[]{:S(2)}, u32[]{:S(2)}) collective-permute-start(bf16[128,1024]{1,0:T(8,128)(2,1)} %bitcast.12), channel_id=1, source_target_pairs={{0,1},{1,0},{2,3},{3,2},{4,5},{5,4},{6,7},{7,6},{8,9},{9,8},{10,11... | collective-permute-start | bytes 786440 | tf_op jit(solution)/shard_map/ppermute | solution.py:548
  0.7 4.1 %collective-permute-start.1 = (bf16[128,1024]{1,0:T(8,128)(2,1)}, bf16[128,1024]{1,0:T(8,128)(2,1)S(1)}, u32[]{:S(2)}, u32[]{:S(2)}) collective-permute-start(bf16[128,1024]{1,0:T(8,128)(2,1)} %bitcast.15), channel_id=1, source_target_pairs={{0,1},{1,0},{2,3},{3,2},{4,5},{5,4},{6,7},{7,6},{8,9},{9,8},{10,11... | collective-permute-start | bytes 786440 | tf_op jit(solution)/shard_map/ppermute | solution.py:548
  2.0 2.9 %copy-start = (bf16[1,1,128,1024]{3,2,1,0:T(8,128)(2,1)S(1)}, bf16[1,1,128,1024]{3,2,1,0:T(8,128)(2,1)}, u32[]{:S(2)}) copy-start(bf16[1,1,128,1024]{3,2,1,0:T(8,128)(2,1)} %param.9) | copy-start | bytes 786436
  2.0 2.9 %copy-start.1 = (bf16[1,1,128,1024]{3,2,1,0:T(8,128)(2,1)S(1)}, bf16[1,1,128,1024]{3,2,1,0:T(8,128)(2,1)}, u32[]{:S(2)}) copy-start(bf16[1,1,128,1024]{3,2,1,0:T(8,128)(2,1)} %param.15) | copy-start | bytes 786436
  2.0 2.9 %copy-start.2 = (f32[1024]{0:T(1024)S(1)}, f32[1024]{0:T(1024)}, u32[]{:S(2)}) copy-start(f32[1024]{0:T(1024)} %param.10) | copy-start | bytes 12292
  8.1 28.8 %all-to-all-start.1 = ((bf16[8,528,128]{2,1,0:T(8,128)(2,1)}), bf16[8,528,128]{2,1,0:T(8,128)(2,1)S(1)}, u32[]{:S(2)}, u32[]{:S(2)}) async-start(bf16[8,528,128]{2,1,0:T(8,128)(2,1)} %bitcast.7), calls=%async_computation.1 | async-start | bytes 2162688 | tf_op jit(solution)/shard_map/all_to_all | solution.py:560
  13.8 36.3 %collective-permute-start.3 = (bf16[2,512,128]{2,1,0:T(8,128)(2,1)S(1)}, bf16[2,512,128]{2,1,0:T(8,128)(2,1)S(1)}, u32[]{:S(2)}, u32[]{:S(2)}) collective-permute-start(bf16[2,512,128]{2,1,0:T(8,128)(2,1)S(1)} %get-tuple-element.47), channel_id=1, source_target_pairs={{0,4},{2,6},{4,0},{6,2},{1,5},{3,7},{5,1},{7,3},{8,12},{10,14},{12... | collective-permute-start | bytes 786440 | tf_op jit(solution)/shard_map/ppermute | solution.py:552
  20.0 34.1 %collective-permute-start.4 = (bf16[2,512,128]{2,1,0:T(8,128)(2,1)S(1)}, bf16[2,512,128]{2,1,0:T(8,128)(2,1)S(1)}, u32[]{:S(2)}, u32[]{:S(2)}) collective-permute-start(bf16[2,512,128]{2,1,0:T(8,128)(2,1)S(1)} %get-tuple-element.48), channel_id=1, source_target_pairs={{0,2},{2,4},{4,6},{6,0},{1,3},{3,5},{5,7},{7,1},{8,10},{10,12},{12... | collective-permute-start | bytes 786440 | tf_op jit(solution)/shard_map/ppermute | solution.py:552
  21.6 32.6 %collective-permute-start.5 = (bf16[2,512,128]{2,1,0:T(8,128)(2,1)S(1)}, bf16[2,512,128]{2,1,0:T(8,128)(2,1)S(1)}, u32[]{:S(2)}, u32[]{:S(2)}) collective-permute-start(bf16[2,512,128]{2,1,0:T(8,128)(2,1)S(1)} %get-tuple-element.49), channel_id=1, source_target_pairs={{0,6},{2,0},{4,2},{6,4},{1,7},{3,1},{5,3},{7,5},{8,14},{10,8},{12,... | collective-permute-start | bytes 786440 | tf_op jit(solution)/shard_map/ppermute | solution.py:552
  37.0 19.7 %collective-permute-start.2 = (bf16[8,272,128]{2,1,0:T(8,128)(2,1)S(1)}, bf16[8,272,128]{2,1,0:T(8,128)(2,1)S(1)}, u32[]{:S(2)}, u32[]{:S(2)}) collective-permute-start(bf16[8,272,128]{2,1,0:T(8,128)(2,1)S(1)} %slice.8), channel_id=1, source_target_pairs={{0,64},{64,128},{128,192},{1,65},{65,129},{129,193},{2,66},{66,130... | collective-permute-start | bytes 1671176 | tf_op jit(solution)/shard_map/ppermute | solution.py:584
  54.2 2.5 %copy-start.3 = (s32[8]{0:T(128)S(1)}, s32[8]{0:T(128)}, u32[]{:S(2)}) copy-start(s32[8]{0:T(128)} %win.1) | copy-start | bytes 100
  79.8 13.2 %collective-permute-start.9 = (bf16[8,256,128]{2,1,0:T(8,128)(2,1)S(1)}, bf16[8,256,128]{2,1,0:T(8,128)(2,1)S(1)}, u32[]{:S(2)}, u32[]{:S(2)}) collective-permute-start(bf16[8,256,128]{2,1,0:T(8,128)(2,1)S(1)} %get-tuple-element.66), channel_id=1, source_target_pairs={{64,0},{128,64},{192,128},{65,1},{129,65},{193,129},{66,2},{130,66... | collective-permute-start | bytes 1572872 | tf_op jit(solution)/shard_map/ppermute | solution.py:589
  85.1 36.3 %collective-permute-start.6 = (bf16[2,512,128]{2,1,0:T(8,128)(2,1)S(1)}, bf16[2,512,128]{2,1,0:T(8,128)(2,1)S(1)}, u32[]{:S(2)}, u32[]{:S(2)}) collective-permute-start(bf16[2,512,128]{2,1,0:T(8,128)(2,1)S(1)} %get-tuple-element.62), channel_id=1, source_target_pairs={{0,4},{2,6},{4,0},{6,2},{1,5},{3,7},{5,1},{7,3},{8,12},{10,14},{12... | collective-permute-start | bytes 786440 | tf_op jit(solution)/shard_map/ppermute | solution.py:552
  88.9 32.5 %collective-permute-start.7 = (bf16[2,512,128]{2,1,0:T(8,128)(2,1)S(1)}, bf16[2,512,128]{2,1,0:T(8,128)(2,1)S(1)}, u32[]{:S(2)}, u32[]{:S(2)}) collective-permute-start(bf16[2,512,128]{2,1,0:T(8,128)(2,1)S(1)} %get-tuple-element.63), channel_id=1, source_target_pairs={{0,6},{2,0},{4,2},{6,4},{1,7},{3,1},{5,3},{7,5},{8,14},{10,8},{12,... | collective-permute-start | bytes 786440 | tf_op jit(solution)/shard_map/ppermute | solution.py:552
  90.3 31.1 %collective-permute-start.8 = (bf16[2,512,128]{2,1,0:T(8,128)(2,1)S(1)}, bf16[2,512,128]{2,1,0:T(8,128)(2,1)S(1)}, u32[]{:S(2)}, u32[]{:S(2)}) collective-permute-start(bf16[2,512,128]{2,1,0:T(8,128)(2,1)S(1)} %get-tuple-element.64), channel_id=1, source_target_pairs={{0,2},{2,4},{4,6},{6,0},{1,3},{3,5},{5,7},{7,1},{8,10},{10,12},{12... | collective-permute-start | bytes 786440 | tf_op jit(solution)/shard_map/ppermute | solution.py:552
  125.8 2.0 %collective-permute-start.10 = (bf16[2,128,1024]{2,1,0:T(8,128)(2,1)S(1)}, bf16[2,128,1024]{2,1,0:T(8,128)(2,1)S(1)}, u32[]{:S(2)}, u32[]{:S(2)}) collective-permute-start(bf16[2,128,1024]{2,1,0:T(8,128)(2,1)S(1)} %get-tuple-element.72), channel_id=1, source_target_pairs={{0,1},{1,0},{2,3},{3,2},{4,5},{5,4},{6,7},{7,6},{8,9},{9,8},{10,11... | collective-permute-start | bytes 1572872 | tf_op jit(solution)/shard_map/ppermute | solution.py:548

commit v9 on v6

--- a/solution.py
+++ b/solution.py
@@ -57,42 +57,56 @@
     return pl.CostEstimate(flops=flops, bytes_accessed=size, transcendentals=exps)
 
 
-def weight_copies(place, w_qkv, w_out, parts, out, sems):
+PIECES = 4
+
+
+def weight_copies(place, w_qkv, w_out, targets, sems):
     begin = pl.multiple_of(place[0] * HALF * DH, HALF * DH)
-    copies = [
-        pltpu.make_async_copy(
-            w_qkv.at[:, pl.ds(pl.multiple_of(begin + part * D, HALF * DH), HALF * DH)],
-            parts[part],
-            sems.at[part],
-        )
-        for part in range(3)
-    ]
-    copies.append(
-        pltpu.make_async_copy(w_out.at[pl.ds(begin, HALF * DH), :], out, sems.at[3])
-    )
-    return copies
-
-
-def stage_kernel(place, w_qkv, w_out, wq, wk, wv, out, sems):
-    copies = weight_copies(place, w_qkv, w_out, (wq, wk, wv), out, sems)
-    for copy in copies:
-        copy.start()
-    for copy in copies:
+    groups = []
+    for part, target in targets:
+        size = target.shape[0] // PIECES
+        group = []
+        for n in range(PIECES):
+            if part < 3:
+                columns = pl.ds(pl.multiple_of(begin + part * D, HALF * DH), HALF * DH)
+                source = w_qkv.at[pl.ds(n * size, size), columns]
+            else:
+                source = w_out.at[pl.ds(pl.multiple_of(begin + n * size, size), size), :]
+            spot = target.at[pl.ds(n * size, size), :]
+            group.append(pltpu.make_async_copy(source, spot, sems.at[part * PIECES + n]))
+        groups.append(group)
+    return groups
+
+
+def start_all(groups):
+    for group in groups:
+        for copy in group:
+            copy.start()
+
+
+def wait_all(group):
+    for copy in group:
         copy.wait()
 
 
-def stage(place, w_qkv, w_out):
+def stage_kernel(place, w_qkv, wq, wk, sems):
+    groups = weight_copies(place, w_qkv, None, ((0, wq), (1, wk)), sems)
+    start_all(groups)
+    for group in groups:
+        wait_all(group)
+
+
+def stage(place, w_qkv):
     return pl.pallas_call(
         stage_kernel,
-        in_specs=[SM] + [ANY] * 2,
-        out_specs=[VM] * 4,
-        out_shape=[jax.ShapeDtypeStruct((D, HALF * DH), BF16)] * 3
-        + [jax.ShapeDtypeStruct((HALF * DH, D), BF16)],
-        scratch_shapes=[pltpu.SemaphoreType.DMA((4,))],
+        in_specs=[SM, ANY],
+        out_specs=[VM] * 2,
+        out_shape=[jax.ShapeDtypeStruct((D, HALF * DH), BF16)] * 2,
+        scratch_shapes=[pltpu.SemaphoreType.DMA((2 * PIECES,))],
         compiler_params=pltpu.CompilerParams(vmem_limit_bytes=STAGE_LIMIT),
         cost_estimate=cost(0, 9_000_000),
         name="stage",
-    )(place, w_qkv, w_out)
+    )(place, w_qkv)
 
 
 STEPS = (0, 2, 1, 3)
@@ -107,43 +121,65 @@
 
 
 def project_kernel(
-    place, valid, own, other, cot_own, cot_other, gain, wq, wk, wv, wo, packed, near0, near1, near2, near3
+    place, valid, own, other, cot_own, cot_other, gain, wq, wk, w_qkv, w_out,
+    packed, near0, near1, near2, near3, made, wv, wo, sems, out_sems,
 ):
+    groups = weight_copies(place, w_qkv, w_out, ((2, wv), (3, wo)), sems)
+    start_all(groups)
+    flags = jnp.full((ROWS - OK0, DH), valid[0], jnp.int32).astype(F32).astype(BF16)
+    for h in range(HALF):
+        for s in range(2):
+            made[h, s, OK0:ROWS, :] = flags
     x = jnp.concatenate([own[...], other[...]], axis=0).astype(F32)
     rinv = lax.rsqrt(jnp.mean(x * x, axis=-1, keepdims=True) + EPS)
     normed = (x * rinv * gain[...]).astype(BF16)
-    cot = jnp.concatenate([cot_own[...], cot_other[...]], axis=0)
-    flags = jnp.full((ROWS - OK0, DH), valid[0], jnp.int32).astype(F32).astype(BF16)
-    for row in (Q0, K0, V0, G0):
+    leaving = []
+    for n, (row, weight) in enumerate(((Q0, wq), (K0, wk), (V0, wv), (G0, wo))):
+        if n >= 2:
+            wait_all(groups[n - 2])
         if row == G0:
-            got = mm_nt(cot, wo[...]).astype(BF16)
+            cots = jnp.concatenate([cot_own[...], cot_other[...]], axis=0)
+            got = mm_nt(cots, weight[...]).astype(BF16)
         else:
-            got = mm(normed, {Q0: wq, K0: wk, V0: wv}[row][...]).astype(BF16)
+            got = mm(normed, weight[...]).astype(BF16)
         for h in range(HALF):
             for s in range(2):
-                packed[slot_of_head(place, h), s, row : row + HW, :] = (
+                made[slot_of_head(place, h), s, row : row + HW, :] = (
                     got[s * HW : (s + 1) * HW, h * DH : (h + 1) * DH]
                 )
-    for h in range(HALF):
-        for s in range(2):
-            packed[h, s, OK0:ROWS, :] = flags
-    for step, near in zip(STEPS, (near0, near1, near2, near3)):
-        slot = lax.rem(place[1] + step, HALF)
-        for s in range(2):
-            near[s] = packed[slot, s, :OK0, :]
-
-
-def project(place, valid, own, other, cot_own, cot_other, gain, weights):
+        end = ROWS if row == V0 else row + HW
+        span = pl.ds(row, end - row)
+        moves = [(made.at[:, :, span, :], packed.at[:, :, span, :])]
+        for step, near in zip(STEPS, (near0, near1, near2, near3)):
+            slot = lax.rem(place[1] + step, HALF)
+            rows = pl.ds(row, HW)
+            moves.append((made.at[slot, :, rows, :], near.at[:, rows, :]))
+        for m, (source, target) in enumerate(moves):
+            copy = pltpu.make_async_copy(source, target, out_sems.at[5 * n + m])
+            copy.start()
+            leaving.append(copy)
+    for copy in leaving:
+        copy.wait()
+
+
+def project(place, valid, own, other, cot_own, cot_other, gain, weights, w_qkv, w_out):
     return pl.pallas_call(
         project_kernel,
-        in_specs=[SM, SM] + [VM] * 9,
-        out_specs=[VM] * 5,
+        in_specs=[SM, SM] + [VM] * 7 + [ANY] * 2,
+        out_specs=[ANY] * 5,
         out_shape=[jax.ShapeDtypeStruct((HALF, 2, ROWS, DH), BF16)]
         + [jax.ShapeDtypeStruct((2, OK0, DH), BF16)] * 4,
-        compiler_params=params(),
+        scratch_shapes=[
+            pltpu.VMEM((HALF, 2, ROWS, DH), BF16),
+            pltpu.VMEM((D, HALF * DH), BF16),
+            pltpu.VMEM((HALF * DH, D), BF16),
+            pltpu.SemaphoreType.DMA((4 * PIECES,)),
+            pltpu.SemaphoreType.DMA((20,)),
+        ],
+        compiler_params=pltpu.CompilerParams(vmem_limit_bytes=STAGE_LIMIT),
         cost_estimate=cost(2 * PAIR * D * 4 * HALF * DH, 7_000_000),
         name="project",
-    )(place, valid, own, other, cot_own, cot_other, gain, *weights)
+    )(place, valid, own, other, cot_own, cot_other, gain, *weights, w_qkv, w_out)
 
 
 def both(block, row):
@@ -372,8 +408,7 @@
         back[j, :HW, :] = (dk[early, :] * SCALE).astype(BF16)
         back[j, HW:, :] = dv[early, :].astype(BF16)
         own[j, 2 * HW : 3 * HW, :] = (dk[late, :] * SCALE).astype(BF16)
-        own[j, 3 * HW : 4 * HW, :] = dv[late, :].astype(BF16)
-        own[j, 4 * HW :, :] = jnp.zeros((ROWS - 4 * HW, DH), BF16)
+        own[j, 3 * HW :, :] = dv[late, :].astype(BF16)
 
 
 def far_backward(place, mine, past, kept, result, sent, told):
@@ -382,7 +417,7 @@
         in_specs=[SM] + [VM] * 6,
         out_specs=[VM, VM],
         out_shape=[
-            jax.ShapeDtypeStruct((GROUP, ROWS, DH), BF16),
+            jax.ShapeDtypeStruct((GROUP, 4 * HW, DH), BF16),
             jax.ShapeDtypeStruct((GROUP, 2 * HW, DH), BF16),
         ],
         scratch_shapes=[
@@ -410,7 +445,7 @@
         add_back_kernel,
         in_specs=[VM] * 2,
         out_specs=VM,
-        out_shape=jax.ShapeDtypeStruct((GROUP, ROWS, DH), BF16),
+        out_shape=jax.ShapeDtypeStruct((GROUP, 4 * HW, DH), BF16),
         input_output_aliases={0: 0},
         compiler_params=params(),
         cost_estimate=cost(GROUP * 2 * HW * DH, 2_500_000),
@@ -421,9 +456,8 @@
 def unproject_kernel(
     place, near0, near1, near2, near3, far, w_qkv, w_out, own, other, close, wq, wk, wv, wo, sems
 ):
-    copies = weight_copies(place, w_qkv, w_out, (wq, wk, wv), wo, sems)
-    for copy in copies:
-        copy.start()
+    groups = weight_copies(place, w_qkv, w_out, ((0, wq), (1, wk), (2, wv), (3, wo)), sems)
+    start_all(groups)
     for step, near in zip(STEPS, (near0, near1, near2, near3)):
         close[head_here(place, step)] = near[...]
     parts = []
@@ -436,13 +470,13 @@
             here = jnp.concatenate([close[h, 0, rows, :], close[h, 1, rows, :]], axis=0)
             pieces.append((away.astype(F32) + here.astype(F32)).astype(BF16))
         parts.append(jnp.concatenate(pieces, axis=1))
-    copies[0].wait()
+    wait_all(groups[0])
     total = mm_nt(parts[1], wq[...])
-    copies[1].wait()
+    wait_all(groups[1])
     total = total + mm_nt(parts[2], wk[...])
-    copies[2].wait()
+    wait_all(groups[2])
     total = total + mm_nt(parts[3], wv[...])
-    copies[3].wait()
+    wait_all(groups[3])
     mixed = mm(parts[0], wo[...])
     own[0] = mixed[:HW]
     own[1] = total[:HW]
@@ -457,7 +491,7 @@
         out_specs=[VM, VM],
         scratch_shapes=[pltpu.VMEM((HALF, 2, 4 * HW, DH), BF16)]
         + [pltpu.VMEM((D, HALF * DH), BF16)] * 3
-        + [pltpu.VMEM((HALF * DH, D), BF16), pltpu.SemaphoreType.DMA((4,))],
+        + [pltpu.VMEM((HALF * DH, D), BF16), pltpu.SemaphoreType.DMA((4 * PIECES,))],
         out_shape=[jax.ShapeDtypeStruct((2, HW, D), F32), jax.ShapeDtypeStruct((2, HW, D), BF16)],
         compiler_params=pltpu.CompilerParams(vmem_limit_bytes=50 * 1024 * 1024),
         cost_estimate=cost(2 * PAIR * D * 4 * HALF * DH, 8_000_000),
@@ -524,9 +558,9 @@
     other_tokens = swap(tokens)
     other_cot = swap(cot)
     gain = gain.reshape(1, D)
-    weights = stage(place, w_qkv, w_out)
+    weights = stage(place, w_qkv)
     packed, *blocks = project(
-        place, valid, tokens, other_tokens, cot, other_cot, gain, weights
+        place, valid, tokens, other_tokens, cot, other_cot, gain, weights, w_qkv, w_out
     )
     blocks = all_round(blocks, 1)
     mine = exchange(packed.reshape(2 * HALF, ROWS, DH), LANE)
@@ -540,7 +574,7 @@
     own, returned = lax.optimization_barrier((own, returned))
     returned = all_round(returned, -1)
     own = add_back(own, back)
-    far = exchange_alone(own, go).reshape(HALF, 2, ROWS, DH)
+    far = exchange_alone(own, go).reshape(HALF, 2, 4 * HW, DH)
     out_own, out_other = unproject(place, returned, far, w_qkv, w_out)
     mixed, d_tokens = finish(tokens, cot, gain, out_own, swap(out_other))
     return mixed.reshape(1, 1, HW, D), d_tokens.reshape(1, 1, HW, D)

time: 130 us -> 130 us (level)
  transfers between devices with their start and end apart: 12 -> 12, of which waited for: 5 -> 5; matrix products, arithmetic and copies ran while one was open for 0% -> 0% of each run, Pallas kernels for 7% -> 6%
where the time goes in v9:
time: 130 us; the launch traced here: 128 us
  blocking collectives  43.1 us (33%)
  waiting for transfers between devices  30 us (23%)
  starting transfers between devices  29 us (22%)
  Pallas kernels  24 us (18%)
  between operations  1.48 us (1%)
    all_to_all x2, blocking collectives, exchange(): lax.all_to_all(value, axes, 0, 0, axis_index_groups=groups, tiled=True)  43.1 us
    ppermute x6, starting transfers between devices, turn_ring(): return lax.ppermute(value, 'zh', [(i, (i + steps) % 4) for i in range(4)])  17.1 us
    ppermute x6, waiting for transfers between devices, turn_ring(): return lax.ppermute(value, 'zh', [(i, (i + steps) % 4) for i in range(4)])  14.1 us
    all_to_all x1, waiting for transfers between devices, exchange(): lax.all_to_all(value, axes, 0, 0, axis_index_groups=groups, tiled=True)  12.7 us
    all_to_all x1, starting transfers between devices, exchange(): lax.all_to_all(value, axes, 0, 0, axis_index_groups=groups, tiled=True)  5.66 us
    pallas_call x1, Pallas kernels, project(): pl.pallas_call(project_kernel, in_specs=[SM, SM] + [VM] * 7 + [ANY] * 2,...  4.39 us
    pallas_call x1, Pallas kernels, unproject(): pl.pallas_call(unproject_kernel, in_specs=[SM] + [VM] * 5 + [ANY] * 2, ou...  3.8 us
    pallas_call x1, Pallas kernels, far_forward(): pl.pallas_call(far_forward_kernel, in_specs=[SM, SM, VM, VM, VM], out_spe...  3.41 us
  transfers between devices with their start and end apart: 12, of which 5 were waited for; matrix products, arithmetic and copies ran while one was open for 0% of the time, Pallas kernels for 6%

profile of v9, /device:TPU:16, one launch (start us, length us, event | category | flops | bytes accessed | tf_op | source)
XLA Modules:
  0.0 127.7 jit_solution(8546753774361795818)
XLA Ops:
  0.6 0.1 collective-permute-start
  0.7 0.5 collective-permute-start.1
  1.9 0.1 pad_add_fusion.place
  2.0 2.1 %stage.1 = (bf16[1024,512]{1,0:T(8,128)(2,1)S(1)}, bf16[1024,512]{1,0:T(8,128)(2,1)S(1)}) custom-call(s32[3]{0:T(128)S(1)} %pad_add_fusion.place, bf16[1024,3072]{1,0:T(8,128)(2,1)} %w_qkv.5), custom_call_target="tpu_custom_call" | custom-call | bytes 9000000 | tf_op jit(solution)/shard_map/stage/pallas_call | solution.py:100
  4.1 0.0 collective-permute-done.other
  4.2 4.4 %project.1 = (bf16[4,2,528,128]{3,2,1,0:T(8,128)(2,1)}, bf16[2,512,128]{2,1,0:T(8,128)(2,1)S(1)}, bf16[2,512,128]{2,1,0:T(8,128)(2,1)S(1)}, bf16[2,512,128]{2,1,0:T(8,128)(2,1)S(1)}, bf16[2,512,128]{2,1,0:T(8,128)(2,1)S(1)}) custom-call(s32[3]{0:T(128)S(1)} %pad_add_fusion.place, s32[1]{0:T(128)S(6)} %copy.13.valid, bf16[128,1024]{1,0:T(8,128)(2,1)S(1)} %bitcast.13, ...), custom_call_target="tpu_custom_call" | custom-call | flops 1073741824 | bytes 7000000 | tf_op jit(solution)/shard_map/project/pallas_call | solution.py:166
  8.6 5.7 %all-to-all-start.1 = ((bf16[8,528,128]{2,1,0:T(8,128)(2,1)}), bf16[8,528,128]{2,1,0:T(8,128)(2,1)S(1)}, u32[]{:S(2)}, u32[]{:S(2)}) async-start(bf16[8,528,128]{2,1,0:T(8,128)(2,1)} %bitcast.7), calls=%async_computation.1 | async-start | bytes 2162688 | tf_op jit(solution)/shard_map/all_to_all | solution.py:543
  14.2 6.3 %collective-permute-start.3 = (bf16[2,512,128]{2,1,0:T(8,128)(2,1)S(1)}, bf16[2,512,128]{2,1,0:T(8,128)(2,1)S(1)}, u32[]{:S(2)}, u32[]{:S(2)}) collective-permute-start(bf16[2,512,128]{2,1,0:T(8,128)(2,1)S(1)} %get-tuple-element.39), channel_id=1, source_target_pairs={{0,4},{2,6},{4,0},{6,2},{1,5},{3,7},{5,1},{7,3},{8,12},{10,14},{12... | collective-permute-start | bytes 786440 | tf_op jit(solution)/shard_map/ppermute | solution.py:535
  20.5 1.5 %collective-permute-start.4 = (bf16[2,512,128]{2,1,0:T(8,128)(2,1)S(1)}, bf16[2,512,128]{2,1,0:T(8,128)(2,1)S(1)}, u32[]{:S(2)}, u32[]{:S(2)}) collective-permute-start(bf16[2,512,128]{2,1,0:T(8,128)(2,1)S(1)} %get-tuple-element.40), channel_id=1, source_target_pairs={{0,2},{2,4},{4,6},{6,0},{1,3},{3,5},{5,7},{7,1},{8,10},{10,12},{12... | collective-permute-start | bytes 786440 | tf_op jit(solution)/shard_map/ppermute | solution.py:535
  22.0 2.7 %collective-permute-start.5 = (bf16[2,512,128]{2,1,0:T(8,128)(2,1)S(1)}, bf16[2,512,128]{2,1,0:T(8,128)(2,1)S(1)}, u32[]{:S(2)}, u32[]{:S(2)}) collective-permute-start(bf16[2,512,128]{2,1,0:T(8,128)(2,1)S(1)} %get-tuple-element.41), channel_id=1, source_target_pairs={{0,6},{2,0},{4,2},{6,4},{1,7},{3,1},{5,3},{7,5},{8,14},{10,8},{12,... | collective-permute-start | bytes 786440 | tf_op jit(solution)/shard_map/ppermute | solution.py:535
  24.6 12.7 %all-to-all-done.1.mine = bf16[8,528,128]{2,1,0:T(8,128)(2,1)S(1)} async-done(((bf16[8,528,128]{2,1,0:T(8,128)(2,1)}), bf16[8,528,128]{2,1,0:T(8,128)(2,1)S(1)}, u32[]{:S(2)}, u32[]{:S(2)}) %all-to-all-start.1) | async-done | bytes 1081376 | tf_op jit(solution)/shard_map/all_to_all | solution.py:543
  37.4 3.2 %collective-permute-start.2 = (bf16[8,272,128]{2,1,0:T(8,128)(2,1)S(1)}, bf16[8,272,128]{2,1,0:T(8,128)(2,1)S(1)}, u32[]{:S(2)}, u32[]{:S(2)}) collective-permute-start(bf16[8,272,128]{2,1,0:T(8,128)(2,1)S(1)} %slice.8), channel_id=1, source_target_pairs={{0,64},{64,128},{128,192},{1,65},{65,129},{129,193},{2,66},{66,130... | collective-permute-start | bytes 1671176 | tf_op jit(solution)/shard_map/ppermute | solution.py:567
  40.6 10.1 %collective-permute-done.3.near1 = bf16[2,512,128]{2,1,0:T(8,128)(2,1)S(1)} collective-permute-done((bf16[2,512,128]{2,1,0:T(8,128)(2,1)S(1)}, bf16[2,512,128]{2,1,0:T(8,128)(2,1)S(1)}, u32[]{:S(2)}, u32[]{:S(2)}) %collective-permute-start.3) | collective-permute-done | bytes 262176 | tf_op jit(solution)/shard_map/ppermute | solution.py:535
  50.7 4.0 %collective-permute-done.4.near2 = bf16[2,512,128]{2,1,0:T(8,128)(2,1)S(1)} collective-permute-done((bf16[2,512,128]{2,1,0:T(8,128)(2,1)S(1)}, bf16[2,512,128]{2,1,0:T(8,128)(2,1)S(1)}, u32[]{:S(2)}, u32[]{:S(2)}) %collective-permute-start.4) | collective-permute-done | bytes 262176 | tf_op jit(solution)/shard_map/ppermute | solution.py:535
  54.7 0.0 collective-permute-done.5.near3
  54.7 2.5 %near_forward.1 = (bf16[1024,1024]{1,0:T(8,128)(2,1)S(1)}, f32[128,1024]{1,0:T(8,128)S(1)}, f32[8,4,128]{2,1,0:T(4,128)S(1)}) custom-call(bf16[2,512,128]{2,1,0:T(8,128)(2,1)S(1)} %get-tuple-element.38.near0, bf16[2,512,128]{2,1,0:T(8,128)(2,1)S(1)} %collective-permute-done.3.near1, bf16[2,512,128]{2,1,0:T(8,128)(2,1)S(1)} %collective-permute-done.4.near2, ...), custom_call_target="tpu_custom_call" | custom-call | flops 10737418240 | bytes 4000000 | tf_op jit(solution)/shard_map/near_forward/pallas_call | solution.py:219
  57.2 3.4 %far_forward.1 = (f32[8,8,128]{2,1,0:T(8,128)S(1)}, bf16[4,1152,256]{2,1,0:T(8,128)(2,1)S(1)}, f32[128,1024]{1,0:T(8,128)S(1)}) custom-call(s32[3]{0:T(128)S(1)} %pad_add_fusion.place, s32[8]{0:T(128)S(1)} %copy-done.3, bf16[8,528,128]{2,1,0:T(8,128)(2,1)S(1)} %all-to-all-done.1.mine, bf16[8,272,128]{2,1,0:T(8,128)(2,1)S(1)} %collective-permute-done.2.past, ...), custom_call_target="tpu_custom_call" | custom-call | flops 603979776 | bytes 5000000 | tf_op jit(solution)/shard_map/far_forward/pallas_call | solution.py:284
  60.6 16.4 %all_to_all.15.told = f32[8,8,128]{2,1,0:T(8,128)S(1)} all-to-all(f32[8,8,128]{2,1,0:T(8,128)S(1)} %get-tuple-element.45.sent), channel_id=1, replica_groups={{0,8,22,30,36,44,50,58},{2,10,16,24,38,46,52,60},{4,12,18,26,32,40,54,6..., dimensions={0} | all-to-all | bytes 65536 | tf_op jit(solution)/shard_map/all_to_all | solution.py:543
  77.0 3.4 %far_backward.1 = (bf16[8,512,128]{2,1,0:T(8,128)(2,1)S(1)}, bf16[8,256,128]{2,1,0:T(8,128)(2,1)S(1)}) custom-call(s32[3]{0:T(128)S(1)} %pad_add_fusion.place, bf16[8,528,128]{2,1,0:T(8,128)(2,1)S(1)} %all-to-all-done.1.mine, bf16[8,272,128]{2,1,0:T(8,128)(2,1)S(1)} %collective-permute-done.2.past, bf16[4,1152,256]{2,1,0:T(8,128)(2,1)S(1)} %get-tuple-element.43.kept, ...), custom_call_target="tpu_custom_call" | custom-call | flops 1207959552 | bytes 6000000 | tf_op jit(solution)/shard_map/far_backward/pallas_call | solution.py:415
  80.4 2.4 %collective-permute-start.9 = (bf16[8,256,128]{2,1,0:T(8,128)(2,1)S(1)}, bf16[8,256,128]{2,1,0:T(8,128)(2,1)S(1)}, u32[]{:S(2)}, u32[]{:S(2)}) collective-permute-start(bf16[8,256,128]{2,1,0:T(8,128)(2,1)S(1)} %get-tuple-element.58), channel_id=1, source_target_pairs={{64,0},{128,64},{192,128},{65,1},{129,65},{193,129},{66,2},{130,66... | collective-permute-start | bytes 1572872 | tf_op jit(solution)/shard_map/ppermute | solution.py:572
  82.7 2.9 %near_backward.1 = (bf16[2,512,128]{2,1,0:T(8,128)(2,1)S(1)}, bf16[2,512,128]{2,1,0:T(8,128)(2,1)S(1)}, bf16[2,512,128]{2,1,0:T(8,128)(2,1)S(1)}, bf16[2,512,128]{2,1,0:T(8,128)(2,1)S(1)}) custom-call(s32[3]{0:T(128)S(1)} %pad_add_fusion.place, bf16[2,512,128]{2,1,0:T(8,128)(2,1)S(1)} %get-tuple-element.38.near0, ...), custom_call_target="tpu_custom_call" | custom-call | flops 1073741824 | bytes 5000000 | tf_op jit(solution)/shard_map/near_backward/pallas_call | solution.py:353
  85.7 3.8 %collective-permute-start.6 = (bf16[2,512,128]{2,1,0:T(8,128)(2,1)S(1)}, bf16[2,512,128]{2,1,0:T(8,128)(2,1)S(1)}, u32[]{:S(2)}, u32[]{:S(2)}) collective-permute-start(bf16[2,512,128]{2,1,0:T(8,128)(2,1)S(1)} %get-tuple-element.54), channel_id=1, source_target_pairs={{0,4},{2,6},{4,0},{6,2},{1,5},{3,7},{5,1},{7,3},{8,12},{10,14},{12... | collective-permute-start | bytes 786440 | tf_op jit(solution)/shard_map/ppermute | solution.py:535
  89.4 1.4 %collective-permute-start.7 = (bf16[2,512,128]{2,1,0:T(8,128)(2,1)S(1)}, bf16[2,512,128]{2,1,0:T(8,128)(2,1)S(1)}, u32[]{:S(2)}, u32[]{:S(2)}) collective-permute-start(bf16[2,512,128]{2,1,0:T(8,128)(2,1)S(1)} %get-tuple-element.55), channel_id=1, source_target_pairs={{0,6},{2,0},{4,2},{6,4},{1,7},{3,1},{5,3},{7,5},{8,14},{10,8},{12,... | collective-permute-start | bytes 786440 | tf_op jit(solution)/shard_map/ppermute | solution.py:535
  90.8 1.5 %collective-permute-start.8 = (bf16[2,512,128]{2,1,0:T(8,128)(2,1)S(1)}, bf16[2,512,128]{2,1,0:T(8,128)(2,1)S(1)}, u32[]{:S(2)}, u32[]{:S(2)}) collective-permute-start(bf16[2,512,128]{2,1,0:T(8,128)(2,1)S(1)} %get-tuple-element.56), channel_id=1, source_target_pairs={{0,2},{2,4},{4,6},{6,0},{1,3},{3,5},{5,7},{7,1},{8,10},{10,12},{12... | collective-permute-start | bytes 786440 | tf_op jit(solution)/shard_map/ppermute | solution.py:535
  92.4 1.3 collective-permute-done.9.back
  93.6 0.4 add_back.1
  94.1 26.8 %conditional.1 = (bf16[4,2,512,128]{3,2,1,0:T(8,128)(2,1)S(1)}) conditional(s32[]{:T(128)} %bitcast.8, () %tuple.18, bf16[8,512,128]{2,1,0:T(8,128)(2,1)S(1)} %add_back.1), branch_computations={%region_0.0_spmd, %region_1.0_spmd} | conditional | bytes 2097160 | solution.py:547
  94.1 26.7 %all_to_all.14 = bf16[8,512,128]{2,1,0:T(8,128)(2,1)S(1)} all-to-all(bf16[8,512,128]{2,1,0:T(8,128)(2,1)S(1)} %param.1), channel_id=1, replica_groups=mesh['y'=4,'x'=4,'zl'=2,'zh'=4,'core'=2] {'x','zl'}, dimensions={0} | all-to-all | bytes 2097152 | tf_op jit(solution)/shard_map/cond/branch_1_fun/all_to_all | solution.py:543
  120.8 3.8 %unproject.1 = (f32[2,128,1024]{2,1,0:T(8,128)S(1)}, bf16[2,128,1024]{2,1,0:T(8,128)(2,1)S(1)}) custom-call(s32[3]{0:T(128)S(1)} %pad_add_fusion.place, bf16[2,512,128]{2,1,0:T(8,128)(2,1)S(1)} %get-tuple-element.53.near0, bf16[2,512,128]{2,1,0:T(8,128)(2,1)S(1)} %collective-permute-done.6.near1, bf16[2,512,128]{2,1,0:T(8,128)(2,1)S(1)} %collective-permute-done.7.near2, ...), custom_call_target="tpu_custom_call" | custom-call | flops 1073741824 | bytes 8000000 | tf_op jit(solution)/shard_map/unproject/pallas_call | solution.py:488
  124.6 0.1 collective-permute-start.10
  124.7 1.9 %collective-permute-done.10.other = bf16[2,128,1024]{2,1,0:T(8,128)(2,1)S(1)} collective-permute-done((bf16[2,128,1024]{2,1,0:T(8,128)(2,1)S(1)}, bf16[2,128,1024]{2,1,0:T(8,128)(2,1)S(1)}, u32[]{:S(2)}, u32[]{:S(2)}) %collective-permute-start.10) | collective-permute-done | bytes 524320 | tf_op jit(solution)/shard_map/ppermute | solution.py:531
  126.6 1.0 finish.1
  (14 shorter events, 0.1 us)
Async XLA Ops:
  0.6 3.5 %collective-permute-start = (bf16[128,1024]{1,0:T(8,128)(2,1)}, bf16[128,1024]{1,0:T(8,128)(2,1)S(1)}, u32[]{:S(2)}, u32[]{:S(2)}) collective-permute-start(bf16[128,1024]{1,0:T(8,128)(2,1)} %bitcast.12), channel_id=1, source_target_pairs={{0,1},{1,0},{2,3},{3,2},{4,5},{5,4},{6,7},{7,6},{8,9},{9,8},{10,11... | collective-permute-start | bytes 786440 | tf_op jit(solution)/shard_map/ppermute | solution.py:531
  0.7 3.4 %collective-permute-start.1 = (bf16[128,1024]{1,0:T(8,128)(2,1)}, bf16[128,1024]{1,0:T(8,128)(2,1)S(1)}, u32[]{:S(2)}, u32[]{:S(2)}) collective-permute-start(bf16[128,1024]{1,0:T(8,128)(2,1)} %bitcast.15), channel_id=1, source_target_pairs={{0,1},{1,0},{2,3},{3,2},{4,5},{5,4},{6,7},{7,6},{8,9},{9,8},{10,11... | collective-permute-start | bytes 786440 | tf_op jit(solution)/shard_map/ppermute | solution.py:531
  2.0 2.2 %copy-start = (bf16[1,1,128,1024]{3,2,1,0:T(8,128)(2,1)S(1)}, bf16[1,1,128,1024]{3,2,1,0:T(8,128)(2,1)}, u32[]{:S(2)}) copy-start(bf16[1,1,128,1024]{3,2,1,0:T(8,128)(2,1)} %param.9) | copy-start | bytes 786436
  2.0 2.2 %copy-start.1 = (bf16[1,1,128,1024]{3,2,1,0:T(8,128)(2,1)S(1)}, bf16[1,1,128,1024]{3,2,1,0:T(8,128)(2,1)}, u32[]{:S(2)}) copy-start(bf16[1,1,128,1024]{3,2,1,0:T(8,128)(2,1)} %param.15) | copy-start | bytes 786436
  2.0 2.2 %copy-start.2 = (f32[1024]{0:T(1024)S(1)}, f32[1024]{0:T(1024)}, u32[]{:S(2)}) copy-start(f32[1024]{0:T(1024)} %param.10) | copy-start | bytes 12292
  8.6 28.8 %all-to-all-start.1 = ((bf16[8,528,128]{2,1,0:T(8,128)(2,1)}), bf16[8,528,128]{2,1,0:T(8,128)(2,1)S(1)}, u32[]{:S(2)}, u32[]{:S(2)}) async-start(bf16[8,528,128]{2,1,0:T(8,128)(2,1)} %bitcast.7), calls=%async_computation.1 | async-start | bytes 2162688 | tf_op jit(solution)/shard_map/all_to_all | solution.py:543
  14.2 36.5 %collective-permute-start.3 = (bf16[2,512,128]{2,1,0:T(8,128)(2,1)S(1)}, bf16[2,512,128]{2,1,0:T(8,128)(2,1)S(1)}, u32[]{:S(2)}, u32[]{:S(2)}) collective-permute-start(bf16[2,512,128]{2,1,0:T(8,128)(2,1)S(1)} %get-tuple-element.39), channel_id=1, source_target_pairs={{0,4},{2,6},{4,0},{6,2},{1,5},{3,7},{5,1},{7,3},{8,12},{10,14},{12... | collective-permute-start | bytes 786440 | tf_op jit(solution)/shard_map/ppermute | solution.py:535
  20.5 34.2 %collective-permute-start.4 = (bf16[2,512,128]{2,1,0:T(8,128)(2,1)S(1)}, bf16[2,512,128]{2,1,0:T(8,128)(2,1)S(1)}, u32[]{:S(2)}, u32[]{:S(2)}) collective-permute-start(bf16[2,512,128]{2,1,0:T(8,128)(2,1)S(1)} %get-tuple-element.40), channel_id=1, source_target_pairs={{0,2},{2,4},{4,6},{6,0},{1,3},{3,5},{5,7},{7,1},{8,10},{10,12},{12... | collective-permute-start | bytes 786440 | tf_op jit(solution)/shard_map/ppermute | solution.py:535
  22.0 32.7 %collective-permute-start.5 = (bf16[2,512,128]{2,1,0:T(8,128)(2,1)S(1)}, bf16[2,512,128]{2,1,0:T(8,128)(2,1)S(1)}, u32[]{:S(2)}, u32[]{:S(2)}) collective-permute-start(bf16[2,512,128]{2,1,0:T(8,128)(2,1)S(1)} %get-tuple-element.41), channel_id=1, source_target_pairs={{0,6},{2,0},{4,2},{6,4},{1,7},{3,1},{5,3},{7,5},{8,14},{10,8},{12,... | collective-permute-start | bytes 786440 | tf_op jit(solution)/shard_map/ppermute | solution.py:535
  37.4 19.8 %collective-permute-start.2 = (bf16[8,272,128]{2,1,0:T(8,128)(2,1)S(1)}, bf16[8,272,128]{2,1,0:T(8,128)(2,1)S(1)}, u32[]{:S(2)}, u32[]{:S(2)}) collective-permute-start(bf16[8,272,128]{2,1,0:T(8,128)(2,1)S(1)} %slice.8), channel_id=1, source_target_pairs={{0,64},{64,128},{128,192},{1,65},{65,129},{129,193},{2,66},{66,130... | collective-permute-start | bytes 1671176 | tf_op jit(solution)/shard_map/ppermute | solution.py:567
  54.7 2.5 %copy-start.3 = (s32[8]{0:T(128)S(1)}, s32[8]{0:T(128)}, u32[]{:S(2)}) copy-start(s32[8]{0:T(128)} %win.1) | copy-start | bytes 100
  80.4 13.3 %collective-permute-start.9 = (bf16[8,256,128]{2,1,0:T(8,128)(2,1)S(1)}, bf16[8,256,128]{2,1,0:T(8,128)(2,1)S(1)}, u32[]{:S(2)}, u32[]{:S(2)}) collective-permute-start(bf16[8,256,128]{2,1,0:T(8,128)(2,1)S(1)} %get-tuple-element.58), channel_id=1, source_target_pairs={{64,0},{128,64},{192,128},{65,1},{129,65},{193,129},{66,2},{130,66... | collective-permute-start | bytes 1572872 | tf_op jit(solution)/shard_map/ppermute | solution.py:572
  85.7 35.2 %collective-permute-start.6 = (bf16[2,512,128]{2,1,0:T(8,128)(2,1)S(1)}, bf16[2,512,128]{2,1,0:T(8,128)(2,1)S(1)}, u32[]{:S(2)}, u32[]{:S(2)}) collective-permute-start(bf16[2,512,128]{2,1,0:T(8,128)(2,1)S(1)} %get-tuple-element.54), channel_id=1, source_target_pairs={{0,4},{2,6},{4,0},{6,2},{1,5},{3,7},{5,1},{7,3},{8,12},{10,14},{12... | collective-permute-start | bytes 786440 | tf_op jit(solution)/shard_map/ppermute | solution.py:535
  89.4 31.4 %collective-permute-start.7 = (bf16[2,512,128]{2,1,0:T(8,128)(2,1)S(1)}, bf16[2,512,128]{2,1,0:T(8,128)(2,1)S(1)}, u32[]{:S(2)}, u32[]{:S(2)}) collective-permute-start(bf16[2,512,128]{2,1,0:T(8,128)(2,1)S(1)} %get-tuple-element.55), channel_id=1, source_target_pairs={{0,6},{2,0},{4,2},{6,4},{1,7},{3,1},{5,3},{7,5},{8,14},{10,8},{12,... | collective-permute-start | bytes 786440 | tf_op jit(solution)/shard_map/ppermute | solution.py:535
  90.8 30.0 %collective-permute-start.8 = (bf16[2,512,128]{2,1,0:T(8,128)(2,1)S(1)}, bf16[2,512,128]{2,1,0:T(8,128)(2,1)S(1)}, u32[]{:S(2)}, u32[]{:S(2)}) collective-permute-start(bf16[2,512,128]{2,1,0:T(8,128)(2,1)S(1)} %get-tuple-element.56), channel_id=1, source_target_pairs={{0,2},{2,4},{4,6},{6,0},{1,3},{3,5},{5,7},{7,1},{8,10},{10,12},{12... | collective-permute-start | bytes 786440 | tf_op jit(solution)/shard_map/ppermute | solution.py:535
  124.6 2.0 %collective-permute-start.10 = (bf16[2,128,1024]{2,1,0:T(8,128)(2,1)S(1)}, bf16[2,128,1024]{2,1,0:T(8,128)(2,1)S(1)}, u32[]{:S(2)}, u32[]{:S(2)}) collective-permute-start(bf16[2,128,1024]{2,1,0:T(8,128)(2,1)S(1)} %get-tuple-element.60), channel_id=1, source_target_pairs={{0,1},{1,0},{2,3},{3,2},{4,5},{5,4},{6,7},{7,6},{8,9},{9,8},{10,11... | collective-permute-start | bytes 1572872 | tf_op jit(solution)/shard_map/ppermute | solution.py:531

commit v10 on v9

--- a/solution.py
+++ b/solution.py
@@ -89,24 +89,25 @@
         copy.wait()
 
 
-def stage_kernel(place, w_qkv, wq, wk, sems):
-    groups = weight_copies(place, w_qkv, None, ((0, wq), (1, wk)), sems)
+def stage_kernel(place, w_qkv, w_out, wq, wk, wv, wo, sems):
+    groups = weight_copies(place, w_qkv, w_out, ((0, wq), (1, wk), (2, wv), (3, wo)), sems)
     start_all(groups)
     for group in groups:
         wait_all(group)
 
 
-def stage(place, w_qkv):
+def stage(place, w_qkv, w_out):
     return pl.pallas_call(
         stage_kernel,
-        in_specs=[SM, ANY],
-        out_specs=[VM] * 2,
-        out_shape=[jax.ShapeDtypeStruct((D, HALF * DH), BF16)] * 2,
-        scratch_shapes=[pltpu.SemaphoreType.DMA((2 * PIECES,))],
+        in_specs=[SM, ANY, ANY],
+        out_specs=[VM] * 4,
+        out_shape=[jax.ShapeDtypeStruct((D, HALF * DH), BF16)] * 3
+        + [jax.ShapeDtypeStruct((HALF * DH, D), BF16)],
+        scratch_shapes=[pltpu.SemaphoreType.DMA((4 * PIECES,))],
         compiler_params=pltpu.CompilerParams(vmem_limit_bytes=STAGE_LIMIT),
         cost_estimate=cost(0, 9_000_000),
         name="stage",
-    )(place, w_qkv)
+    )(place, w_qkv, w_out)
 
 
 STEPS = (0, 2, 1, 3)
@@ -121,11 +122,9 @@
 
 
 def project_kernel(
-    place, valid, own, other, cot_own, cot_other, gain, wq, wk, w_qkv, w_out,
-    packed, near0, near1, near2, near3, made, wv, wo, sems, out_sems,
+    place, valid, own, other, cot_own, cot_other, gain, wq, wk, wv, wo,
+    packed, near0, near1, near2, near3, made, out_sems,
 ):
-    groups = weight_copies(place, w_qkv, w_out, ((2, wv), (3, wo)), sems)
-    start_all(groups)
     flags = jnp.full((ROWS - OK0, DH), valid[0], jnp.int32).astype(F32).astype(BF16)
     for h in range(HALF):
         for s in range(2):
@@ -135,8 +134,6 @@
     normed = (x * rinv * gain[...]).astype(BF16)
     leaving = []
     for n, (row, weight) in enumerate(((Q0, wq), (K0, wk), (V0, wv), (G0, wo))):
-        if n >= 2:
-            wait_all(groups[n - 2])
         if row == G0:
             cots = jnp.concatenate([cot_own[...], cot_other[...]], axis=0)
             got = mm_nt(cots, weight[...]).astype(BF16)
@@ -162,24 +159,21 @@
         copy.wait()
 
 
-def project(place, valid, own, other, cot_own, cot_other, gain, weights, w_qkv, w_out):
+def project(place, valid, own, other, cot_own, cot_other, gain, weights):
     return pl.pallas_call(
         project_kernel,
-        in_specs=[SM, SM] + [VM] * 7 + [ANY] * 2,
+        in_specs=[SM, SM] + [VM] * 9,
         out_specs=[ANY] * 5,
         out_shape=[jax.ShapeDtypeStruct((HALF, 2, ROWS, DH), BF16)]
         + [jax.ShapeDtypeStruct((2, OK0, DH), BF16)] * 4,
         scratch_shapes=[
             pltpu.VMEM((HALF, 2, ROWS, DH), BF16),
-            pltpu.VMEM((D, HALF * DH), BF16),
-            pltpu.VMEM((HALF * DH, D), BF16),
-            pltpu.SemaphoreType.DMA((4 * PIECES,)),
             pltpu.SemaphoreType.DMA((20,)),
         ],
-        compiler_params=pltpu.CompilerParams(vmem_limit_bytes=STAGE_LIMIT),
+        compiler_params=params(),
         cost_estimate=cost(2 * PAIR * D * 4 * HALF * DH, 7_000_000),
         name="project",
-    )(place, valid, own, other, cot_own, cot_other, gain, *weights, w_qkv, w_out)
+    )(place, valid, own, other, cot_own, cot_other, gain, *weights)
 
 
 def both(block, row):
@@ -189,28 +183,29 @@
 def near_forward_kernel(near0, near1, near2, near3, kept, result, stats, scores):
     blocks = (near0, near1, near2, near3)
     turned = [turn(both(block, V0)).astype(BF16) for block in blocks]
+    query = jnp.concatenate([both(block, Q0) for block in blocks], axis=0)
+    peak = jnp.full((1, TOKENS), -jnp.inf, F32)
+    for b in range(8):
+        keys = blocks[b // 2][b % 2, K0 : K0 + HW, :]
+        block = mm_nt(keys, query)
+        scores[b * HW : (b + 1) * HW, :] = block
+        peak = jnp.maximum(peak, jnp.max(block, axis=0, keepdims=True))
+    peak = peak * SCALE2
+    total = jnp.zeros((1, TOKENS), F32)
+    for b in range(32):
+        rows = slice(b * 32, (b + 1) * 32)
+        block = jnp.exp2(scores[rows, :] * SCALE2 - peak)
+        total = total + jnp.sum(block, axis=0, keepdims=True)
+        kept[rows, :] = block.astype(BF16)
+    turned = jnp.concatenate(turned, axis=1)
     for g in range(4):
         cols = slice(g * PAIR, (g + 1) * PAIR)
-        query = both(blocks[g], Q0)
-        grad_t = turn(both(blocks[g], G0))
-        peak = jnp.full((1, PAIR), -jnp.inf, F32)
-        for z in range(4):
-            block = mm_nt(both(blocks[z], K0), query)
-            scores[z * PAIR : (z + 1) * PAIR, :] = block
-            peak = jnp.maximum(peak, jnp.max(block, axis=0, keepdims=True))
-        peak = peak * SCALE2
-        total = jnp.zeros((1, PAIR), F32)
-        for b in range(8):
-            rows = slice(b * HW, (b + 1) * HW)
-            block = jnp.exp2(scores[rows, :] * SCALE2 - peak)
-            total = total + jnp.sum(block, axis=0, keepdims=True)
-            kept[rows, cols] = block.astype(BF16)
-        got = jnp.zeros((DH, PAIR), F32)
-        for z in range(4):
-            got = got + mm(turned[z], kept[z * PAIR : (z + 1) * PAIR, cols])
+        got = mm(turned, kept[:, cols])
         result[:, cols] = got
-        delta = jnp.sum(got * grad_t, axis=0, keepdims=True)
-        told = jnp.concatenate([peak, total, delta, jnp.zeros((1, PAIR), F32)], axis=0)
+        delta = jnp.sum(got * turn(both(blocks[g], G0)), axis=0, keepdims=True)
+        told = jnp.concatenate(
+            [peak[:, cols], total[:, cols], delta, jnp.zeros((1, PAIR), F32)], axis=0
+        )
         stats[2 * g] = told[:, :HW]
         stats[2 * g + 1] = told[:, HW:]
 
@@ -225,7 +220,7 @@
             jax.ShapeDtypeStruct((DH, TOKENS), F32),
             jax.ShapeDtypeStruct((8, 4, HW), F32),
         ],
-        scratch_shapes=[pltpu.VMEM((TOKENS, PAIR), F32)],
+        scratch_shapes=[pltpu.VMEM((TOKENS, TOKENS), F32)],
         compiler_params=params(),
         cost_estimate=cost(80 * TOKENS * TOKENS * DH, 4_000_000, TOKENS * TOKENS),
         name="near_forward",
@@ -236,14 +231,12 @@
     return lax.rem(place[1] + step, 4) * 2 + s
 
 
-def far_forward_kernel(place, win, mine, past, close, told, kept, result, keys, values_t, scores):
+def far_forward_kernel(place, win, mine, past, close, told, kept, result, values_t, scores):
     width = win[place[0] * HALF + head_here(place)]
     for g in range(4):
         for s in range(2):
             told[slot_of_near(place, STEPS[g], s), 0:4, :] = close[2 * g + s]
     for j in range(GROUP):
-        keys[j * HW : (j + 1) * HW, :] = past[j, :HW, :]
-        keys[(GROUP + j) * HW : (GROUP + j + 1) * HW, :] = mine[j, K0 : K0 + HW, :]
         values_t[:, j * HW : (j + 1) * HW] = turn(past[j, HW : 2 * HW, :]).astype(BF16)
         values_t[:, (GROUP + j) * HW : (GROUP + j + 1) * HW] = turn(
             mine[j, V0 : V0 + HW, :]
@@ -257,13 +250,15 @@
         for b in range(WIN + 1):
             j = 2 * p + b
             if j < GROUP:
+                keys = past[j, :HW, :]
                 flag = past[j, 2 * HW : 2 * HW + 1, :].astype(F32)
             else:
+                keys = mine[j - GROUP, K0 : K0 + HW, :]
                 flag = mine[j - GROUP, OK0 : OK0 + 1, :].astype(F32)
             lower = jnp.where((flag > 0.5) & (b >= WIN - width) & (b < WIN), 0.0, -jnp.inf)
             upper = jnp.where((flag > 0.5) & (b >= WIN + 1 - width), 0.0, -jnp.inf)
             bias = jnp.concatenate([lower, upper], axis=1)
-            block = mm_nt(keys[j * HW : (j + 1) * HW, :], query) + bias
+            block = mm_nt(keys, query) + bias
             scores[b * HW : (b + 1) * HW, :] = block
             peak = jnp.maximum(peak, jnp.max(block, axis=0, keepdims=True))
         peak = jnp.maximum(peak * SCALE2, FLOOR)
@@ -291,7 +286,6 @@
             jax.ShapeDtypeStruct((DH, GROUP * HW), F32),
         ],
         scratch_shapes=[
-            pltpu.VMEM((2 * GROUP * HW, DH), BF16),
             pltpu.VMEM((DH, 2 * GROUP * HW), BF16),
             pltpu.VMEM((KEYS, PAIR), F32),
         ],
@@ -558,9 +552,9 @@
     other_tokens = swap(tokens)
     other_cot = swap(cot)
     gain = gain.reshape(1, D)
-    weights = stage(place, w_qkv)
+    weights = stage(place, w_qkv, w_out)
     packed, *blocks = project(
-        place, valid, tokens, other_tokens, cot, other_cot, gain, weights, w_qkv, w_out
+        place, valid, tokens, other_tokens, cot, other_cot, gain, weights
     )
     blocks = all_round(blocks, 1)
     mine = exchange(packed.reshape(2 * HALF, ROWS, DH), LANE)

time: 130 us -> 129 us (level)
  transfers between devices with their start and end apart: 12 -> 12, of which waited for: 5 -> 5; matrix products, arithmetic and copies ran while one was open for 0% -> 0% of each run, Pallas kernels for 6% -> 7%
where the time goes in v10:
time: 129 us; the launch traced here: 127 us
  blocking collectives  43.1 us (33%)
  waiting for transfers between devices  29.8 us (23%)
  starting transfers between devices  29 us (22%)
  Pallas kernels  23.8 us (18%)
  between operations  1.48 us (1%)
    all_to_all x2, blocking collectives, exchange(): lax.all_to_all(value, axes, 0, 0, axis_index_groups=groups, tiled=True)  43.1 us
    ppermute x6, starting transfers between devices, turn_ring(): return lax.ppermute(value, 'zh', [(i, (i + steps) % 4) for i in range(4)])  17.1 us
    ppermute x6, waiting for transfers between devices, turn_ring(): return lax.ppermute(value, 'zh', [(i, (i + steps) % 4) for i in range(4)])  14 us
    all_to_all x1, waiting for transfers between devices, exchange(): lax.all_to_all(value, axes, 0, 0, axis_index_groups=groups, tiled=True)  12.7 us
    all_to_all x1, starting transfers between devices, exchange(): lax.all_to_all(value, axes, 0, 0, axis_index_groups=groups, tiled=True)  5.67 us
    pallas_call x1, Pallas kernels, project(): pl.pallas_call(project_kernel, in_specs=[SM, SM] + [VM] * 9, out_specs=[A...  3.89 us
    pallas_call x1, Pallas kernels, unproject(): pl.pallas_call(unproject_kernel, in_specs=[SM] + [VM] * 5 + [ANY] * 2, ou...  3.8 us
    pallas_call x1, Pallas kernels, far_backward(): pl.pallas_call(far_backward_kernel, in_specs=[SM] + [VM] * 6, out_specs=[...  3.37 us
  transfers between devices with their start and end apart: 12, of which 5 were waited for; matrix products, arithmetic and copies ran while one was open for 0% of the time, Pallas kernels for 7%

profile of v10, /device:TPU:16, one launch (start us, length us, event | category | flops | bytes accessed | tf_op | source)
XLA Modules:
  0.0 127.3 jit_solution(171567909196905493)
XLA Ops:
  0.6 0.1 collective-permute-start
  0.7 0.5 collective-permute-start.1
  1.9 0.1 pad_add_fusion.place
  2.0 2.8 %stage.1 = (bf16[1024,512]{1,0:T(8,128)(2,1)S(1)}, bf16[1024,512]{1,0:T(8,128)(2,1)S(1)}, bf16[1024,512]{1,0:T(8,128)(2,1)S(1)}, bf16[512,1024]{1,0:T(8,128)(2,1)S(1)}) custom-call(s32[3]{0:T(128)S(1)} %pad_add_fusion.place, bf16[1024,3072]{1,0:T(8,128)(2,1)} %w_qkv.3, bf16[1024,1024]{1,0:T(8,128)(2,1)} %w_out.3), custom_call_target="tpu_custom_call" | custom-call | bytes 9000000 | tf_op jit(solution)/shard_map/stage/pallas_call | solution.py:100
  4.8 0.0 collective-permute-done.1.cot_other
  4.9 3.9 %project.1 = (bf16[4,2,528,128]{3,2,1,0:T(8,128)(2,1)}, bf16[2,512,128]{2,1,0:T(8,128)(2,1)S(1)}, bf16[2,512,128]{2,1,0:T(8,128)(2,1)S(1)}, bf16[2,512,128]{2,1,0:T(8,128)(2,1)S(1)}, bf16[2,512,128]{2,1,0:T(8,128)(2,1)S(1)}) custom-call(s32[3]{0:T(128)S(1)} %pad_add_fusion.place, s32[1]{0:T(128)S(6)} %copy.13.valid, bf16[128,1024]{1,0:T(8,128)(2,1)S(1)} %bitcast.13, ...), custom_call_target="tpu_custom_call" | custom-call | flops 1073741824 | bytes 7000000 | tf_op jit(solution)/shard_map/project/pallas_call | solution.py:163
  8.8 5.7 %all-to-all-start.1 = ((bf16[8,528,128]{2,1,0:T(8,128)(2,1)}), bf16[8,528,128]{2,1,0:T(8,128)(2,1)S(1)}, u32[]{:S(2)}, u32[]{:S(2)}) async-start(bf16[8,528,128]{2,1,0:T(8,128)(2,1)} %bitcast.7), calls=%async_computation.1 | async-start | bytes 2162688 | tf_op jit(solution)/shard_map/all_to_all | solution.py:537
  14.4 6.3 %collective-permute-start.3 = (bf16[2,512,128]{2,1,0:T(8,128)(2,1)S(1)}, bf16[2,512,128]{2,1,0:T(8,128)(2,1)S(1)}, u32[]{:S(2)}, u32[]{:S(2)}) collective-permute-start(bf16[2,512,128]{2,1,0:T(8,128)(2,1)S(1)} %get-tuple-element.43), channel_id=1, source_target_pairs={{0,4},{2,6},{4,0},{6,2},{1,5},{3,7},{5,1},{7,3},{8,12},{10,14},{12... | collective-permute-start | bytes 786440 | tf_op jit(solution)/shard_map/ppermute | solution.py:529
  20.7 1.5 %collective-permute-start.4 = (bf16[2,512,128]{2,1,0:T(8,128)(2,1)S(1)}, bf16[2,512,128]{2,1,0:T(8,128)(2,1)S(1)}, u32[]{:S(2)}, u32[]{:S(2)}) collective-permute-start(bf16[2,512,128]{2,1,0:T(8,128)(2,1)S(1)} %get-tuple-element.44), channel_id=1, source_target_pairs={{0,2},{2,4},{4,6},{6,0},{1,3},{3,5},{5,7},{7,1},{8,10},{10,12},{12... | collective-permute-start | bytes 786440 | tf_op jit(solution)/shard_map/ppermute | solution.py:529
  22.2 2.7 %collective-permute-start.5 = (bf16[2,512,128]{2,1,0:T(8,128)(2,1)S(1)}, bf16[2,512,128]{2,1,0:T(8,128)(2,1)S(1)}, u32[]{:S(2)}, u32[]{:S(2)}) collective-permute-start(bf16[2,512,128]{2,1,0:T(8,128)(2,1)S(1)} %get-tuple-element.45), channel_id=1, source_target_pairs={{0,6},{2,0},{4,2},{6,4},{1,7},{3,1},{5,3},{7,5},{8,14},{10,8},{12,... | collective-permute-start | bytes 786440 | tf_op jit(solution)/shard_map/ppermute | solution.py:529
  24.9 12.7 %all-to-all-done.1.mine = bf16[8,528,128]{2,1,0:T(8,128)(2,1)S(1)} async-done(((bf16[8,528,128]{2,1,0:T(8,128)(2,1)}), bf16[8,528,128]{2,1,0:T(8,128)(2,1)S(1)}, u32[]{:S(2)}, u32[]{:S(2)}) %all-to-all-start.1) | async-done | bytes 1081376 | tf_op jit(solution)/shard_map/all_to_all | solution.py:537
  37.6 3.2 %collective-permute-start.2 = (bf16[8,272,128]{2,1,0:T(8,128)(2,1)S(1)}, bf16[8,272,128]{2,1,0:T(8,128)(2,1)S(1)}, u32[]{:S(2)}, u32[]{:S(2)}) collective-permute-start(bf16[8,272,128]{2,1,0:T(8,128)(2,1)S(1)} %slice.8), channel_id=1, source_target_pairs={{0,64},{64,128},{128,192},{1,65},{65,129},{129,193},{2,66},{66,130... | collective-permute-start | bytes 1671176 | tf_op jit(solution)/shard_map/ppermute | solution.py:561
  40.8 10.1 %collective-permute-done.3.near1 = bf16[2,512,128]{2,1,0:T(8,128)(2,1)S(1)} collective-permute-done((bf16[2,512,128]{2,1,0:T(8,128)(2,1)S(1)}, bf16[2,512,128]{2,1,0:T(8,128)(2,1)S(1)}, u32[]{:S(2)}, u32[]{:S(2)}) %collective-permute-start.3) | collective-permute-done | bytes 262176 | tf_op jit(solution)/shard_map/ppermute | solution.py:529
  50.9 3.9 %collective-permute-done.4.near2 = bf16[2,512,128]{2,1,0:T(8,128)(2,1)S(1)} collective-permute-done((bf16[2,512,128]{2,1,0:T(8,128)(2,1)S(1)}, bf16[2,512,128]{2,1,0:T(8,128)(2,1)S(1)}, u32[]{:S(2)}, u32[]{:S(2)}) %collective-permute-start.4) | collective-permute-done | bytes 262176 | tf_op jit(solution)/shard_map/ppermute | solution.py:529
  54.8 0.0 collective-permute-done.5.near3
  54.8 2.2 %near_forward.1 = (bf16[1024,1024]{1,0:T(8,128)(2,1)S(1)}, f32[128,1024]{1,0:T(8,128)S(1)}, f32[8,4,128]{2,1,0:T(4,128)S(1)}) custom-call(bf16[2,512,128]{2,1,0:T(8,128)(2,1)S(1)} %get-tuple-element.42.near0, bf16[2,512,128]{2,1,0:T(8,128)(2,1)S(1)} %collective-permute-done.3.near1, bf16[2,512,128]{2,1,0:T(8,128)(2,1)S(1)} %collective-permute-done.4.near2, ...), custom_call_target="tpu_custom_call" | custom-call | flops 10737418240 | bytes 4000000 | tf_op jit(solution)/shard_map/near_forward/pallas_call | solution.py:214
  57.0 3.4 %far_forward.1 = (f32[8,8,128]{2,1,0:T(8,128)S(1)}, bf16[4,1152,256]{2,1,0:T(8,128)(2,1)S(1)}, f32[128,1024]{1,0:T(8,128)S(1)}) custom-call(s32[3]{0:T(128)S(1)} %pad_add_fusion.place, s32[8]{0:T(128)S(1)} %copy-done.3, bf16[8,528,128]{2,1,0:T(8,128)(2,1)S(1)} %all-to-all-done.1.mine, bf16[8,272,128]{2,1,0:T(8,128)(2,1)S(1)} %collective-permute-done.2.past, ...), custom_call_target="tpu_custom_call" | custom-call | flops 603979776 | bytes 5000000 | tf_op jit(solution)/shard_map/far_forward/pallas_call | solution.py:279
  60.4 16.4 %all_to_all.15.told = f32[8,8,128]{2,1,0:T(8,128)S(1)} all-to-all(f32[8,8,128]{2,1,0:T(8,128)S(1)} %get-tuple-element.49.sent), channel_id=1, replica_groups={{0,8,22,30,36,44,50,58},{2,10,16,24,38,46,52,60},{4,12,18,26,32,40,54,6..., dimensions={0} | all-to-all | bytes 65536 | tf_op jit(solution)/shard_map/all_to_all | solution.py:537
  76.8 3.4 %far_backward.1 = (bf16[8,512,128]{2,1,0:T(8,128)(2,1)S(1)}, bf16[8,256,128]{2,1,0:T(8,128)(2,1)S(1)}) custom-call(s32[3]{0:T(128)S(1)} %pad_add_fusion.place, bf16[8,528,128]{2,1,0:T(8,128)(2,1)S(1)} %all-to-all-done.1.mine, bf16[8,272,128]{2,1,0:T(8,128)(2,1)S(1)} %collective-permute-done.2.past, bf16[4,1152,256]{2,1,0:T(8,128)(2,1)S(1)} %get-tuple-element.47.kept, ...), custom_call_target="tpu_custom_call" | custom-call | flops 1207959552 | bytes 6000000 | tf_op jit(solution)/shard_map/far_backward/pallas_call | solution.py:409
  80.1 2.3 %collective-permute-start.9 = (bf16[8,256,128]{2,1,0:T(8,128)(2,1)S(1)}, bf16[8,256,128]{2,1,0:T(8,128)(2,1)S(1)}, u32[]{:S(2)}, u32[]{:S(2)}) collective-permute-start(bf16[8,256,128]{2,1,0:T(8,128)(2,1)S(1)} %get-tuple-element.62), channel_id=1, source_target_pairs={{64,0},{128,64},{192,128},{65,1},{129,65},{193,129},{66,2},{130,66... | collective-permute-start | bytes 1572872 | tf_op jit(solution)/shard_map/ppermute | solution.py:566
  82.5 2.9 %near_backward.1 = (bf16[2,512,128]{2,1,0:T(8,128)(2,1)S(1)}, bf16[2,512,128]{2,1,0:T(8,128)(2,1)S(1)}, bf16[2,512,128]{2,1,0:T(8,128)(2,1)S(1)}, bf16[2,512,128]{2,1,0:T(8,128)(2,1)S(1)}) custom-call(s32[3]{0:T(128)S(1)} %pad_add_fusion.place, bf16[2,512,128]{2,1,0:T(8,128)(2,1)S(1)} %get-tuple-element.42.near0, ...), custom_call_target="tpu_custom_call" | custom-call | flops 1073741824 | bytes 5000000 | tf_op jit(solution)/shard_map/near_backward/pallas_call | solution.py:347
  85.4 3.8 %collective-permute-start.6 = (bf16[2,512,128]{2,1,0:T(8,128)(2,1)S(1)}, bf16[2,512,128]{2,1,0:T(8,128)(2,1)S(1)}, u32[]{:S(2)}, u32[]{:S(2)}) collective-permute-start(bf16[2,512,128]{2,1,0:T(8,128)(2,1)S(1)} %get-tuple-element.58), channel_id=1, source_target_pairs={{0,4},{2,6},{4,0},{6,2},{1,5},{3,7},{5,1},{7,3},{8,12},{10,14},{12... | collective-permute-start | bytes 786440 | tf_op jit(solution)/shard_map/ppermute | solution.py:529
  89.2 1.4 %collective-permute-start.7 = (bf16[2,512,128]{2,1,0:T(8,128)(2,1)S(1)}, bf16[2,512,128]{2,1,0:T(8,128)(2,1)S(1)}, u32[]{:S(2)}, u32[]{:S(2)}) collective-permute-start(bf16[2,512,128]{2,1,0:T(8,128)(2,1)S(1)} %get-tuple-element.59), channel_id=1, source_target_pairs={{0,6},{2,0},{4,2},{6,4},{1,7},{3,1},{5,3},{7,5},{8,14},{10,8},{12,... | collective-permute-start | bytes 786440 | tf_op jit(solution)/shard_map/ppermute | solution.py:529
  90.6 1.5 %collective-permute-start.8 = (bf16[2,512,128]{2,1,0:T(8,128)(2,1)S(1)}, bf16[2,512,128]{2,1,0:T(8,128)(2,1)S(1)}, u32[]{:S(2)}, u32[]{:S(2)}) collective-permute-start(bf16[2,512,128]{2,1,0:T(8,128)(2,1)S(1)} %get-tuple-element.60), channel_id=1, source_target_pairs={{0,2},{2,4},{4,6},{6,0},{1,3},{3,5},{5,7},{7,1},{8,10},{10,12},{12... | collective-permute-start | bytes 786440 | tf_op jit(solution)/shard_map/ppermute | solution.py:529
  92.2 1.2 collective-permute-done.9.back
  93.3 0.4 add_back.1
  93.7 26.8 %conditional.1 = (bf16[4,2,512,128]{3,2,1,0:T(8,128)(2,1)S(1)}) conditional(s32[]{:T(128)} %bitcast.8, () %tuple.18, bf16[8,512,128]{2,1,0:T(8,128)(2,1)S(1)} %add_back.1), branch_computations={%region_0.0_spmd, %region_1.0_spmd} | conditional | bytes 2097160 | solution.py:541
  93.7 26.7 %all_to_all.14 = bf16[8,512,128]{2,1,0:T(8,128)(2,1)S(1)} all-to-all(bf16[8,512,128]{2,1,0:T(8,128)(2,1)S(1)} %param.1), channel_id=1, replica_groups=mesh['y'=4,'x'=4,'zl'=2,'zh'=4,'core'=2] {'x','zl'}, dimensions={0} | all-to-all | bytes 2097152 | tf_op jit(solution)/shard_map/cond/branch_1_fun/all_to_all | solution.py:537
  120.5 3.8 %unproject.1 = (f32[2,128,1024]{2,1,0:T(8,128)S(1)}, bf16[2,128,1024]{2,1,0:T(8,128)(2,1)S(1)}) custom-call(s32[3]{0:T(128)S(1)} %pad_add_fusion.place, bf16[2,512,128]{2,1,0:T(8,128)(2,1)S(1)} %get-tuple-element.57.near0, bf16[2,512,128]{2,1,0:T(8,128)(2,1)S(1)} %collective-permute-done.6.near1, bf16[2,512,128]{2,1,0:T(8,128)(2,1)S(1)} %collective-permute-done.7.near2, ...), custom_call_target="tpu_custom_call" | custom-call | flops 1073741824 | bytes 8000000 | tf_op jit(solution)/shard_map/unproject/pallas_call | solution.py:482
  124.3 0.1 collective-permute-start.10
  124.4 1.9 %collective-permute-done.10.other = bf16[2,128,1024]{2,1,0:T(8,128)(2,1)S(1)} collective-permute-done((bf16[2,128,1024]{2,1,0:T(8,128)(2,1)S(1)}, bf16[2,128,1024]{2,1,0:T(8,128)(2,1)S(1)}, u32[]{:S(2)}, u32[]{:S(2)}) %collective-permute-start.10) | collective-permute-done | bytes 524320 | tf_op jit(solution)/shard_map/ppermute | solution.py:525
  126.3 1.0 finish.1
  (14 shorter events, 0.1 us)
Async XLA Ops:
  0.6 4.2 %collective-permute-start = (bf16[128,1024]{1,0:T(8,128)(2,1)}, bf16[128,1024]{1,0:T(8,128)(2,1)S(1)}, u32[]{:S(2)}, u32[]{:S(2)}) collective-permute-start(bf16[128,1024]{1,0:T(8,128)(2,1)} %bitcast.12), channel_id=1, source_target_pairs={{0,1},{1,0},{2,3},{3,2},{4,5},{5,4},{6,7},{7,6},{8,9},{9,8},{10,11... | collective-permute-start | bytes 786440 | tf_op jit(solution)/shard_map/ppermute | solution.py:525
  0.7 4.1 %collective-permute-start.1 = (bf16[128,1024]{1,0:T(8,128)(2,1)}, bf16[128,1024]{1,0:T(8,128)(2,1)S(1)}, u32[]{:S(2)}, u32[]{:S(2)}) collective-permute-start(bf16[128,1024]{1,0:T(8,128)(2,1)} %bitcast.15), channel_id=1, source_target_pairs={{0,1},{1,0},{2,3},{3,2},{4,5},{5,4},{6,7},{7,6},{8,9},{9,8},{10,11... | collective-permute-start | bytes 786440 | tf_op jit(solution)/shard_map/ppermute | solution.py:525
  2.0 2.9 %copy-start = (bf16[1,1,128,1024]{3,2,1,0:T(8,128)(2,1)S(1)}, bf16[1,1,128,1024]{3,2,1,0:T(8,128)(2,1)}, u32[]{:S(2)}) copy-start(bf16[1,1,128,1024]{3,2,1,0:T(8,128)(2,1)} %param.9) | copy-start | bytes 786436
  2.0 2.9 %copy-start.1 = (bf16[1,1,128,1024]{3,2,1,0:T(8,128)(2,1)S(1)}, bf16[1,1,128,1024]{3,2,1,0:T(8,128)(2,1)}, u32[]{:S(2)}) copy-start(bf16[1,1,128,1024]{3,2,1,0:T(8,128)(2,1)} %param.15) | copy-start | bytes 786436
  2.0 2.9 %copy-start.2 = (f32[1024]{0:T(1024)S(1)}, f32[1024]{0:T(1024)}, u32[]{:S(2)}) copy-start(f32[1024]{0:T(1024)} %param.10) | copy-start | bytes 12292
  8.8 28.8 %all-to-all-start.1 = ((bf16[8,528,128]{2,1,0:T(8,128)(2,1)}), bf16[8,528,128]{2,1,0:T(8,128)(2,1)S(1)}, u32[]{:S(2)}, u32[]{:S(2)}) async-start(bf16[8,528,128]{2,1,0:T(8,128)(2,1)} %bitcast.7), calls=%async_computation.1 | async-start | bytes 2162688 | tf_op jit(solution)/shard_map/all_to_all | solution.py:537
  14.4 36.5 %collective-permute-start.3 = (bf16[2,512,128]{2,1,0:T(8,128)(2,1)S(1)}, bf16[2,512,128]{2,1,0:T(8,128)(2,1)S(1)}, u32[]{:S(2)}, u32[]{:S(2)}) collective-permute-start(bf16[2,512,128]{2,1,0:T(8,128)(2,1)S(1)} %get-tuple-element.43), channel_id=1, source_target_pairs={{0,4},{2,6},{4,0},{6,2},{1,5},{3,7},{5,1},{7,3},{8,12},{10,14},{12... | collective-permute-start | bytes 786440 | tf_op jit(solution)/shard_map/ppermute | solution.py:529
  20.7 34.1 %collective-permute-start.4 = (bf16[2,512,128]{2,1,0:T(8,128)(2,1)S(1)}, bf16[2,512,128]{2,1,0:T(8,128)(2,1)S(1)}, u32[]{:S(2)}, u32[]{:S(2)}) collective-permute-start(bf16[2,512,128]{2,1,0:T(8,128)(2,1)S(1)} %get-tuple-element.44), channel_id=1, source_target_pairs={{0,2},{2,4},{4,6},{6,0},{1,3},{3,5},{5,7},{7,1},{8,10},{10,12},{12... | collective-permute-start | bytes 786440 | tf_op jit(solution)/shard_map/ppermute | solution.py:529
  22.2 32.6 %collective-permute-start.5 = (bf16[2,512,128]{2,1,0:T(8,128)(2,1)S(1)}, bf16[2,512,128]{2,1,0:T(8,128)(2,1)S(1)}, u32[]{:S(2)}, u32[]{:S(2)}) collective-permute-start(bf16[2,512,128]{2,1,0:T(8,128)(2,1)S(1)} %get-tuple-element.45), channel_id=1, source_target_pairs={{0,6},{2,0},{4,2},{6,4},{1,7},{3,1},{5,3},{7,5},{8,14},{10,8},{12,... | collective-permute-start | bytes 786440 | tf_op jit(solution)/shard_map/ppermute | solution.py:529
  37.6 19.4 %collective-permute-start.2 = (bf16[8,272,128]{2,1,0:T(8,128)(2,1)S(1)}, bf16[8,272,128]{2,1,0:T(8,128)(2,1)S(1)}, u32[]{:S(2)}, u32[]{:S(2)}) collective-permute-start(bf16[8,272,128]{2,1,0:T(8,128)(2,1)S(1)} %slice.8), channel_id=1, source_target_pairs={{0,64},{64,128},{128,192},{1,65},{65,129},{129,193},{2,66},{66,130... | collective-permute-start | bytes 1671176 | tf_op jit(solution)/shard_map/ppermute | solution.py:561
  54.8 2.2 %copy-start.3 = (s32[8]{0:T(128)S(1)}, s32[8]{0:T(128)}, u32[]{:S(2)}) copy-start(s32[8]{0:T(128)} %win.1) | copy-start | bytes 100
  80.1 13.2 %collective-permute-start.9 = (bf16[8,256,128]{2,1,0:T(8,128)(2,1)S(1)}, bf16[8,256,128]{2,1,0:T(8,128)(2,1)S(1)}, u32[]{:S(2)}, u32[]{:S(2)}) collective-permute-start(bf16[8,256,128]{2,1,0:T(8,128)(2,1)S(1)} %get-tuple-element.62), channel_id=1, source_target_pairs={{64,0},{128,64},{192,128},{65,1},{129,65},{193,129},{66,2},{130,66... | collective-permute-start | bytes 1572872 | tf_op jit(solution)/shard_map/ppermute | solution.py:566
  85.4 35.1 %collective-permute-start.6 = (bf16[2,512,128]{2,1,0:T(8,128)(2,1)S(1)}, bf16[2,512,128]{2,1,0:T(8,128)(2,1)S(1)}, u32[]{:S(2)}, u32[]{:S(2)}) collective-permute-start(bf16[2,512,128]{2,1,0:T(8,128)(2,1)S(1)} %get-tuple-element.58), channel_id=1, source_target_pairs={{0,4},{2,6},{4,0},{6,2},{1,5},{3,7},{5,1},{7,3},{8,12},{10,14},{12... | collective-permute-start | bytes 786440 | tf_op jit(solution)/shard_map/ppermute | solution.py:529
  89.2 31.3 %collective-permute-start.7 = (bf16[2,512,128]{2,1,0:T(8,128)(2,1)S(1)}, bf16[2,512,128]{2,1,0:T(8,128)(2,1)S(1)}, u32[]{:S(2)}, u32[]{:S(2)}) collective-permute-start(bf16[2,512,128]{2,1,0:T(8,128)(2,1)S(1)} %get-tuple-element.59), channel_id=1, source_target_pairs={{0,6},{2,0},{4,2},{6,4},{1,7},{3,1},{5,3},{7,5},{8,14},{10,8},{12,... | collective-permute-start | bytes 786440 | tf_op jit(solution)/shard_map/ppermute | solution.py:529
  90.6 29.9 %collective-permute-start.8 = (bf16[2,512,128]{2,1,0:T(8,128)(2,1)S(1)}, bf16[2,512,128]{2,1,0:T(8,128)(2,1)S(1)}, u32[]{:S(2)}, u32[]{:S(2)}) collective-permute-start(bf16[2,512,128]{2,1,0:T(8,128)(2,1)S(1)} %get-tuple-element.60), channel_id=1, source_target_pairs={{0,2},{2,4},{4,6},{6,0},{1,3},{3,5},{5,7},{7,1},{8,10},{10,12},{12... | collective-permute-start | bytes 786440 | tf_op jit(solution)/shard_map/ppermute | solution.py:529
  124.3 2.0 %collective-permute-start.10 = (bf16[2,128,1024]{2,1,0:T(8,128)(2,1)S(1)}, bf16[2,128,1024]{2,1,0:T(8,128)(2,1)S(1)}, u32[]{:S(2)}, u32[]{:S(2)}) collective-permute-start(bf16[2,128,1024]{2,1,0:T(8,128)(2,1)S(1)} %get-tuple-element.64), channel_id=1, source_target_pairs={{0,1},{1,0},{2,3},{3,2},{4,5},{5,4},{6,7},{7,6},{8,9},{9,8},{10,11... | collective-permute-start | bytes 1572872 | tf_op jit(solution)/shard_map/ppermute | solution.py:525

commit v11 on v10

--- a/solution.py
+++ b/solution.py
@@ -122,54 +122,39 @@
 
 
 def project_kernel(
-    place, valid, own, other, cot_own, cot_other, gain, wq, wk, wv, wo,
-    packed, near0, near1, near2, near3, made, out_sems,
+    place, valid, own, other, cot_own, cot_other, gain, wq, wk, wv, wo, packed, near0, near1, near2, near3
 ):
-    flags = jnp.full((ROWS - OK0, DH), valid[0], jnp.int32).astype(F32).astype(BF16)
-    for h in range(HALF):
-        for s in range(2):
-            made[h, s, OK0:ROWS, :] = flags
     x = jnp.concatenate([own[...], other[...]], axis=0).astype(F32)
     rinv = lax.rsqrt(jnp.mean(x * x, axis=-1, keepdims=True) + EPS)
     normed = (x * rinv * gain[...]).astype(BF16)
-    leaving = []
-    for n, (row, weight) in enumerate(((Q0, wq), (K0, wk), (V0, wv), (G0, wo))):
+    cot = jnp.concatenate([cot_own[...], cot_other[...]], axis=0)
+    flags = jnp.full((ROWS - OK0, DH), valid[0], jnp.int32).astype(F32).astype(BF16)
+    for row in (Q0, K0, V0, G0):
         if row == G0:
-            cots = jnp.concatenate([cot_own[...], cot_other[...]], axis=0)
-            got = mm_nt(cots, weight[...]).astype(BF16)
+            got = mm_nt(cot, wo[...]).astype(BF16)
         else:
-            got = mm(normed, weight[...]).astype(BF16)
+            got = mm(normed, {Q0: wq, K0: wk, V0: wv}[row][...]).astype(BF16)
         for h in range(HALF):
             for s in range(2):
-                made[slot_of_head(place, h), s, row : row + HW, :] = (
+                packed[slot_of_head(place, h), s, row : row + HW, :] = (
                     got[s * HW : (s + 1) * HW, h * DH : (h + 1) * DH]
                 )
-        end = ROWS if row == V0 else row + HW
-        span = pl.ds(row, end - row)
-        moves = [(made.at[:, :, span, :], packed.at[:, :, span, :])]
-        for step, near in zip(STEPS, (near0, near1, near2, near3)):
-            slot = lax.rem(place[1] + step, HALF)
-            rows = pl.ds(row, HW)
-            moves.append((made.at[slot, :, rows, :], near.at[:, rows, :]))
-        for m, (source, target) in enumerate(moves):
-            copy = pltpu.make_async_copy(source, target, out_sems.at[5 * n + m])
-            copy.start()
-            leaving.append(copy)
-    for copy in leaving:
-        copy.wait()
+    for h in range(HALF):
+        for s in range(2):
+            packed[h, s, OK0:ROWS, :] = flags
+    for step, near in zip(STEPS, (near0, near1, near2, near3)):
+        slot = lax.rem(place[1] + step, HALF)
+        for s in range(2):
+            near[s] = packed[slot, s, :OK0, :]
 
 
 def project(place, valid, own, other, cot_own, cot_other, gain, weights):
     return pl.pallas_call(
         project_kernel,
         in_specs=[SM, SM] + [VM] * 9,
-        out_specs=[ANY] * 5,
+        out_specs=[VM] * 5,
         out_shape=[jax.ShapeDtypeStruct((HALF, 2, ROWS, DH), BF16)]
         + [jax.ShapeDtypeStruct((2, OK0, DH), BF16)] * 4,
-        scratch_shapes=[
-            pltpu.VMEM((HALF, 2, ROWS, DH), BF16),
-            pltpu.SemaphoreType.DMA((20,)),
-        ],
         compiler_params=params(),
         cost_estimate=cost(2 * PAIR * D * 4 * HALF * DH, 7_000_000),
         name="project",

time: 129 us -> 128 us (level)
  no operation moved by 1% of the time
where the time goes in v11:
time: 128 us; the launch traced here: 127 us
  blocking collectives  43 us (34%)
  waiting for transfers between devices  29.9 us (23%)
  starting transfers between devices  29 us (23%)
  Pallas kernels  23.1 us (18%)
  between operations  1.47 us (1%)
    all_to_all x2, blocking collectives, exchange(): lax.all_to_all(value, axes, 0, 0, axis_index_groups=groups, tiled=True)  43 us
    ppermute x6, starting transfers between devices, turn_ring(): return lax.ppermute(value, 'zh', [(i, (i + steps) % 4) for i in range(4)])  17.1 us
    ppermute x6, waiting for transfers between devices, turn_ring(): return lax.ppermute(value, 'zh', [(i, (i + steps) % 4) for i in range(4)])  14 us
    all_to_all x1, waiting for transfers between devices, exchange(): lax.all_to_all(value, axes, 0, 0, axis_index_groups=groups, tiled=True)  12.8 us
    all_to_all x1, starting transfers between devices, exchange(): lax.all_to_all(value, axes, 0, 0, axis_index_groups=groups, tiled=True)  5.7 us
    pallas_call x1, Pallas kernels, unproject(): pl.pallas_call(unproject_kernel, in_specs=[SM] + [VM] * 5 + [ANY] * 2, ou...  3.8 us
    pallas_call x1, Pallas kernels, far_backward(): pl.pallas_call(far_backward_kernel, in_specs=[SM] + [VM] * 6, out_specs=[...  3.37 us
    pallas_call x1, Pallas kernels, far_forward(): pl.pallas_call(far_forward_kernel, in_specs=[SM, SM, VM, VM, VM], out_spe...  3.36 us
  transfers between devices with their start and end apart: 12, of which 5 were waited for; matrix products, arithmetic and copies ran while one was open for 0% of the time, Pallas kernels for 7%

profile of v11, /device:TPU:16, one launch (start us, length us, event | category | flops | bytes accessed | tf_op | source)
XLA Modules:
  0.0 126.7 jit_solution(1873467425101155559)
XLA Ops:
  0.6 0.1 collective-permute-start
  0.7 0.5 collective-permute-start.1
  1.9 0.1 pad_add_fusion.place
  2.0 2.8 %stage.1 = (bf16[1024,512]{1,0:T(8,128)(2,1)S(1)}, bf16[1024,512]{1,0:T(8,128)(2,1)S(1)}, bf16[1024,512]{1,0:T(8,128)(2,1)S(1)}, bf16[512,1024]{1,0:T(8,128)(2,1)S(1)}) custom-call(s32[3]{0:T(128)S(1)} %pad_add_fusion.place, bf16[1024,3072]{1,0:T(8,128)(2,1)} %w_qkv.3, bf16[1024,1024]{1,0:T(8,128)(2,1)} %w_out.3), custom_call_target="tpu_custom_call" | custom-call | bytes 9000000 | tf_op jit(solution)/shard_map/stage/pallas_call | solution.py:100
  4.8 0.0 collective-permute-done.other
  4.8 0.0 collective-permute-done.1.cot_other
  4.9 3.2 %project.1 = (bf16[4,2,528,128]{3,2,1,0:T(8,128)(2,1)}, bf16[2,512,128]{2,1,0:T(8,128)(2,1)S(1)}, bf16[2,512,128]{2,1,0:T(8,128)(2,1)S(1)}, bf16[2,512,128]{2,1,0:T(8,128)(2,1)S(1)}, bf16[2,512,128]{2,1,0:T(8,128)(2,1)S(1)}) custom-call(s32[3]{0:T(128)S(1)} %pad_add_fusion.place, s32[1]{0:T(128)S(6)} %copy.13.valid, bf16[128,1024]{1,0:T(8,128)(2,1)S(1)} %bitcast.13, ...), custom_call_target="tpu_custom_call" | custom-call | flops 1073741824 | bytes 7000000 | tf_op jit(solution)/shard_map/project/pallas_call | solution.py:152
  8.1 5.7 %all-to-all-start.1 = ((bf16[8,528,128]{2,1,0:T(8,128)(2,1)}), bf16[8,528,128]{2,1,0:T(8,128)(2,1)S(1)}, u32[]{:S(2)}, u32[]{:S(2)}) async-start(bf16[8,528,128]{2,1,0:T(8,128)(2,1)} %bitcast.7), calls=%async_computation.1 | async-start | bytes 2162688 | tf_op jit(solution)/shard_map/all_to_all | solution.py:522
  13.8 6.2 %collective-permute-start.3 = (bf16[2,512,128]{2,1,0:T(8,128)(2,1)S(1)}, bf16[2,512,128]{2,1,0:T(8,128)(2,1)S(1)}, u32[]{:S(2)}, u32[]{:S(2)}) collective-permute-start(bf16[2,512,128]{2,1,0:T(8,128)(2,1)S(1)} %get-tuple-element.43), channel_id=1, source_target_pairs={{0,4},{2,6},{4,0},{6,2},{1,5},{3,7},{5,1},{7,3},{8,12},{10,14},{12... | collective-permute-start | bytes 786440 | tf_op jit(solution)/shard_map/ppermute | solution.py:514
  20.0 1.5 %collective-permute-start.4 = (bf16[2,512,128]{2,1,0:T(8,128)(2,1)S(1)}, bf16[2,512,128]{2,1,0:T(8,128)(2,1)S(1)}, u32[]{:S(2)}, u32[]{:S(2)}) collective-permute-start(bf16[2,512,128]{2,1,0:T(8,128)(2,1)S(1)} %get-tuple-element.44), channel_id=1, source_target_pairs={{0,2},{2,4},{4,6},{6,0},{1,3},{3,5},{5,7},{7,1},{8,10},{10,12},{12... | collective-permute-start | bytes 786440 | tf_op jit(solution)/shard_map/ppermute | solution.py:514
  21.6 2.6 %collective-permute-start.5 = (bf16[2,512,128]{2,1,0:T(8,128)(2,1)S(1)}, bf16[2,512,128]{2,1,0:T(8,128)(2,1)S(1)}, u32[]{:S(2)}, u32[]{:S(2)}) collective-permute-start(bf16[2,512,128]{2,1,0:T(8,128)(2,1)S(1)} %get-tuple-element.45), channel_id=1, source_target_pairs={{0,6},{2,0},{4,2},{6,4},{1,7},{3,1},{5,3},{7,5},{8,14},{10,8},{12,... | collective-permute-start | bytes 786440 | tf_op jit(solution)/shard_map/ppermute | solution.py:514
  24.1 12.8 %all-to-all-done.1.mine = bf16[8,528,128]{2,1,0:T(8,128)(2,1)S(1)} async-done(((bf16[8,528,128]{2,1,0:T(8,128)(2,1)}), bf16[8,528,128]{2,1,0:T(8,128)(2,1)S(1)}, u32[]{:S(2)}, u32[]{:S(2)}) %all-to-all-start.1) | async-done | bytes 1081376 | tf_op jit(solution)/shard_map/all_to_all | solution.py:522
  37.0 3.2 %collective-permute-start.2 = (bf16[8,272,128]{2,1,0:T(8,128)(2,1)S(1)}, bf16[8,272,128]{2,1,0:T(8,128)(2,1)S(1)}, u32[]{:S(2)}, u32[]{:S(2)}) collective-permute-start(bf16[8,272,128]{2,1,0:T(8,128)(2,1)S(1)} %slice.8), channel_id=1, source_target_pairs={{0,64},{64,128},{128,192},{1,65},{65,129},{129,193},{2,66},{66,130... | collective-permute-start | bytes 1671176 | tf_op jit(solution)/shard_map/ppermute | solution.py:546
  40.1 9.9 %collective-permute-done.3.near1 = bf16[2,512,128]{2,1,0:T(8,128)(2,1)S(1)} collective-permute-done((bf16[2,512,128]{2,1,0:T(8,128)(2,1)S(1)}, bf16[2,512,128]{2,1,0:T(8,128)(2,1)S(1)}, u32[]{:S(2)}, u32[]{:S(2)}) %collective-permute-start.3) | collective-permute-done | bytes 262176 | tf_op jit(solution)/shard_map/ppermute | solution.py:514
  50.1 4.1 %collective-permute-done.4.near2 = bf16[2,512,128]{2,1,0:T(8,128)(2,1)S(1)} collective-permute-done((bf16[2,512,128]{2,1,0:T(8,128)(2,1)S(1)}, bf16[2,512,128]{2,1,0:T(8,128)(2,1)S(1)}, u32[]{:S(2)}, u32[]{:S(2)}) %collective-permute-start.4) | collective-permute-done | bytes 262176 | tf_op jit(solution)/shard_map/ppermute | solution.py:514
  54.2 2.2 %near_forward.1 = (bf16[1024,1024]{1,0:T(8,128)(2,1)S(1)}, f32[128,1024]{1,0:T(8,128)S(1)}, f32[8,4,128]{2,1,0:T(4,128)S(1)}) custom-call(bf16[2,512,128]{2,1,0:T(8,128)(2,1)S(1)} %get-tuple-element.42.near0, bf16[2,512,128]{2,1,0:T(8,128)(2,1)S(1)} %collective-permute-done.3.near1, bf16[2,512,128]{2,1,0:T(8,128)(2,1)S(1)} %collective-permute-done.4.near2, ...), custom_call_target="tpu_custom_call" | custom-call | flops 10737418240 | bytes 4000000 | tf_op jit(solution)/shard_map/near_forward/pallas_call | solution.py:199
  56.4 3.4 %far_forward.1 = (f32[8,8,128]{2,1,0:T(8,128)S(1)}, bf16[4,1152,256]{2,1,0:T(8,128)(2,1)S(1)}, f32[128,1024]{1,0:T(8,128)S(1)}) custom-call(s32[3]{0:T(128)S(1)} %pad_add_fusion.place, s32[8]{0:T(128)S(1)} %copy-done.3, bf16[8,528,128]{2,1,0:T(8,128)(2,1)S(1)} %all-to-all-done.1.mine, bf16[8,272,128]{2,1,0:T(8,128)(2,1)S(1)} %collective-permute-done.2.past, ...), custom_call_target="tpu_custom_call" | custom-call | flops 603979776 | bytes 5000000 | tf_op jit(solution)/shard_map/far_forward/pallas_call | solution.py:264
  59.7 16.3 %all_to_all.15.told = f32[8,8,128]{2,1,0:T(8,128)S(1)} all-to-all(f32[8,8,128]{2,1,0:T(8,128)S(1)} %get-tuple-element.49.sent), channel_id=1, replica_groups={{0,8,22,30,36,44,50,58},{2,10,16,24,38,46,52,60},{4,12,18,26,32,40,54,6..., dimensions={0} | all-to-all | bytes 65536 | tf_op jit(solution)/shard_map/all_to_all | solution.py:522
  76.1 3.4 %far_backward.1 = (bf16[8,512,128]{2,1,0:T(8,128)(2,1)S(1)}, bf16[8,256,128]{2,1,0:T(8,128)(2,1)S(1)}) custom-call(s32[3]{0:T(128)S(1)} %pad_add_fusion.place, bf16[8,528,128]{2,1,0:T(8,128)(2,1)S(1)} %all-to-all-done.1.mine, bf16[8,272,128]{2,1,0:T(8,128)(2,1)S(1)} %collective-permute-done.2.past, bf16[4,1152,256]{2,1,0:T(8,128)(2,1)S(1)} %get-tuple-element.47.kept, ...), custom_call_target="tpu_custom_call" | custom-call | flops 1207959552 | bytes 6000000 | tf_op jit(solution)/shard_map/far_backward/pallas_call | solution.py:394
  79.4 2.4 %collective-permute-start.9 = (bf16[8,256,128]{2,1,0:T(8,128)(2,1)S(1)}, bf16[8,256,128]{2,1,0:T(8,128)(2,1)S(1)}, u32[]{:S(2)}, u32[]{:S(2)}) collective-permute-start(bf16[8,256,128]{2,1,0:T(8,128)(2,1)S(1)} %get-tuple-element.62), channel_id=1, source_target_pairs={{64,0},{128,64},{192,128},{65,1},{129,65},{193,129},{66,2},{130,66... | collective-permute-start | bytes 1572872 | tf_op jit(solution)/shard_map/ppermute | solution.py:551
  81.8 2.9 %near_backward.1 = (bf16[2,512,128]{2,1,0:T(8,128)(2,1)S(1)}, bf16[2,512,128]{2,1,0:T(8,128)(2,1)S(1)}, bf16[2,512,128]{2,1,0:T(8,128)(2,1)S(1)}, bf16[2,512,128]{2,1,0:T(8,128)(2,1)S(1)}) custom-call(s32[3]{0:T(128)S(1)} %pad_add_fusion.place, bf16[2,512,128]{2,1,0:T(8,128)(2,1)S(1)} %get-tuple-element.42.near0, ...), custom_call_target="tpu_custom_call" | custom-call | flops 1073741824 | bytes 5000000 | tf_op jit(solution)/shard_map/near_backward/pallas_call | solution.py:332
  84.8 3.8 %collective-permute-start.6 = (bf16[2,512,128]{2,1,0:T(8,128)(2,1)S(1)}, bf16[2,512,128]{2,1,0:T(8,128)(2,1)S(1)}, u32[]{:S(2)}, u32[]{:S(2)}) collective-permute-start(bf16[2,512,128]{2,1,0:T(8,128)(2,1)S(1)} %get-tuple-element.58), channel_id=1, source_target_pairs={{0,4},{2,6},{4,0},{6,2},{1,5},{3,7},{5,1},{7,3},{8,12},{10,14},{12... | collective-permute-start | bytes 786440 | tf_op jit(solution)/shard_map/ppermute | solution.py:514
  88.5 1.5 %collective-permute-start.7 = (bf16[2,512,128]{2,1,0:T(8,128)(2,1)S(1)}, bf16[2,512,128]{2,1,0:T(8,128)(2,1)S(1)}, u32[]{:S(2)}, u32[]{:S(2)}) collective-permute-start(bf16[2,512,128]{2,1,0:T(8,128)(2,1)S(1)} %get-tuple-element.59), channel_id=1, source_target_pairs={{0,6},{2,0},{4,2},{6,4},{1,7},{3,1},{5,3},{7,5},{8,14},{10,8},{12,... | collective-permute-start | bytes 786440 | tf_op jit(solution)/shard_map/ppermute | solution.py:514
  90.0 1.5 %collective-permute-start.8 = (bf16[2,512,128]{2,1,0:T(8,128)(2,1)S(1)}, bf16[2,512,128]{2,1,0:T(8,128)(2,1)S(1)}, u32[]{:S(2)}, u32[]{:S(2)}) collective-permute-start(bf16[2,512,128]{2,1,0:T(8,128)(2,1)S(1)} %get-tuple-element.60), channel_id=1, source_target_pairs={{0,2},{2,4},{4,6},{6,0},{1,3},{3,5},{5,7},{7,1},{8,10},{10,12},{12... | collective-permute-start | bytes 786440 | tf_op jit(solution)/shard_map/ppermute | solution.py:514
  91.5 1.2 collective-permute-done.9.back
  92.7 0.4 add_back.1
  93.1 26.7 %conditional.1 = (bf16[4,2,512,128]{3,2,1,0:T(8,128)(2,1)S(1)}) conditional(s32[]{:T(128)} %bitcast.8, () %tuple.18, bf16[8,512,128]{2,1,0:T(8,128)(2,1)S(1)} %add_back.1), branch_computations={%region_0.0_spmd, %region_1.0_spmd} | conditional | bytes 2097160 | solution.py:526
  93.1 26.7 %all_to_all.14 = bf16[8,512,128]{2,1,0:T(8,128)(2,1)S(1)} all-to-all(bf16[8,512,128]{2,1,0:T(8,128)(2,1)S(1)} %param.1), channel_id=1, replica_groups=mesh['y'=4,'x'=4,'zl'=2,'zh'=4,'core'=2] {'x','zl'}, dimensions={0} | all-to-all | bytes 2097152 | tf_op jit(solution)/shard_map/cond/branch_1_fun/all_to_all | solution.py:522
  119.8 3.8 %unproject.1 = (f32[2,128,1024]{2,1,0:T(8,128)S(1)}, bf16[2,128,1024]{2,1,0:T(8,128)(2,1)S(1)}) custom-call(s32[3]{0:T(128)S(1)} %pad_add_fusion.place, bf16[2,512,128]{2,1,0:T(8,128)(2,1)S(1)} %get-tuple-element.57.near0, bf16[2,512,128]{2,1,0:T(8,128)(2,1)S(1)} %collective-permute-done.6.near1, bf16[2,512,128]{2,1,0:T(8,128)(2,1)S(1)} %collective-permute-done.7.near2, ...), custom_call_target="tpu_custom_call" | custom-call | flops 1073741824 | bytes 8000000 | tf_op jit(solution)/shard_map/unproject/pallas_call | solution.py:467
  123.6 0.1 collective-permute-start.10
  123.7 1.9 %collective-permute-done.10.other = bf16[2,128,1024]{2,1,0:T(8,128)(2,1)S(1)} collective-permute-done((bf16[2,128,1024]{2,1,0:T(8,128)(2,1)S(1)}, bf16[2,128,1024]{2,1,0:T(8,128)(2,1)S(1)}, u32[]{:S(2)}, u32[]{:S(2)}) %collective-permute-start.10) | collective-permute-done | bytes 524320 | tf_op jit(solution)/shard_map/ppermute | solution.py:510
  125.6 1.0 finish.1
  (14 shorter events, 0.1 us)
Async XLA Ops:
  0.6 4.2 %collective-permute-start = (bf16[128,1024]{1,0:T(8,128)(2,1)}, bf16[128,1024]{1,0:T(8,128)(2,1)S(1)}, u32[]{:S(2)}, u32[]{:S(2)}) collective-permute-start(bf16[128,1024]{1,0:T(8,128)(2,1)} %bitcast.12), channel_id=1, source_target_pairs={{0,1},{1,0},{2,3},{3,2},{4,5},{5,4},{6,7},{7,6},{8,9},{9,8},{10,11... | collective-permute-start | bytes 786440 | tf_op jit(solution)/shard_map/ppermute | solution.py:510
  0.7 4.1 %collective-permute-start.1 = (bf16[128,1024]{1,0:T(8,128)(2,1)}, bf16[128,1024]{1,0:T(8,128)(2,1)S(1)}, u32[]{:S(2)}, u32[]{:S(2)}) collective-permute-start(bf16[128,1024]{1,0:T(8,128)(2,1)} %bitcast.15), channel_id=1, source_target_pairs={{0,1},{1,0},{2,3},{3,2},{4,5},{5,4},{6,7},{7,6},{8,9},{9,8},{10,11... | collective-permute-start | bytes 786440 | tf_op jit(solution)/shard_map/ppermute | solution.py:510
  2.0 2.9 %copy-start = (bf16[1,1,128,1024]{3,2,1,0:T(8,128)(2,1)S(1)}, bf16[1,1,128,1024]{3,2,1,0:T(8,128)(2,1)}, u32[]{:S(2)}) copy-start(bf16[1,1,128,1024]{3,2,1,0:T(8,128)(2,1)} %param.9) | copy-start | bytes 786436
  2.0 2.9 %copy-start.1 = (bf16[1,1,128,1024]{3,2,1,0:T(8,128)(2,1)S(1)}, bf16[1,1,128,1024]{3,2,1,0:T(8,128)(2,1)}, u32[]{:S(2)}) copy-start(bf16[1,1,128,1024]{3,2,1,0:T(8,128)(2,1)} %param.15) | copy-start | bytes 786436
  2.0 2.9 %copy-start.2 = (f32[1024]{0:T(1024)S(1)}, f32[1024]{0:T(1024)}, u32[]{:S(2)}) copy-start(f32[1024]{0:T(1024)} %param.10) | copy-start | bytes 12292
  8.1 28.8 %all-to-all-start.1 = ((bf16[8,528,128]{2,1,0:T(8,128)(2,1)}), bf16[8,528,128]{2,1,0:T(8,128)(2,1)S(1)}, u32[]{:S(2)}, u32[]{:S(2)}) async-start(bf16[8,528,128]{2,1,0:T(8,128)(2,1)} %bitcast.7), calls=%async_computation.1 | async-start | bytes 2162688 | tf_op jit(solution)/shard_map/all_to_all | solution.py:522
  13.8 36.3 %collective-permute-start.3 = (bf16[2,512,128]{2,1,0:T(8,128)(2,1)S(1)}, bf16[2,512,128]{2,1,0:T(8,128)(2,1)S(1)}, u32[]{:S(2)}, u32[]{:S(2)}) collective-permute-start(bf16[2,512,128]{2,1,0:T(8,128)(2,1)S(1)} %get-tuple-element.43), channel_id=1, source_target_pairs={{0,4},{2,6},{4,0},{6,2},{1,5},{3,7},{5,1},{7,3},{8,12},{10,14},{12... | collective-permute-start | bytes 786440 | tf_op jit(solution)/shard_map/ppermute | solution.py:514
  20.0 34.1 %collective-permute-start.4 = (bf16[2,512,128]{2,1,0:T(8,128)(2,1)S(1)}, bf16[2,512,128]{2,1,0:T(8,128)(2,1)S(1)}, u32[]{:S(2)}, u32[]{:S(2)}) collective-permute-start(bf16[2,512,128]{2,1,0:T(8,128)(2,1)S(1)} %get-tuple-element.44), channel_id=1, source_target_pairs={{0,2},{2,4},{4,6},{6,0},{1,3},{3,5},{5,7},{7,1},{8,10},{10,12},{12... | collective-permute-start | bytes 786440 | tf_op jit(solution)/shard_map/ppermute | solution.py:514
  21.6 32.6 %collective-permute-start.5 = (bf16[2,512,128]{2,1,0:T(8,128)(2,1)S(1)}, bf16[2,512,128]{2,1,0:T(8,128)(2,1)S(1)}, u32[]{:S(2)}, u32[]{:S(2)}) collective-permute-start(bf16[2,512,128]{2,1,0:T(8,128)(2,1)S(1)} %get-tuple-element.45), channel_id=1, source_target_pairs={{0,6},{2,0},{4,2},{6,4},{1,7},{3,1},{5,3},{7,5},{8,14},{10,8},{12,... | collective-permute-start | bytes 786440 | tf_op jit(solution)/shard_map/ppermute | solution.py:514
  37.0 19.4 %collective-permute-start.2 = (bf16[8,272,128]{2,1,0:T(8,128)(2,1)S(1)}, bf16[8,272,128]{2,1,0:T(8,128)(2,1)S(1)}, u32[]{:S(2)}, u32[]{:S(2)}) collective-permute-start(bf16[8,272,128]{2,1,0:T(8,128)(2,1)S(1)} %slice.8), channel_id=1, source_target_pairs={{0,64},{64,128},{128,192},{1,65},{65,129},{129,193},{2,66},{66,130... | collective-permute-start | bytes 1671176 | tf_op jit(solution)/shard_map/ppermute | solution.py:546
  54.2 2.2 %copy-start.3 = (s32[8]{0:T(128)S(1)}, s32[8]{0:T(128)}, u32[]{:S(2)}) copy-start(s32[8]{0:T(128)} %win.1) | copy-start | bytes 100
  79.4 13.2 %collective-permute-start.9 = (bf16[8,256,128]{2,1,0:T(8,128)(2,1)S(1)}, bf16[8,256,128]{2,1,0:T(8,128)(2,1)S(1)}, u32[]{:S(2)}, u32[]{:S(2)}) collective-permute-start(bf16[8,256,128]{2,1,0:T(8,128)(2,1)S(1)} %get-tuple-element.62), channel_id=1, source_target_pairs={{64,0},{128,64},{192,128},{65,1},{129,65},{193,129},{66,2},{130,66... | collective-permute-start | bytes 1572872 | tf_op jit(solution)/shard_map/ppermute | solution.py:551
  84.8 35.1 %collective-permute-start.6 = (bf16[2,512,128]{2,1,0:T(8,128)(2,1)S(1)}, bf16[2,512,128]{2,1,0:T(8,128)(2,1)S(1)}, u32[]{:S(2)}, u32[]{:S(2)}) collective-permute-start(bf16[2,512,128]{2,1,0:T(8,128)(2,1)S(1)} %get-tuple-element.58), channel_id=1, source_target_pairs={{0,4},{2,6},{4,0},{6,2},{1,5},{3,7},{5,1},{7,3},{8,12},{10,14},{12... | collective-permute-start | bytes 786440 | tf_op jit(solution)/shard_map/ppermute | solution.py:514
  88.5 31.3 %collective-permute-start.7 = (bf16[2,512,128]{2,1,0:T(8,128)(2,1)S(1)}, bf16[2,512,128]{2,1,0:T(8,128)(2,1)S(1)}, u32[]{:S(2)}, u32[]{:S(2)}) collective-permute-start(bf16[2,512,128]{2,1,0:T(8,128)(2,1)S(1)} %get-tuple-element.59), channel_id=1, source_target_pairs={{0,6},{2,0},{4,2},{6,4},{1,7},{3,1},{5,3},{7,5},{8,14},{10,8},{12,... | collective-permute-start | bytes 786440 | tf_op jit(solution)/shard_map/ppermute | solution.py:514
  90.0 29.8 %collective-permute-start.8 = (bf16[2,512,128]{2,1,0:T(8,128)(2,1)S(1)}, bf16[2,512,128]{2,1,0:T(8,128)(2,1)S(1)}, u32[]{:S(2)}, u32[]{:S(2)}) collective-permute-start(bf16[2,512,128]{2,1,0:T(8,128)(2,1)S(1)} %get-tuple-element.60), channel_id=1, source_target_pairs={{0,2},{2,4},{4,6},{6,0},{1,3},{3,5},{5,7},{7,1},{8,10},{10,12},{12... | collective-permute-start | bytes 786440 | tf_op jit(solution)/shard_map/ppermute | solution.py:514
  123.6 2.0 %collective-permute-start.10 = (bf16[2,128,1024]{2,1,0:T(8,128)(2,1)S(1)}, bf16[2,128,1024]{2,1,0:T(8,128)(2,1)S(1)}, u32[]{:S(2)}, u32[]{:S(2)}) collective-permute-start(bf16[2,128,1024]{2,1,0:T(8,128)(2,1)S(1)} %get-tuple-element.64), channel_id=1, source_target_pairs={{0,1},{1,0},{2,3},{3,2},{4,5},{5,4},{6,7},{7,6},{8,9},{9,8},{10,11... | collective-permute-start | bytes 1572872 | tf_op jit(solution)/shard_map/ppermute | solution.py:510

commit v12 on v11

--- a/solution.py
+++ b/solution.py
@@ -176,20 +176,19 @@
         scores[b * HW : (b + 1) * HW, :] = block
         peak = jnp.maximum(peak, jnp.max(block, axis=0, keepdims=True))
     peak = peak * SCALE2
-    total = jnp.zeros((1, TOKENS), F32)
     for b in range(32):
         rows = slice(b * 32, (b + 1) * 32)
         block = jnp.exp2(scores[rows, :] * SCALE2 - peak)
-        total = total + jnp.sum(block, axis=0, keepdims=True)
         kept[rows, :] = block.astype(BF16)
     turned = jnp.concatenate(turned, axis=1)
     for g in range(4):
         cols = slice(g * PAIR, (g + 1) * PAIR)
         got = mm(turned, kept[:, cols])
+        total = mm(jnp.ones((8, TOKENS), BF16), kept[:, cols])[0:1]
         result[:, cols] = got
         delta = jnp.sum(got * turn(both(blocks[g], G0)), axis=0, keepdims=True)
         told = jnp.concatenate(
-            [peak[:, cols], total[:, cols], delta, jnp.zeros((1, PAIR), F32)], axis=0
+            [peak[:, cols], total, delta, jnp.zeros((1, PAIR), F32)], axis=0
         )
         stats[2 * g] = told[:, :HW]
         stats[2 * g + 1] = told[:, HW:]
@@ -247,12 +246,11 @@
             scores[b * HW : (b + 1) * HW, :] = block
             peak = jnp.maximum(peak, jnp.max(block, axis=0, keepdims=True))
         peak = jnp.maximum(peak * SCALE2, FLOOR)
-        total = jnp.zeros((1, PAIR), F32)
         for b in range(WIN + 1):
             block = jnp.exp2(scores[b * HW : (b + 1) * HW, :] * SCALE2 - peak)
-            total = total + jnp.sum(block, axis=0, keepdims=True)
             kept[p, b * HW : (b + 1) * HW, :] = block.astype(BF16)
         got = mm(values_t[:, p * PAIR : p * PAIR + KEYS], kept[p])
+        total = mm(jnp.ones((8, KEYS), BF16), kept[p])[0:1]
         result[:, p * PAIR : (p + 1) * PAIR] = got
         delta = jnp.sum(got * grad_t, axis=0, keepdims=True)
         stats = jnp.concatenate([peak, total, delta, jnp.zeros((1, PAIR), F32)], axis=0)

time: 128 us -> 128 us (level)
  no operation moved by 1% of the time
where the time goes in v12:
time: 128 us; the launch traced here: 126 us
  blocking collectives  43 us (34%)
  waiting for transfers between devices  29.9 us (23%)
  starting transfers between devices  29 us (23%)
  Pallas kernels  22.9 us (18%)
  between operations  1.47 us (1%)
    all_to_all x2, blocking collectives, exchange(): lax.all_to_all(value, axes, 0, 0, axis_index_groups=groups, tiled=True)  43 us
    ppermute x6, starting transfers between devices, turn_ring(): return lax.ppermute(value, 'zh', [(i, (i + steps) % 4) for i in range(4)])  17.1 us
    ppermute x6, waiting for transfers between devices, turn_ring(): return lax.ppermute(value, 'zh', [(i, (i + steps) % 4) for i in range(4)])  14 us
    all_to_all x1, waiting for transfers between devices, exchange(): lax.all_to_all(value, axes, 0, 0, axis_index_groups=groups, tiled=True)  12.8 us
    all_to_all x1, starting transfers between devices, exchange(): lax.all_to_all(value, axes, 0, 0, axis_index_groups=groups, tiled=True)  5.7 us
    pallas_call x1, Pallas kernels, unproject(): pl.pallas_call(unproject_kernel, in_specs=[SM] + [VM] * 5 + [ANY] * 2, ou...  3.8 us
    pallas_call x1, Pallas kernels, far_backward(): pl.pallas_call(far_backward_kernel, in_specs=[SM] + [VM] * 6, out_specs=[...  3.37 us
    pallas_call x1, Pallas kernels, far_forward(): pl.pallas_call(far_forward_kernel, in_specs=[SM, SM, VM, VM, VM], out_spe...  3.28 us
  transfers between devices with their start and end apart: 12, of which 5 were waited for; matrix products, arithmetic and copies ran while one was open for 0% of the time, Pallas kernels for 7%

profile of v12, /device:TPU:16, one launch (start us, length us, event | category | flops | bytes accessed | tf_op | source)
XLA Modules:
  0.0 126.4 jit_solution(6166754373474841072)
XLA Ops:
  0.6 0.1 collective-permute-start
  0.7 0.5 collective-permute-start.1
  1.9 0.1 pad_add_fusion.place
  2.0 2.8 %stage.1 = (bf16[1024,512]{1,0:T(8,128)(2,1)S(1)}, bf16[1024,512]{1,0:T(8,128)(2,1)S(1)}, bf16[1024,512]{1,0:T(8,128)(2,1)S(1)}, bf16[512,1024]{1,0:T(8,128)(2,1)S(1)}) custom-call(s32[3]{0:T(128)S(1)} %pad_add_fusion.place, bf16[1024,3072]{1,0:T(8,128)(2,1)} %w_qkv.3, bf16[1024,1024]{1,0:T(8,128)(2,1)} %w_out.3), custom_call_target="tpu_custom_call" | custom-call | bytes 9000000 | tf_op jit(solution)/shard_map/stage/pallas_call | solution.py:100
  4.8 0.0 collective-permute-done.other
  4.9 3.2 %project.1 = (bf16[4,2,528,128]{3,2,1,0:T(8,128)(2,1)}, bf16[2,512,128]{2,1,0:T(8,128)(2,1)S(1)}, bf16[2,512,128]{2,1,0:T(8,128)(2,1)S(1)}, bf16[2,512,128]{2,1,0:T(8,128)(2,1)S(1)}, bf16[2,512,128]{2,1,0:T(8,128)(2,1)S(1)}) custom-call(s32[3]{0:T(128)S(1)} %pad_add_fusion.place, s32[1]{0:T(128)S(6)} %copy.13.valid, bf16[128,1024]{1,0:T(8,128)(2,1)S(1)} %bitcast.13, ...), custom_call_target="tpu_custom_call" | custom-call | flops 1073741824 | bytes 7000000 | tf_op jit(solution)/shard_map/project/pallas_call | solution.py:152
  8.1 5.7 %all-to-all-start.1 = ((bf16[8,528,128]{2,1,0:T(8,128)(2,1)}), bf16[8,528,128]{2,1,0:T(8,128)(2,1)S(1)}, u32[]{:S(2)}, u32[]{:S(2)}) async-start(bf16[8,528,128]{2,1,0:T(8,128)(2,1)} %bitcast.7), calls=%async_computation.1 | async-start | bytes 2162688 | tf_op jit(solution)/shard_map/all_to_all | solution.py:520
  13.8 6.2 %collective-permute-start.3 = (bf16[2,512,128]{2,1,0:T(8,128)(2,1)S(1)}, bf16[2,512,128]{2,1,0:T(8,128)(2,1)S(1)}, u32[]{:S(2)}, u32[]{:S(2)}) collective-permute-start(bf16[2,512,128]{2,1,0:T(8,128)(2,1)S(1)} %get-tuple-element.43), channel_id=1, source_target_pairs={{0,4},{2,6},{4,0},{6,2},{1,5},{3,7},{5,1},{7,3},{8,12},{10,14},{12... | collective-permute-start | bytes 786440 | tf_op jit(solution)/shard_map/ppermute | solution.py:512
  20.0 1.5 %collective-permute-start.4 = (bf16[2,512,128]{2,1,0:T(8,128)(2,1)S(1)}, bf16[2,512,128]{2,1,0:T(8,128)(2,1)S(1)}, u32[]{:S(2)}, u32[]{:S(2)}) collective-permute-start(bf16[2,512,128]{2,1,0:T(8,128)(2,1)S(1)} %get-tuple-element.44), channel_id=1, source_target_pairs={{0,2},{2,4},{4,6},{6,0},{1,3},{3,5},{5,7},{7,1},{8,10},{10,12},{12... | collective-permute-start | bytes 786440 | tf_op jit(solution)/shard_map/ppermute | solution.py:512
  21.6 2.6 %collective-permute-start.5 = (bf16[2,512,128]{2,1,0:T(8,128)(2,1)S(1)}, bf16[2,512,128]{2,1,0:T(8,128)(2,1)S(1)}, u32[]{:S(2)}, u32[]{:S(2)}) collective-permute-start(bf16[2,512,128]{2,1,0:T(8,128)(2,1)S(1)} %get-tuple-element.45), channel_id=1, source_target_pairs={{0,6},{2,0},{4,2},{6,4},{1,7},{3,1},{5,3},{7,5},{8,14},{10,8},{12,... | collective-permute-start | bytes 786440 | tf_op jit(solution)/shard_map/ppermute | solution.py:512
  24.1 12.8 %all-to-all-done.1.mine = bf16[8,528,128]{2,1,0:T(8,128)(2,1)S(1)} async-done(((bf16[8,528,128]{2,1,0:T(8,128)(2,1)}), bf16[8,528,128]{2,1,0:T(8,128)(2,1)S(1)}, u32[]{:S(2)}, u32[]{:S(2)}) %all-to-all-start.1) | async-done | bytes 1081376 | tf_op jit(solution)/shard_map/all_to_all | solution.py:520
  37.0 3.2 %collective-permute-start.2 = (bf16[8,272,128]{2,1,0:T(8,128)(2,1)S(1)}, bf16[8,272,128]{2,1,0:T(8,128)(2,1)S(1)}, u32[]{:S(2)}, u32[]{:S(2)}) collective-permute-start(bf16[8,272,128]{2,1,0:T(8,128)(2,1)S(1)} %slice.8), channel_id=1, source_target_pairs={{0,64},{64,128},{128,192},{1,65},{65,129},{129,193},{2,66},{66,130... | collective-permute-start | bytes 1671176 | tf_op jit(solution)/shard_map/ppermute | solution.py:544
  40.1 9.9 %collective-permute-done.3.near1 = bf16[2,512,128]{2,1,0:T(8,128)(2,1)S(1)} collective-permute-done((bf16[2,512,128]{2,1,0:T(8,128)(2,1)S(1)}, bf16[2,512,128]{2,1,0:T(8,128)(2,1)S(1)}, u32[]{:S(2)}, u32[]{:S(2)}) %collective-permute-start.3) | collective-permute-done | bytes 262176 | tf_op jit(solution)/shard_map/ppermute | solution.py:512
  50.1 4.1 %collective-permute-done.4.near2 = bf16[2,512,128]{2,1,0:T(8,128)(2,1)S(1)} collective-permute-done((bf16[2,512,128]{2,1,0:T(8,128)(2,1)S(1)}, bf16[2,512,128]{2,1,0:T(8,128)(2,1)S(1)}, u32[]{:S(2)}, u32[]{:S(2)}) %collective-permute-start.4) | collective-permute-done | bytes 262176 | tf_op jit(solution)/shard_map/ppermute | solution.py:512
  54.2 2.0 %near_forward.1 = (bf16[1024,1024]{1,0:T(8,128)(2,1)S(1)}, f32[128,1024]{1,0:T(8,128)S(1)}, f32[8,4,128]{2,1,0:T(4,128)S(1)}) custom-call(bf16[2,512,128]{2,1,0:T(8,128)(2,1)S(1)} %get-tuple-element.42.near0, bf16[2,512,128]{2,1,0:T(8,128)(2,1)S(1)} %collective-permute-done.3.near1, bf16[2,512,128]{2,1,0:T(8,128)(2,1)S(1)} %collective-permute-done.4.near2, ...), custom_call_target="tpu_custom_call" | custom-call | flops 10737418240 | bytes 4000000 | tf_op jit(solution)/shard_map/near_forward/pallas_call | solution.py:198
  56.2 0.0 collective-permute-done.2.past
  56.2 3.3 %far_forward.1 = (f32[8,8,128]{2,1,0:T(8,128)S(1)}, bf16[4,1152,256]{2,1,0:T(8,128)(2,1)S(1)}, f32[128,1024]{1,0:T(8,128)S(1)}) custom-call(s32[3]{0:T(128)S(1)} %pad_add_fusion.place, s32[8]{0:T(128)S(1)} %copy-done.3, bf16[8,528,128]{2,1,0:T(8,128)(2,1)S(1)} %all-to-all-done.1.mine, bf16[8,272,128]{2,1,0:T(8,128)(2,1)S(1)} %collective-permute-done.2.past, ...), custom_call_target="tpu_custom_call" | custom-call | flops 603979776 | bytes 5000000 | tf_op jit(solution)/shard_map/far_forward/pallas_call | solution.py:262
  59.5 16.3 %all_to_all.15.told = f32[8,8,128]{2,1,0:T(8,128)S(1)} all-to-all(f32[8,8,128]{2,1,0:T(8,128)S(1)} %get-tuple-element.49.sent), channel_id=1, replica_groups={{0,8,22,30,36,44,50,58},{2,10,16,24,38,46,52,60},{4,12,18,26,32,40,54,6..., dimensions={0} | all-to-all | bytes 65536 | tf_op jit(solution)/shard_map/all_to_all | solution.py:520
  75.8 3.4 %far_backward.1 = (bf16[8,512,128]{2,1,0:T(8,128)(2,1)S(1)}, bf16[8,256,128]{2,1,0:T(8,128)(2,1)S(1)}) custom-call(s32[3]{0:T(128)S(1)} %pad_add_fusion.place, bf16[8,528,128]{2,1,0:T(8,128)(2,1)S(1)} %all-to-all-done.1.mine, bf16[8,272,128]{2,1,0:T(8,128)(2,1)S(1)} %collective-permute-done.2.past, bf16[4,1152,256]{2,1,0:T(8,128)(2,1)S(1)} %get-tuple-element.47.kept, ...), custom_call_target="tpu_custom_call" | custom-call | flops 1207959552 | bytes 6000000 | tf_op jit(solution)/shard_map/far_backward/pallas_call | solution.py:392
  79.2 2.3 %collective-permute-start.9 = (bf16[8,256,128]{2,1,0:T(8,128)(2,1)S(1)}, bf16[8,256,128]{2,1,0:T(8,128)(2,1)S(1)}, u32[]{:S(2)}, u32[]{:S(2)}) collective-permute-start(bf16[8,256,128]{2,1,0:T(8,128)(2,1)S(1)} %get-tuple-element.62), channel_id=1, source_target_pairs={{64,0},{128,64},{192,128},{65,1},{129,65},{193,129},{66,2},{130,66... | collective-permute-start | bytes 1572872 | tf_op jit(solution)/shard_map/ppermute | solution.py:549
  81.6 2.9 %near_backward.1 = (bf16[2,512,128]{2,1,0:T(8,128)(2,1)S(1)}, bf16[2,512,128]{2,1,0:T(8,128)(2,1)S(1)}, bf16[2,512,128]{2,1,0:T(8,128)(2,1)S(1)}, bf16[2,512,128]{2,1,0:T(8,128)(2,1)S(1)}) custom-call(s32[3]{0:T(128)S(1)} %pad_add_fusion.place, bf16[2,512,128]{2,1,0:T(8,128)(2,1)S(1)} %get-tuple-element.42.near0, ...), custom_call_target="tpu_custom_call" | custom-call | flops 1073741824 | bytes 5000000 | tf_op jit(solution)/shard_map/near_backward/pallas_call | solution.py:330
  84.5 3.8 %collective-permute-start.6 = (bf16[2,512,128]{2,1,0:T(8,128)(2,1)S(1)}, bf16[2,512,128]{2,1,0:T(8,128)(2,1)S(1)}, u32[]{:S(2)}, u32[]{:S(2)}) collective-permute-start(bf16[2,512,128]{2,1,0:T(8,128)(2,1)S(1)} %get-tuple-element.58), channel_id=1, source_target_pairs={{0,4},{2,6},{4,0},{6,2},{1,5},{3,7},{5,1},{7,3},{8,12},{10,14},{12... | collective-permute-start | bytes 786440 | tf_op jit(solution)/shard_map/ppermute | solution.py:512
  88.3 1.5 %collective-permute-start.7 = (bf16[2,512,128]{2,1,0:T(8,128)(2,1)S(1)}, bf16[2,512,128]{2,1,0:T(8,128)(2,1)S(1)}, u32[]{:S(2)}, u32[]{:S(2)}) collective-permute-start(bf16[2,512,128]{2,1,0:T(8,128)(2,1)S(1)} %get-tuple-element.59), channel_id=1, source_target_pairs={{0,6},{2,0},{4,2},{6,4},{1,7},{3,1},{5,3},{7,5},{8,14},{10,8},{12,... | collective-permute-start | bytes 786440 | tf_op jit(solution)/shard_map/ppermute | solution.py:512
  89.7 1.5 %collective-permute-start.8 = (bf16[2,512,128]{2,1,0:T(8,128)(2,1)S(1)}, bf16[2,512,128]{2,1,0:T(8,128)(2,1)S(1)}, u32[]{:S(2)}, u32[]{:S(2)}) collective-permute-start(bf16[2,512,128]{2,1,0:T(8,128)(2,1)S(1)} %get-tuple-element.60), channel_id=1, source_target_pairs={{0,2},{2,4},{4,6},{6,0},{1,3},{3,5},{5,7},{7,1},{8,10},{10,12},{12... | collective-permute-start | bytes 786440 | tf_op jit(solution)/shard_map/ppermute | solution.py:512
  91.2 1.2 collective-permute-done.9.back
  92.5 0.4 add_back.1
  92.9 26.7 %conditional.1 = (bf16[4,2,512,128]{3,2,1,0:T(8,128)(2,1)S(1)}) conditional(s32[]{:T(128)} %bitcast.8, () %tuple.18, bf16[8,512,128]{2,1,0:T(8,128)(2,1)S(1)} %add_back.1), branch_computations={%region_0.0_spmd, %region_1.0_spmd} | conditional | bytes 2097160 | solution.py:524
  92.9 26.7 %all_to_all.14 = bf16[8,512,128]{2,1,0:T(8,128)(2,1)S(1)} all-to-all(bf16[8,512,128]{2,1,0:T(8,128)(2,1)S(1)} %param.1), channel_id=1, replica_groups=mesh['y'=4,'x'=4,'zl'=2,'zh'=4,'core'=2] {'x','zl'}, dimensions={0} | all-to-all | bytes 2097152 | tf_op jit(solution)/shard_map/cond/branch_1_fun/all_to_all | solution.py:520
  119.6 3.8 %unproject.1 = (f32[2,128,1024]{2,1,0:T(8,128)S(1)}, bf16[2,128,1024]{2,1,0:T(8,128)(2,1)S(1)}) custom-call(s32[3]{0:T(128)S(1)} %pad_add_fusion.place, bf16[2,512,128]{2,1,0:T(8,128)(2,1)S(1)} %get-tuple-element.57.near0, bf16[2,512,128]{2,1,0:T(8,128)(2,1)S(1)} %collective-permute-done.6.near1, bf16[2,512,128]{2,1,0:T(8,128)(2,1)S(1)} %collective-permute-done.7.near2, ...), custom_call_target="tpu_custom_call" | custom-call | flops 1073741824 | bytes 8000000 | tf_op jit(solution)/shard_map/unproject/pallas_call | solution.py:465
  123.4 0.1 collective-permute-start.10
  123.5 1.9 %collective-permute-done.10.other = bf16[2,128,1024]{2,1,0:T(8,128)(2,1)S(1)} collective-permute-done((bf16[2,128,1024]{2,1,0:T(8,128)(2,1)S(1)}, bf16[2,128,1024]{2,1,0:T(8,128)(2,1)S(1)}, u32[]{:S(2)}, u32[]{:S(2)}) %collective-permute-start.10) | collective-permute-done | bytes 524320 | tf_op jit(solution)/shard_map/ppermute | solution.py:508
  125.4 1.0 finish.1
  (14 shorter events, 0.1 us)
Async XLA Ops:
  0.6 4.2 %collective-permute-start = (bf16[128,1024]{1,0:T(8,128)(2,1)}, bf16[128,1024]{1,0:T(8,128)(2,1)S(1)}, u32[]{:S(2)}, u32[]{:S(2)}) collective-permute-start(bf16[128,1024]{1,0:T(8,128)(2,1)} %bitcast.12), channel_id=1, source_target_pairs={{0,1},{1,0},{2,3},{3,2},{4,5},{5,4},{6,7},{7,6},{8,9},{9,8},{10,11... | collective-permute-start | bytes 786440 | tf_op jit(solution)/shard_map/ppermute | solution.py:508
  0.7 4.1 %collective-permute-start.1 = (bf16[128,1024]{1,0:T(8,128)(2,1)}, bf16[128,1024]{1,0:T(8,128)(2,1)S(1)}, u32[]{:S(2)}, u32[]{:S(2)}) collective-permute-start(bf16[128,1024]{1,0:T(8,128)(2,1)} %bitcast.15), channel_id=1, source_target_pairs={{0,1},{1,0},{2,3},{3,2},{4,5},{5,4},{6,7},{7,6},{8,9},{9,8},{10,11... | collective-permute-start | bytes 786440 | tf_op jit(solution)/shard_map/ppermute | solution.py:508
  2.0 2.9 %copy-start = (bf16[1,1,128,1024]{3,2,1,0:T(8,128)(2,1)S(1)}, bf16[1,1,128,1024]{3,2,1,0:T(8,128)(2,1)}, u32[]{:S(2)}) copy-start(bf16[1,1,128,1024]{3,2,1,0:T(8,128)(2,1)} %param.9) | copy-start | bytes 786436
  2.0 2.9 %copy-start.1 = (bf16[1,1,128,1024]{3,2,1,0:T(8,128)(2,1)S(1)}, bf16[1,1,128,1024]{3,2,1,0:T(8,128)(2,1)}, u32[]{:S(2)}) copy-start(bf16[1,1,128,1024]{3,2,1,0:T(8,128)(2,1)} %param.15) | copy-start | bytes 786436
  2.0 2.9 %copy-start.2 = (f32[1024]{0:T(1024)S(1)}, f32[1024]{0:T(1024)}, u32[]{:S(2)}) copy-start(f32[1024]{0:T(1024)} %param.10) | copy-start | bytes 12292
  8.1 28.8 %all-to-all-start.1 = ((bf16[8,528,128]{2,1,0:T(8,128)(2,1)}), bf16[8,528,128]{2,1,0:T(8,128)(2,1)S(1)}, u32[]{:S(2)}, u32[]{:S(2)}) async-start(bf16[8,528,128]{2,1,0:T(8,128)(2,1)} %bitcast.7), calls=%async_computation.1 | async-start | bytes 2162688 | tf_op jit(solution)/shard_map/all_to_all | solution.py:520
  13.8 36.3 %collective-permute-start.3 = (bf16[2,512,128]{2,1,0:T(8,128)(2,1)S(1)}, bf16[2,512,128]{2,1,0:T(8,128)(2,1)S(1)}, u32[]{:S(2)}, u32[]{:S(2)}) collective-permute-start(bf16[2,512,128]{2,1,0:T(8,128)(2,1)S(1)} %get-tuple-element.43), channel_id=1, source_target_pairs={{0,4},{2,6},{4,0},{6,2},{1,5},{3,7},{5,1},{7,3},{8,12},{10,14},{12... | collective-permute-start | bytes 786440 | tf_op jit(solution)/shard_map/ppermute | solution.py:512
  20.0 34.1 %collective-permute-start.4 = (bf16[2,512,128]{2,1,0:T(8,128)(2,1)S(1)}, bf16[2,512,128]{2,1,0:T(8,128)(2,1)S(1)}, u32[]{:S(2)}, u32[]{:S(2)}) collective-permute-start(bf16[2,512,128]{2,1,0:T(8,128)(2,1)S(1)} %get-tuple-element.44), channel_id=1, source_target_pairs={{0,2},{2,4},{4,6},{6,0},{1,3},{3,5},{5,7},{7,1},{8,10},{10,12},{12... | collective-permute-start | bytes 786440 | tf_op jit(solution)/shard_map/ppermute | solution.py:512
  21.6 32.6 %collective-permute-start.5 = (bf16[2,512,128]{2,1,0:T(8,128)(2,1)S(1)}, bf16[2,512,128]{2,1,0:T(8,128)(2,1)S(1)}, u32[]{:S(2)}, u32[]{:S(2)}) collective-permute-start(bf16[2,512,128]{2,1,0:T(8,128)(2,1)S(1)} %get-tuple-element.45), channel_id=1, source_target_pairs={{0,6},{2,0},{4,2},{6,4},{1,7},{3,1},{5,3},{7,5},{8,14},{10,8},{12,... | collective-permute-start | bytes 786440 | tf_op jit(solution)/shard_map/ppermute | solution.py:512
  37.0 19.2 %collective-permute-start.2 = (bf16[8,272,128]{2,1,0:T(8,128)(2,1)S(1)}, bf16[8,272,128]{2,1,0:T(8,128)(2,1)S(1)}, u32[]{:S(2)}, u32[]{:S(2)}) collective-permute-start(bf16[8,272,128]{2,1,0:T(8,128)(2,1)S(1)} %slice.8), channel_id=1, source_target_pairs={{0,64},{64,128},{128,192},{1,65},{65,129},{129,193},{2,66},{66,130... | collective-permute-start | bytes 1671176 | tf_op jit(solution)/shard_map/ppermute | solution.py:544
  54.2 2.0 %copy-start.3 = (s32[8]{0:T(128)S(1)}, s32[8]{0:T(128)}, u32[]{:S(2)}) copy-start(s32[8]{0:T(128)} %win.1) | copy-start | bytes 100
  79.2 13.2 %collective-permute-start.9 = (bf16[8,256,128]{2,1,0:T(8,128)(2,1)S(1)}, bf16[8,256,128]{2,1,0:T(8,128)(2,1)S(1)}, u32[]{:S(2)}, u32[]{:S(2)}) collective-permute-start(bf16[8,256,128]{2,1,0:T(8,128)(2,1)S(1)} %get-tuple-element.62), channel_id=1, source_target_pairs={{64,0},{128,64},{192,128},{65,1},{129,65},{193,129},{66,2},{130,66... | collective-permute-start | bytes 1572872 | tf_op jit(solution)/shard_map/ppermute | solution.py:549
  84.5 35.1 %collective-permute-start.6 = (bf16[2,512,128]{2,1,0:T(8,128)(2,1)S(1)}, bf16[2,512,128]{2,1,0:T(8,128)(2,1)S(1)}, u32[]{:S(2)}, u32[]{:S(2)}) collective-permute-start(bf16[2,512,128]{2,1,0:T(8,128)(2,1)S(1)} %get-tuple-element.58), channel_id=1, source_target_pairs={{0,4},{2,6},{4,0},{6,2},{1,5},{3,7},{5,1},{7,3},{8,12},{10,14},{12... | collective-permute-start | bytes 786440 | tf_op jit(solution)/shard_map/ppermute | solution.py:512
  88.3 31.3 %collective-permute-start.7 = (bf16[2,512,128]{2,1,0:T(8,128)(2,1)S(1)}, bf16[2,512,128]{2,1,0:T(8,128)(2,1)S(1)}, u32[]{:S(2)}, u32[]{:S(2)}) collective-permute-start(bf16[2,512,128]{2,1,0:T(8,128)(2,1)S(1)} %get-tuple-element.59), channel_id=1, source_target_pairs={{0,6},{2,0},{4,2},{6,4},{1,7},{3,1},{5,3},{7,5},{8,14},{10,8},{12,... | collective-permute-start | bytes 786440 | tf_op jit(solution)/shard_map/ppermute | solution.py:512
  89.7 29.8 %collective-permute-start.8 = (bf16[2,512,128]{2,1,0:T(8,128)(2,1)S(1)}, bf16[2,512,128]{2,1,0:T(8,128)(2,1)S(1)}, u32[]{:S(2)}, u32[]{:S(2)}) collective-permute-start(bf16[2,512,128]{2,1,0:T(8,128)(2,1)S(1)} %get-tuple-element.60), channel_id=1, source_target_pairs={{0,2},{2,4},{4,6},{6,0},{1,3},{3,5},{5,7},{7,1},{8,10},{10,12},{12... | collective-permute-start | bytes 786440 | tf_op jit(solution)/shard_map/ppermute | solution.py:512
  123.4 2.0 %collective-permute-start.10 = (bf16[2,128,1024]{2,1,0:T(8,128)(2,1)S(1)}, bf16[2,128,1024]{2,1,0:T(8,128)(2,1)S(1)}, u32[]{:S(2)}, u32[]{:S(2)}) collective-permute-start(bf16[2,128,1024]{2,1,0:T(8,128)(2,1)S(1)} %get-tuple-element.64), channel_id=1, source_target_pairs={{0,1},{1,0},{2,3},{3,2},{4,5},{5,4},{6,7},{7,6},{8,9},{9,8},{10,11... | collective-permute-start | bytes 1572872 | tf_op jit(solution)/shard_map/ppermute | solution.py:508
